TPU v7x, 32 devices: a whole 2x2x4 slice. The times are simulated.
32 devices in a mesh: group: 2 (over y), gx: 4 (over z), gy: 2 (over x), gz: 2 (over core).
Axes of the slice: x: 2, y: 2, z: 4, core: 2. Of those that a mesh axis runs over, the one named last changes fastest.
Arguments:
- node_latent: bfloat16 [16, 4, 2, 128, 128], P(('group', 'gx'), 'gy', 'gz'), parts along dimension 0, may hold values from -6 to 6
- edge_latent: bfloat16 [16, 4, 2, 12, 128, 128], P(('group', 'gx'), 'gy', 'gz'), parts along dimension 0, may hold values from -6 to 6
- positions: float32 [3, 16, 4, 2, 128], P(None, ('group', 'gx'), 'gy', 'gz'), parts along dimension 1, may hold values from 0 to 8, as said below
- velocity: float32 [3, 16, 4, 2, 128], P(None, ('group', 'gx'), 'gy', 'gz'), parts along dimension 1, may hold values from -2 to 2
- fill: int32 [16, 4, 2], P(('group', 'gx'), 'gy', 'gz'), parts along dimension 0, may hold values from 64 to 128, as said below
- neighbours: int32 [16, 4, 2, 12, 128], P(('group', 'gx'), 'gy', 'gz'), parts along dimension 0, may hold values from 0 to 6143, as said below
- owners: int32 [16, 4, 2, 128], P(('group', 'gx'), 'gy', 'gz'), parts along dimension 0, may hold values from 0 to 15, as said below
- edge_weights: bfloat16 [5, 128, 128], replicated, may hold values from -0.5 to 0.5
- node_in: bfloat16 [256, 128], replicated, may hold values from -0.375 to 0.375
- node_weights: bfloat16 [2, 128, 128], replicated, may hold values from -0.5 to 0.5
- decoder_weights: bfloat16 [2, 128, 128], replicated, may hold values from -0.5 to 0.5
- decoder_out: bfloat16 [3, 128], replicated, may hold values from -0.5 to 0.5
- encoder_in: bfloat16 [12, 128], replicated, may hold values from -1.75 to 1.75
- encoder_weights: bfloat16 [2, 128, 128], replicated, may hold values from -0.5 to 0.5
Outputs:
- kept_latent: bfloat16 [16, 4, 2, 128, 128], P(('group', 'gx'), 'gy', 'gz'), parts along dimension 0
- kept_state: float32 [9, 16, 4, 2, 128], P(None, ('group', 'gx'), 'gy', 'gz'), parts along dimension 1
- arrived_latent: bfloat16 [8, 2, 2, 208, 128], P(('group', 'gx'), 'gy', 'gz'), parts along dimension 0
- arrived_state: float32 [9, 8, 2, 2, 208], P(None, ('group', 'gx'), 'gy', 'gz'), parts along dimension 1
There are 2 independent parts, one for each index of `group`. A program takes and returns all parts, laid end to end along the dimension named above; an argument that names none is the same for every part. Nothing has to cross between parts.
Inputs may be any that keep to these rules, and one draw needn't show every extreme that they name: live particles fill the first fill slots of their cell; in every draw some cell is full. `neighbours`: every entry of a live particle names a live slot of its own cell or of a cell beside it (faces, edges or corners) inside the domain. `owners`: the owner of a live particle is its own device or one whose block of cells touches it; from one device at most 8 live particles go to any one other device, and in every draw each device sends exactly 8 to some other; slots without a particle name their own device. `positions`: each position lies within its own cell, cell (X, Y, Z) covering [X, X + 1) x [Y, Y + 1) x [Z, Z + 1).
All inputs are finite; a program needn't handle non-finite values.
Results may differ from a plain program's by a relative error of at most 0.0077.
Values may be sent and summed in bfloat16 or wider, within the bound.
No kernel may reach another device: no remote copies, remote signals or barrier semaphores. Data moves between devices by JAX's collectives and lax.ppermute only.
A program may use at most 64 MiB of HBM per device.

v0:
```python
import jax
import jax.numpy as jnp
from jax import lax
from jax.sharding import PartitionSpec as P

CAP = 8


def padded(cells, sides, width):
    for axis, dim in sides:
        count = lax.axis_size(axis)
        ends = count - 1
        head = lax.slice_in_dim(cells, 0, width, axis=dim)
        tail = lax.slice_in_dim(cells, cells.shape[dim] - width, cells.shape[dim], axis=dim)
        cells = jnp.concatenate(
            [
                lax.ppermute(tail, axis, [(i, (i + 1) % count) for i in range(ends)]),
                cells,
                lax.ppermute(head, axis, [((i + 1) % count, i) for i in range(ends)]),
            ],
            axis=dim,
        )
    return cells


def layer_norm(values):
    centred = values - jnp.mean(values, axis=-1, keepdims=True)
    spread = jnp.mean(centred * centred, axis=-1, keepdims=True)
    return centred * lax.rsqrt(spread + 1e-05)


def mlp_tail(pre_act, middle_w, final_w):
    hidden = jax.nn.relu(pre_act).astype(jnp.bfloat16)
    hidden = jax.nn.relu(jnp.dot(hidden, middle_w, preferred_element_type=jnp.float32)).astype(
        jnp.bfloat16
    )
    return layer_norm(jnp.dot(hidden, final_w, preferred_element_type=jnp.float32))


def decode_step(updated, decoder_weights, decoder_out):
    hidden = jax.nn.relu(
        jnp.dot(updated, decoder_weights[0], preferred_element_type=jnp.float32)
    ).astype(jnp.bfloat16)
    hidden = jax.nn.relu(
        jnp.dot(hidden, decoder_weights[1], preferred_element_type=jnp.float32)
    ).astype(jnp.bfloat16)
    return jnp.dot(hidden, decoder_out.T, preferred_element_type=jnp.float32).T


def encode(new_state, alive_mask, encoder_in, encoder_weights, extent):
    position = new_state[0:3]
    features = jnp.concatenate(
        [new_state[3:9], jnp.clip(position, -1.0, 1.0), jnp.clip(extent - position, -1.0, 1.0)],
        axis=0,
    )
    pre_act = jnp.dot(features.T, encoder_in.astype(jnp.float32), precision=lax.Precision.HIGHEST)
    latent = mlp_tail(pre_act, encoder_weights[0], encoder_weights[1]) * alive_mask[:, None]
    return latent.astype(jnp.bfloat16)


def ranks_within(groups, moving, group_count, tile_rows):
    member = (groups[:, None] == jnp.arange(group_count, dtype=jnp.int32)[None, :]) & moving[
        :, None
    ]
    tiles = member.astype(jnp.bfloat16).reshape(-1, tile_rows, group_count)
    tile_count = tiles.shape[0]
    inner_tri = (
        jnp.arange(tile_rows, dtype=jnp.int32)[:, None]
        >= jnp.arange(tile_rows, dtype=jnp.int32)[None, :]
    ).astype(jnp.bfloat16)
    inside = jnp.einsum("ij,bjg->big", inner_tri, tiles, preferred_element_type=jnp.float32)
    totals = jnp.sum(tiles.astype(jnp.float32), axis=1)
    outer_tri = (
        jnp.arange(tile_count, dtype=jnp.int32)[:, None]
        > jnp.arange(tile_count, dtype=jnp.int32)[None, :]
    ).astype(jnp.float32)
    before = jnp.dot(outer_tri, totals, precision=lax.Precision.HIGHEST)
    counted = (inside + before[:, None, :]).reshape(-1, group_count)
    return (jnp.sum(counted * member.astype(jnp.float32), axis=1) - 1.0).astype(jnp.int32)


def body(
    node_latent,
    edge_latent,
    positions,
    velocity,
    fill,
    neighbours,
    owners,
    edge_weights,
    node_in,
    node_weights,
    decoder_weights,
    decoder_out,
    encoder_in,
    encoder_weights,
):
    width = node_latent.shape[-1]
    cells_x, cells_y, cells_z, slot_count = node_latent.shape[:4]
    neighbour_count = edge_latent.shape[3]
    count_x = lax.axis_size("gx")
    count_y = lax.axis_size("gy")
    count_z = lax.axis_size("gz")
    index_x = lax.axis_index("gx")
    index_y = lax.axis_index("gy")
    index_z = lax.axis_index("gz")
    occupied = jnp.arange(slot_count, dtype=jnp.int32)[None, None, None, :] < fill[..., None]
    flat_latent = node_latent.reshape(-1, width)
    near_term = jnp.dot(flat_latent, edge_weights[1], preferred_element_type=jnp.float32).reshape(
        node_latent.shape
    )
    extended = padded(node_latent, (("gx", 0), ("gy", 1), ("gz", 2)), 1)
    far_term = (
        jnp.dot(extended.reshape(-1, width), edge_weights[2], preferred_element_type=jnp.float32)
        .astype(jnp.bfloat16)
        .reshape(extended.shape)
    )
    outer_cell = neighbours // slot_count
    target_slot = neighbours % slot_count
    outer_z = outer_cell % (cells_z + 2)
    outer_y = outer_cell // (cells_z + 2) % (cells_y + 2)
    outer_x = outer_cell // ((cells_y + 2) * (cells_z + 2))
    window_rows = 27 * slot_count
    window_ids = jnp.arange(window_rows, dtype=jnp.int32)[None, :]
    gathered_cells = []
    for cell_a in range(cells_x):
        for cell_b in range(cells_y):
            local = (
                ((outer_x[cell_a, cell_b, 0] - cell_a) * 3 + outer_y[cell_a, cell_b, 0] - cell_b)
                * 3
                + outer_z[cell_a, cell_b, 0]
                - 0
            ) * slot_count + target_slot[cell_a, cell_b, 0]
            window = far_term[cell_a : cell_a + 3, cell_b : cell_b + 3, 0:3].reshape(
                window_rows, width
            )
            picker = (local.reshape(-1, 1) == window_ids).astype(jnp.bfloat16)
            picked = jnp.dot(picker, window, preferred_element_type=jnp.float32)
            gathered_cells.append(picked.reshape(neighbour_count, slot_count, width))
    gathered = jnp.stack(gathered_cells, axis=0).reshape(edge_latent.shape)
    pre_act = jnp.dot(
        edge_latent.reshape(-1, width), edge_weights[0], preferred_element_type=jnp.float32
    ).reshape(edge_latent.shape)
    pre_act = pre_act + near_term[:, :, :, None] + gathered
    message = mlp_tail(pre_act.reshape(-1, width), edge_weights[3], edge_weights[4]).reshape(
        edge_latent.shape
    )
    message = message * occupied[:, :, :, None, :, None].astype(jnp.float32)
    aggregate = jnp.sum(message, axis=3).astype(jnp.bfloat16).reshape(-1, width)
    pre_node = jnp.dot(flat_latent, node_in[:width], preferred_element_type=jnp.float32) + jnp.dot(
        aggregate, node_in[width:], preferred_element_type=jnp.float32
    )
    updated = (
        flat_latent.astype(jnp.float32) + mlp_tail(pre_node, node_weights[0], node_weights[1])
    ).astype(jnp.bfloat16)
    acceleration = decode_step(updated, decoder_weights, decoder_out)
    flat_velocity = velocity.reshape(3, -1)
    new_velocity = flat_velocity + acceleration
    new_position = positions.reshape(3, -1) + new_velocity
    new_state = jnp.concatenate([new_position, new_velocity, flat_velocity], axis=0)
    extent = jnp.array(
        [cells_x * count_x, cells_y * count_y, cells_z * count_z], dtype=jnp.float32
    )[:, None]
    own_block = (index_x * count_y + index_y) * count_z + index_z
    flat_owner = owners.reshape(-1)
    flat_alive = occupied.reshape(-1)
    staying = flat_alive & (flat_owner == own_block)
    moving = flat_alive & (flat_owner != own_block)
    stay_mask = staying.astype(jnp.float32)
    move_mask = moving.astype(jnp.float32)
    kept_latent = encode(new_state, stay_mask, encoder_in, encoder_weights, extent).reshape(
        node_latent.shape
    )
    kept_state = (new_state * stay_mask[None, :]).reshape((9,) + node_latent.shape[:4])
    payload = jnp.concatenate([new_state, move_mask[None, :]], axis=0)
    owner_x = flat_owner // (count_y * count_z)
    owner_y = flat_owner // count_z % count_y
    owner_z = flat_owner % count_z
    direction = (owner_x - index_x + 1) * 9 + (owner_y - index_y + 1) * 3 + (owner_z - index_z + 1)
    order_rank = ranks_within(direction, moving, 27, slot_count)
    column = jnp.where(moving, direction * CAP + order_rank, 27 * CAP)
    placer = (column[:, None] == jnp.arange(27 * CAP, dtype=jnp.int32)[None, :]).astype(jnp.float32)
    buckets = jnp.dot(payload, placer, precision=lax.Precision.HIGHEST).reshape(10, 3, 3, 3, CAP)
    beside_all = padded(buckets, (("gx", 1), ("gy", 2), ("gz", 3)), 1)
    arrived = beside_all[:, ::2, ::2, ::2, :].reshape(10, 27, CAP)
    arrived = jnp.concatenate([arrived[:, :13], arrived[:, 14:]], axis=1).reshape(10, 26 * CAP)
    arrived_state = arrived[:9]
    arrived_latent = encode(arrived_state, arrived[9], encoder_in, encoder_weights, extent)
    return (
        kept_latent,
        kept_state,
        arrived_latent.reshape(1, 1, 1, 26 * CAP, width),
        arrived_state.reshape(9, 1, 1, 1, 26 * CAP),
    )


def solution(mesh):
    placed = (
        P(("group", "gx"), "gy", "gz", None, None),
        P(("group", "gx"), "gy", "gz", None, None, None),
        P(None, ("group", "gx"), "gy", "gz", None),
        P(None, ("group", "gx"), "gy", "gz", None),
        P(("group", "gx"), "gy", "gz"),
        P(("group", "gx"), "gy", "gz", None, None),
        P(("group", "gx"), "gy", "gz", None),
        P(),
        P(),
        P(),
        P(),
        P(),
        P(),
        P(),
    )
    return jax.shard_map(
        body,
        mesh=mesh,
        in_specs=placed,
        out_specs=(
            P(("group", "gx"), "gy", "gz", None, None),
            P(None, ("group", "gx"), "gy", "gz", None),
            P(("group", "gx"), "gy", "gz", None, None),
            P(None, ("group", "gx"), "gy", "gz", None),
        ),
        check_vma=False,
    )
```

profile of v0, /device:TPU:0, one launch (start us, length us, event | category | flops | bytes accessed | tf_op | source)
XLA Modules:
  0.0 105.9 jit_solution(12379769722123948133)
XLA Ops:
  1.7 4.9 %collective-permute-start = (bf16[1,2,1,128,128]{4,3,2,1,0:T(8,128)(2,1)S(1)}, bf16[1,2,1,128,128]{4,3,2,1,0:T(8,128)(2,1)S(1)}, u32[]{:S(2)}, u32[]{:S(2)}) collective-permute-start(bf16[1,2,1,128,128]{4,3,2,1,0:T(8,128)(2,1)S(1)} %get-tuple-element.34), channel_id=1, source_target_pairs={{0,4},{4,8},{8,12},{1,5},{5,9},{9,13},{2,6},{6,10},{10,14},{3,7},{... | collective-permute-start | bytes 196616 | tf_op jit(solution)/shard_map/ppermute | solution.py:17
  6.6 1.3 %collective-permute-start.1 = (bf16[1,2,1,128,128]{4,3,2,1,0:T(8,128)(2,1)S(1)}, bf16[1,2,1,128,128]{4,3,2,1,0:T(8,128)(2,1)S(1)}, u32[]{:S(2)}, u32[]{:S(2)}) collective-permute-start(bf16[1,2,1,128,128]{4,3,2,1,0:T(8,128)(2,1)S(1)} %get-tuple-element.33), channel_id=1, source_target_pairs={{4,0},{8,4},{12,8},{5,1},{9,5},{13,9},{6,2},{10,6},{14,10},{7,3},{... | collective-permute-start | bytes 196616 | tf_op jit(solution)/shard_map/ppermute | solution.py:19
  9.4 1.3 %reduce.15 = s32[2,2]{1,0:T(2,128)S(1)} reduce(s32[2,2,1]{1,2,0:T(1,128)} %param.19, s32[]{:T(128)} %broadcast.687), dimensions={2}, to_apply=%param.19.reduce_sub_computation.3 | reduce | bytes 36 | tf_op args[4]
  11.6 1.3 %and_convert_fusion = (f32[2,2,1,128]{3,2,1,0:T(1,128)}, pred[2,2,1,128]{3,2,1,0:T(4,128)(4,1)S(1)}, pred[2,2,128]{2,1,0:T(4,128)(4,1)S(1)}) fusion(s32[2,2,1,128]{3,2,1,0:T(1,128)} %param.21, s32[]{:T(128)S(6)} %add.357, s32[2,2]{1,0:T(2,128)} %bitcast.198), kind=kLoop, calls=%fused_computation.171 | loop fusion | flops 2560 | bytes 5140 | tf_op jit(solution)/shard_map/convert_element_type | solution.py:170
  16.8 3.4 %collective-permute-start.2 = (bf16[4,1,1,128,128]{4,3,2,1,0:T(8,128)(2,1)S(1)}, bf16[4,1,1,128,128]{4,3,2,1,0:T(8,128)(2,1)S(1)}, u32[]{:S(2)}, u32[]{:S(2)}) collective-permute-start(bf16[4,1,1,128,128]{4,3,2,1,0:T(8,128)(2,1)S(1)} %get-tuple-element.29), channel_id=1, source_target_pairs={{0,2},{1,3},{4,6},{5,7},{8,10},{9,11},{12,14},{13,15},{16,18},{17,... | collective-permute-start | bytes 393224 | tf_op jit(solution)/shard_map/ppermute | solution.py:17
  21.5 1.3 %fusion.138 = (f32[2,2,128]{2,1,0:T(2,128)}, f32[2,2,128]{2,1,0:T(2,128)}) fusion(pred[2,2,1,128]{3,2,1,0:T(4,128)(4,1)S(1)} %get-tuple-element.46, s32[2,2]{1,0:T(2,128)} %bitcast.199), kind=kLoop, calls=%fused_computation.203 | loop fusion | flops 2048 | bytes 4624 | tf_op jit(solution)/shard_map/convert_element_type | solution.py:169
  22.8 4.3 %collective-permute-done.3 = bf16[4,1,1,128,128]{4,3,2,1,0:T(8,128)(2,1)} collective-permute-done((bf16[4,1,1,128,128]{4,3,2,1,0:T(8,128)(2,1)S(1)}, bf16[4,1,1,128,128]{4,3,2,1,0:T(8,128)(2,1)}, u32[]{:S(2)}, u32[]{:S(2)}) %collective-permute-start.3) | collective-permute-done | bytes 131104 | tf_op jit(solution)/shard_map/ppermute | solution.py:19
  28.1 1.3 %collective-permute-start.4 = (bf16[4,4,1,128,128]{4,3,2,1,0:T(8,128)(2,1)S(1)}, bf16[4,4,1,128,128]{4,3,2,1,0:T(8,128)(2,1)S(1)}, u32[]{:S(2)}, u32[]{:S(2)}) collective-permute-start(bf16[4,4,1,128,128]{4,3,2,1,0:T(8,128)(2,1)S(1)} %pad_maximum_fusion.3), channel_id=1, source_target_pairs={{0,1},{2,3},{4,5},{6,7},{8,9},{10,11},{12,13},{14,15},{16,17},{18,... | collective-permute-start | bytes 1572872 | tf_op jit(solution)/shard_map/ppermute | solution.py:17
  40.5 1.3 %convolution_convert_fusion = bf16[6144,128]{1,0:T(8,128)(2,1)S(1)} fusion(bf16[6144,128]{1,0:T(8,128)(2,1)S(1)} %bitcast.181, bf16[5,128,128]{2,1,0:T(8,128)(2,1)} %param.22), kind=kOutput, calls=%fused_computation.18 | convolution fusion | flops 202113024 | bytes 3178496 | tf_op jit(solution)/shard_map/dot_general | solution.py:114
  42.7 3.8 %fusion.19 = f32[1,12,128,128]{3,2,1,0:T(8,128)S(1)} fusion(bf16[3456,128,1]{1,0,2:T(8,128)(2,1)S(1)} %bitcast.188, s32[12,128]{1,0:T(8,128)S(1)} %bitcast.203), kind=kOutput, calls=%fused_computation.27 | convolution fusion | flops 1364262912 | bytes 1677312 | tf_op jit(solution)/shard_map/dot_general | solution.py:138
  46.4 3.8 %fusion.22 = f32[1,12,128,128]{3,2,1,0:T(8,128)S(1)} fusion(bf16[3456,128,1]{1,0,2:T(8,128)(2,1)S(1)} %bitcast.187, s32[12,128]{1,0:T(8,128)S(1)} %bitcast.202), kind=kOutput, calls=%fused_computation.28 | convolution fusion | flops 1364262912 | bytes 1677312 | tf_op jit(solution)/shard_map/dot_general | solution.py:138
  50.2 3.9 %fusion.25 = f32[1,12,128,128]{3,2,1,0:T(8,128)S(1)} fusion(bf16[3456,128,1]{1,0,2:T(8,128)(2,1)S(1)} %bitcast.186, s32[12,128]{1,0:T(8,128)S(1)} %bitcast.201), kind=kOutput, calls=%fused_computation.29 | convolution fusion | flops 1364262912 | bytes 1677312 | tf_op jit(solution)/shard_map/dot_general | solution.py:138
  54.2 3.8 %fusion.28 = f32[1,12,128,128]{3,2,1,0:T(8,128)S(1)} fusion(bf16[3456,128,1]{1,0,2:T(8,128)(2,1)S(1)} %bitcast.185, s32[12,128]{1,0:T(8,128)S(1)} %bitcast.200), kind=kOutput, calls=%fused_computation.30 | convolution fusion | flops 1364262912 | bytes 1677312 | tf_op jit(solution)/shard_map/dot_general | solution.py:138
  58.2 1.4 %maximum_convert_fusion = bf16[2,2,12,128,128]{4,3,2,1,0:T(8,128)(2,1)S(1)} fusion(f32[2,2,12,128,128]{4,3,2,1,0:T(8,128)S(1)} %bitcast.179, bf16[2,2,1,12,128,128]{5,4,3,2,1,0:T(8,128)(2,1)S(1)} %copy-done, f32[2,2,128,128]{3,2,1,0:T(8,128)S(1)} %fusion.48, bf16[5,128,128]{2,1,0:T(8,128)(2,1)} %param.22), kind=kOutput, calls=%fused_computation.22 | convolution fusion | flops 204472320 | bytes 6586368 | tf_op jit(solution)/shard_map/dot_general | solution.py:141
  59.6 4.1 %fusion.183 = (f32[6144]{0:T(1024)}, f32[6144,128]{1,0:T(8,128)}) fusion(bf16[5,128,128]{2,1,0:T(8,128)(2,1)} %param.22, bf16[6144,128]{1,0:T(8,128)(2,1)S(1)} %bitcast.182), kind=kOutput, calls=%fused_computation.285 | convolution fusion | flops 405006336 | bytes 4808704 | tf_op jit(solution)/shard_map/dot_general | solution.py:37
  64.6 3.3 %multiply_reduce_fusion.1 = f32[6144]{0:T(1024)S(1)} fusion(f32[6144,128]{1,0:T(8,128)} %get-tuple-element.51, f32[6144]{0:T(1024)S(1)} %broadcast_multiply_fusion), kind=kLoop, calls=%fused_computation.21 | loop fusion | flops 2353152 | bytes 3194880 | tf_op jit(solution)/shard_map/reduce_sum | solution.py:28
  67.9 3.3 %subtract_multiply_fusion = f32[6144,128]{1,0:T(8,128)S(1)} fusion(f32[6144,128]{1,0:T(8,128)S(1)} %copy-done.1, f32[6144]{0:T(1024)S(1)} %add_rsqrt_fusion, f32[6144]{0:T(1024)S(1)} %broadcast_multiply_fusion), kind=kLoop, calls=%fused_computation.23 | loop fusion | flops 1572864 | bytes 6340608 | tf_op jit(solution)/shard_map/mul | solution.py:29
  73.8 4.6 %collective-permute-start.6 = (f32[10,1,3,3,8]{4,3,2,1,0:T(4,128)S(1)}, f32[10,1,3,3,8]{4,3,2,1,0:T(4,128)S(1)}, u32[]{:S(2)}, u32[]{:S(2)}) collective-permute-start(f32[10,1,3,3,8]{4,3,2,1,0:T(4,128)S(1)} %get-tuple-element.32), channel_id=1, source_target_pairs={{0,4},{4,8},{8,12},{1,5},{5,9},{9,13},{2,6},{6,10},{10,14},{3,7},{... | collective-permute-start | bytes 8648 | tf_op jit(solution)/shard_map/ppermute | solution.py:17
  81.0 3.5 %collective-permute-done.7 = f32[10,1,3,3,8]{4,3,2,1,0:T(4,128)S(1)} collective-permute-done((f32[10,1,3,3,8]{4,3,2,1,0:T(4,128)S(1)}, f32[10,1,3,3,8]{4,3,2,1,0:T(4,128)S(1)}, u32[]{:S(2)}, u32[]{:S(2)}) %collective-permute-start.7) | collective-permute-done | bytes 2912 | tf_op jit(solution)/shard_map/ppermute | solution.py:19
  84.6 1.4 %collective-permute-start.8 = (f32[10,5,1,3,8]{4,3,2,1,0:T(4,128)S(1)}, f32[10,5,1,3,8]{4,3,2,1,0:T(4,128)S(1)}, u32[]{:S(2)}, u32[]{:S(2)}) collective-permute-start(f32[10,5,1,3,8]{4,3,2,1,0:T(4,128)S(1)} %get-tuple-element.27), channel_id=1, source_target_pairs={{0,2},{1,3},{4,6},{5,7},{8,10},{9,11},{12,14},{13,15},{16,18},{17,... | collective-permute-start | bytes 14408 | tf_op jit(solution)/shard_map/ppermute | solution.py:17
  86.0 1.3 %collective-permute-start.9 = (f32[10,5,1,3,8]{4,3,2,1,0:T(4,128)S(1)}, f32[10,5,1,3,8]{4,3,2,1,0:T(4,128)S(1)}, u32[]{:S(2)}, u32[]{:S(2)}) collective-permute-start(f32[10,5,1,3,8]{4,3,2,1,0:T(4,128)S(1)} %get-tuple-element.28), channel_id=1, source_target_pairs={{2,0},{3,1},{6,4},{7,5},{10,8},{11,9},{14,12},{15,13},{18,16},{19,... | collective-permute-start | bytes 14408 | tf_op jit(solution)/shard_map/ppermute | solution.py:19
  88.9 4.2 %collective-permute-done.9 = f32[10,5,1,3,8]{4,3,2,1,0:T(4,128)S(1)} collective-permute-done((f32[10,5,1,3,8]{4,3,2,1,0:T(4,128)S(1)}, f32[10,5,1,3,8]{4,3,2,1,0:T(4,128)S(1)}, u32[]{:S(2)}, u32[]{:S(2)}) %collective-permute-start.9) | collective-permute-done | bytes 4832 | tf_op jit(solution)/shard_map/ppermute | solution.py:19
  93.3 1.5 %collective-permute-start.10 = (f32[10,5,5,1,8]{4,3,2,1,0:T(1,128)S(1)}, f32[10,5,5,1,8]{4,3,2,1,0:T(1,128)S(1)}, u32[]{:S(2)}, u32[]{:S(2)}) collective-permute-start(f32[10,5,5,1,8]{4,3,2,1,0:T(1,128)S(1)} %get-tuple-element.25), channel_id=1, source_target_pairs={{0,1},{2,3},{4,5},{6,7},{8,9},{10,11},{12,13},{14,15},{16,17},{18,... | collective-permute-start | bytes 24008 | tf_op jit(solution)/shard_map/ppermute | solution.py:17
  98.5 3.2 %slice.207 = f32[10,3,3,3,8]{4,3,2,1,0:T(4,128)S(1)} slice(f32[10,5,5,5,8]{4,3,2,1,0:T(8,128)S(1)} %pad_maximum_fusion.2), slice={[0:10:1], [0:5:2], [0:5:2], [0:5:2], [0:8:1]} | slice | bytes 17280 | tf_op jit(solution)/shard_map/slice | solution.py:185
  (149 shorter events, 36.8 us)
Async XLA Ops:
  0.6 57.5 %copy-start = (bf16[2,2,1,12,128,128]{5,4,3,2,1,0:T(8,128)(2,1)S(1)}, bf16[2,2,1,12,128,128]{5,4,3,2,1,0:T(8,128)(2,1)}, u32[]{:S(2)}) copy-start(bf16[2,2,1,12,128,128]{5,4,3,2,1,0:T(8,128)(2,1)} %param.16) | copy-start | bytes 4718596
  0.6 36.7 %copy-start.2 = (bf16[2,2,1,128,128]{4,3,2,1,0:T(8,128)(2,1)S(1)}, bf16[2,2,1,128,128]{4,3,2,1,0:T(8,128)(2,1)}, u32[]{:S(2)}) copy-start(bf16[2,2,1,128,128]{4,3,2,1,0:T(8,128)(2,1)} %param.15) | copy-start | bytes 393220
  0.7 35.3 %copy-start.8 = (f32[3,2,2,1,128]{4,3,2,1,0:T(1,128)S(1)}, f32[3,2,2,1,128]{4,3,2,1,0:T(1,128)}, u32[]{:S(2)}) copy-start(f32[3,2,2,1,128]{4,3,2,1,0:T(1,128)} %param.18) | copy-start | bytes 18436
  0.7 36.0 %copy-start.19 = (f32[3,2,2,1,128]{4,3,2,1,0:T(1,128)S(1)}, f32[3,2,2,1,128]{4,3,2,1,0:T(1,128)}, u32[]{:S(2)}) copy-start(f32[3,2,2,1,128]{4,3,2,1,0:T(1,128)} %param.17) | copy-start | bytes 18436
  1.7 14.1 %collective-permute-start = (bf16[1,2,1,128,128]{4,3,2,1,0:T(8,128)(2,1)S(1)}, bf16[1,2,1,128,128]{4,3,2,1,0:T(8,128)(2,1)S(1)}, u32[]{:S(2)}, u32[]{:S(2)}) collective-permute-start(bf16[1,2,1,128,128]{4,3,2,1,0:T(8,128)(2,1)S(1)} %get-tuple-element.34), channel_id=1, source_target_pairs={{0,4},{4,8},{8,12},{1,5},{5,9},{9,13},{2,6},{6,10},{10,14},{3,7},{... | collective-permute-start | bytes 196616 | tf_op jit(solution)/shard_map/ppermute | solution.py:17
  6.6 10.1 %collective-permute-start.1 = (bf16[1,2,1,128,128]{4,3,2,1,0:T(8,128)(2,1)S(1)}, bf16[1,2,1,128,128]{4,3,2,1,0:T(8,128)(2,1)S(1)}, u32[]{:S(2)}, u32[]{:S(2)}) collective-permute-start(bf16[1,2,1,128,128]{4,3,2,1,0:T(8,128)(2,1)S(1)} %get-tuple-element.33), channel_id=1, source_target_pairs={{4,0},{8,4},{12,8},{5,1},{9,5},{13,9},{6,2},{10,6},{14,10},{7,3},{... | collective-permute-start | bytes 196616 | tf_op jit(solution)/shard_map/ppermute | solution.py:19
  16.8 6.0 %collective-permute-start.2 = (bf16[4,1,1,128,128]{4,3,2,1,0:T(8,128)(2,1)S(1)}, bf16[4,1,1,128,128]{4,3,2,1,0:T(8,128)(2,1)S(1)}, u32[]{:S(2)}, u32[]{:S(2)}) collective-permute-start(bf16[4,1,1,128,128]{4,3,2,1,0:T(8,128)(2,1)S(1)} %get-tuple-element.29), channel_id=1, source_target_pairs={{0,2},{1,3},{4,6},{5,7},{8,10},{9,11},{12,14},{13,15},{16,18},{17,... | collective-permute-start | bytes 393224 | tf_op jit(solution)/shard_map/ppermute | solution.py:17
  20.2 7.0 %collective-permute-start.3 = (bf16[4,1,1,128,128]{4,3,2,1,0:T(8,128)(2,1)S(1)}, bf16[4,1,1,128,128]{4,3,2,1,0:T(8,128)(2,1)}, u32[]{:S(2)}, u32[]{:S(2)}) collective-permute-start(bf16[4,1,1,128,128]{4,3,2,1,0:T(8,128)(2,1)S(1)} %get-tuple-element.30), channel_id=1, source_target_pairs={{2,0},{3,1},{6,4},{7,5},{10,8},{11,9},{14,12},{15,13},{18,16},{19,... | collective-permute-start | bytes 393224 | tf_op jit(solution)/shard_map/ppermute | solution.py:19
  28.1 11.1 %collective-permute-start.4 = (bf16[4,4,1,128,128]{4,3,2,1,0:T(8,128)(2,1)S(1)}, bf16[4,4,1,128,128]{4,3,2,1,0:T(8,128)(2,1)S(1)}, u32[]{:S(2)}, u32[]{:S(2)}) collective-permute-start(bf16[4,4,1,128,128]{4,3,2,1,0:T(8,128)(2,1)S(1)} %pad_maximum_fusion.3), channel_id=1, source_target_pairs={{0,1},{2,3},{4,5},{6,7},{8,9},{10,11},{12,13},{14,15},{16,17},{18,... | collective-permute-start | bytes 1572872 | tf_op jit(solution)/shard_map/ppermute | solution.py:17
  29.4 9.8 %collective-permute-start.5 = (bf16[4,4,1,128,128]{4,3,2,1,0:T(8,128)(2,1)S(1)}, bf16[4,4,1,128,128]{4,3,2,1,0:T(8,128)(2,1)}, u32[]{:S(2)}, u32[]{:S(2)}) collective-permute-start(bf16[4,4,1,128,128]{4,3,2,1,0:T(8,128)(2,1)S(1)} %pad_maximum_fusion.3), channel_id=1, source_target_pairs={{1,0},{3,2},{5,4},{7,6},{9,8},{11,10},{13,12},{15,14},{17,16},{19,... | collective-permute-start | bytes 1572872 | tf_op jit(solution)/shard_map/ppermute | solution.py:19
  71.3 8.5 %copy-start.10 = (bf16[12,128]{1,0:T(8,128)(2,1)S(1)}, bf16[12,128]{1,0:T(8,128)(2,1)}, u32[]{:S(2)}) copy-start(bf16[12,128]{1,0:T(8,128)(2,1)} %param.27) | copy-start | bytes 9220
  71.3 8.9 %copy-start.3 = (bf16[2,128,128]{2,1,0:T(8,128)(2,1)S(1)}, bf16[2,128,128]{2,1,0:T(8,128)(2,1)}, u32[]{:S(2)}) copy-start(bf16[2,128,128]{2,1,0:T(8,128)(2,1)} %param.28) | copy-start | bytes 196612
  71.7 15.6 %copy-start.12 = (f32[512]{0:T(512)S(1)}, f32[512]{0:T(512)}, u32[]{:S(2)}) copy-start(f32[512]{0:T(512)} %and_convert_fusion.1) | copy-start | bytes 6148
  71.7 24.5 %copy-start.9 = (f32[3,2,2,1,128]{4,3,2,1,0:T(1,128)S(1)}, f32[3,2,2,1,128]{4,3,2,1,0:T(1,128)}, u32[]{:S(2)}) copy-start(f32[3,2,2,1,128]{4,3,2,1,0:T(1,128)} %param.18) | copy-start | bytes 18436
  71.7 24.5 %copy-start.13 = (f32[2,2,128]{2,1,0:T(2,128)S(1)}, f32[2,2,128]{2,1,0:T(2,128)}, u32[]{:S(2)}) copy-start(f32[2,2,128]{2,1,0:T(2,128)} %get-tuple-element.48) | copy-start | bytes 6148
  73.8 7.1 %collective-permute-start.6 = (f32[10,1,3,3,8]{4,3,2,1,0:T(4,128)S(1)}, f32[10,1,3,3,8]{4,3,2,1,0:T(4,128)S(1)}, u32[]{:S(2)}, u32[]{:S(2)}) collective-permute-start(f32[10,1,3,3,8]{4,3,2,1,0:T(4,128)S(1)} %get-tuple-element.32), channel_id=1, source_target_pairs={{0,4},{4,8},{8,12},{1,5},{5,9},{9,13},{2,6},{6,10},{10,14},{3,7},{... | collective-permute-start | bytes 8648 | tf_op jit(solution)/shard_map/ppermute | solution.py:17
  78.4 6.1 %collective-permute-start.7 = (f32[10,1,3,3,8]{4,3,2,1,0:T(4,128)S(1)}, f32[10,1,3,3,8]{4,3,2,1,0:T(4,128)S(1)}, u32[]{:S(2)}, u32[]{:S(2)}) collective-permute-start(f32[10,1,3,3,8]{4,3,2,1,0:T(4,128)S(1)} %get-tuple-element.31), channel_id=1, source_target_pairs={{4,0},{8,4},{12,8},{5,1},{9,5},{13,9},{6,2},{10,6},{14,10},{7,3},{... | collective-permute-start | bytes 8648 | tf_op jit(solution)/shard_map/ppermute | solution.py:19
  80.9 23.0 %copy-start.23 = (f32[3]{0:T(128)S(1)}, f32[3]{0:T(128)}, u32[]{:S(2)}) copy-start(f32[3]{0:T(128)} %constant.158.clone) | copy-start | bytes 40
  80.9 23.1 %copy-start.11 = (bf16[12,128]{1,0:T(8,128)(2,1)S(1)}, bf16[12,128]{1,0:T(8,128)(2,1)}, u32[]{:S(2)}) copy-start(bf16[12,128]{1,0:T(8,128)(2,1)} %param.27) | copy-start | bytes 9220
  80.9 23.4 %copy-start.4 = (bf16[2,128,128]{2,1,0:T(8,128)(2,1)S(1)}, bf16[2,128,128]{2,1,0:T(8,128)(2,1)}, u32[]{:S(2)}) copy-start(bf16[2,128,128]{2,1,0:T(8,128)(2,1)} %param.28) | copy-start | bytes 196612
  84.6 4.3 %collective-permute-start.8 = (f32[10,5,1,3,8]{4,3,2,1,0:T(4,128)S(1)}, f32[10,5,1,3,8]{4,3,2,1,0:T(4,128)S(1)}, u32[]{:S(2)}, u32[]{:S(2)}) collective-permute-start(f32[10,5,1,3,8]{4,3,2,1,0:T(4,128)S(1)} %get-tuple-element.27), channel_id=1, source_target_pairs={{0,2},{1,3},{4,6},{5,7},{8,10},{9,11},{12,14},{13,15},{16,18},{17,... | collective-permute-start | bytes 14408 | tf_op jit(solution)/shard_map/ppermute | solution.py:17
  86.0 7.1 %collective-permute-start.9 = (f32[10,5,1,3,8]{4,3,2,1,0:T(4,128)S(1)}, f32[10,5,1,3,8]{4,3,2,1,0:T(4,128)S(1)}, u32[]{:S(2)}, u32[]{:S(2)}) collective-permute-start(f32[10,5,1,3,8]{4,3,2,1,0:T(4,128)S(1)} %get-tuple-element.28), channel_id=1, source_target_pairs={{2,0},{3,1},{6,4},{7,5},{10,8},{11,9},{14,12},{15,13},{18,16},{19,... | collective-permute-start | bytes 14408 | tf_op jit(solution)/shard_map/ppermute | solution.py:19
  93.3 3.5 %collective-permute-start.10 = (f32[10,5,5,1,8]{4,3,2,1,0:T(1,128)S(1)}, f32[10,5,5,1,8]{4,3,2,1,0:T(1,128)S(1)}, u32[]{:S(2)}, u32[]{:S(2)}) collective-permute-start(f32[10,5,5,1,8]{4,3,2,1,0:T(1,128)S(1)} %get-tuple-element.25), channel_id=1, source_target_pairs={{0,1},{2,3},{4,5},{6,7},{8,9},{10,11},{12,13},{14,15},{16,17},{18,... | collective-permute-start | bytes 24008 | tf_op jit(solution)/shard_map/ppermute | solution.py:17
  94.9 3.2 %collective-permute-start.11 = (f32[10,5,5,1,8]{4,3,2,1,0:T(1,128)S(1)}, f32[10,5,5,1,8]{4,3,2,1,0:T(1,128)S(1)}, u32[]{:S(2)}, u32[]{:S(2)}) collective-permute-start(f32[10,5,5,1,8]{4,3,2,1,0:T(1,128)S(1)} %get-tuple-element.26), channel_id=1, source_target_pairs={{1,0},{3,2},{5,4},{7,6},{9,8},{11,10},{13,12},{15,14},{17,16},{19,... | collective-permute-start | bytes 24008 | tf_op jit(solution)/shard_map/ppermute | solution.py:19
  (13 other events, 37.5 us)
where the time goes:
time: 107 us; the launch traced here: 106 us
  matrix products  27.1 us (25%)
  other arithmetic  25 us (23%)
  starting transfers between devices  24.9 us (23%)
  waiting for transfers between devices  14 us (13%)
  local copies, waits for them, and re-layouts  13.5 us (13%)
  between operations  1.42 us (1%)
    ppermute x6, starting transfers between devices, padded(): lax.ppermute(tail, axis, [(i, (i + 1) % count) for i in range(ends)])  17.1 us
    dot_general x4, matrix products, body(): picked = jnp.dot(picker, window, preferred_element_type=jnp.float32)  15.2 us
    ppermute x6, waiting for transfers between devices, padded(): lax.ppermute(head, axis, [((i + 1) % count, i) for i in range(ends)])  13.3 us
    ppermute x6, starting transfers between devices, padded(): lax.ppermute(head, axis, [((i + 1) % count, i) for i in range(ends)])  7.75 us
    dot_general x4, matrix products, mlp_tail(): jnp.dot(hidden, final_w, preferred_element_type=jnp.float32)  5.12 us
    unnamed x60, local copies, waits for them, and re-layouts  5.02 us
    reduce_sum x4, other arithmetic, layer_norm(): spread = jnp.mean(centred * centred, axis=-1, keepdims=True)  3.77 us
    slice x2, local copies, waits for them, and re-layouts, body(): arrived = beside_all[:, ::2, ::2, ::2, :].reshape(10, 27, CAP)  3.48 us
  transfers between devices with their start and end apart: 12, of which 5 were waited for; matrix products, arithmetic and copies ran while one was open for 20% of the time, Pallas kernels for 0%

commit v1 on v0

v1 whole, which is shorter than its diff:
```python
import functools

import jax
import jax.numpy as jnp
from jax import lax
from jax.experimental import pallas as pl
from jax.experimental.pallas import tpu as pltpu
from jax.sharding import PartitionSpec as P

CAP = 8
F32 = jnp.float32
BF16 = jnp.bfloat16
ROWS = 16


def dot(left, right):
    return jnp.dot(left, right, preferred_element_type=F32)


def dot_nt(left, right):
    return lax.dot_general(
        left, right, (((1,), (1,)), ((), ())), preferred_element_type=F32
    )


def relu16(values):
    return jnp.maximum(values, 0.0).astype(BF16)


def norm_rows(values):
    scale = 1.0 / values.shape[0]
    centred = values - jnp.sum(values, axis=0, keepdims=True) * scale
    spread = jnp.sum(centred * centred, axis=0, keepdims=True) * scale
    return centred * lax.rsqrt(spread + 1e-05)


def thirds(values):
    high = values.astype(BF16)
    rest = values - high.astype(F32)
    middle = rest.astype(BF16)
    low = (rest - middle.astype(F32)).astype(BF16)
    return high, middle, low


def quotient(values, count):
    if count & (count - 1) == 0:
        return values >> (count.bit_length() - 1)
    return lax.div(values, jnp.full_like(values, count))


def flip(weights):
    return weights.astype(F32).T.astype(BF16)


def encode(state, encoder_in, first, second, extent):
    width = state.shape[1]
    position = state[0:3]
    row = lax.broadcasted_iota(jnp.int32, (3, width), 0)
    size = jnp.where(row == 0, extent[0], jnp.where(row == 1, extent[1], extent[2]))
    features = jnp.concatenate(
        [
            state[3:9],
            jnp.clip(position, -1.0, 1.0),
            jnp.clip(size - position, -1.0, 1.0),
            jnp.zeros((4, width), F32),
        ],
        axis=0,
    )
    inward = jnp.concatenate([encoder_in.astype(F32), jnp.zeros((4, encoder_in.shape[1]), F32)], axis=0)
    inward = jnp.concatenate([inward, inward, inward], axis=0).T.astype(BF16)
    hidden = relu16(dot(inward, jnp.concatenate(thirds(features), axis=0)))
    hidden = relu16(dot(first, hidden))
    return norm_rows(dot(second, hidden))


def step_kernel(
    sizes,
    fill_ref,
    own_ref,
    zed_ref,
    side_refs,
    left_ref,
    right_ref,
    edge_ref,
    positions_ref,
    velocity_ref,
    neighbours_ref,
    owners_ref,
    edge_w_ref,
    node_in_ref,
    node_w_ref,
    decoder_w_ref,
    decoder_out_ref,
    encoder_in_ref,
    encoder_w_ref,
    kept_latent_ref,
    kept_state_ref,
    bucket_ref,
    far_ref,
    gather_ref,
):
    count_x, count_y, count_z = sizes
    fold_y = count_y == 2
    index_x = lax.axis_index("gx")
    index_y = lax.axis_index("gy")
    index_z = lax.axis_index("gz")
    slots, width = own_ref.shape[-2:]
    neighbour_count = edge_ref.shape[3]
    middle_t = flip(edge_w_ref[3])
    final_t = flip(edge_w_ref[4])
    edge_t = flip(edge_w_ref[0])
    near_t = flip(edge_w_ref[1])
    far_t = flip(edge_w_ref[2])

    if fold_y:
        row_count = 3
        own_rows = (0, 1)
        outer = {2: 0}
    else:
        row_count = 4
        own_rows = (1, 2)
        outer = {0: 0, 3: 1}
    for ex in range(4):
        for row in range(row_count):
            if ex == 0:
                pair = (left_ref[0, row], left_ref[1, row])
            elif ex == 3:
                pair = (right_ref[0, row], right_ref[1, row])
            elif row in own_rows:
                b = own_rows.index(row)
                pair = (own_ref[ex - 1, b, 0], zed_ref[ex - 1, b, 0])
            else:
                side = side_refs[outer[row]]
                pair = (side[0, ex - 1], side[1, ex - 1])
            far_ref[ex * row_count + row] = dot_nt(
                far_t, jnp.concatenate(pair, axis=0)
            ).astype(BF16)

    lane = lax.broadcasted_iota(jnp.int32, (1, slots), 1)
    key_rows = lax.broadcasted_iota(jnp.int32, (2 * slots, 2 * slots), 0)
    chunk = 32
    for a in range(2):
        for bt in range(2):
            if fold_y:
                b = index_y if bt == 0 else 1 - index_y
                rows = (0, 1) if bt == 0 else (0, 1, 2)
            else:
                b = bt
                rows = (bt, bt + 1, bt + 2)
            columns = [(ex, row) for ex in range(a, a + 3) for row in rows]
            near = dot_nt(near_t, own_ref[a, b, 0])
            near = jnp.concatenate([near, near], axis=1)
            total = jnp.zeros((width, slots), F32)
            window = jnp.concatenate(
                [
                    far_ref[ex * row_count + row, f : f + chunk]
                    for f in range(0, width, chunk)
                    for ex, row in columns
                ],
                axis=0,
            )
            for k in range(0, neighbour_count, 2):
                ids = jnp.concatenate(
                    [neighbours_ref[a, b, k], neighbours_ref[a, b, k + 1]], axis=1
                )
                cell = ids >> 7
                plane = (cell * 43) >> 7
                ez = cell - plane * 3
                ey = plane & 3
                ex = plane >> 2
                if fold_y:
                    row = jnp.where(ey == 1, 0, jnp.where(ey == 2, 1, 2))
                else:
                    row = ey
                place = ex * 4 + row
                key = (ids & 127) + jnp.where(ez == 1, 0, slots)
                picker = (key_rows == key).astype(F32).astype(BF16)
                found = dot(window, picker)
                edges = jnp.concatenate([edge_ref[a, b, 0, k], edge_ref[a, b, 0, k + 1]], axis=0)
                pre = dot_nt(edge_t, edges) + near
                parts = []
                at = 0
                for f in range(0, width, chunk):
                    part = jnp.zeros((chunk, 2 * slots), F32)
                    for ex_at, row_at in columns:
                        part = jnp.where(
                            place == ex_at * 4 + row_at, found[at : at + chunk], part
                        )
                        at += chunk
                    parts.append(part)
                hidden = relu16(pre + jnp.concatenate(parts, axis=0))
                hidden = relu16(dot(middle_t, hidden))
                message = norm_rows(dot(final_t, hidden))
                total = total + message[:, :slots] + message[:, slots:]
            total = jnp.where(lane < fill_ref[a * 2 + b], total, 0.0)
            gather_ref[a * 2 + b] = total.astype(BF16)

    cells = [(a, b) for a in range(2) for b in range(2)]
    aggregate = jnp.concatenate([gather_ref[i] for i in range(4)], axis=1)
    latent = jnp.concatenate([own_ref[a, b, 0] for a, b in cells], axis=0)
    pre = dot_nt(flip(node_in_ref[:width]), latent) + dot(flip(node_in_ref[width:]), aggregate)
    hidden = relu16(dot(flip(node_w_ref[0]), relu16(pre)))
    updated = (latent.astype(F32).T + norm_rows(dot(flip(node_w_ref[1]), hidden))).astype(BF16)
    hidden = relu16(dot(flip(decoder_w_ref[0]), updated))
    hidden = relu16(dot(flip(decoder_w_ref[1]), hidden))
    acceleration = dot(decoder_out_ref[...], hidden)

    def flat(ref, i):
        return jnp.concatenate([ref[i, a, b] for a, b in cells], axis=1)

    old = jnp.concatenate([flat(velocity_ref, i) for i in range(3)], axis=0)
    new_velocity = old + acceleration
    new_position = jnp.concatenate([flat(positions_ref, i) for i in range(3)], axis=0) + new_velocity
    state = jnp.concatenate([new_position, new_velocity, old], axis=0)

    owner = jnp.concatenate([owners_ref[a, b] for a, b in cells], axis=1)
    alive = jnp.concatenate(
        [(lane < fill_ref[i]).astype(jnp.int32) for i in range(4)], axis=1
    )
    own_block = (index_x * count_y + index_y) * count_z + index_z
    stays = jnp.where((alive == 1) & (owner == own_block), 1.0, 0.0)
    moving = jnp.where((alive == 1) & (owner != own_block), 1, 0)

    extent = (2.0 * count_x, 2.0 * count_y, 1.0 * count_z)
    latents = encode(
        state, encoder_in_ref[...], flip(encoder_w_ref[0]), flip(encoder_w_ref[1]), extent
    )
    latents = (latents * stays).T.astype(BF16)
    kept = state * stays
    for i, (a, b) in enumerate(cells):
        kept_latent_ref[a, b, 0] = latents[i * slots : (i + 1) * slots]
        for j in range(9):
            kept_state_ref[j, a, b] = kept[j : j + 1, i * slots : (i + 1) * slots]

    owner_x = quotient(owner, count_y * count_z)
    rest = owner - owner_x * (count_y * count_z)
    owner_y = quotient(rest, count_z)
    owner_z = rest - owner_y * count_z
    step_y = owner_y - index_y
    side_y = jnp.where(step_y == 0, 0, 1) if fold_y else jnp.where(step_y < 0, 1, 2 * step_y)
    options_y = 2 if fold_y else 3
    group = ((owner_x - index_x + 1) * options_y + side_y) * 2 + jnp.where(owner_z == index_z, 0, 1)
    groups = 3 * options_y * 2
    group_rows = (groups + 15) // 16 * 16
    particles = owner.shape[1]
    member = jnp.where(
        (lax.broadcasted_iota(jnp.int32, (group_rows, particles), 0) == group) & (moving == 1),
        1.0,
        0.0,
    )
    triangle = jnp.where(
        lax.broadcasted_iota(jnp.int32, (slots, slots), 0)
        <= lax.broadcasted_iota(jnp.int32, (slots, slots), 1),
        1.0,
        0.0,
    ).astype(BF16)
    counted = []
    before = jnp.zeros((group_rows, 1), F32)
    for i in range(4):
        inside = member[:, i * slots : (i + 1) * slots]
        counted.append(dot(inside.astype(BF16), triangle) + before)
        before = before + jnp.sum(inside, axis=1, keepdims=True)
    counted = jnp.concatenate(counted, axis=1)
    rank = (jnp.sum(counted * member, axis=0, keepdims=True) - 1.0).astype(jnp.int32)
    column = jnp.where(moving == 1, group * CAP + rank, -1)
    placer = (
        (lax.broadcasted_iota(jnp.int32, (groups * CAP, particles), 0) == column)
        .astype(F32)
        .astype(BF16)
    )
    payload = jnp.concatenate(
        [state, moving.astype(F32), jnp.zeros((ROWS - 10, particles), F32)], axis=0
    )
    placed = dot_nt(jnp.concatenate(thirds(payload), axis=0), placer)
    bucket_ref[...] = placed[:ROWS] + placed[ROWS : 2 * ROWS] + placed[2 * ROWS :]


def arrive_kernel(
    sizes,
    middle_ref,
    left_ref,
    right_ref,
    encoder_in_ref,
    encoder_w_ref,
    arrived_latent_ref,
    arrived_state_ref,
):
    count_x, count_y, count_z = sizes
    fold_y = count_y == 2
    index_y = lax.axis_index("gy")
    index_z = lax.axis_index("gz")
    options_y = 2 if fold_y else 3
    lanes = middle_ref.shape[-1]
    group = lax.broadcasted_iota(jnp.int32, (ROWS, lanes), 1) >> 3
    found = jnp.zeros((ROWS, lanes), F32)
    for source_x, ref in ((-1, left_ref), (0, middle_ref), (1, right_ref)):
        for from_y in range(options_y):
            for from_z in range(2):
                if source_x == 0 and from_y == 0 and from_z == 0:
                    continue
                side_y = from_y if fold_y or from_y == 0 else 3 - from_y
                target = ((1 - source_x) * options_y + side_y) * 2 + from_z
                found = jnp.where(group == target, ref[from_y * 2 + from_z], found)
    out_lanes = arrived_state_ref.shape[-1]
    spread_shape = (lanes, out_lanes)
    line = lax.broadcasted_iota(jnp.int32, spread_shape, 0)
    from_group = line >> 3
    plane = quotient(from_group, 2)
    from_x = 1 - quotient(plane, options_y) if fold_y else 1 - ((plane * 43) >> 7)
    side_y = plane - (1 - from_x) * options_y
    if fold_y:
        from_y = jnp.where(side_y == 0, 0, jnp.where(index_y == 0, 1, -1))
    else:
        from_y = jnp.where(side_y == 0, 0, jnp.where(side_y == 1, 1, -1))
    from_z = jnp.where((from_group & 1) == 0, 0, jnp.where(index_z == 0, 1, -1))
    direction = (from_x + 1) * 9 + (from_y + 1) * 3 + from_z + 1
    direction = direction - jnp.where(direction > 13, 1, 0)
    column = direction * CAP + (line & 7)
    valid = (lax.broadcasted_iota(jnp.int32, spread_shape, 1) == column) & (
        (from_x != 0) | (from_y != 0) | (from_z != 0)
    )
    spread = jnp.where(valid, 1.0, 0.0).astype(BF16)
    arrived = dot(jnp.concatenate(thirds(found), axis=0), spread)
    arrived = arrived[:ROWS] + arrived[ROWS : 2 * ROWS] + arrived[2 * ROWS :]
    for j in range(9):
        arrived_state_ref[j, 0, 0] = arrived[j : j + 1]
    extent = (2.0 * count_x, 2.0 * count_y, 1.0 * count_z)
    latents = encode(
        arrived[:9], encoder_in_ref[...], flip(encoder_w_ref[0]), flip(encoder_w_ref[1]), extent
    )
    arrived_latent_ref[0, 0, 0] = (latents * arrived[9:10]).T.astype(BF16)


def along(count):
    up = [(i, i + 1) for i in range(count - 1)]
    return up, [(j, i) for i, j in up]


def swap(values, axis):
    return lax.ppermute(values, axis, [(0, 1), (1, 0)])


def shift(values, axis, way):
    return lax.ppermute(values, axis, along(lax.axis_size(axis))[way])


def body(
    node_latent,
    edge_latent,
    positions,
    velocity,
    fill,
    neighbours,
    owners,
    edge_weights,
    node_in,
    node_weights,
    decoder_weights,
    decoder_out,
    encoder_in,
    encoder_weights,
):
    sizes = tuple(lax.axis_size(axis) for axis in ("gx", "gy", "gz"))
    fold_y = sizes[1] == 2
    slots, width = node_latent.shape[-2:]
    zed = swap(node_latent, "gz")
    both = jnp.stack([node_latent[:, :, 0], zed[:, :, 0]], axis=0)
    if fold_y:
        inner = 1 - lax.axis_index("gy")
        sides = [swap(lax.dynamic_index_in_dim(both, inner, 2, keepdims=False), "gy")]
        layers = jnp.concatenate([both, sides[0][:, :, None]], axis=2)
    else:
        sides = [shift(both[:, :, 1], "gy", 0), shift(both[:, :, 0], "gy", 1)]
        layers = jnp.concatenate([sides[0][:, :, None], both, sides[1][:, :, None]], axis=2)
    left = shift(layers[:, 1], "gx", 0)
    right = shift(layers[:, 0], "gx", 1)

    options_y = 2 if fold_y else 3
    lanes = 3 * options_y * 2 * CAP
    rows = layers.shape[2]
    vmem = pl.BlockSpec(memory_space=pltpu.VMEM)
    smem = pl.BlockSpec(memory_space=pltpu.SMEM)
    side_count = len(sides)

    def step(fill_ref, own_ref, zed_ref, *refs):
        step_kernel(sizes, fill_ref, own_ref, zed_ref, refs[:side_count], *refs[side_count:])

    kept_latent, kept_state, bucket = pl.pallas_call(
        step,
        out_shape=(
            jax.ShapeDtypeStruct(node_latent.shape, BF16),
            jax.ShapeDtypeStruct((9,) + node_latent.shape[:4], F32),
            jax.ShapeDtypeStruct((ROWS, lanes), F32),
        ),
        in_specs=[smem] + [vmem] * (17 + side_count - 1),
        out_specs=(vmem, vmem, vmem),
        scratch_shapes=[
            pltpu.VMEM((4 * rows, width, 2 * slots), BF16),
            pltpu.VMEM((4, width, slots), BF16),
        ],
        compiler_params=pltpu.CompilerParams(vmem_limit_bytes=40 * 1024 * 1024),
        name="step",
    )(
        fill.reshape(-1),
        node_latent,
        zed,
        *sides,
        left,
        right,
        edge_latent,
        positions,
        velocity,
        neighbours.reshape(2, 2, neighbours.shape[3], 1, slots),
        owners,
        edge_weights,
        node_in,
        node_weights,
        decoder_weights,
        decoder_out,
        encoder_in,
        encoder_weights,
    )

    tiles = jnp.stack([bucket, swap(bucket, "gz")], axis=0)
    if fold_y:
        tiles = jnp.concatenate([tiles, swap(tiles, "gy")], axis=0)
    else:
        tiles = jnp.concatenate([tiles, shift(tiles, "gy", 0), shift(tiles, "gy", 1)], axis=0)
    tiles_left = shift(tiles, "gx", 0)
    tiles_right = shift(tiles, "gx", 1)
    arrived_latent, arrived_state = pl.pallas_call(
        functools.partial(arrive_kernel, sizes),
        out_shape=(
            jax.ShapeDtypeStruct((1, 1, 1, 26 * CAP, width), BF16),
            jax.ShapeDtypeStruct((9, 1, 1, 1, 26 * CAP), F32),
        ),
        in_specs=[vmem] * 5,
        out_specs=(vmem, vmem),
        name="arrive",
    )(tiles, tiles_left, tiles_right, encoder_in, encoder_weights)
    return kept_latent, kept_state, arrived_latent, arrived_state


def solution(mesh):
    placed = (
        P(("group", "gx"), "gy", "gz", None, None),
        P(("group", "gx"), "gy", "gz", None, None, None),
        P(None, ("group", "gx"), "gy", "gz", None),
        P(None, ("group", "gx"), "gy", "gz", None),
        P(("group", "gx"), "gy", "gz"),
        P(("group", "gx"), "gy", "gz", None, None),
        P(("group", "gx"), "gy", "gz", None),
        P(),
        P(),
        P(),
        P(),
        P(),
        P(),
        P(),
    )
    return jax.shard_map(
        body,
        mesh=mesh,
        in_specs=placed,
        out_specs=(
            P(("group", "gx"), "gy", "gz", None, None),
            P(None, ("group", "gx"), "gy", "gz", None),
            P(("group", "gx"), "gy", "gz", None, None),
            P(None, ("group", "gx"), "gy", "gz", None),
        ),
        check_vma=False,
    )
```

time: 107 us -> 56.4 us (0.53)
  matrix products: 27.1 us -> 0 us
  other arithmetic: 25 us -> 2.48 us
  Pallas kernels: 0 us -> 18.6 us
  local copies, waits for them, and re-layouts: 13.5 us -> 1.31 us
  starting transfers between devices: 24.9 us -> 14.7 us
  waiting for transfers between devices: 14 us -> 18.1 us
    dot_general x20 -> x0, matrix products: 27.1 us -> none  [the longest x4 15.2 us: body(): picked = jnp.dot(picker, window, preferred_element_type=jnp.float32)]
    pallas_call x0 -> x2, Pallas kernels: none -> 18.6 us  [the longest x1 16.2 us: body(): pl.pallas_call(step, out_shape=(jax.ShapeDtypeStruct(node_latent.shape, B...]
    ppermute x12 -> x8, starting transfers between devices: 24.9 us -> 14.7 us  [the longest x4 9.8 us: shift(): return lax.ppermute(values, axis, along(lax.axis_size(axis))[way])]
    slice x16 -> x0, local copies, waits for them, and re-layouts: 6.3 us -> none  [the longest x2 3.48 us: body(): arrived = beside_all[:, ::2, ::2, ::2, :].reshape(10, 27, CAP)]
    convert_element_type x4 -> x0, other arithmetic: 4.86 us -> none  [the longest x2 2.59 us: body(): stay_mask = staying.astype(jnp.float32)]
    reduce_sum x6 -> x0, other arithmetic: 4.2 us -> none  [the longest x4 3.77 us: layer_norm(): spread = jnp.mean(centred * centred, axis=-1, keepdims=True)]
    ppermute x12 -> x8, waiting for transfers between devices: 14 us -> 18.1 us  [the longest x4 9.67 us: shift(): return lax.ppermute(values, axis, along(lax.axis_size(axis))[way])]
    mul x2 -> x0, other arithmetic: 3.94 us -> none  [the longest x1 3.32 us: layer_norm(): return centred * lax.rsqrt(spread + 1e-05)]
  transfers between devices with their start and end apart: 12 -> 8, of which waited for: 5 -> 8; matrix products, arithmetic and copies ran while one was open for 20% -> 2% of each run, Pallas kernels for 0% -> 0%
where the time goes in v1:
time: 56.4 us; the launch traced here: 56.1 us
  Pallas kernels  18.6 us (33%)
  waiting for transfers between devices  18.1 us (32%)
  starting transfers between devices  14.7 us (26%)
  other arithmetic  2.48 us (4%)
  local copies, waits for them, and re-layouts  1.31 us (2%)
  between operations  0.89 us (2%)
    pallas_call x1, Pallas kernels, body(): pl.pallas_call(step, out_shape=(jax.ShapeDtypeStruct(node_latent.shape, B...  16.2 us
    ppermute x4, starting transfers between devices, shift(): return lax.ppermute(values, axis, along(lax.axis_size(axis))[way])  9.8 us
    ppermute x4, waiting for transfers between devices, shift(): return lax.ppermute(values, axis, along(lax.axis_size(axis))[way])  9.67 us
    ppermute x4, waiting for transfers between devices, swap(): return lax.ppermute(values, axis, [(0, 1), (1, 0)])  8.42 us
    ppermute x4, starting transfers between devices, swap(): return lax.ppermute(values, axis, [(0, 1), (1, 0)])  4.93 us
    pallas_call x1, Pallas kernels, body(): pl.pallas_call(functools.partial(arrive_kernel, sizes), out_shape=(jax.Sh...  2.33 us
    unnamed x35, local copies, waits for them, and re-layouts  1.19 us
  transfers between devices with their start and end apart: 8, of which 8 were waited for; matrix products, arithmetic and copies ran while one was open for 2% of the time, Pallas kernels for 0%

profile of v1, /device:TPU:0, one launch (start us, length us, event | category | flops | bytes accessed | tf_op | source)
XLA Modules:
  0.0 56.1 jit_solution(4523555486235119062)
XLA Ops:
  0.6 0.0 copy-start.1
  0.8 0.5 collective-permute-start
  1.3 1.2 %collective-permute-done = bf16[2,2,1,128,128]{4,3,1,0,2:T(8,128)(2,1)S(1)} collective-permute-done((bf16[2,2,1,128,128]{4,3,1,0,2:T(8,128)(2,1)}, bf16[2,2,1,128,128]{4,3,1,0,2:T(8,128)(2,1)S(1)}, u32[]{:S(2)}, u32[]{:S(2)}) %collective-permute-start) | collective-permute-done | bytes 131104 | tf_op jit(solution)/shard_map/ppermute | solution.py:340
  2.5 0.9 %fusion.1 = bf16[2,2,128,128]{3,2,0,1:T(8,128)(2,1)S(1)} fusion(s32[]{:T(128)S(6)} %select_n.4, bf16[1,2,2,128,128]{4,3,2,0,1:T(8,128)(2,1)} %bitcast.16, bf16[1,2,2,128,128]{4,3,2,0,1:T(8,128)(2,1)S(1)} %bitcast.18), kind=kLoop, calls=%fused_computation.6 | loop fusion | flops 65536 | bytes 393220 | tf_op jit(solution)/shard_map/jit(dynamic_index_in_dim)/squeeze | solution.py:370
  3.4 2.9 %collective-permute-start.1 = (bf16[2,2,128,128]{3,2,0,1:T(8,128)(2,1)S(1)}, bf16[2,2,128,128]{3,2,0,1:T(8,128)(2,1)S(1)}, u32[]{:S(2)}, u32[]{:S(2)}) collective-permute-start(bf16[2,2,128,128]{3,2,0,1:T(8,128)(2,1)S(1)} %fusion.1), channel_id=1, source_target_pairs={{0,2},{2,0},{1,3},{3,1},{4,6},{6,4},{5,7},{7,5},{8,10},{10,8},{9,1... | collective-permute-start | bytes 393224 | tf_op jit(solution)/shard_map/ppermute | solution.py:340
  6.3 3.8 %collective-permute-done.1 = bf16[2,2,128,128]{3,2,0,1:T(8,128)(2,1)S(1)} collective-permute-done((bf16[2,2,128,128]{3,2,0,1:T(8,128)(2,1)S(1)}, bf16[2,2,128,128]{3,2,0,1:T(8,128)(2,1)S(1)}, u32[]{:S(2)}, u32[]{:S(2)}) %collective-permute-start.1) | collective-permute-done | bytes 131104 | tf_op jit(solution)/shard_map/ppermute | solution.py:340
  10.1 0.9 %pad_maximum_fusion = bf16[2,2,3,128,128]{4,3,2,0,1:T(8,128)(2,1)S(1)} fusion(bf16[2,2,1,128,128]{4,3,2,0,1:T(8,128)(2,1)S(1)} %bitcast.24, bf16[1,2,2,128,128]{4,3,2,0,1:T(8,128)(2,1)S(1)} %bitcast.19, bf16[1,2,2,128,128]{4,3,2,0,1:T(8,128)(2,1)} %bitcast.17), kind=kLoop, calls=%fused_computation | loop fusion | flops 393216 | bytes 786432 | tf_op jit(solution)/shard_map/concatenate | solution.py:371
  11.1 3.7 %collective-permute-start.2 = (bf16[2,3,128,128]{3,2,1,0:T(8,128)(2,1)S(1)}, bf16[2,3,128,128]{3,2,1,0:T(8,128)(2,1)S(1)}, u32[]{:S(2)}, u32[]{:S(2)}) collective-permute-start(bf16[2,3,128,128]{3,2,1,0:T(8,128)(2,1)S(1)} %get-tuple-element.15), channel_id=1, source_target_pairs={{0,4},{4,8},{8,12},{1,5},{5,9},{9,13},{2,6},{6,10},{10,14},{3,7},{... | collective-permute-start | bytes 589832 | tf_op jit(solution)/shard_map/ppermute | solution.py:344
  14.8 1.3 %collective-permute-start.3 = (bf16[2,3,128,128]{3,2,1,0:T(8,128)(2,1)S(1)}, bf16[2,3,128,128]{3,2,1,0:T(8,128)(2,1)S(1)}, u32[]{:S(2)}, u32[]{:S(2)}) collective-permute-start(bf16[2,3,128,128]{3,2,1,0:T(8,128)(2,1)S(1)} %get-tuple-element.14), channel_id=1, source_target_pairs={{4,0},{8,4},{12,8},{5,1},{9,5},{13,9},{6,2},{10,6},{14,10},{7,3},{... | collective-permute-start | bytes 589832 | tf_op jit(solution)/shard_map/ppermute | solution.py:344
  16.1 0.5 broadcast.3
  16.6 0.7 %reduce.3 = s32[2,2]{1,0:T(2,128)S(1)} reduce(s32[2,2,1]{1,2,0:T(1,128)S(1)} %copy-done.16, s32[]{:T(128)} %broadcast.3), dimensions={2}, to_apply=%param.18.reduce_sub_computation.3 | reduce | bytes 36 | tf_op args[4]
  17.3 0.1 reshape.14.fill_ref
  17.4 1.0 %collective-permute-done.2.refs_1_ = bf16[2,3,128,128]{3,2,1,0:T(8,128)(2,1)S(1)} collective-permute-done((bf16[2,3,128,128]{3,2,1,0:T(8,128)(2,1)S(1)}, bf16[2,3,128,128]{3,2,1,0:T(8,128)(2,1)S(1)}, u32[]{:S(2)}, u32[]{:S(2)}) %collective-permute-start.2) | collective-permute-done | bytes 196640 | tf_op jit(solution)/shard_map/ppermute | solution.py:344
  18.4 4.1 %collective-permute-done.3.refs_2_ = bf16[2,3,128,128]{3,2,1,0:T(8,128)(2,1)S(1)} collective-permute-done((bf16[2,3,128,128]{3,2,1,0:T(8,128)(2,1)S(1)}, bf16[2,3,128,128]{3,2,1,0:T(8,128)(2,1)S(1)}, u32[]{:S(2)}, u32[]{:S(2)}) %collective-permute-start.3) | collective-permute-done | bytes 196640 | tf_op jit(solution)/shard_map/ppermute | solution.py:344
  22.7 16.2 %step.1 = (bf16[2,2,1,128,128]{4,3,2,1,0:T(8,128)(2,1)}, f32[9,2,2,1,128]{4,3,2,1,0:T(1,128)}, f32[16,96]{1,0:T(8,128)S(1)}) custom-call(s32[4]{0:T(128)S(1)} %reshape.14.fill_ref, bf16[2,2,1,128,128]{4,3,2,1,0:T(8,128)(2,1)S(1)} %copy-done.1, bf16[2,2,1,128,128]{4,3,2,1,0:T(8,128)(2,1)S(1)} %bitcast.20, bf16[2,2,128,128]{3,2,1,0:T(8,128)(2,1)S(1)} %copy.20.refs_0_, ...), custom_call_target="tpu_custom_call" | custom-call | tf_op jit(solution)/shard_map/step/pallas_call | solution.py:388
  38.9 1.2 %collective-permute-done.4 = f32[16,96]{1,0:T(8,128)S(1)} collective-permute-done((f32[16,96]{1,0:T(8,128)S(1)}, f32[16,96]{1,0:T(8,128)S(1)}, u32[]{:S(2)}, u32[]{:S(2)}) %collective-permute-start.4) | collective-permute-done | bytes 6176 | tf_op jit(solution)/shard_map/ppermute | solution.py:340
  40.1 1.5 %collective-permute-start.5 = (f32[2,16,96]{2,1,0:T(8,128)S(1)}, f32[2,16,96]{2,1,0:T(8,128)S(1)}, u32[]{:S(2)}, u32[]{:S(2)}) collective-permute-start(f32[2,16,96]{2,1,0:T(8,128)S(1)} %pad_maximum_fusion.2), channel_id=1, source_target_pairs={{0,2},{2,0},{1,3},{3,1},{4,6},{6,4},{5,7},{7,5},{8,10},{10,8},{9,1... | collective-permute-start | bytes 36872 | tf_op jit(solution)/shard_map/ppermute | solution.py:340
  41.6 2.2 %collective-permute-done.5 = f32[2,16,96]{2,1,0:T(8,128)S(1)} collective-permute-done((f32[2,16,96]{2,1,0:T(8,128)S(1)}, f32[2,16,96]{2,1,0:T(8,128)S(1)}, u32[]{:S(2)}, u32[]{:S(2)}) %collective-permute-start.5) | collective-permute-done | bytes 12320 | tf_op jit(solution)/shard_map/ppermute | solution.py:340
  43.8 3.5 %collective-permute-start.6 = (f32[4,16,96]{2,1,0:T(8,128)S(1)}, f32[4,16,96]{2,1,0:T(8,128)S(1)}, u32[]{:S(2)}, u32[]{:S(2)}) collective-permute-start(f32[4,16,96]{2,1,0:T(8,128)S(1)} %pad_maximum_fusion.1.middle_ref), channel_id=1, source_target_pairs={{0,4},{4,8},{8,12},{1,5},{5,9},{9,13},{2,6},{6,10},{10,14},{3,7},{... | collective-permute-start | bytes 73736 | tf_op jit(solution)/shard_map/ppermute | solution.py:344
  47.3 1.3 %collective-permute-start.7 = (f32[4,16,96]{2,1,0:T(8,128)S(1)}, f32[4,16,96]{2,1,0:T(8,128)S(1)}, u32[]{:S(2)}, u32[]{:S(2)}) collective-permute-start(f32[4,16,96]{2,1,0:T(8,128)S(1)} %pad_maximum_fusion.1.middle_ref), channel_id=1, source_target_pairs={{4,0},{8,4},{12,8},{5,1},{9,5},{13,9},{6,2},{10,6},{14,10},{7,3},{... | collective-permute-start | bytes 73736 | tf_op jit(solution)/shard_map/ppermute | solution.py:344
  48.6 0.3 collective-permute-done.6.left_ref
  48.9 4.2 %collective-permute-done.7.right_ref = f32[4,16,96]{2,1,0:T(8,128)S(1)} collective-permute-done((f32[4,16,96]{2,1,0:T(8,128)S(1)}, f32[4,16,96]{2,1,0:T(8,128)S(1)}, u32[]{:S(2)}, u32[]{:S(2)}) %collective-permute-start.7) | collective-permute-done | bytes 24608 | tf_op jit(solution)/shard_map/ppermute | solution.py:344
  53.1 0.6 %copy-done.15 = f32[4,16,96]{2,1,0:T(8,128)} copy-done((f32[4,16,96]{2,1,0:T(8,128)}, f32[4,16,96]{2,1,0:T(8,128)S(1)}, u32[]{:S(2)}) %copy-start.15) | copy-done | bytes 24600
  53.7 2.3 %arrive.1 = (bf16[1,1,1,208,128]{4,3,2,1,0:T(8,128)(2,1)}, f32[9,1,1,1,208]{4,3,2,1,0:T(1,128)}) custom-call(f32[4,16,96]{2,1,0:T(8,128)} %copy-done.13, f32[4,16,96]{2,1,0:T(8,128)} %copy-done.14, f32[4,16,96]{2,1,0:T(8,128)} %copy-done.15, bf16[12,128]{1,0:T(8,128)(2,1)} %encoder_in_ref.1, bf16[2,128,128]{2,1,0:T(8,128)(2,1)} %encoder_w_ref.1), custom_call_target="tpu_custom_call" | custom-call | tf_op jit(solution)/shard_map/arrive/pallas_call | solution.py:431
  (37 shorter events, 0.1 us)
Async XLA Ops:
  0.6 21.9 %copy-start.1 = (bf16[2,2,1,128,128]{4,3,2,1,0:T(8,128)(2,1)S(1)}, bf16[2,2,1,128,128]{4,3,2,1,0:T(8,128)(2,1)}, u32[]{:S(2)}) copy-start(bf16[2,2,1,128,128]{4,3,2,1,0:T(8,128)(2,1)} %own_ref.1) | copy-start | bytes 393220
  0.6 16.0 %copy-start.16 = (s32[2,2,1]{1,2,0:T(1,128)S(1)}, s32[2,2,1]{1,2,0:T(1,128)}, u32[]{:S(2)}) copy-start(s32[2,2,1]{1,2,0:T(1,128)} %param.18) | copy-start | bytes 52
  0.7 21.9 %copy-start.7 = (s32[2,2,1,12,128]{4,2,3,1,0:T(1,128)S(1)}, s32[2,2,1,12,128]{4,2,3,1,0:T(1,128)}, u32[]{:S(2)}) copy-start(s32[2,2,1,12,128]{4,2,3,1,0:T(1,128)} %param.19) | copy-start | bytes 73732
  0.7 21.9 %copy-start = (bf16[2,2,1,12,128,128]{5,4,3,2,1,0:T(8,128)(2,1)S(1)}, bf16[2,2,1,12,128,128]{5,4,3,2,1,0:T(8,128)(2,1)}, u32[]{:S(2)}) copy-start(bf16[2,2,1,12,128,128]{5,4,3,2,1,0:T(8,128)(2,1)} %refs_3_.1) | copy-start | bytes 4718596
  0.7 21.9 %copy-start.9 = (f32[3,2,2,1,128]{4,3,2,1,0:T(1,128)S(1)}, f32[3,2,2,1,128]{4,3,2,1,0:T(1,128)}, u32[]{:S(2)}) copy-start(f32[3,2,2,1,128]{4,3,2,1,0:T(1,128)} %refs_4_.1) | copy-start | bytes 18436
  0.7 21.9 %copy-start.10 = (f32[3,2,2,1,128]{4,3,2,1,0:T(1,128)S(1)}, f32[3,2,2,1,128]{4,3,2,1,0:T(1,128)}, u32[]{:S(2)}) copy-start(f32[3,2,2,1,128]{4,3,2,1,0:T(1,128)} %refs_5_.1) | copy-start | bytes 18436
  0.7 21.9 %copy-start.11 = (s32[2,2,1,128]{3,2,1,0:T(1,128)S(1)}, s32[2,2,1,128]{3,2,1,0:T(1,128)}, u32[]{:S(2)}) copy-start(s32[2,2,1,128]{3,2,1,0:T(1,128)} %refs_7_.1) | copy-start | bytes 6148
  0.7 21.9 %copy-start.3 = (bf16[5,128,128]{2,1,0:T(8,128)(2,1)S(1)}, bf16[5,128,128]{2,1,0:T(8,128)(2,1)}, u32[]{:S(2)}) copy-start(bf16[5,128,128]{2,1,0:T(8,128)(2,1)} %refs_8_.1) | copy-start | bytes 491524
  0.7 21.9 %copy-start.4 = (bf16[256,128]{1,0:T(8,128)(2,1)S(1)}, bf16[256,128]{1,0:T(8,128)(2,1)}, u32[]{:S(2)}) copy-start(bf16[256,128]{1,0:T(8,128)(2,1)} %refs_9_.1) | copy-start | bytes 196612
  0.7 21.9 %copy-start.5 = (bf16[2,128,128]{2,1,0:T(8,128)(2,1)S(1)}, bf16[2,128,128]{2,1,0:T(8,128)(2,1)}, u32[]{:S(2)}) copy-start(bf16[2,128,128]{2,1,0:T(8,128)(2,1)} %refs_10_.1) | copy-start | bytes 196612
  0.7 21.9 %copy-start.6 = (bf16[2,128,128]{2,1,0:T(8,128)(2,1)S(1)}, bf16[2,128,128]{2,1,0:T(8,128)(2,1)}, u32[]{:S(2)}) copy-start(bf16[2,128,128]{2,1,0:T(8,128)(2,1)} %refs_11_.1) | copy-start | bytes 196612
  0.7 21.9 %copy-start.12 = (bf16[3,128]{1,0:T(4,128)(2,1)S(1)}, bf16[3,128]{1,0:T(4,128)(2,1)}, u32[]{:S(2)}) copy-start(bf16[3,128]{1,0:T(4,128)(2,1)} %refs_12_.1) | copy-start | bytes 2308
  0.8 21.9 %copy-start.8 = (bf16[12,128]{1,0:T(8,128)(2,1)S(1)}, bf16[12,128]{1,0:T(8,128)(2,1)}, u32[]{:S(2)}) copy-start(bf16[12,128]{1,0:T(8,128)(2,1)} %encoder_in_ref.1) | copy-start | bytes 9220
  0.8 21.9 %copy-start.2 = (bf16[2,128,128]{2,1,0:T(8,128)(2,1)S(1)}, bf16[2,128,128]{2,1,0:T(8,128)(2,1)}, u32[]{:S(2)}) copy-start(bf16[2,128,128]{2,1,0:T(8,128)(2,1)} %encoder_w_ref.1) | copy-start | bytes 196612
  0.8 1.7 %collective-permute-start = (bf16[2,2,1,128,128]{4,3,1,0,2:T(8,128)(2,1)}, bf16[2,2,1,128,128]{4,3,1,0,2:T(8,128)(2,1)S(1)}, u32[]{:S(2)}, u32[]{:S(2)}) collective-permute-start(bf16[2,2,1,128,128]{4,3,1,0,2:T(8,128)(2,1)} %bitcast.15), channel_id=1, source_target_pairs={{0,1},{1,0},{2,3},{3,2},{4,5},{5,4},{6,7},{7,6},{8,9},{9,8},{10,11... | collective-permute-start | bytes 393224 | tf_op jit(solution)/shard_map/ppermute | solution.py:340
  3.4 6.7 %collective-permute-start.1 = (bf16[2,2,128,128]{3,2,0,1:T(8,128)(2,1)S(1)}, bf16[2,2,128,128]{3,2,0,1:T(8,128)(2,1)S(1)}, u32[]{:S(2)}, u32[]{:S(2)}) collective-permute-start(bf16[2,2,128,128]{3,2,0,1:T(8,128)(2,1)S(1)} %fusion.1), channel_id=1, source_target_pairs={{0,2},{2,0},{1,3},{3,1},{4,6},{6,4},{5,7},{7,5},{8,10},{10,8},{9,1... | collective-permute-start | bytes 393224 | tf_op jit(solution)/shard_map/ppermute | solution.py:340
  11.1 7.4 %collective-permute-start.2 = (bf16[2,3,128,128]{3,2,1,0:T(8,128)(2,1)S(1)}, bf16[2,3,128,128]{3,2,1,0:T(8,128)(2,1)S(1)}, u32[]{:S(2)}, u32[]{:S(2)}) collective-permute-start(bf16[2,3,128,128]{3,2,1,0:T(8,128)(2,1)S(1)} %get-tuple-element.15), channel_id=1, source_target_pairs={{0,4},{4,8},{8,12},{1,5},{5,9},{9,13},{2,6},{6,10},{10,14},{3,7},{... | collective-permute-start | bytes 589832 | tf_op jit(solution)/shard_map/ppermute | solution.py:344
  14.8 7.7 %collective-permute-start.3 = (bf16[2,3,128,128]{3,2,1,0:T(8,128)(2,1)S(1)}, bf16[2,3,128,128]{3,2,1,0:T(8,128)(2,1)S(1)}, u32[]{:S(2)}, u32[]{:S(2)}) collective-permute-start(bf16[2,3,128,128]{3,2,1,0:T(8,128)(2,1)S(1)} %get-tuple-element.14), channel_id=1, source_target_pairs={{4,0},{8,4},{12,8},{5,1},{9,5},{13,9},{6,2},{10,6},{14,10},{7,3},{... | collective-permute-start | bytes 589832 | tf_op jit(solution)/shard_map/ppermute | solution.py:344
  38.9 1.2 %collective-permute-start.4 = (f32[16,96]{1,0:T(8,128)S(1)}, f32[16,96]{1,0:T(8,128)S(1)}, u32[]{:S(2)}, u32[]{:S(2)}) collective-permute-start(f32[16,96]{1,0:T(8,128)S(1)} %get-tuple-element.11), channel_id=1, source_target_pairs={{0,1},{1,0},{2,3},{3,2},{4,5},{5,4},{6,7},{7,6},{8,9},{9,8},{10,11... | collective-permute-start | bytes 18440 | tf_op jit(solution)/shard_map/ppermute | solution.py:340
  40.1 3.7 %collective-permute-start.5 = (f32[2,16,96]{2,1,0:T(8,128)S(1)}, f32[2,16,96]{2,1,0:T(8,128)S(1)}, u32[]{:S(2)}, u32[]{:S(2)}) collective-permute-start(f32[2,16,96]{2,1,0:T(8,128)S(1)} %pad_maximum_fusion.2), channel_id=1, source_target_pairs={{0,2},{2,0},{1,3},{3,1},{4,6},{6,4},{5,7},{7,5},{8,10},{10,8},{9,1... | collective-permute-start | bytes 36872 | tf_op jit(solution)/shard_map/ppermute | solution.py:340
  43.8 9.3 %copy-start.13 = (f32[4,16,96]{2,1,0:T(8,128)}, f32[4,16,96]{2,1,0:T(8,128)S(1)}, u32[]{:S(2)}) copy-start(f32[4,16,96]{2,1,0:T(8,128)S(1)} %pad_maximum_fusion.1.middle_ref) | copy-start | bytes 73732
  43.8 5.1 %collective-permute-start.6 = (f32[4,16,96]{2,1,0:T(8,128)S(1)}, f32[4,16,96]{2,1,0:T(8,128)S(1)}, u32[]{:S(2)}, u32[]{:S(2)}) collective-permute-start(f32[4,16,96]{2,1,0:T(8,128)S(1)} %pad_maximum_fusion.1.middle_ref), channel_id=1, source_target_pairs={{0,4},{4,8},{8,12},{1,5},{5,9},{9,13},{2,6},{6,10},{10,14},{3,7},{... | collective-permute-start | bytes 73736 | tf_op jit(solution)/shard_map/ppermute | solution.py:344
  47.3 5.8 %collective-permute-start.7 = (f32[4,16,96]{2,1,0:T(8,128)S(1)}, f32[4,16,96]{2,1,0:T(8,128)S(1)}, u32[]{:S(2)}, u32[]{:S(2)}) collective-permute-start(f32[4,16,96]{2,1,0:T(8,128)S(1)} %pad_maximum_fusion.1.middle_ref), channel_id=1, source_target_pairs={{4,0},{8,4},{12,8},{5,1},{9,5},{13,9},{6,2},{10,6},{14,10},{7,3},{... | collective-permute-start | bytes 73736 | tf_op jit(solution)/shard_map/ppermute | solution.py:344
  48.9 4.2 %copy-start.14 = (f32[4,16,96]{2,1,0:T(8,128)}, f32[4,16,96]{2,1,0:T(8,128)S(1)}, u32[]{:S(2)}) copy-start(f32[4,16,96]{2,1,0:T(8,128)S(1)} %collective-permute-done.6.left_ref) | copy-start | bytes 73732
  (1 other events, 0.6 us)

commit v2 on v1

--- a/solution.py
+++ b/solution.py
@@ -23,6 +23,12 @@
     )
 
 
+def dot_tn(left, right):
+    return lax.dot_general(
+        left, right, (((0,), (0,)), ((), ())), preferred_element_type=F32
+    )
+
+
 def relu16(values):
     return jnp.maximum(values, 0.0).astype(BF16)
 
@@ -52,7 +58,14 @@
     return weights.astype(F32).T.astype(BF16)
 
 
-def encode(state, encoder_in, first, second, extent):
+def norm_lanes(values):
+    scale = 1.0 / values.shape[1]
+    centred = values - jnp.sum(values, axis=1, keepdims=True) * scale
+    spread = jnp.sum(centred * centred, axis=1, keepdims=True) * scale
+    return centred * lax.rsqrt(spread + 1e-05)
+
+
+def encode(state, mask, encoder_in, encoder_w, extent):
     width = state.shape[1]
     position = state[0:3]
     row = lax.broadcasted_iota(jnp.int32, (3, width), 0)
@@ -66,21 +79,24 @@
         ],
         axis=0,
     )
-    inward = jnp.concatenate([encoder_in.astype(F32), jnp.zeros((4, encoder_in.shape[1]), F32)], axis=0)
-    inward = jnp.concatenate([inward, inward, inward], axis=0).T.astype(BF16)
-    hidden = relu16(dot(inward, jnp.concatenate(thirds(features), axis=0)))
-    hidden = relu16(dot(first, hidden))
-    return norm_rows(dot(second, hidden))
+    inward = jnp.concatenate(
+        [encoder_in.astype(F32), jnp.zeros((4, encoder_in.shape[1]), F32)], axis=0
+    ).astype(BF16)
+    inward = jnp.concatenate([inward, inward, inward], axis=0)
+    hidden = relu16(dot_tn(jnp.concatenate(thirds(features), axis=0), inward))
+    hidden = relu16(dot(hidden, encoder_w[0]))
+    column = jnp.broadcast_to(mask, (8, width)).T[:, 0:1]
+    return (norm_lanes(dot(hidden, encoder_w[1])) * column).astype(BF16)
 
 
 def step_kernel(
     sizes,
     fill_ref,
     own_ref,
-    zed_ref,
     side_refs,
-    left_ref,
-    right_ref,
+    even_ref,
+    odd_ref,
+    zed_refs,
     edge_ref,
     positions_ref,
     velocity_ref,
@@ -120,21 +136,23 @@
         row_count = 4
         own_rows = (1, 2)
         outer = {0: 0, 3: 1}
-    for ex in range(4):
-        for row in range(row_count):
-            if ex == 0:
-                pair = (left_ref[0, row], left_ref[1, row])
-            elif ex == 3:
-                pair = (right_ref[0, row], right_ref[1, row])
-            elif row in own_rows:
+    own_zed, side_zeds, even_zed, odd_zed = zed_refs
+    parity = index_x & 1
+
+    def far(place, here, beside):
+        pair = jnp.concatenate([here, beside], axis=0)
+        far_ref[place] = dot_nt(far_t, pair).astype(BF16)
+
+    for row in range(row_count):
+        for ex in (1, 2):
+            if row in own_rows:
                 b = own_rows.index(row)
-                pair = (own_ref[ex - 1, b, 0], zed_ref[ex - 1, b, 0])
+                far(ex * row_count + row, own_ref[ex - 1, b, 0], own_zed[ex - 1, b, 0])
             else:
-                side = side_refs[outer[row]]
-                pair = (side[0, ex - 1], side[1, ex - 1])
-            far_ref[ex * row_count + row] = dot_nt(
-                far_t, jnp.concatenate(pair, axis=0)
-            ).astype(BF16)
+                side = outer[row]
+                far(ex * row_count + row, side_refs[side][ex - 1], side_zeds[side][ex - 1])
+        far(3 * (1 - parity) * row_count + row, even_ref[row], even_zed[row])
+        far(3 * parity * row_count + row, odd_ref[row], odd_zed[row])
 
     lane = lax.broadcasted_iota(jnp.int32, (1, slots), 1)
     key_rows = lax.broadcasted_iota(jnp.int32, (2 * slots, 2 * slots), 0)
@@ -192,7 +210,7 @@
                 hidden = relu16(dot(middle_t, hidden))
                 message = norm_rows(dot(final_t, hidden))
                 total = total + message[:, :slots] + message[:, slots:]
-            total = jnp.where(lane < fill_ref[a * 2 + b], total, 0.0)
+            total = jnp.where(lane < fill_ref[a, 0, b], total, 0.0)
             gather_ref[a * 2 + b] = total.astype(BF16)
 
     cells = [(a, b) for a in range(2) for b in range(2)]
@@ -215,17 +233,14 @@
 
     owner = jnp.concatenate([owners_ref[a, b] for a, b in cells], axis=1)
     alive = jnp.concatenate(
-        [(lane < fill_ref[i]).astype(jnp.int32) for i in range(4)], axis=1
+        [(lane < fill_ref[a, 0, b]).astype(jnp.int32) for a, b in cells], axis=1
     )
     own_block = (index_x * count_y + index_y) * count_z + index_z
     stays = jnp.where((alive == 1) & (owner == own_block), 1.0, 0.0)
     moving = jnp.where((alive == 1) & (owner != own_block), 1, 0)
 
     extent = (2.0 * count_x, 2.0 * count_y, 1.0 * count_z)
-    latents = encode(
-        state, encoder_in_ref[...], flip(encoder_w_ref[0]), flip(encoder_w_ref[1]), extent
-    )
-    latents = (latents * stays).T.astype(BF16)
+    latents = encode(state, stays, encoder_in_ref[...], encoder_w_ref[...], extent)
     kept = state * stays
     for i, (a, b) in enumerate(cells):
         kept_latent_ref[a, b, 0] = latents[i * slots : (i + 1) * slots]
@@ -277,9 +292,12 @@
 
 def arrive_kernel(
     sizes,
-    middle_ref,
-    left_ref,
-    right_ref,
+    own_ref,
+    even_ref,
+    odd_ref,
+    own_zed,
+    even_zed,
+    odd_zed,
     encoder_in_ref,
     encoder_w_ref,
     arrived_latent_ref,
@@ -287,20 +305,32 @@
 ):
     count_x, count_y, count_z = sizes
     fold_y = count_y == 2
+    index_x = lax.axis_index("gx")
     index_y = lax.axis_index("gy")
     index_z = lax.axis_index("gz")
     options_y = 2 if fold_y else 3
-    lanes = middle_ref.shape[-1]
+    lanes = own_ref.shape[-1]
     group = lax.broadcasted_iota(jnp.int32, (ROWS, lanes), 1) >> 3
+    even = (index_x & 1) == 0
     found = jnp.zeros((ROWS, lanes), F32)
-    for source_x, ref in ((-1, left_ref), (0, middle_ref), (1, right_ref)):
+    for source_x in (-1, 0, 1):
         for from_y in range(options_y):
             for from_z in range(2):
                 if source_x == 0 and from_y == 0 and from_z == 0:
                     continue
+                own, first, second = (own_ref, even_ref, odd_ref) if from_z == 0 else (own_zed, even_zed, odd_zed)
                 side_y = from_y if fold_y or from_y == 0 else 3 - from_y
                 target = ((1 - source_x) * options_y + side_y) * 2 + from_z
-                found = jnp.where(group == target, ref[from_y * 2 + from_z], found)
+                if source_x == 0:
+                    tile = own[from_y]
+                    there = group == target
+                elif source_x == -1:
+                    tile = jnp.where(even, second[from_y], first[from_y])
+                    there = (group == target) & (index_x > 0)
+                else:
+                    tile = jnp.where(even, first[from_y], second[from_y])
+                    there = (group == target) & (index_x < count_x - 1)
+                found = jnp.where(there, tile, found)
     out_lanes = arrived_state_ref.shape[-1]
     spread_shape = (lanes, out_lanes)
     line = lax.broadcasted_iota(jnp.int32, spread_shape, 0)
@@ -325,10 +355,9 @@
     for j in range(9):
         arrived_state_ref[j, 0, 0] = arrived[j : j + 1]
     extent = (2.0 * count_x, 2.0 * count_y, 1.0 * count_z)
-    latents = encode(
-        arrived[:9], encoder_in_ref[...], flip(encoder_w_ref[0]), flip(encoder_w_ref[1]), extent
-    )
-    arrived_latent_ref[0, 0, 0] = (latents * arrived[9:10]).T.astype(BF16)
+    arrived_latent_ref[0, 0, 0] = encode(
+        arrived[:9], arrived[9:10], encoder_in_ref[...], encoder_w_ref[...], extent
+    )
 
 
 def along(count):
@@ -342,6 +371,19 @@
 
 def shift(values, axis, way):
     return lax.ppermute(values, axis, along(lax.axis_size(axis))[way])
+
+
+def swap_x(values, first):
+    count = lax.axis_size("gx")
+    pairs = []
+    for x in range(count):
+        partner = x + 1 if (x - first) % 2 == 0 else x - 1
+        for z in range(2):
+            if 0 <= partner < count:
+                pairs.append((x * 2 + z, partner * 2 + z))
+            else:
+                pairs.append((x * 2 + z, x * 2 + 1 - z))
+    return lax.ppermute(values, ("gx", "gz"), pairs)
 
 
 def body(
@@ -363,27 +405,46 @@
     sizes = tuple(lax.axis_size(axis) for axis in ("gx", "gy", "gz"))
     fold_y = sizes[1] == 2
     slots, width = node_latent.shape[-2:]
-    zed = swap(node_latent, "gz")
-    both = jnp.stack([node_latent[:, :, 0], zed[:, :, 0]], axis=0)
+    parity = lax.axis_index("gx") & 1
+    cells = node_latent[:, :, 0]
     if fold_y:
         inner = 1 - lax.axis_index("gy")
-        sides = [swap(lax.dynamic_index_in_dim(both, inner, 2, keepdims=False), "gy")]
-        layers = jnp.concatenate([both, sides[0][:, :, None]], axis=2)
+        sides = [swap(lax.dynamic_index_in_dim(cells, inner, 1, keepdims=False), "gy")]
+        layers = [cells, sides[0][:, None]]
     else:
-        sides = [shift(both[:, :, 1], "gy", 0), shift(both[:, :, 0], "gy", 1)]
-        layers = jnp.concatenate([sides[0][:, :, None], both, sides[1][:, :, None]], axis=2)
-    left = shift(layers[:, 1], "gx", 0)
-    right = shift(layers[:, 0], "gx", 1)
+        sides = [shift(cells[:, 1], "gy", 0), shift(cells[:, 0], "gy", 1)]
+        layers = [sides[0][:, None], cells, sides[1][:, None]]
+
+    def layer(a):
+        return jnp.concatenate(
+            [lax.dynamic_index_in_dim(part, a, 0, keepdims=False) for part in layers], axis=0
+        )
+
+    even = swap_x(layer(1 - parity), 0)
+    odd = swap_x(layer(parity), 1)
+    halo = [node_latent, *sides, even, odd]
+    halo = halo + [swap(part, "gz") for part in halo]
 
     options_y = 2 if fold_y else 3
     lanes = 3 * options_y * 2 * CAP
-    rows = layers.shape[2]
+    rows = 3 if fold_y else 4
     vmem = pl.BlockSpec(memory_space=pltpu.VMEM)
     smem = pl.BlockSpec(memory_space=pltpu.SMEM)
-    side_count = len(sides)
-
-    def step(fill_ref, own_ref, zed_ref, *refs):
-        step_kernel(sizes, fill_ref, own_ref, zed_ref, refs[:side_count], *refs[side_count:])
+    count = len(sides)
+
+    def step(fill_ref, *refs):
+        own_ref, *side_refs, even_ref, odd_ref = refs[: count + 3]
+        own_zed, *side_zeds, even_zed, odd_zed = refs[count + 3 : 2 * count + 6]
+        step_kernel(
+            sizes,
+            fill_ref,
+            own_ref,
+            side_refs,
+            even_ref,
+            odd_ref,
+            (own_zed, side_zeds, even_zed, odd_zed),
+            *refs[2 * count + 6 :],
+        )
 
     kept_latent, kept_state, bucket = pl.pallas_call(
         step,
@@ -392,7 +453,7 @@
             jax.ShapeDtypeStruct((9,) + node_latent.shape[:4], F32),
             jax.ShapeDtypeStruct((ROWS, lanes), F32),
         ),
-        in_specs=[smem] + [vmem] * (17 + side_count - 1),
+        in_specs=[smem] + [vmem] * (len(halo) + 12),
         out_specs=(vmem, vmem, vmem),
         scratch_shapes=[
             pltpu.VMEM((4 * rows, width, 2 * slots), BF16),
@@ -401,12 +462,8 @@
         compiler_params=pltpu.CompilerParams(vmem_limit_bytes=40 * 1024 * 1024),
         name="step",
     )(
-        fill.reshape(-1),
-        node_latent,
-        zed,
-        *sides,
-        left,
-        right,
+        jnp.transpose(fill, (0, 2, 1)),
+        *halo,
         edge_latent,
         positions,
         velocity,
@@ -421,23 +478,22 @@
         encoder_weights,
     )
 
-    tiles = jnp.stack([bucket, swap(bucket, "gz")], axis=0)
     if fold_y:
-        tiles = jnp.concatenate([tiles, swap(tiles, "gy")], axis=0)
+        tiles = jnp.stack([bucket, swap(bucket, "gy")], axis=0)
     else:
-        tiles = jnp.concatenate([tiles, shift(tiles, "gy", 0), shift(tiles, "gy", 1)], axis=0)
-    tiles_left = shift(tiles, "gx", 0)
-    tiles_right = shift(tiles, "gx", 1)
+        tiles = jnp.stack([bucket, shift(bucket, "gy", 0), shift(bucket, "gy", 1)], axis=0)
+    tiles = [tiles, swap_x(tiles, 0), swap_x(tiles, 1)]
+    tiles = tiles + [swap(part, "gz") for part in tiles]
     arrived_latent, arrived_state = pl.pallas_call(
         functools.partial(arrive_kernel, sizes),
         out_shape=(
             jax.ShapeDtypeStruct((1, 1, 1, 26 * CAP, width), BF16),
             jax.ShapeDtypeStruct((9, 1, 1, 1, 26 * CAP), F32),
         ),
-        in_specs=[vmem] * 5,
+        in_specs=[vmem] * 8,
         out_specs=(vmem, vmem),
         name="arrive",
-    )(tiles, tiles_left, tiles_right, encoder_in, encoder_weights)
+    )(*tiles, encoder_in, encoder_weights)
     return kept_latent, kept_state, arrived_latent, arrived_state
 
 

time: 56.4 us -> 56.3 us (level)
  local copies, waits for them, and re-layouts: 1.31 us -> 13.8 us
  waiting for transfers between devices: 18.1 us -> 8.69 us
  other arithmetic: 2.48 us -> 0.03 us
  starting transfers between devices: 14.7 us -> 13.5 us
    unnamed x35 -> x40, local copies, waits for them, and re-layouts: 1.19 us -> 12 us
    ppermute x4, waiting for transfers between devices: 9.67 us -> 3.21 us  [swap_x(): return lax.ppermute(values, ('gx', 'gz'), pairs)]
    ppermute x4 -> x9, waiting for transfers between devices: 8.42 us -> 5.48 us  [swap(): return lax.ppermute(values, axis, [(0, 1), (1, 0)])]
    ppermute x4, starting transfers between devices: 9.8 us -> 7.14 us  [swap_x(): return lax.ppermute(values, ('gx', 'gz'), pairs)]
    squeeze x1 -> x3, local copies, waits for them, and re-layouts: 0.03 us -> 1.74 us  [the longest x2 0.89 us: layer(): lax.dynamic_index_in_dim(part, a, 0, keepdims=False)]
    ppermute x4 -> x9, starting transfers between devices: 4.93 us -> 6.39 us  [swap(): return lax.ppermute(values, axis, [(0, 1), (1, 0)])]
    concatenate x2, other arithmetic: 0.95 us -> 0.02 us  [layer(): jnp.concatenate([lax.dynamic_index_in_dim(part, a, 0, keepdims=False) for...]
    squeeze x1 -> x0, other arithmetic: 0.85 us -> none  [body(): lax.dynamic_index_in_dim(both, inner, 2, keepdims=False)]
  transfers between devices with their start and end apart: 8 -> 13, of which waited for: 8 -> 6; matrix products, arithmetic and copies ran while one was open for 2% -> 2% of each run, Pallas kernels for 0% -> 0%
where the time goes in v2:
time: 56.3 us; the launch traced here: 55.5 us
  Pallas kernels  18.8 us (33%)
  local copies, waits for them, and re-layouts  13.8 us (25%)
  starting transfers between devices  13.5 us (24%)
  waiting for transfers between devices  8.69 us (15%)
  between operations  0.76 us (1%)
    pallas_call x1, Pallas kernels, body(): pl.pallas_call(step, out_shape=(jax.ShapeDtypeStruct(node_latent.shape, B...  16.3 us
    unnamed x40, local copies, waits for them, and re-layouts  12 us
    ppermute x4, starting transfers between devices, swap_x(): return lax.ppermute(values, ('gx', 'gz'), pairs)  7.14 us
    ppermute x9, starting transfers between devices, swap(): return lax.ppermute(values, axis, [(0, 1), (1, 0)])  6.39 us
    ppermute x9, waiting for transfers between devices, swap(): return lax.ppermute(values, axis, [(0, 1), (1, 0)])  5.48 us
    ppermute x4, waiting for transfers between devices, swap_x(): return lax.ppermute(values, ('gx', 'gz'), pairs)  3.21 us
    pallas_call x1, Pallas kernels, body(): pl.pallas_call(functools.partial(arrive_kernel, sizes), out_shape=(jax.Sh...  2.42 us
  transfers between devices with their start and end apart: 13, of which 6 were waited for; matrix products, arithmetic and copies ran while one was open for 2% of the time, Pallas kernels for 0%

profile of v2, /device:TPU:0, one launch (start us, length us, event | category | flops | bytes accessed | tf_op | source)
XLA Modules:
  0.0 55.5 jit_solution(10836455316738259671)
XLA Ops:
  0.6 0.9 %dynamic-slice_bitcast_fusion.2 = bf16[2,128,128]{2,1,0:T(8,128)(2,1)S(1)} fusion(bf16[2,2,1,128,128]{4,3,2,1,0:T(8,128)(2,1)} %refs_0_.1, s32[]{:T(128)S(6)} %select_n.14), kind=kLoop, calls=%fused_computation.4 | loop fusion | bytes 131076 | tf_op jit(solution)/shard_map/jit(dynamic_index_in_dim)/squeeze | solution.py:412
  1.5 2.9 %collective-permute-start = (bf16[2,128,128]{2,1,0:T(8,128)(2,1)S(1)}, bf16[2,128,128]{2,1,0:T(8,128)(2,1)S(1)}, u32[]{:S(2)}, u32[]{:S(2)}) collective-permute-start(bf16[2,128,128]{2,1,0:T(8,128)(2,1)S(1)} %dynamic-slice_bitcast_fusion.2), channel_id=1, source_target_pairs={{0,2},{2,0},{1,3},{3,1},{4,6},{6,4},{5,7},{7,5},{8,10},{10,8},{9,1... | collective-permute-start | bytes 196616 | tf_op jit(solution)/shard_map/ppermute | solution.py:369
  4.4 0.9 %dynamic-slice_bitcast_fusion = (bf16[2,128,128]{2,1,0:T(8,128)(2,1)S(1)}, bf16[2,128,128]{2,1,0:T(8,128)(2,1)S(1)}) fusion(bf16[2,2,1,128,128]{4,3,2,1,0:T(8,128)(2,1)} %refs_0_.1, s32[]{:T(128)S(6)} %select_n.16, s32[]{:T(128)S(6)} %select_n.15), kind=kLoop, calls=%fused_computation.2 | loop fusion | bytes 262152 | tf_op jit(solution)/shard_map/jit(dynamic_index_in_dim)/squeeze | solution.py:420
  5.3 1.4 %collective-permute-done.refs_1_ = bf16[2,128,128]{2,1,0:T(8,128)(2,1)S(1)} collective-permute-done((bf16[2,128,128]{2,1,0:T(8,128)(2,1)S(1)}, bf16[2,128,128]{2,1,0:T(8,128)(2,1)S(1)}, u32[]{:S(2)}, u32[]{:S(2)}) %collective-permute-start) | collective-permute-done | bytes 65568 | tf_op jit(solution)/shard_map/ppermute | solution.py:369
  6.7 2.2 %collective-permute-start.1 = (bf16[3,128,128]{2,1,0:T(8,128)(2,1)S(1)}, bf16[3,128,128]{2,1,0:T(8,128)(2,1)S(1)}, u32[]{:S(2)}, u32[]{:S(2)}) collective-permute-start(bf16[3,128,128]{2,1,0:T(8,128)(2,1)S(1)} %pad_maximum_fusion), channel_id=1, source_target_pairs={{0,4},{1,5},{4,0},{5,1},{8,12},{9,13},{12,8},{13,9},{2,6},{3,7},{6... | collective-permute-start | bytes 294920 | tf_op jit(solution)/shard_map/ppermute | solution.py:386
  9.5 2.0 %collective-permute-done.1.refs_2_ = bf16[3,128,128]{2,1,0:T(8,128)(2,1)S(1)} collective-permute-done((bf16[3,128,128]{2,1,0:T(8,128)(2,1)S(1)}, bf16[3,128,128]{2,1,0:T(8,128)(2,1)S(1)}, u32[]{:S(2)}, u32[]{:S(2)}) %collective-permute-start.1) | collective-permute-done | bytes 98336 | tf_op jit(solution)/shard_map/ppermute | solution.py:386
  12.0 1.3 %collective-permute-done.4.refs_5_ = bf16[2,128,128]{2,1,0:T(8,128)(2,1)S(1)} collective-permute-done((bf16[2,128,128]{2,1,0:T(8,128)(2,1)S(1)}, bf16[2,128,128]{2,1,0:T(8,128)(2,1)S(1)}, u32[]{:S(2)}, u32[]{:S(2)}) %collective-permute-start.4) | collective-permute-done | bytes 65568 | tf_op jit(solution)/shard_map/ppermute | solution.py:369
  13.3 1.4 %copy-done = bf16[2,2,1,12,128,128]{5,4,3,2,1,0:T(8,128)(2,1)S(1)} copy-done((bf16[2,2,1,12,128,128]{5,4,3,2,1,0:T(8,128)(2,1)S(1)}, bf16[2,2,1,12,128,128]{5,4,3,2,1,0:T(8,128)(2,1)}, u32[]{:S(2)}) %copy-start) | copy-done | bytes 1572888
  14.7 0.9 %copy-done.1 = bf16[2,2,1,128,128]{4,3,2,1,0:T(8,128)(2,1)S(1)} copy-done((bf16[2,2,1,128,128]{4,3,2,1,0:T(8,128)(2,1)S(1)}, bf16[2,2,1,128,128]{4,3,2,1,0:T(8,128)(2,1)}, u32[]{:S(2)}) %copy-start.1) | copy-done | bytes 131096
  15.6 0.8 %copy-done.2 = bf16[2,128,128]{2,1,0:T(8,128)(2,1)S(1)} copy-done((bf16[2,128,128]{2,1,0:T(8,128)(2,1)S(1)}, bf16[2,128,128]{2,1,0:T(8,128)(2,1)}, u32[]{:S(2)}) %copy-start.2) | copy-done | bytes 65560
  16.4 0.9 %copy-done.3 = bf16[5,128,128]{2,1,0:T(8,128)(2,1)S(1)} copy-done((bf16[5,128,128]{2,1,0:T(8,128)(2,1)S(1)}, bf16[5,128,128]{2,1,0:T(8,128)(2,1)}, u32[]{:S(2)}) %copy-start.3) | copy-done | bytes 163864
  17.3 0.8 %copy-done.4 = bf16[256,128]{1,0:T(8,128)(2,1)S(1)} copy-done((bf16[256,128]{1,0:T(8,128)(2,1)S(1)}, bf16[256,128]{1,0:T(8,128)(2,1)}, u32[]{:S(2)}) %copy-start.4) | copy-done | bytes 65560
  18.2 0.8 %copy-done.5 = bf16[2,128,128]{2,1,0:T(8,128)(2,1)S(1)} copy-done((bf16[2,128,128]{2,1,0:T(8,128)(2,1)S(1)}, bf16[2,128,128]{2,1,0:T(8,128)(2,1)}, u32[]{:S(2)}) %copy-start.5) | copy-done | bytes 65560
  19.0 0.8 %copy-done.6 = bf16[2,128,128]{2,1,0:T(8,128)(2,1)S(1)} copy-done((bf16[2,128,128]{2,1,0:T(8,128)(2,1)S(1)}, bf16[2,128,128]{2,1,0:T(8,128)(2,1)}, u32[]{:S(2)}) %copy-start.6) | copy-done | bytes 65560
  19.8 0.7 %copy-done.7 = s32[2,2,1,12,128]{4,2,3,1,0:T(1,128)S(1)} copy-done((s32[2,2,1,12,128]{4,2,3,1,0:T(1,128)S(1)}, s32[2,2,1,12,128]{4,2,3,1,0:T(1,128)}, u32[]{:S(2)}) %copy-start.7) | copy-done | bytes 24600
  21.3 0.7 %copy-done.9 = f32[3,2,2,1,128]{4,3,2,1,0:T(1,128)S(1)} copy-done((f32[3,2,2,1,128]{4,3,2,1,0:T(1,128)S(1)}, f32[3,2,2,1,128]{4,3,2,1,0:T(1,128)}, u32[]{:S(2)}) %copy-start.9) | copy-done | bytes 6168
  22.0 0.7 %copy-done.10 = f32[3,2,2,1,128]{4,3,2,1,0:T(1,128)S(1)} copy-done((f32[3,2,2,1,128]{4,3,2,1,0:T(1,128)S(1)}, f32[3,2,2,1,128]{4,3,2,1,0:T(1,128)}, u32[]{:S(2)}) %copy-start.10) | copy-done | bytes 6168
  24.7 16.3 %step.1 = (bf16[2,2,1,128,128]{4,3,2,1,0:T(8,128)(2,1)}, f32[9,2,2,1,128]{4,3,2,1,0:T(1,128)}, f32[16,96]{1,0:T(8,128)S(1)}) custom-call(s32[2,1,2]{2,1,0:T(1,128)S(1)} %bitcast.14, bf16[2,2,1,128,128]{4,3,2,1,0:T(8,128)(2,1)S(1)} %copy-done.1, bf16[2,128,128]{2,1,0:T(8,128)(2,1)S(1)} %collective-permute-done.refs_1_, ...), custom_call_target="tpu_custom_call" | custom-call | tf_op jit(solution)/shard_map/step/pallas_call | solution.py:449
  41.0 1.9 %collective-permute-start.7 = (f32[16,96]{1,0:T(8,128)S(1)}, f32[16,96]{1,0:T(8,128)S(1)}, u32[]{:S(2)}, u32[]{:S(2)}) collective-permute-start(f32[16,96]{1,0:T(8,128)S(1)} %get-tuple-element.11), channel_id=1, source_target_pairs={{0,2},{2,0},{1,3},{3,1},{4,6},{6,4},{5,7},{7,5},{8,10},{10,8},{9,1... | collective-permute-start | bytes 18440 | tf_op jit(solution)/shard_map/ppermute | solution.py:369
  43.0 1.7 %collective-permute-done.7 = f32[16,96]{1,0:T(8,128)S(1)} collective-permute-done((f32[16,96]{1,0:T(8,128)S(1)}, f32[16,96]{1,0:T(8,128)S(1)}, u32[]{:S(2)}, u32[]{:S(2)}) %collective-permute-start.7) | collective-permute-done | bytes 6176 | tf_op jit(solution)/shard_map/ppermute | solution.py:369
  44.7 4.9 %collective-permute-start.8 = (f32[2,16,96]{2,1,0:T(8,128)S(1)}, f32[2,16,96]{2,1,0:T(8,128)S(1)}, u32[]{:S(2)}, u32[]{:S(2)}) collective-permute-start(f32[2,16,96]{2,1,0:T(8,128)S(1)} %pad_maximum_fusion.2.own_ref), channel_id=1, source_target_pairs={{0,4},{1,5},{4,0},{5,1},{8,12},{9,13},{12,8},{13,9},{2,6},{3,7},{6... | collective-permute-start | bytes 36872 | tf_op jit(solution)/shard_map/ppermute | solution.py:386
  50.1 1.2 %collective-permute-done.8.even_ref = f32[2,16,96]{2,1,0:T(8,128)S(1)} collective-permute-done((f32[2,16,96]{2,1,0:T(8,128)S(1)}, f32[2,16,96]{2,1,0:T(8,128)S(1)}, u32[]{:S(2)}, u32[]{:S(2)}) %collective-permute-start.8) | collective-permute-done | bytes 12320 | tf_op jit(solution)/shard_map/ppermute | solution.py:386
  51.3 1.1 %collective-permute-done.11.even_zed = f32[2,16,96]{2,1,0:T(8,128)S(1)} collective-permute-done((f32[2,16,96]{2,1,0:T(8,128)S(1)}, f32[2,16,96]{2,1,0:T(8,128)S(1)}, u32[]{:S(2)}, u32[]{:S(2)}) %collective-permute-start.11) | collective-permute-done | bytes 12320 | tf_op jit(solution)/shard_map/ppermute | solution.py:369
  53.1 2.4 %arrive.1 = (bf16[1,1,1,208,128]{4,3,2,1,0:T(8,128)(2,1)}, f32[9,1,1,1,208]{4,3,2,1,0:T(1,128)}) custom-call(f32[2,16,96]{2,1,0:T(8,128)} %copy-done.14, f32[2,16,96]{2,1,0:T(8,128)} %copy-done.16, f32[2,16,96]{2,1,0:T(8,128)} %copy-done.15, f32[2,16,96]{2,1,0:T(8,128)} %copy-done.17, f32[2,16,96]{2,1,0:T(8,128)} %copy-done.19, f32[2,16,96]{2,1,0:T(8,128)} %copy-done.18, ...), custom_call_target="tpu_custom_call" | custom-call | tf_op jit(solution)/shard_map/arrive/pallas_call | solution.py:487
  (50 shorter events, 5.0 us)
Async XLA Ops:
  1.5 5.2 %collective-permute-start = (bf16[2,128,128]{2,1,0:T(8,128)(2,1)S(1)}, bf16[2,128,128]{2,1,0:T(8,128)(2,1)S(1)}, u32[]{:S(2)}, u32[]{:S(2)}) collective-permute-start(bf16[2,128,128]{2,1,0:T(8,128)(2,1)S(1)} %dynamic-slice_bitcast_fusion.2), channel_id=1, source_target_pairs={{0,2},{2,0},{1,3},{3,1},{4,6},{6,4},{5,7},{7,5},{8,10},{10,8},{9,1... | collective-permute-start | bytes 196616 | tf_op jit(solution)/shard_map/ppermute | solution.py:369
  6.7 4.8 %collective-permute-start.1 = (bf16[3,128,128]{2,1,0:T(8,128)(2,1)S(1)}, bf16[3,128,128]{2,1,0:T(8,128)(2,1)S(1)}, u32[]{:S(2)}, u32[]{:S(2)}) collective-permute-start(bf16[3,128,128]{2,1,0:T(8,128)(2,1)S(1)} %pad_maximum_fusion), channel_id=1, source_target_pairs={{0,4},{1,5},{4,0},{5,1},{8,12},{9,13},{12,8},{13,9},{2,6},{3,7},{6... | collective-permute-start | bytes 294920 | tf_op jit(solution)/shard_map/ppermute | solution.py:386
  8.9 2.6 %collective-permute-start.2 = (bf16[3,128,128]{2,1,0:T(8,128)(2,1)S(1)}, bf16[3,128,128]{2,1,0:T(8,128)(2,1)S(1)}, u32[]{:S(2)}, u32[]{:S(2)}) collective-permute-start(bf16[3,128,128]{2,1,0:T(8,128)(2,1)S(1)} %pad_maximum_fusion.1), channel_id=1, source_target_pairs={{0,1},{1,0},{4,8},{5,9},{8,4},{9,5},{12,13},{13,12},{2,3},{3,2},{6... | collective-permute-start | bytes 294920 | tf_op jit(solution)/shard_map/ppermute | solution.py:386
  9.0 4.3 %collective-permute-start.3 = (bf16[2,2,1,128,128]{4,3,2,1,0:T(8,128)(2,1)}, bf16[2,2,1,128,128]{4,3,2,1,0:T(8,128)(2,1)S(1)}, u32[]{:S(2)}, u32[]{:S(2)}) collective-permute-start(bf16[2,2,1,128,128]{4,3,2,1,0:T(8,128)(2,1)} %refs_0_.1), channel_id=1, source_target_pairs={{0,1},{1,0},{2,3},{3,2},{4,5},{5,4},{6,7},{7,6},{8,9},{9,8},{10,11... | collective-permute-start | bytes 393224 | tf_op jit(solution)/shard_map/ppermute | solution.py:369
  11.5 1.8 %collective-permute-start.5 = (bf16[3,128,128]{2,1,0:T(8,128)(2,1)S(1)}, bf16[3,128,128]{2,1,0:T(8,128)(2,1)S(1)}, u32[]{:S(2)}, u32[]{:S(2)}) collective-permute-start(bf16[3,128,128]{2,1,0:T(8,128)(2,1)S(1)} %collective-permute-done.1.refs_2_), channel_id=1, source_target_pairs={{0,1},{1,0},{2,3},{3,2},{4,5},{5,4},{6,7},{7,6},{8,9},{9,8},{10,11... | collective-permute-start | bytes 294920 | tf_op jit(solution)/shard_map/ppermute | solution.py:369
  11.5 1.8 %collective-permute-start.6 = (bf16[3,128,128]{2,1,0:T(8,128)(2,1)S(1)}, bf16[3,128,128]{2,1,0:T(8,128)(2,1)S(1)}, u32[]{:S(2)}, u32[]{:S(2)}) collective-permute-start(bf16[3,128,128]{2,1,0:T(8,128)(2,1)S(1)} %collective-permute-done.2.refs_3_), channel_id=1, source_target_pairs={{0,1},{1,0},{2,3},{3,2},{4,5},{5,4},{6,7},{7,6},{8,9},{9,8},{10,11... | collective-permute-start | bytes 294920 | tf_op jit(solution)/shard_map/ppermute | solution.py:369
  12.0 1.3 %collective-permute-start.4 = (bf16[2,128,128]{2,1,0:T(8,128)(2,1)S(1)}, bf16[2,128,128]{2,1,0:T(8,128)(2,1)S(1)}, u32[]{:S(2)}, u32[]{:S(2)}) collective-permute-start(bf16[2,128,128]{2,1,0:T(8,128)(2,1)S(1)} %collective-permute-done.refs_1_), channel_id=1, source_target_pairs={{0,1},{1,0},{2,3},{3,2},{4,5},{5,4},{6,7},{7,6},{8,9},{9,8},{10,11... | collective-permute-start | bytes 196616 | tf_op jit(solution)/shard_map/ppermute | solution.py:369
  13.2 1.4 %copy-start = (bf16[2,2,1,12,128,128]{5,4,3,2,1,0:T(8,128)(2,1)S(1)}, bf16[2,2,1,12,128,128]{5,4,3,2,1,0:T(8,128)(2,1)}, u32[]{:S(2)}) copy-start(bf16[2,2,1,12,128,128]{5,4,3,2,1,0:T(8,128)(2,1)} %refs_8_.1) | copy-start | bytes 4718596
  14.7 0.9 %copy-start.1 = (bf16[2,2,1,128,128]{4,3,2,1,0:T(8,128)(2,1)S(1)}, bf16[2,2,1,128,128]{4,3,2,1,0:T(8,128)(2,1)}, u32[]{:S(2)}) copy-start(bf16[2,2,1,128,128]{4,3,2,1,0:T(8,128)(2,1)} %refs_0_.1) | copy-start | bytes 393220
  15.6 0.8 %copy-start.2 = (bf16[2,128,128]{2,1,0:T(8,128)(2,1)S(1)}, bf16[2,128,128]{2,1,0:T(8,128)(2,1)}, u32[]{:S(2)}) copy-start(bf16[2,128,128]{2,1,0:T(8,128)(2,1)} %encoder_w_ref.1) | copy-start | bytes 196612
  16.4 0.9 %copy-start.3 = (bf16[5,128,128]{2,1,0:T(8,128)(2,1)S(1)}, bf16[5,128,128]{2,1,0:T(8,128)(2,1)}, u32[]{:S(2)}) copy-start(bf16[5,128,128]{2,1,0:T(8,128)(2,1)} %refs_13_.1) | copy-start | bytes 491524
  17.3 0.8 %copy-start.4 = (bf16[256,128]{1,0:T(8,128)(2,1)S(1)}, bf16[256,128]{1,0:T(8,128)(2,1)}, u32[]{:S(2)}) copy-start(bf16[256,128]{1,0:T(8,128)(2,1)} %refs_14_.1) | copy-start | bytes 196612
  18.2 0.8 %copy-start.5 = (bf16[2,128,128]{2,1,0:T(8,128)(2,1)S(1)}, bf16[2,128,128]{2,1,0:T(8,128)(2,1)}, u32[]{:S(2)}) copy-start(bf16[2,128,128]{2,1,0:T(8,128)(2,1)} %refs_15_.1) | copy-start | bytes 196612
  41.0 3.7 %collective-permute-start.7 = (f32[16,96]{1,0:T(8,128)S(1)}, f32[16,96]{1,0:T(8,128)S(1)}, u32[]{:S(2)}, u32[]{:S(2)}) collective-permute-start(f32[16,96]{1,0:T(8,128)S(1)} %get-tuple-element.11), channel_id=1, source_target_pairs={{0,2},{2,0},{1,3},{3,1},{4,6},{6,4},{5,7},{7,5},{8,10},{10,8},{9,1... | collective-permute-start | bytes 18440 | tf_op jit(solution)/shard_map/ppermute | solution.py:369
  44.7 7.8 %copy-start.14 = (f32[2,16,96]{2,1,0:T(8,128)}, f32[2,16,96]{2,1,0:T(8,128)S(1)}, u32[]{:S(2)}) copy-start(f32[2,16,96]{2,1,0:T(8,128)S(1)} %pad_maximum_fusion.2.own_ref) | copy-start | bytes 36868
  44.7 4.9 %collective-permute-start.9 = (f32[2,16,96]{2,1,0:T(8,128)S(1)}, f32[2,16,96]{2,1,0:T(8,128)S(1)}, u32[]{:S(2)}, u32[]{:S(2)}) collective-permute-start(f32[2,16,96]{2,1,0:T(8,128)S(1)} %pad_maximum_fusion.2.own_ref), channel_id=1, source_target_pairs={{0,1},{1,0},{4,8},{5,9},{8,4},{9,5},{12,13},{13,12},{2,3},{3,2},{6... | collective-permute-start | bytes 36872 | tf_op jit(solution)/shard_map/ppermute | solution.py:386
  44.7 6.6 %collective-permute-start.8 = (f32[2,16,96]{2,1,0:T(8,128)S(1)}, f32[2,16,96]{2,1,0:T(8,128)S(1)}, u32[]{:S(2)}, u32[]{:S(2)}) collective-permute-start(f32[2,16,96]{2,1,0:T(8,128)S(1)} %pad_maximum_fusion.2.own_ref), channel_id=1, source_target_pairs={{0,4},{1,5},{4,0},{5,1},{8,12},{9,13},{12,8},{13,9},{2,6},{3,7},{6... | collective-permute-start | bytes 36872 | tf_op jit(solution)/shard_map/ppermute | solution.py:386
  49.6 1.7 %collective-permute-start.10 = (f32[2,16,96]{2,1,0:T(8,128)S(1)}, f32[2,16,96]{2,1,0:T(8,128)S(1)}, u32[]{:S(2)}, u32[]{:S(2)}) collective-permute-start(f32[2,16,96]{2,1,0:T(8,128)S(1)} %pad_maximum_fusion.2.own_ref), channel_id=1, source_target_pairs={{0,1},{1,0},{2,3},{3,2},{4,5},{5,4},{6,7},{7,6},{8,9},{9,8},{10,11... | collective-permute-start | bytes 36872 | tf_op jit(solution)/shard_map/ppermute | solution.py:369
  49.6 2.9 %copy-start.15 = (f32[2,16,96]{2,1,0:T(8,128)}, f32[2,16,96]{2,1,0:T(8,128)S(1)}, u32[]{:S(2)}) copy-start(f32[2,16,96]{2,1,0:T(8,128)S(1)} %collective-permute-done.9.odd_ref) | copy-start | bytes 36868
  49.6 1.7 %collective-permute-start.12 = (f32[2,16,96]{2,1,0:T(8,128)S(1)}, f32[2,16,96]{2,1,0:T(8,128)S(1)}, u32[]{:S(2)}, u32[]{:S(2)}) collective-permute-start(f32[2,16,96]{2,1,0:T(8,128)S(1)} %collective-permute-done.9.odd_ref), channel_id=1, source_target_pairs={{0,1},{1,0},{2,3},{3,2},{4,5},{5,4},{6,7},{7,6},{8,9},{9,8},{10,11... | collective-permute-start | bytes 36872 | tf_op jit(solution)/shard_map/ppermute | solution.py:369
  51.3 1.2 %copy-start.16 = (f32[2,16,96]{2,1,0:T(8,128)}, f32[2,16,96]{2,1,0:T(8,128)S(1)}, u32[]{:S(2)}) copy-start(f32[2,16,96]{2,1,0:T(8,128)S(1)} %collective-permute-done.8.even_ref) | copy-start | bytes 36868
  51.3 1.2 %collective-permute-start.11 = (f32[2,16,96]{2,1,0:T(8,128)S(1)}, f32[2,16,96]{2,1,0:T(8,128)S(1)}, u32[]{:S(2)}, u32[]{:S(2)}) collective-permute-start(f32[2,16,96]{2,1,0:T(8,128)S(1)} %collective-permute-done.8.even_ref), channel_id=1, source_target_pairs={{0,1},{1,0},{2,3},{3,2},{4,5},{5,4},{6,7},{7,6},{8,9},{9,8},{10,11... | collective-permute-start | bytes 36872 | tf_op jit(solution)/shard_map/ppermute | solution.py:369
  51.3 1.2 %copy-start.17 = (f32[2,16,96]{2,1,0:T(8,128)}, f32[2,16,96]{2,1,0:T(8,128)S(1)}, u32[]{:S(2)}) copy-start(f32[2,16,96]{2,1,0:T(8,128)S(1)} %collective-permute-done.10.own_zed) | copy-start | bytes 36868
  51.3 1.2 %copy-start.18 = (f32[2,16,96]{2,1,0:T(8,128)}, f32[2,16,96]{2,1,0:T(8,128)S(1)}, u32[]{:S(2)}) copy-start(f32[2,16,96]{2,1,0:T(8,128)S(1)} %collective-permute-done.12.odd_zed) | copy-start | bytes 36868
  (9 other events, 6.3 us)

commit v3 on v2

v3 whole, which is shorter than its diff:
```python
import functools

import jax
import jax.numpy as jnp
from jax import lax
from jax.experimental import pallas as pl
from jax.experimental.pallas import tpu as pltpu
from jax.sharding import PartitionSpec as P

CAP = 8
F32 = jnp.float32
BF16 = jnp.bfloat16
I32 = jnp.int32
ROWS = 16
TILE = 256
CELLS = [(a, b) for a in range(2) for b in range(2)]
EDGE, NEAR, FAR, MIDDLE, FINAL, NODE_OLD, NODE_NEW, NODE_0, NODE_1, DECODE_0, DECODE_1 = range(11)

VMEM = pl.BlockSpec(memory_space=pltpu.VMEM)
SMEM = pl.BlockSpec(memory_space=pltpu.SMEM)
ANY = pl.BlockSpec(memory_space=pl.ANY)


def dot(left, right):
    return jnp.dot(left, right, preferred_element_type=F32)


def dot_nt(left, right):
    return lax.dot_general(left, right, (((1,), (1,)), ((), ())), preferred_element_type=F32)


def dot_tn(left, right):
    return lax.dot_general(left, right, (((0,), (0,)), ((), ())), preferred_element_type=F32)


def relu16(values):
    return jnp.maximum(values, 0.0).astype(BF16)


def norm(values, axis):
    scale = 1.0 / values.shape[axis]
    centred = values - jnp.sum(values, axis=axis, keepdims=True) * scale
    spread = jnp.sum(centred * centred, axis=axis, keepdims=True) * scale
    return centred * lax.rsqrt(spread + 1e-05)


def thirds(values):
    high = values.astype(BF16)
    rest = values - high.astype(F32)
    middle = rest.astype(BF16)
    low = (rest - middle.astype(F32)).astype(BF16)
    return jnp.concatenate([high, middle, low], axis=0)


def joined(values):
    rows = values.shape[0] // 3
    return values[:rows] + values[rows : 2 * rows] + values[2 * rows :]


def quotient(values, count):
    if count & (count - 1) == 0:
        return values >> (count.bit_length() - 1)
    return lax.div(values, jnp.full_like(values, count))


def flip(weights):
    return weights.astype(F32).T.astype(BF16)


def fetch(pairs, sems):
    copies = [pltpu.make_async_copy(src, dst, sems.at[i]) for i, (src, dst) in enumerate(pairs)]
    for copy in copies:
        copy.start()
    return copies


def encode(state, mask, inward, encoder_w, extent):
    width = state.shape[1]
    position = state[0:3]
    row = lax.broadcasted_iota(I32, (3, width), 0)
    size = jnp.where(row == 0, extent[0], jnp.where(row == 1, extent[1], extent[2]))
    features = jnp.concatenate(
        [
            state[3:9],
            jnp.clip(position, -1.0, 1.0),
            jnp.clip(size - position, -1.0, 1.0),
            jnp.zeros((4, width), F32),
        ],
        axis=0,
    )
    hidden = relu16(dot_tn(thirds(features), inward))
    hidden = relu16(dot(hidden, encoder_w[0]))
    column = jnp.broadcast_to(mask, (8, width)).T[:, 0:1]
    return (norm(dot(hidden, encoder_w[1]), 1) * column).astype(BF16)


def places(ids_low, ids_high, fold_y):
    plane = (ids_high * 43) >> 7
    ez = ids_high - plane * 3
    ey = plane & 3
    ex = plane >> 2
    if fold_y:
        row = jnp.where(ey == 1, 0, jnp.where(ey == 2, 1, 2))
    else:
        row = ey
    return ex * 4 + row, ids_low + jnp.where(ez == 1, 0, 128)


def messages(far_ref, columns, row_count, place, key, pre, middle_t, final_t, hidden_ref):
    width = far_ref.shape[1]
    chunk = 32
    window = jnp.concatenate(
        [
            far_ref[ex * row_count + row, f : f + chunk]
            for f in range(0, width, chunk)
            for ex, row in columns
        ],
        axis=0,
    )
    key_rows = lax.broadcasted_iota(I32, (TILE, TILE), 0)
    lanes = place.shape[1]
    for tile in range(lanes // TILE):
        at = slice(tile * TILE, (tile + 1) * TILE)
        picker = jnp.where(key_rows == key[:, at], 1.0, 0.0).astype(BF16)
        found = dot(window, picker).reshape(width // chunk, len(columns), chunk // 8, 8, TILE)
        where = jnp.broadcast_to(place[:, at], (8, TILE))
        parts = []
        for f in range(width // chunk):
            part = jnp.zeros((chunk // 8, 8, TILE), F32)
            for i, (ex, row) in enumerate(columns):
                part = jnp.where((where == ex * 4 + row)[None], found[f, i], part)
            parts.append(part.reshape(chunk, TILE))
        hidden_ref[:, at] = relu16(pre(tile) + jnp.concatenate(parts, axis=0))
    hidden = relu16(dot(middle_t, hidden_ref[...]))
    return norm(dot(final_t, hidden), 0)


def slot_sum(message, step):
    total = message[:, :step]
    for at in range(step, message.shape[1], step):
        total = total + message[:, at : at + step]
    return total


def advance(pre, aggregate, latent_t, weights_ref, decoder_out):
    pre = pre + dot(weights_ref[NODE_NEW], aggregate)
    hidden = relu16(dot(weights_ref[NODE_0], relu16(pre)))
    updated = (latent_t + norm(dot(weights_ref[NODE_1], hidden), 0)).astype(BF16)
    hidden = relu16(dot(weights_ref[DECODE_0], updated))
    hidden = relu16(dot(weights_ref[DECODE_1], hidden))
    return dot(decoder_out, hidden)


def moved(position, velocity, acceleration):
    new_velocity = velocity + acceleration
    return jnp.concatenate([position + new_velocity, new_velocity, velocity], axis=0)


def prepare_kernel(
    sizes,
    fill_ref,
    latent_any,
    edge_any,
    positions_any,
    velocity_any,
    neighbours_any,
    owners_any,
    edge_w_any,
    node_in_any,
    node_w_any,
    decoder_w_any,
    decoder_out_any,
    encoder_in_any,
    encoder_w_any,
    weights_ref,
    decoder_out_ref,
    inward_ref,
    encoder_w_ref,
    latent_t_ref,
    node_pre_ref,
    state_ref,
    mover_pre_ref,
    mover_place_ref,
    mover_key_ref,
    mover_node_pre_ref,
    mover_latent_ref,
    mover_state_ref,
    latent_ref,
    edge_ref,
    positions_ref,
    velocity_ref,
    neighbours_ref,
    owners_ref,
    edge_w_ref,
    node_in_ref,
    node_w_ref,
    decoder_w_ref,
    encoder_in_ref,
    sems,
):
    count_x, count_y, count_z = sizes
    fold_y = count_y == 2
    copies = fetch(
        [
            (owners_any, owners_ref),
            (edge_w_any, edge_w_ref),
            (neighbours_any, neighbours_ref),
            (positions_any, positions_ref),
            (velocity_any, velocity_ref),
            (latent_any, latent_ref),
            (edge_any, edge_ref),
            (node_in_any, node_in_ref),
            (node_w_any, node_w_ref),
            (decoder_w_any, decoder_w_ref),
            (decoder_out_any, decoder_out_ref),
            (encoder_in_any, encoder_in_ref),
            (encoder_w_any, encoder_w_ref),
        ],
        sems,
    )
    for copy in copies:
        copy.wait()
    index_x = lax.axis_index("gx")
    index_y = lax.axis_index("gy")
    index_z = lax.axis_index("gz")
    slots, width = latent_ref.shape[-2:]
    neighbour_count = edge_ref.shape[3]

    lane = lax.broadcasted_iota(I32, (1, slots), 1)
    owner = jnp.concatenate([owners_ref[a, b] for a, b in CELLS], axis=1)
    alive = jnp.concatenate([jnp.where(lane < fill_ref[a, 0, b], 1, 0) for a, b in CELLS], axis=1)
    own_block = (index_x * count_y + index_y) * count_z + index_z
    stays = jnp.where((alive == 1) & (owner == own_block), 1.0, 0.0)
    moving = jnp.where((alive == 1) & (owner != own_block), 1, 0)
    owner_x = quotient(owner, count_y * count_z)
    rest = owner - owner_x * (count_y * count_z)
    owner_y = quotient(rest, count_z)
    owner_z = rest - owner_y * count_z
    step_y = owner_y - index_y
    side_y = jnp.where(step_y == 0, 0, 1) if fold_y else jnp.where(step_y < 0, 1, 2 * step_y)
    options_y = 2 if fold_y else 3
    group = ((owner_x - index_x + 1) * options_y + side_y) * 2 + jnp.where(owner_z == index_z, 0, 1)
    group_rows = (3 * options_y * 2 + 15) // 16 * 16
    particles = owner.shape[1]
    member = jnp.where(
        (lax.broadcasted_iota(I32, (group_rows, particles), 0) == group) & (moving == 1), 1.0, 0.0
    )
    triangle = jnp.where(
        lax.broadcasted_iota(I32, (slots, slots), 0) <= lax.broadcasted_iota(I32, (slots, slots), 1),
        1.0,
        0.0,
    ).astype(BF16)
    counted = []
    before = jnp.zeros((group_rows, 1), F32)
    for i in range(4):
        inside = member[:, i * slots : (i + 1) * slots]
        counted.append(dot(inside.astype(BF16), triangle) + before)
        before = before + jnp.sum(inside, axis=1, keepdims=True)
    counted = jnp.concatenate(counted, axis=1)
    rank = (jnp.sum(counted * member, axis=0, keepdims=True) - 1.0).astype(I32)
    column = jnp.where(moving == 1, group * CAP + rank, -1)
    movers = mover_state_ref.shape[1]
    placer = jnp.where(
        lax.broadcasted_iota(I32, (movers, particles), 0) == column, 1.0, 0.0
    ).astype(BF16)

    for i in range(5):
        weights_ref[i] = flip(edge_w_ref[i])
    weights_ref[NODE_OLD] = flip(node_in_ref[:width])
    weights_ref[NODE_NEW] = flip(node_in_ref[width:])
    for i in range(2):
        weights_ref[NODE_0 + i] = flip(node_w_ref[i])
        weights_ref[DECODE_0 + i] = flip(decoder_w_ref[i])
    inward = jnp.concatenate([encoder_in_ref[...].astype(F32), jnp.zeros((4, width), F32)], axis=0)
    inward = inward.astype(BF16)
    inward_ref[...] = jnp.concatenate([inward, inward, inward], axis=0)

    latent = jnp.concatenate([latent_ref[a, b, 0] for a, b in CELLS], axis=0)
    latent_t_ref[...] = latent.astype(F32).T
    node_pre_ref[...] = dot_nt(weights_ref[NODE_OLD], latent)

    def flat(ref, i):
        return jnp.concatenate([ref[i, a, b] for a, b in CELLS], axis=1)

    state = [flat(positions_ref, i) for i in range(3)] + [flat(velocity_ref, i) for i in range(3)]
    state_ref[...] = jnp.concatenate(state + [stays, jnp.zeros_like(stays)], axis=0)

    mover_latent = dot(placer, latent).astype(BF16)
    mover_latent_ref[...] = mover_latent.astype(F32).T
    mover_node_pre_ref[...] = dot_nt(weights_ref[NODE_OLD], mover_latent)
    near = dot_nt(weights_ref[NEAR], mover_latent)
    state = jnp.concatenate(state + [moving.astype(F32), jnp.zeros_like(stays)], axis=0)
    mover_state_ref[...] = joined(dot_nt(thirds(state), placer))
    ids = jnp.concatenate(
        [
            jnp.concatenate([neighbours_ref[a, b, k] for a, b in CELLS], axis=1)
            for k in range(neighbour_count)
        ],
        axis=0,
    )
    ids = jnp.concatenate([ids & 127, ids >> 7, jnp.zeros((8, particles), I32)], axis=0)
    ids = dot_nt(ids.astype(F32).astype(BF16), placer).astype(I32)
    place, key = places(ids[:neighbour_count], ids[neighbour_count : 2 * neighbour_count], fold_y)
    mover_place_ref[...] = place
    mover_key_ref[...] = key
    for k in range(neighbour_count):
        edges = jnp.concatenate([edge_ref[a, b, 0, k] for a, b in CELLS], axis=0)
        edges = dot(placer, edges).astype(BF16)
        mover_pre_ref[:, k * movers : (k + 1) * movers] = dot_nt(weights_ref[EDGE], edges) + near


def movers_kernel(
    sizes,
    side_count,
    latent_any,
    *refs,
):
    count_x, count_y, _ = sizes
    fold_y = count_y == 2
    side_refs, refs = refs[:side_count], refs[side_count:]
    even_ref, odd_ref, own_zed, refs = refs[0], refs[1], refs[2], refs[3:]
    side_zeds, refs = refs[:side_count], refs[side_count:]
    even_zed, odd_zed, refs = refs[0], refs[1], refs[2:]
    (
        weights_ref,
        decoder_out_ref,
        pre_ref,
        place_ref,
        key_ref,
        node_pre_ref,
        latent_t_ref,
        state_ref,
        far_ref,
        bucket_ref,
        own_ref,
        hidden_ref,
        sems,
    ) = refs
    copies = fetch([(latent_any, own_ref)], sems)
    row_count = 3 if fold_y else 4
    own_rows = (0, 1) if fold_y else (1, 2)
    outer = {2: 0} if fold_y else {0: 0, 3: 1}
    parity = lax.axis_index("gx") & 1
    far_t = weights_ref[FAR]

    def far(at, here, beside):
        pair = jnp.concatenate([here, beside], axis=0)
        far_ref[at] = dot_nt(far_t, pair).astype(BF16)

    copies[0].wait()
    for row in range(row_count):
        for ex in (1, 2):
            if row in own_rows:
                b = own_rows.index(row)
                far(ex * row_count + row, own_ref[ex - 1, b, 0], own_zed[ex - 1, b, 0])
            else:
                side = outer[row]
                far(ex * row_count + row, side_refs[side][ex - 1], side_zeds[side][ex - 1])
        far(3 * (1 - parity) * row_count + row, even_ref[row], even_zed[row])
        far(3 * parity * row_count + row, odd_ref[row], odd_zed[row])

    movers = state_ref.shape[1]
    neighbour_count = place_ref.shape[0]
    place = jnp.concatenate([place_ref[k : k + 1] for k in range(neighbour_count)], axis=1)
    key = jnp.concatenate([key_ref[k : k + 1] for k in range(neighbour_count)], axis=1)
    columns = [(ex, row) for ex in range(4) for row in range(row_count)]
    message = messages(
        far_ref,
        columns,
        row_count,
        place,
        key,
        lambda tile: pre_ref[:, tile * TILE : (tile + 1) * TILE],
        weights_ref[MIDDLE],
        weights_ref[FINAL],
        hidden_ref,
    )
    aggregate = slot_sum(message, movers).astype(BF16)
    acceleration = advance(
        node_pre_ref[...], aggregate, latent_t_ref[...], weights_ref, decoder_out_ref[...]
    )
    mask = state_ref[6:7]
    state = moved(state_ref[0:3], state_ref[3:6], acceleration) * mask
    bucket_ref[...] = jnp.concatenate([state, mask, jnp.zeros((ROWS - 10, movers), F32)], axis=0)


def edges_kernel(
    sizes,
    a,
    fill_ref,
    latent_any,
    edge_any,
    neighbours_any,
    far_ref,
    weights_ref,
    total_ref,
    latent_ref,
    edge_ref,
    neighbours_ref,
    hidden_ref,
    sems,
):
    fold_y = sizes[1] == 2
    row_count = 3 if fold_y else 4
    index_y = lax.axis_index("gy")
    copies = fetch(
        [
            (neighbours_any.at[a], neighbours_ref),
            (latent_any.at[a], latent_ref),
            (edge_any.at[a], edge_ref),
        ],
        sems,
    )
    for copy in copies:
        copy.wait()
    slots, width = latent_ref.shape[-2:]
    neighbour_count = edge_ref.shape[2]
    lane = lax.broadcasted_iota(I32, (1, slots), 1)
    for bt in range(2):
        if fold_y:
            b = index_y if bt == 0 else 1 - index_y
            rows = (0, 1) if bt == 0 else (0, 1, 2)
        else:
            b = bt
            rows = (bt, bt + 1, bt + 2)
        columns = [(ex, row) for ex in range(a, a + 3) for row in rows]
        near = dot_nt(weights_ref[NEAR], latent_ref[b, 0])
        near = jnp.concatenate([near, near], axis=1)
        ids = jnp.concatenate([neighbours_ref[b, k] for k in range(neighbour_count)], axis=1)
        place, key = places(ids & 127, ids >> 7, fold_y)

        def pre(tile, b=b, near=near):
            edges = jnp.concatenate([edge_ref[b, 0, 2 * tile], edge_ref[b, 0, 2 * tile + 1]], axis=0)
            return dot_nt(weights_ref[EDGE], edges) + near

        message = messages(
            far_ref,
            columns,
            row_count,
            place,
            key,
            pre,
            weights_ref[MIDDLE],
            weights_ref[FINAL],
            hidden_ref.at[bt],
        )
        total = jnp.where(lane < fill_ref[a, 0, b], slot_sum(message, slots), 0.0)
        total_ref[b] = total.astype(BF16)


def nodes_kernel(
    sizes,
    first_ref,
    second_ref,
    node_pre_ref,
    latent_t_ref,
    state_ref,
    weights_ref,
    decoder_out_ref,
    inward_ref,
    encoder_w_ref,
    kept_latent_ref,
    kept_state_ref,
):
    slots = first_ref.shape[-1]
    aggregate = jnp.concatenate([first_ref[0], first_ref[1], second_ref[0], second_ref[1]], axis=1)
    acceleration = advance(
        node_pre_ref[...], aggregate, latent_t_ref[...], weights_ref, decoder_out_ref[...]
    )
    stays = state_ref[6:7]
    state = moved(state_ref[0:3], state_ref[3:6], acceleration)
    extent = (2.0 * sizes[0], 2.0 * sizes[1], 1.0 * sizes[2])
    latents = encode(state, stays, inward_ref[...], encoder_w_ref[...], extent)
    kept = state * stays
    for i, (a, b) in enumerate(CELLS):
        kept_latent_ref[a, b, 0] = latents[i * slots : (i + 1) * slots]
        for j in range(9):
            kept_state_ref[j, a, b] = kept[j : j + 1, i * slots : (i + 1) * slots]


def arrive_kernel(
    sizes,
    own_ref,
    even_ref,
    odd_ref,
    own_zed,
    even_zed,
    odd_zed,
    inward_ref,
    encoder_w_ref,
    arrived_latent_ref,
    arrived_state_ref,
):
    count_x, count_y, count_z = sizes
    fold_y = count_y == 2
    index_x = lax.axis_index("gx")
    index_y = lax.axis_index("gy")
    index_z = lax.axis_index("gz")
    options_y = 2 if fold_y else 3
    lanes = own_ref.shape[-1]
    group = lax.broadcasted_iota(I32, (ROWS, lanes), 1) >> 3
    even = (index_x & 1) == 0
    found = jnp.zeros((ROWS, lanes), F32)
    for source_x in (-1, 0, 1):
        for from_y in range(options_y):
            for from_z in range(2):
                if source_x == 0 and from_y == 0 and from_z == 0:
                    continue
                if from_z == 0:
                    own, first, second = own_ref, even_ref, odd_ref
                else:
                    own, first, second = own_zed, even_zed, odd_zed
                side_y = from_y if fold_y or from_y == 0 else 3 - from_y
                target = ((1 - source_x) * options_y + side_y) * 2 + from_z
                if source_x == 0:
                    tile = own[from_y]
                    there = group == target
                elif source_x == -1:
                    tile = jnp.where(even, second[from_y], first[from_y])
                    there = (group == target) & (index_x > 0)
                else:
                    tile = jnp.where(even, first[from_y], second[from_y])
                    there = (group == target) & (index_x < count_x - 1)
                found = jnp.where(there, tile, found)
    out_lanes = arrived_state_ref.shape[-1]
    spread_shape = (lanes, out_lanes)
    line = lax.broadcasted_iota(I32, spread_shape, 0)
    from_group = line >> 3
    plane = from_group >> 1
    from_x = 1 - ((plane >> 1) if fold_y else ((plane * 43) >> 7))
    side_y = plane - (1 - from_x) * options_y
    if fold_y:
        from_y = jnp.where(side_y == 0, 0, jnp.where(index_y == 0, 1, -1))
    else:
        from_y = jnp.where(side_y == 0, 0, jnp.where(side_y == 1, 1, -1))
    from_z = jnp.where((from_group & 1) == 0, 0, jnp.where(index_z == 0, 1, -1))
    direction = (from_x + 1) * 9 + (from_y + 1) * 3 + from_z + 1
    direction = direction - jnp.where(direction > 13, 1, 0)
    column = direction * CAP + (line & 7)
    valid = (lax.broadcasted_iota(I32, spread_shape, 1) == column) & (
        (from_x != 0) | (from_y != 0) | (from_z != 0)
    )
    spread = jnp.where(valid, 1.0, 0.0).astype(BF16)
    arrived = joined(dot(thirds(found), spread))
    for j in range(9):
        arrived_state_ref[j, 0, 0] = arrived[j : j + 1]
    extent = (2.0 * count_x, 2.0 * count_y, 1.0 * count_z)
    arrived_latent_ref[0, 0, 0] = encode(
        arrived[:9], arrived[9:10], inward_ref[...], encoder_w_ref[...], extent
    )


def swap(values, axis):
    return lax.ppermute(values, axis, [(0, 1), (1, 0)])


def shift(values, axis, way):
    pairs = [(i, i + 1) for i in range(lax.axis_size(axis) - 1)]
    return lax.ppermute(values, axis, [(j, i) for i, j in pairs] if way else pairs)


def swap_x(values, first):
    count = lax.axis_size("gx")
    pairs = []
    for x in range(count):
        partner = x + 1 if (x - first) % 2 == 0 else x - 1
        for z in range(2):
            if 0 <= partner < count:
                pairs.append((x * 2 + z, partner * 2 + z))
            else:
                pairs.append((x * 2 + z, x * 2 + 1 - z))
    return lax.ppermute(values, ("gx", "gz"), pairs)


def call(kernel, name, in_specs, outs, scratch, operands, flops):
    return pl.pallas_call(
        kernel,
        out_shape=tuple(jax.ShapeDtypeStruct(shape, kind) for shape, kind in outs),
        in_specs=in_specs,
        out_specs=tuple(VMEM for _ in outs),
        scratch_shapes=scratch,
        compiler_params=pltpu.CompilerParams(vmem_limit_bytes=32 * 1024 * 1024),
        cost_estimate=pl.CostEstimate(flops=flops, bytes_accessed=0, transcendentals=0),
        name=name,
    )(*operands)


def like(array):
    return pltpu.VMEM(array.shape, array.dtype)


def body(
    node_latent,
    edge_latent,
    positions,
    velocity,
    fill,
    neighbours,
    owners,
    edge_weights,
    node_in,
    node_weights,
    decoder_weights,
    decoder_out,
    encoder_in,
    encoder_weights,
):
    sizes = tuple(lax.axis_size(axis) for axis in ("gx", "gy", "gz"))
    fold_y = sizes[1] == 2
    slots, width = node_latent.shape[-2:]
    neighbour_count = neighbours.shape[3]
    particles = 4 * slots
    options_y = 2 if fold_y else 3
    movers = (3 * options_y * 2 * CAP + 127) // 128 * 128
    rows = 3 if fold_y else 4
    fill = jnp.transpose(fill, (0, 2, 1))
    neighbours = neighbours.reshape(2, 2, neighbour_count, 1, slots)

    parity = lax.axis_index("gx") & 1
    cells = node_latent[:, :, 0]
    if fold_y:
        inner = 1 - lax.axis_index("gy")
        sides = [swap(lax.dynamic_index_in_dim(cells, inner, 1, keepdims=False), "gy")]
    else:
        sides = [shift(cells[:, 1], "gy", 0), shift(cells[:, 0], "gy", 1)]

    prepared = call(
        functools.partial(prepare_kernel, sizes),
        "prepare",
        [SMEM] + [ANY] * 13,
        [
            ((11, width, width), BF16),
            (decoder_out.shape, BF16),
            ((48, width), BF16),
            (encoder_weights.shape, BF16),
            ((width, particles), F32),
            ((width, particles), F32),
            ((8, particles), F32),
            ((width, neighbour_count * movers), F32),
            ((neighbour_count, movers), I32),
            ((neighbour_count, movers), I32),
            ((width, movers), F32),
            ((width, movers), F32),
            ((8, movers), F32),
        ],
        [
            like(node_latent),
            like(edge_latent),
            like(positions),
            like(velocity),
            like(neighbours),
            like(owners),
            like(edge_weights),
            like(node_in),
            like(node_weights),
            like(decoder_weights),
            like(encoder_in),
            pltpu.SemaphoreType.DMA((13,)),
        ],
        (
            fill,
            node_latent,
            edge_latent,
            positions,
            velocity,
            neighbours,
            owners,
            edge_weights,
            node_in,
            node_weights,
            decoder_weights,
            decoder_out,
            encoder_in,
            encoder_weights,
        ),
        2_000_000_000,
    )
    sides, prepared = lax.optimization_barrier((sides, prepared))
    (
        weights,
        decoder_out,
        inward,
        encoder_weights,
        latent_t,
        node_pre,
        state,
        mover_pre,
        mover_place,
        mover_key,
        mover_node_pre,
        mover_latent,
        mover_state,
    ) = prepared

    if fold_y:
        layers = [cells, sides[0][:, None]]
    else:
        layers = [sides[0][:, None], cells, sides[1][:, None]]

    def layer(a):
        return jnp.concatenate(
            [lax.dynamic_index_in_dim(part, a, 0, keepdims=False) for part in layers], axis=0
        )

    halo = [*sides, swap_x(layer(1 - parity), 0), swap_x(layer(parity), 1)]
    halo = halo + [swap(part, "gz") for part in [node_latent] + halo]

    far, bucket = call(
        functools.partial(movers_kernel, sizes, len(sides)),
        "movers",
        [ANY] + [VMEM] * (len(halo) + 8),
        [((4 * rows, width, 2 * slots), BF16), ((ROWS, movers), F32)],
        [
            like(node_latent),
            pltpu.VMEM((width, neighbour_count * movers), BF16),
            pltpu.SemaphoreType.DMA((1,)),
        ],
        (
            node_latent,
            *halo,
            weights,
            decoder_out,
            mover_pre,
            mover_place,
            mover_key,
            mover_node_pre,
            mover_latent,
            mover_state,
        ),
        3_000_000_000,
    )

    def edges(a):
        return call(
            functools.partial(edges_kernel, sizes, a),
            "edges",
            [SMEM] + [ANY] * 3 + [VMEM] * 2,
            [((2, width, slots), BF16)],
            [
                pltpu.VMEM(node_latent.shape[1:], BF16),
                pltpu.VMEM(edge_latent.shape[1:], BF16),
                pltpu.VMEM(neighbours.shape[1:], I32),
                pltpu.VMEM((2, width, neighbour_count * slots), BF16),
                pltpu.SemaphoreType.DMA((3,)),
            ],
            (fill, node_latent, edge_latent, neighbours, far, weights),
            4_000_000_000,
        )[0]

    first = edges(0)
    if fold_y:
        tiles = [swap(bucket, "gy")]
    else:
        tiles = [shift(bucket, "gy", 0), shift(bucket, "gy", 1)]
    tiles, first = lax.optimization_barrier((tiles, first))
    tiles = jnp.stack([bucket, *tiles], axis=0)
    second = edges(1)
    sided = [swap_x(tiles, 0), swap_x(tiles, 1)]
    sided, second = lax.optimization_barrier((sided, second))
    tiles = [tiles, *sided]
    tiles = tiles + [swap(part, "gz") for part in tiles]
    kept_latent, kept_state = call(
        functools.partial(nodes_kernel, sizes),
        "nodes",
        [VMEM] * 9,
        [(node_latent.shape, BF16), ((9,) + node_latent.shape[:4], F32)],
        [],
        (
            first,
            second,
            node_pre,
            latent_t,
            state,
            weights,
            decoder_out,
            inward,
            encoder_weights,
        ),
        2_000_000_000,
    )
    arrived_latent, arrived_state = call(
        functools.partial(arrive_kernel, sizes),
        "arrive",
        [VMEM] * 8,
        [((1, 1, 1, 26 * CAP, width), BF16), ((9, 1, 1, 1, 26 * CAP), F32)],
        [],
        (*tiles, inward, encoder_weights),
        1_000_000_000,
    )
    return kept_latent, kept_state, arrived_latent, arrived_state


def solution(mesh):
    placed = (
        P(("group", "gx"), "gy", "gz", None, None),
        P(("group", "gx"), "gy", "gz", None, None, None),
        P(None, ("group", "gx"), "gy", "gz", None),
        P(None, ("group", "gx"), "gy", "gz", None),
        P(("group", "gx"), "gy", "gz"),
        P(("group", "gx"), "gy", "gz", None, None),
        P(("group", "gx"), "gy", "gz", None),
        P(),
        P(),
        P(),
        P(),
        P(),
        P(),
        P(),
    )
    return jax.shard_map(
        body,
        mesh=mesh,
        in_specs=placed,
        out_specs=(
            P(("group", "gx"), "gy", "gz", None, None),
            P(None, ("group", "gx"), "gy", "gz", None),
            P(("group", "gx"), "gy", "gz", None, None),
            P(None, ("group", "gx"), "gy", "gz", None),
        ),
        check_vma=False,
    )
```

time: 56.3 us -> 47.5 us (0.84)
  waiting for transfers between devices: 8.69 us -> 3.7 us
  starting transfers between devices: 13.5 us -> 11.5 us
  local copies, waits for them, and re-layouts: 13.8 us -> 12.3 us
    ppermute x9, waiting for transfers between devices: 5.48 us -> 1.27 us  [swap(): return lax.ppermute(values, axis, [(0, 1), (1, 0)])]
    ppermute x9, starting transfers between devices: 6.39 us -> 4.75 us  [swap(): return lax.ppermute(values, axis, [(0, 1), (1, 0)])]
    squeeze x2, local copies, waits for them, and re-layouts: 0.89 us -> 0.03 us  [layer(): lax.dynamic_index_in_dim(part, a, 0, keepdims=False)]
    ppermute x4, waiting for transfers between devices: 3.21 us -> 2.43 us  [swap_x(): return lax.ppermute(values, ('gx', 'gz'), pairs)]
    unnamed x40 -> x34, local copies, waits for them, and re-layouts: 12 us -> 11.4 us
    pallas_call x2 -> x6, Pallas kernels: 18.8 us -> 18.6 us  [call(): pl.pallas_call(kernel, out_shape=tuple((jax.ShapeDtypeStruct(shape, kind)...]
  transfers between devices with their start and end apart: 13 -> 13, of which waited for: 6 -> 2; matrix products, arithmetic and copies ran while one was open for 2% -> 0% of each run, Pallas kernels for 0% -> 29%
where the time goes in v3:
time: 47.5 us; the launch traced here: 46.9 us
  Pallas kernels  18.6 us (39%)
  local copies, waits for them, and re-layouts  12.3 us (26%)
  starting transfers between devices  11.5 us (24%)
  waiting for transfers between devices  3.7 us (8%)
  between operations  0.8 us (2%)
    pallas_call x6, Pallas kernels, call(): pl.pallas_call(kernel, out_shape=tuple((jax.ShapeDtypeStruct(shape, kind)...  18.6 us
    unnamed x34, local copies, waits for them, and re-layouts  11.4 us
    ppermute x4, starting transfers between devices, swap_x(): return lax.ppermute(values, ('gx', 'gz'), pairs)  6.7 us
    ppermute x9, starting transfers between devices, swap(): return lax.ppermute(values, axis, [(0, 1), (1, 0)])  4.75 us
    ppermute x4, waiting for transfers between devices, swap_x(): return lax.ppermute(values, ('gx', 'gz'), pairs)  2.43 us
    ppermute x9, waiting for transfers between devices, swap(): return lax.ppermute(values, axis, [(0, 1), (1, 0)])  1.27 us
  transfers between devices with their start and end apart: 13, of which 2 were waited for; matrix products, arithmetic and copies ran while one was open for 0% of the time, Pallas kernels for 29%

profile of v3, /device:TPU:0, one launch (start us, length us, event | category | flops | bytes accessed | tf_op | source)
XLA Modules:
  0.0 46.9 jit_solution(5384456244926185641)
XLA Ops:
  0.6 0.9 %dynamic-slice_bitcast_fusion.2 = bf16[2,128,128]{2,1,0:T(8,128)(2,1)S(1)} fusion(bf16[2,2,1,128,128]{4,3,2,1,0:T(8,128)(2,1)} %latent_any.7, s32[]{:T(128)S(6)} %select_n.14), kind=kLoop, calls=%fused_computation.4 | loop fusion | bytes 131076 | tf_op jit(solution)/shard_map/jit(dynamic_index_in_dim)/squeeze | solution.py:623
  1.5 2.9 %collective-permute-start = (bf16[2,128,128]{2,1,0:T(8,128)(2,1)S(1)}, bf16[2,128,128]{2,1,0:T(8,128)(2,1)S(1)}, u32[]{:S(2)}, u32[]{:S(2)}) collective-permute-start(bf16[2,128,128]{2,1,0:T(8,128)(2,1)S(1)} %dynamic-slice_bitcast_fusion.2), channel_id=1, source_target_pairs={{0,2},{2,0},{1,3},{3,1},{4,6},{6,4},{5,7},{7,5},{8,10},{10,8},{9,1... | collective-permute-start | bytes 196616 | tf_op jit(solution)/shard_map/ppermute | solution.py:554
  4.4 0.9 %copy-done = bf16[2,2,1,128,128]{4,3,2,1,0:T(8,128)(2,1)S(1)} copy-done((bf16[2,2,1,128,128]{4,3,2,1,0:T(8,128)(2,1)S(1)}, bf16[2,2,1,128,128]{4,3,2,1,0:T(8,128)(2,1)}, u32[]{:S(2)}) %copy-start) | copy-done | bytes 131096
  5.3 1.4 %copy-done.2 = bf16[2,2,1,12,128,128]{5,4,3,2,1,0:T(8,128)(2,1)S(1)} copy-done((bf16[2,2,1,12,128,128]{5,4,3,2,1,0:T(8,128)(2,1)S(1)}, bf16[2,2,1,12,128,128]{5,4,3,2,1,0:T(8,128)(2,1)}, u32[]{:S(2)}) %copy-start.2) | copy-done | bytes 1572888
  6.7 0.9 %copy-done.4 = bf16[5,128,128]{2,1,0:T(8,128)(2,1)S(1)} copy-done((bf16[5,128,128]{2,1,0:T(8,128)(2,1)S(1)}, bf16[5,128,128]{2,1,0:T(8,128)(2,1)}, u32[]{:S(2)}) %copy-start.4) | copy-done | bytes 163864
  7.7 0.8 %copy-done.5 = bf16[256,128]{1,0:T(8,128)(2,1)S(1)} copy-done((bf16[256,128]{1,0:T(8,128)(2,1)S(1)}, bf16[256,128]{1,0:T(8,128)(2,1)}, u32[]{:S(2)}) %copy-start.5) | copy-done | bytes 65560
  8.5 0.8 %copy-done.6 = bf16[2,128,128]{2,1,0:T(8,128)(2,1)S(1)} copy-done((bf16[2,128,128]{2,1,0:T(8,128)(2,1)S(1)}, bf16[2,128,128]{2,1,0:T(8,128)(2,1)}, u32[]{:S(2)}) %copy-start.6) | copy-done | bytes 65560
  9.3 0.8 %copy-done.7 = bf16[2,128,128]{2,1,0:T(8,128)(2,1)S(1)} copy-done((bf16[2,128,128]{2,1,0:T(8,128)(2,1)S(1)}, bf16[2,128,128]{2,1,0:T(8,128)(2,1)}, u32[]{:S(2)}) %copy-start.7) | copy-done | bytes 65560
  10.2 0.8 %copy-done.8 = bf16[2,128,128]{2,1,0:T(8,128)(2,1)S(1)} copy-done((bf16[2,128,128]{2,1,0:T(8,128)(2,1)S(1)}, bf16[2,128,128]{2,1,0:T(8,128)(2,1)}, u32[]{:S(2)}) %copy-start.8) | copy-done | bytes 65560
  11.0 0.7 %copy-done.9 = s32[2,2,1,12,128]{4,2,3,1,0:T(1,128)S(1)} copy-done((s32[2,2,1,12,128]{4,2,3,1,0:T(1,128)S(1)}, s32[2,2,1,12,128]{4,2,3,1,0:T(1,128)}, u32[]{:S(2)}) %copy-start.9) | copy-done | bytes 24600
  11.8 0.7 %copy-done.11 = f32[3,2,2,1,128]{4,3,2,1,0:T(1,128)S(1)} copy-done((f32[3,2,2,1,128]{4,3,2,1,0:T(1,128)S(1)}, f32[3,2,2,1,128]{4,3,2,1,0:T(1,128)}, u32[]{:S(2)}) %copy-start.11) | copy-done | bytes 6168
  12.4 0.7 %copy-done.12 = f32[3,2,2,1,128]{4,3,2,1,0:T(1,128)S(1)} copy-done((f32[3,2,2,1,128]{4,3,2,1,0:T(1,128)S(1)}, f32[3,2,2,1,128]{4,3,2,1,0:T(1,128)}, u32[]{:S(2)}) %copy-start.12) | copy-done | bytes 6168
  13.1 0.7 %copy-done.13 = bf16[12,128]{1,0:T(8,128)(2,1)S(1)} copy-done((bf16[12,128]{1,0:T(8,128)(2,1)S(1)}, bf16[12,128]{1,0:T(8,128)(2,1)}, u32[]{:S(2)}) %copy-start.13) | copy-done | bytes 3096
  13.8 0.7 %copy-done.14 = s32[2,2,1,128]{3,2,1,0:T(1,128)S(1)} copy-done((s32[2,2,1,128]{3,2,1,0:T(1,128)S(1)}, s32[2,2,1,128]{3,2,1,0:T(1,128)}, u32[]{:S(2)}) %copy-start.14) | copy-done | bytes 2072
  15.9 4.4 %prepare.1 = (bf16[11,128,128]{2,1,0:T(8,128)(2,1)S(1)}, bf16[3,128]{1,0:T(4,128)(2,1)S(1)}, bf16[48,128]{1,0:T(8,128)(2,1)S(1)}, bf16[2,128,128]{2,1,0:T(8,128)...) custom-call(s32[2,1,2]{2,1,0:T(1,128)S(1)} %bitcast.16, ...), custom_call_target="tpu_custom_call" | custom-call | flops 2000000000 | tf_op jit(solution)/shard_map/prepare/pallas_call | solution.py:576
  20.3 1.6 %collective-permute-start.1 = (bf16[3,128,128]{2,1,0:T(8,128)(2,1)S(1)}, bf16[3,128,128]{2,1,0:T(8,128)(2,1)S(1)}, u32[]{:S(2)}, u32[]{:S(2)}) collective-permute-start(bf16[3,128,128]{2,1,0:T(8,128)(2,1)S(1)} %pad_maximum_fusion), channel_id=1, source_target_pairs={{0,4},{1,5},{4,0},{5,1},{8,12},{9,13},{12,8},{13,9},{2,6},{3,7},{6... | collective-permute-start | bytes 294920 | tf_op jit(solution)/shard_map/ppermute | solution.py:572
  22.6 2.4 %collective-permute-done.1.refs_1_ = bf16[3,128,128]{2,1,0:T(8,128)(2,1)S(1)} collective-permute-done((bf16[3,128,128]{2,1,0:T(8,128)(2,1)S(1)}, bf16[3,128,128]{2,1,0:T(8,128)(2,1)S(1)}, u32[]{:S(2)}, u32[]{:S(2)}) %collective-permute-start.1) | collective-permute-done | bytes 98336 | tf_op jit(solution)/shard_map/ppermute | solution.py:572
  25.5 1.2 %collective-permute-done.4.refs_4_ = bf16[2,128,128]{2,1,0:T(8,128)(2,1)S(1)} collective-permute-done((bf16[2,128,128]{2,1,0:T(8,128)(2,1)S(1)}, bf16[2,128,128]{2,1,0:T(8,128)(2,1)S(1)}, u32[]{:S(2)}, u32[]{:S(2)}) %collective-permute-start.4) | collective-permute-done | bytes 65568 | tf_op jit(solution)/shard_map/ppermute | solution.py:554
  26.8 3.3 %movers.1 = (bf16[12,128,256]{2,1,0:T(8,128)(2,1)S(1)}, f32[16,128]{1,0:T(8,128)S(1)}) custom-call(bf16[2,2,1,128,128]{4,3,2,1,0:T(8,128)(2,1)S(1)} %copy-done.1, bf16[2,128,128]{2,1,0:T(8,128)(2,1)S(1)} %collective-permute-done.refs_0_, bf16[3,128,128]{2,1,0:T(8,128)(2,1)S(1)} %collective-permute-done.1.refs_1_, ...), custom_call_target="tpu_custom_call" | custom-call | flops 3000000000 | tf_op jit(solution)/shard_map/movers/pallas_call | solution.py:576
  30.2 3.6 %edges.2.first_ref = bf16[2,128,128]{2,1,0:T(8,128)(2,1)S(1)} custom-call(s32[2,1,2]{2,1,0:T(1,128)S(1)} %bitcast.17, bf16[2,2,1,128,128]{4,3,2,1,0:T(8,128)(2,1)S(1)} %copy-done.1, bf16[2,2,1,12,128,128]{5,4,3,2,1,0:T(8,128)(2,1)S(1)} %copy-done.3, s32[2,2,12,1,128]{4,3,2,1,0:T(1,128)S(1)} %bitcast.14, bf16[12,128,256]{2,1,0:T(8,128)(2,1)S(1)} %get-tuple-element.65.far_ref, ...), custom_call_target="tpu_custom_call" | custom-call | flops 4000000000 | tf_op jit(solution)/shard_map/edges/pallas_call | solution.py:576
  34.0 4.8 %collective-permute-start.8 = (f32[2,16,128]{2,1,0:T(8,128)S(1)}, f32[2,16,128]{2,1,0:T(8,128)S(1)}, u32[]{:S(2)}, u32[]{:S(2)}) collective-permute-start(f32[2,16,128]{2,1,0:T(8,128)S(1)} %pad_maximum_fusion.2.own_ref), channel_id=1, source_target_pairs={{0,4},{1,5},{4,0},{5,1},{8,12},{9,13},{12,8},{13,9},{2,6},{3,7},{6... | collective-permute-start | bytes 49160 | tf_op jit(solution)/shard_map/ppermute | solution.py:572
  38.8 3.6 %edges.3.second_ref = bf16[2,128,128]{2,1,0:T(8,128)(2,1)S(1)} custom-call(s32[2,1,2]{2,1,0:T(1,128)S(1)} %bitcast.18, bf16[2,2,1,128,128]{4,3,2,1,0:T(8,128)(2,1)S(1)} %copy-done.1, bf16[2,2,1,12,128,128]{5,4,3,2,1,0:T(8,128)(2,1)S(1)} %copy-done.3, s32[2,2,12,1,128]{4,3,2,1,0:T(1,128)S(1)} %bitcast.15, ...), custom_call_target="tpu_custom_call" | custom-call | flops 4000000000 | tf_op jit(solution)/shard_map/edges/pallas_call | solution.py:576
  43.0 2.4 %nodes.1 = (bf16[2,2,1,128,128]{4,3,2,1,0:T(8,128)(2,1)}, f32[9,2,2,1,128]{4,3,2,1,0:T(1,128)}) custom-call(bf16[2,128,128]{2,1,0:T(8,128)(2,1)S(1)} %edges.2.first_ref, bf16[2,128,128]{2,1,0:T(8,128)(2,1)S(1)} %edges.3.second_ref, f32[128,512]{1,0:T(8,128)S(1)} %get-tuple-element.69.node_pre_ref, f32[128,512]{1,0:T(8,128)S(1)} %get-tuple-element.70.latent_t_ref, ...), custom_call_target="tpu_custom_call" | custom-call | flops 2000000000 | tf_op jit(solution)/shard_map/nodes/pallas_call | solution.py:576
  45.4 1.5 %arrive.1 = (bf16[1,1,1,208,128]{4,3,2,1,0:T(8,128)(2,1)}, f32[9,1,1,1,208]{4,3,2,1,0:T(1,128)}) custom-call(f32[2,16,128]{2,1,0:T(8,128)S(1)} %pad_maximum_fusion.2.own_ref, f32[2,16,128]{2,1,0:T(8,128)S(1)} %collective-permute-done.8.even_ref, f32[2,16,128]{2,1,0:T(8,128)S(1)} %collective-permute-done.9.odd_ref, ...), custom_call_target="tpu_custom_call" | custom-call | flops 1000000000 | tf_op jit(solution)/shard_map/arrive/pallas_call | solution.py:576
  (48 shorter events, 3.5 us)
Async XLA Ops:
  1.5 18.8 %collective-permute-start = (bf16[2,128,128]{2,1,0:T(8,128)(2,1)S(1)}, bf16[2,128,128]{2,1,0:T(8,128)(2,1)S(1)}, u32[]{:S(2)}, u32[]{:S(2)}) collective-permute-start(bf16[2,128,128]{2,1,0:T(8,128)(2,1)S(1)} %dynamic-slice_bitcast_fusion.2), channel_id=1, source_target_pairs={{0,2},{2,0},{1,3},{3,1},{4,6},{6,4},{5,7},{7,5},{8,10},{10,8},{9,1... | collective-permute-start | bytes 196616 | tf_op jit(solution)/shard_map/ppermute | solution.py:554
  4.4 0.9 %copy-start = (bf16[2,2,1,128,128]{4,3,2,1,0:T(8,128)(2,1)S(1)}, bf16[2,2,1,128,128]{4,3,2,1,0:T(8,128)(2,1)}, u32[]{:S(2)}) copy-start(bf16[2,2,1,128,128]{4,3,2,1,0:T(8,128)(2,1)} %latent_any.7) | copy-start | bytes 393220
  5.3 1.4 %copy-start.2 = (bf16[2,2,1,12,128,128]{5,4,3,2,1,0:T(8,128)(2,1)S(1)}, bf16[2,2,1,12,128,128]{5,4,3,2,1,0:T(8,128)(2,1)}, u32[]{:S(2)}) copy-start(bf16[2,2,1,12,128,128]{5,4,3,2,1,0:T(8,128)(2,1)} %edge_any.5) | copy-start | bytes 4718596
  6.7 0.9 %copy-start.4 = (bf16[5,128,128]{2,1,0:T(8,128)(2,1)S(1)}, bf16[5,128,128]{2,1,0:T(8,128)(2,1)}, u32[]{:S(2)}) copy-start(bf16[5,128,128]{2,1,0:T(8,128)(2,1)} %edge_w_any.1) | copy-start | bytes 491524
  7.7 0.8 %copy-start.5 = (bf16[256,128]{1,0:T(8,128)(2,1)S(1)}, bf16[256,128]{1,0:T(8,128)(2,1)}, u32[]{:S(2)}) copy-start(bf16[256,128]{1,0:T(8,128)(2,1)} %node_in_any.1) | copy-start | bytes 196612
  8.5 0.8 %copy-start.6 = (bf16[2,128,128]{2,1,0:T(8,128)(2,1)S(1)}, bf16[2,128,128]{2,1,0:T(8,128)(2,1)}, u32[]{:S(2)}) copy-start(bf16[2,128,128]{2,1,0:T(8,128)(2,1)} %node_w_any.1) | copy-start | bytes 196612
  9.3 0.8 %copy-start.7 = (bf16[2,128,128]{2,1,0:T(8,128)(2,1)S(1)}, bf16[2,128,128]{2,1,0:T(8,128)(2,1)}, u32[]{:S(2)}) copy-start(bf16[2,128,128]{2,1,0:T(8,128)(2,1)} %decoder_w_any.1) | copy-start | bytes 196612
  10.2 0.8 %copy-start.8 = (bf16[2,128,128]{2,1,0:T(8,128)(2,1)S(1)}, bf16[2,128,128]{2,1,0:T(8,128)(2,1)}, u32[]{:S(2)}) copy-start(bf16[2,128,128]{2,1,0:T(8,128)(2,1)} %encoder_w_any.1) | copy-start | bytes 196612
  11.0 0.7 %copy-start.9 = (s32[2,2,1,12,128]{4,2,3,1,0:T(1,128)S(1)}, s32[2,2,1,12,128]{4,2,3,1,0:T(1,128)}, u32[]{:S(2)}) copy-start(s32[2,2,1,12,128]{4,2,3,1,0:T(1,128)} %param.19) | copy-start | bytes 73732
  15.9 10.9 %copy-start.1 = (bf16[2,2,1,128,128]{4,3,2,1,0:T(8,128)(2,1)S(1)}, bf16[2,2,1,128,128]{4,3,2,1,0:T(8,128)(2,1)}, u32[]{:S(2)}) copy-start(bf16[2,2,1,128,128]{4,3,2,1,0:T(8,128)(2,1)} %latent_any.7) | copy-start | bytes 393220
  20.3 4.7 %collective-permute-start.1 = (bf16[3,128,128]{2,1,0:T(8,128)(2,1)S(1)}, bf16[3,128,128]{2,1,0:T(8,128)(2,1)S(1)}, u32[]{:S(2)}, u32[]{:S(2)}) collective-permute-start(bf16[3,128,128]{2,1,0:T(8,128)(2,1)S(1)} %pad_maximum_fusion), channel_id=1, source_target_pairs={{0,4},{1,5},{4,0},{5,1},{8,12},{9,13},{12,8},{13,9},{2,6},{3,7},{6... | collective-permute-start | bytes 294920 | tf_op jit(solution)/shard_map/ppermute | solution.py:572
  22.0 8.3 %copy-start.3 = (bf16[2,2,1,12,128,128]{5,4,3,2,1,0:T(8,128)(2,1)S(1)}, bf16[2,2,1,12,128,128]{5,4,3,2,1,0:T(8,128)(2,1)}, u32[]{:S(2)}) copy-start(bf16[2,2,1,12,128,128]{5,4,3,2,1,0:T(8,128)(2,1)} %edge_any.5) | copy-start | bytes 4718596
  22.0 8.2 %copy-start.10 = (s32[2,2,1,12,128]{4,2,3,1,0:T(1,128)S(1)}, s32[2,2,1,12,128]{4,2,3,1,0:T(1,128)}, u32[]{:S(2)}) copy-start(s32[2,2,1,12,128]{4,2,3,1,0:T(1,128)} %param.19) | copy-start | bytes 73732
  22.0 3.0 %collective-permute-start.2 = (bf16[3,128,128]{2,1,0:T(8,128)(2,1)S(1)}, bf16[3,128,128]{2,1,0:T(8,128)(2,1)S(1)}, u32[]{:S(2)}, u32[]{:S(2)}) collective-permute-start(bf16[3,128,128]{2,1,0:T(8,128)(2,1)S(1)} %pad_maximum_fusion.1), channel_id=1, source_target_pairs={{0,1},{1,0},{4,8},{5,9},{8,4},{9,5},{12,13},{13,12},{2,3},{3,2},{6... | collective-permute-start | bytes 294920 | tf_op jit(solution)/shard_map/ppermute | solution.py:572
  22.1 3.4 %collective-permute-start.3 = (bf16[2,2,1,128,128]{4,3,2,1,0:T(8,128)(2,1)S(1)}, bf16[2,2,1,128,128]{4,3,2,1,0:T(8,128)(2,1)S(1)}, u32[]{:S(2)}, u32[]{:S(2)}) collective-permute-start(bf16[2,2,1,128,128]{4,3,2,1,0:T(8,128)(2,1)S(1)} %copy-done), channel_id=1, source_target_pairs={{0,1},{1,0},{2,3},{3,2},{4,5},{5,4},{6,7},{7,6},{8,9},{9,8},{10,11... | collective-permute-start | bytes 393224 | tf_op jit(solution)/shard_map/ppermute | solution.py:554
  25.0 1.8 %collective-permute-start.5 = (bf16[3,128,128]{2,1,0:T(8,128)(2,1)S(1)}, bf16[3,128,128]{2,1,0:T(8,128)(2,1)S(1)}, u32[]{:S(2)}, u32[]{:S(2)}) collective-permute-start(bf16[3,128,128]{2,1,0:T(8,128)(2,1)S(1)} %collective-permute-done.1.refs_1_), channel_id=1, source_target_pairs={{0,1},{1,0},{2,3},{3,2},{4,5},{5,4},{6,7},{7,6},{8,9},{9,8},{10,11... | collective-permute-start | bytes 294920 | tf_op jit(solution)/shard_map/ppermute | solution.py:554
  25.0 1.8 %collective-permute-start.6 = (bf16[3,128,128]{2,1,0:T(8,128)(2,1)S(1)}, bf16[3,128,128]{2,1,0:T(8,128)(2,1)S(1)}, u32[]{:S(2)}, u32[]{:S(2)}) collective-permute-start(bf16[3,128,128]{2,1,0:T(8,128)(2,1)S(1)} %collective-permute-done.2.refs_2_), channel_id=1, source_target_pairs={{0,1},{1,0},{2,3},{3,2},{4,5},{5,4},{6,7},{7,6},{8,9},{9,8},{10,11... | collective-permute-start | bytes 294920 | tf_op jit(solution)/shard_map/ppermute | solution.py:554
  25.5 1.3 %collective-permute-start.4 = (bf16[2,128,128]{2,1,0:T(8,128)(2,1)S(1)}, bf16[2,128,128]{2,1,0:T(8,128)(2,1)S(1)}, u32[]{:S(2)}, u32[]{:S(2)}) collective-permute-start(bf16[2,128,128]{2,1,0:T(8,128)(2,1)S(1)} %collective-permute-done.refs_0_), channel_id=1, source_target_pairs={{0,1},{1,0},{2,3},{3,2},{4,5},{5,4},{6,7},{7,6},{8,9},{9,8},{10,11... | collective-permute-start | bytes 196616 | tf_op jit(solution)/shard_map/ppermute | solution.py:554
  30.1 3.7 %collective-permute-start.7 = (f32[16,128]{1,0:T(8,128)S(1)}, f32[16,128]{1,0:T(8,128)S(1)}, u32[]{:S(2)}, u32[]{:S(2)}) collective-permute-start(f32[16,128]{1,0:T(8,128)S(1)} %get-tuple-element.64), channel_id=1, source_target_pairs={{0,2},{2,0},{1,3},{3,1},{4,6},{6,4},{5,7},{7,5},{8,10},{10,8},{9,1... | collective-permute-start | bytes 24584 | tf_op jit(solution)/shard_map/ppermute | solution.py:554
  33.8 8.6 %collective-permute-start.9 = (f32[2,16,128]{2,1,0:T(8,128)S(1)}, f32[2,16,128]{2,1,0:T(8,128)S(1)}, u32[]{:S(2)}, u32[]{:S(2)}) collective-permute-start(f32[2,16,128]{2,1,0:T(8,128)S(1)} %pad_maximum_fusion.2.own_ref), channel_id=1, source_target_pairs={{0,1},{1,0},{4,8},{5,9},{8,4},{9,5},{12,13},{13,12},{2,3},{3,2},{6... | collective-permute-start | bytes 49160 | tf_op jit(solution)/shard_map/ppermute | solution.py:572
  34.0 8.5 %collective-permute-start.8 = (f32[2,16,128]{2,1,0:T(8,128)S(1)}, f32[2,16,128]{2,1,0:T(8,128)S(1)}, u32[]{:S(2)}, u32[]{:S(2)}) collective-permute-start(f32[2,16,128]{2,1,0:T(8,128)S(1)} %pad_maximum_fusion.2.own_ref), channel_id=1, source_target_pairs={{0,4},{1,5},{4,0},{5,1},{8,12},{9,13},{12,8},{13,9},{2,6},{3,7},{6... | collective-permute-start | bytes 49160 | tf_op jit(solution)/shard_map/ppermute | solution.py:572
  42.4 3.0 %collective-permute-start.10 = (f32[2,16,128]{2,1,0:T(8,128)S(1)}, f32[2,16,128]{2,1,0:T(8,128)S(1)}, u32[]{:S(2)}, u32[]{:S(2)}) collective-permute-start(f32[2,16,128]{2,1,0:T(8,128)S(1)} %pad_maximum_fusion.2.own_ref), channel_id=1, source_target_pairs={{0,1},{1,0},{2,3},{3,2},{4,5},{5,4},{6,7},{7,6},{8,9},{9,8},{10,11... | collective-permute-start | bytes 49160 | tf_op jit(solution)/shard_map/ppermute | solution.py:554
  42.5 2.9 %collective-permute-start.11 = (f32[2,16,128]{2,1,0:T(8,128)S(1)}, f32[2,16,128]{2,1,0:T(8,128)S(1)}, u32[]{:S(2)}, u32[]{:S(2)}) collective-permute-start(f32[2,16,128]{2,1,0:T(8,128)S(1)} %collective-permute-done.8.even_ref), channel_id=1, source_target_pairs={{0,1},{1,0},{2,3},{3,2},{4,5},{5,4},{6,7},{7,6},{8,9},{9,8},{10,11... | collective-permute-start | bytes 49160 | tf_op jit(solution)/shard_map/ppermute | solution.py:554
  43.0 2.5 %collective-permute-start.12 = (f32[2,16,128]{2,1,0:T(8,128)S(1)}, f32[2,16,128]{2,1,0:T(8,128)S(1)}, u32[]{:S(2)}, u32[]{:S(2)}) collective-permute-start(f32[2,16,128]{2,1,0:T(8,128)S(1)} %collective-permute-done.9.odd_ref), channel_id=1, source_target_pairs={{0,1},{1,0},{2,3},{3,2},{4,5},{5,4},{6,7},{7,6},{8,9},{9,8},{10,11... | collective-permute-start | bytes 49160 | tf_op jit(solution)/shard_map/ppermute | solution.py:554
  (6 other events, 4.1 us)

commit v4 on v3

--- a/solution.py
+++ b/solution.py
@@ -156,14 +156,9 @@
     return jnp.concatenate([position + new_velocity, new_velocity, velocity], axis=0)
 
 
-def prepare_kernel(
+def ranks_kernel(
     sizes,
     fill_ref,
-    latent_any,
-    edge_any,
-    positions_any,
-    velocity_any,
-    neighbours_any,
     owners_any,
     edge_w_any,
     node_in_any,
@@ -176,20 +171,8 @@
     decoder_out_ref,
     inward_ref,
     encoder_w_ref,
-    latent_t_ref,
-    node_pre_ref,
-    state_ref,
-    mover_pre_ref,
-    mover_place_ref,
-    mover_key_ref,
-    mover_node_pre_ref,
-    mover_latent_ref,
-    mover_state_ref,
-    latent_ref,
-    edge_ref,
-    positions_ref,
-    velocity_ref,
-    neighbours_ref,
+    placer_ref,
+    masks_ref,
     owners_ref,
     edge_w_ref,
     node_in_ref,
@@ -204,11 +187,6 @@
         [
             (owners_any, owners_ref),
             (edge_w_any, edge_w_ref),
-            (neighbours_any, neighbours_ref),
-            (positions_any, positions_ref),
-            (velocity_any, velocity_ref),
-            (latent_any, latent_ref),
-            (edge_any, edge_ref),
             (node_in_any, node_in_ref),
             (node_w_any, node_w_ref),
             (decoder_w_any, decoder_w_ref),
@@ -223,8 +201,8 @@
     index_x = lax.axis_index("gx")
     index_y = lax.axis_index("gy")
     index_z = lax.axis_index("gz")
-    slots, width = latent_ref.shape[-2:]
-    neighbour_count = edge_ref.shape[3]
+    slots = owners_ref.shape[-1]
+    width = node_in_ref.shape[-1]
 
     lane = lax.broadcasted_iota(I32, (1, slots), 1)
     owner = jnp.concatenate([owners_ref[a, b] for a, b in CELLS], axis=1)
@@ -259,10 +237,13 @@
     counted = jnp.concatenate(counted, axis=1)
     rank = (jnp.sum(counted * member, axis=0, keepdims=True) - 1.0).astype(I32)
     column = jnp.where(moving == 1, group * CAP + rank, -1)
-    movers = mover_state_ref.shape[1]
-    placer = jnp.where(
+    movers = placer_ref.shape[0]
+    placer_ref[...] = jnp.where(
         lax.broadcasted_iota(I32, (movers, particles), 0) == column, 1.0, 0.0
     ).astype(BF16)
+    masks_ref[...] = jnp.concatenate(
+        [stays, moving.astype(F32), jnp.zeros((6, particles), F32)], axis=0
+    )
 
     for i in range(5):
         weights_ref[i] = flip(edge_w_ref[i])
@@ -275,6 +256,51 @@
     inward = inward.astype(BF16)
     inward_ref[...] = jnp.concatenate([inward, inward, inward], axis=0)
 
+
+def prepare_kernel(
+    sizes,
+    latent_any,
+    edge_any,
+    positions_any,
+    velocity_any,
+    neighbours_any,
+    weights_ref,
+    placer_ref,
+    masks_ref,
+    latent_t_ref,
+    node_pre_ref,
+    state_ref,
+    mover_pre_ref,
+    mover_place_ref,
+    mover_key_ref,
+    mover_node_pre_ref,
+    mover_latent_ref,
+    mover_state_ref,
+    latent_ref,
+    edge_ref,
+    positions_ref,
+    velocity_ref,
+    neighbours_ref,
+    sems,
+):
+    fold_y = sizes[1] == 2
+    copies = fetch(
+        [
+            (neighbours_any, neighbours_ref),
+            (positions_any, positions_ref),
+            (velocity_any, velocity_ref),
+            (latent_any, latent_ref),
+            (edge_any, edge_ref),
+        ],
+        sems,
+    )
+    for copy in copies[:4]:
+        copy.wait()
+    neighbour_count = edge_ref.shape[3]
+    placer = placer_ref[...]
+    movers, particles = placer.shape
+    stays, moving = masks_ref[0:1], masks_ref[1:2]
+
     latent = jnp.concatenate([latent_ref[a, b, 0] for a, b in CELLS], axis=0)
     latent_t_ref[...] = latent.astype(F32).T
     node_pre_ref[...] = dot_nt(weights_ref[NODE_OLD], latent)
@@ -289,7 +315,7 @@
     mover_latent_ref[...] = mover_latent.astype(F32).T
     mover_node_pre_ref[...] = dot_nt(weights_ref[NODE_OLD], mover_latent)
     near = dot_nt(weights_ref[NEAR], mover_latent)
-    state = jnp.concatenate(state + [moving.astype(F32), jnp.zeros_like(stays)], axis=0)
+    state = jnp.concatenate(state + [moving, jnp.zeros_like(stays)], axis=0)
     mover_state_ref[...] = joined(dot_nt(thirds(state), placer))
     ids = jnp.concatenate(
         [
@@ -303,6 +329,7 @@
     place, key = places(ids[:neighbour_count], ids[neighbour_count : 2 * neighbour_count], fold_y)
     mover_place_ref[...] = place
     mover_key_ref[...] = key
+    copies[4].wait()
     for k in range(neighbour_count):
         edges = jnp.concatenate([edge_ref[a, b, 0, k] for a, b in CELLS], axis=0)
         edges = dot(placer, edges).astype(BF16)
@@ -585,6 +612,10 @@
     )(*operands)
 
 
+def in_hbm(array):
+    return pltpu.with_memory_space_constraint(array, pltpu.HBM)
+
+
 def like(array):
     return pltpu.VMEM(array.shape, array.dtype)
 
@@ -624,15 +655,62 @@
     else:
         sides = [shift(cells[:, 1], "gy", 0), shift(cells[:, 0], "gy", 1)]
 
-    prepared = call(
-        functools.partial(prepare_kernel, sizes),
-        "prepare",
-        [SMEM] + [ANY] * 13,
+    ranked = call(
+        functools.partial(ranks_kernel, sizes),
+        "ranks",
+        [SMEM] + [ANY] * 8,
         [
             ((11, width, width), BF16),
             (decoder_out.shape, BF16),
             ((48, width), BF16),
             (encoder_weights.shape, BF16),
+            ((movers, particles), BF16),
+            ((8, particles), F32),
+        ],
+        [
+            like(owners),
+            like(edge_weights),
+            like(node_in),
+            like(node_weights),
+            like(decoder_weights),
+            like(encoder_in),
+            pltpu.SemaphoreType.DMA((8,)),
+        ],
+        [
+            in_hbm(array)
+            for array in (
+                fill,
+                owners,
+                edge_weights,
+                node_in,
+                node_weights,
+                decoder_weights,
+                decoder_out,
+                encoder_in,
+                encoder_weights,
+            )
+        ],
+        500_000_000,
+    )
+    sides, ranked = lax.optimization_barrier((sides, ranked))
+    weights, decoder_out, inward, encoder_weights, placer, masks = ranked
+
+    if fold_y:
+        layers = [cells, sides[0][:, None]]
+    else:
+        layers = [sides[0][:, None], cells, sides[1][:, None]]
+
+    def layer(a):
+        return jnp.concatenate(
+            [lax.dynamic_index_in_dim(part, a, 0, keepdims=False) for part in layers], axis=0
+        )
+
+    ends = [swap_x(layer(1 - parity), 0), swap_x(layer(parity), 1)]
+    prepared = call(
+        functools.partial(prepare_kernel, sizes),
+        "prepare",
+        [ANY] * 5 + [VMEM] * 3,
+        [
             ((width, particles), F32),
             ((width, particles), F32),
             ((8, particles), F32),
@@ -649,38 +727,17 @@
             like(positions),
             like(velocity),
             like(neighbours),
-            like(owners),
-            like(edge_weights),
-            like(node_in),
-            like(node_weights),
-            like(decoder_weights),
-            like(encoder_in),
-            pltpu.SemaphoreType.DMA((13,)),
-        ],
-        (
-            fill,
-            node_latent,
-            edge_latent,
-            positions,
-            velocity,
-            neighbours,
-            owners,
-            edge_weights,
-            node_in,
-            node_weights,
-            decoder_weights,
-            decoder_out,
-            encoder_in,
-            encoder_weights,
-        ),
-        2_000_000_000,
-    )
-    sides, prepared = lax.optimization_barrier((sides, prepared))
+            pltpu.SemaphoreType.DMA((5,)),
+        ],
+        [
+            in_hbm(array)
+            for array in (node_latent, edge_latent, positions, velocity, neighbours)
+        ]
+        + [weights, placer, masks],
+        500_000_000,
+    )
+    ends, prepared = lax.optimization_barrier((ends, prepared))
     (
-        weights,
-        decoder_out,
-        inward,
-        encoder_weights,
         latent_t,
         node_pre,
         state,
@@ -691,18 +748,7 @@
         mover_latent,
         mover_state,
     ) = prepared
-
-    if fold_y:
-        layers = [cells, sides[0][:, None]]
-    else:
-        layers = [sides[0][:, None], cells, sides[1][:, None]]
-
-    def layer(a):
-        return jnp.concatenate(
-            [lax.dynamic_index_in_dim(part, a, 0, keepdims=False) for part in layers], axis=0
-        )
-
-    halo = [*sides, swap_x(layer(1 - parity), 0), swap_x(layer(parity), 1)]
+    halo = [*sides, *ends]
     halo = halo + [swap(part, "gz") for part in [node_latent] + halo]
 
     far, bucket = call(
@@ -743,7 +789,7 @@
                 pltpu.VMEM((2, width, neighbour_count * slots), BF16),
                 pltpu.SemaphoreType.DMA((3,)),
             ],
-            (fill, node_latent, edge_latent, neighbours, far, weights),
+            (in_hbm(fill), in_hbm(node_latent), in_hbm(edge_latent), in_hbm(neighbours), far, weights),
             4_000_000_000,
         )[0]
 

time: 47.5 us -> 37.9 us (0.80)
  local copies, waits for them, and re-layouts: 12.3 us -> 1.81 us
  Pallas kernels: 18.6 us -> 22.4 us
  waiting for transfers between devices: 3.7 us -> 1.19 us
    unnamed x34 -> x4, local copies, waits for them, and re-layouts: 11.4 us -> 0.01 us
    pallas_call x6 -> x7, Pallas kernels: 18.6 us -> 22.4 us  [call(): pl.pallas_call(kernel, out_shape=tuple((jax.ShapeDtypeStruct(shape, kind)...]
    ppermute x4, waiting for transfers between devices: 2.43 us -> 0.01 us  [swap_x(): return lax.ppermute(values, ('gx', 'gz'), pairs)]
    ppermute x4, starting transfers between devices: 6.7 us -> 5.17 us  [swap_x(): return lax.ppermute(values, ('gx', 'gz'), pairs)]
    ppermute x9, starting transfers between devices: 4.75 us -> 6.08 us  [swap(): return lax.ppermute(values, axis, [(0, 1), (1, 0)])]
    squeeze x2, local copies, waits for them, and re-layouts: 0.03 us -> 0.9 us  [layer(): lax.dynamic_index_in_dim(part, a, 0, keepdims=False)]
  transfers between devices with their start and end apart: 13 -> 13, of which waited for: 2 -> 1; matrix products, arithmetic and copies ran while one was open for 0% -> 2% of each run, Pallas kernels for 29% -> 47%
where the time goes in v4:
time: 37.9 us; the launch traced here: 37.5 us
  Pallas kernels  22.4 us (59%)
  starting transfers between devices  11.2 us (30%)
  local copies, waits for them, and re-layouts  1.81 us (5%)
  waiting for transfers between devices  1.19 us (3%)
  between operations  0.82 us (2%)
    pallas_call x7, Pallas kernels, call(): pl.pallas_call(kernel, out_shape=tuple((jax.ShapeDtypeStruct(shape, kind)...  22.4 us
    ppermute x9, starting transfers between devices, swap(): return lax.ppermute(values, axis, [(0, 1), (1, 0)])  6.08 us
    ppermute x4, starting transfers between devices, swap_x(): return lax.ppermute(values, ('gx', 'gz'), pairs)  5.17 us
    ppermute x9, waiting for transfers between devices, swap(): return lax.ppermute(values, axis, [(0, 1), (1, 0)])  1.18 us
    squeeze x1, local copies, waits for them, and re-layouts, body(): lax.dynamic_index_in_dim(cells, inner, 1, keepdims=False)  0.9 us
    squeeze x2, local copies, waits for them, and re-layouts, layer(): lax.dynamic_index_in_dim(part, a, 0, keepdims=False)  0.9 us
  transfers between devices with their start and end apart: 13, of which 1 were waited for; matrix products, arithmetic and copies ran while one was open for 2% of the time, Pallas kernels for 47%

profile of v4, /device:TPU:0, one launch (start us, length us, event | category | flops | bytes accessed | tf_op | source)
XLA Modules:
  0.0 37.5 jit_solution(16848577046704432232)
XLA Ops:
  0.6 0.0 copy-start
  0.6 0.9 %dynamic-slice_bitcast_fusion.2 = bf16[2,128,128]{2,1,0:T(8,128)(2,1)S(1)} fusion(bf16[2,2,1,128,128]{4,3,2,1,0:T(8,128)(2,1)} %latent_any.7, s32[]{:T(128)S(6)} %select_n.14), kind=kLoop, calls=%fused_computation.4 | loop fusion | bytes 131076 | tf_op jit(solution)/shard_map/jit(dynamic_index_in_dim)/squeeze | solution.py:654
  1.6 2.9 %collective-permute-start = (bf16[2,128,128]{2,1,0:T(8,128)(2,1)S(1)}, bf16[2,128,128]{2,1,0:T(8,128)(2,1)S(1)}, u32[]{:S(2)}, u32[]{:S(2)}) collective-permute-start(bf16[2,128,128]{2,1,0:T(8,128)(2,1)S(1)} %dynamic-slice_bitcast_fusion.2), channel_id=1, source_target_pairs={{0,2},{2,0},{1,3},{3,1},{4,6},{6,4},{5,7},{7,5},{8,10},{10,8},{9,1... | collective-permute-start | bytes 196616 | tf_op jit(solution)/shard_map/ppermute | solution.py:581
  4.5 0.9 %dynamic-slice_bitcast_fusion = (bf16[2,128,128]{2,1,0:T(8,128)(2,1)S(1)}, bf16[2,128,128]{2,1,0:T(8,128)(2,1)S(1)}) fusion(bf16[2,2,1,128,128]{4,3,2,1,0:T(8,128)(2,1)} %latent_any.7, s32[]{:T(128)S(6)} %select_n.16, s32[]{:T(128)S(6)} %select_n.15), kind=kLoop, calls=%fused_computation.2 | loop fusion | bytes 262152 | tf_op jit(solution)/shard_map/jit(dynamic_index_in_dim)/squeeze | solution.py:705
  5.4 2.1 %ranks.1 = (bf16[11,128,128]{2,1,0:T(8,128)(2,1)S(1)}, bf16[3,128]{1,0:T(4,128)(2,1)S(1)}, bf16[48,128]{1,0:T(8,128)(2,1)S(1)}, bf16[2,128,128]{2,1,0:T(8,128)(2...) custom-call(s32[2,1,2]{2,1,0:T(1,128)} %bitcast.17, s32[2,2,1,128]{3,2,1,0:T(1,128)} %owners_any.1, ...), custom_call_target="tpu_custom_call" | custom-call | flops 500000000 | tf_op jit(solution)/shard_map/ranks/pallas_call | solution.py:603
  7.5 1.6 %collective-permute-start.1 = (bf16[3,128,128]{2,1,0:T(8,128)(2,1)S(1)}, bf16[3,128,128]{2,1,0:T(8,128)(2,1)S(1)}, u32[]{:S(2)}, u32[]{:S(2)}) collective-permute-start(bf16[3,128,128]{2,1,0:T(8,128)(2,1)S(1)} %pad_maximum_fusion), channel_id=1, source_target_pairs={{0,4},{1,5},{4,0},{5,1},{8,12},{9,13},{12,8},{13,9},{2,6},{3,7},{6... | collective-permute-start | bytes 294920 | tf_op jit(solution)/shard_map/ppermute | solution.py:599
  9.2 0.1 collective-permute-start.2
  9.3 0.5 %collective-permute-start.3 = (bf16[2,2,1,128,128]{4,3,2,1,0:T(8,128)(2,1)S(1)}, bf16[2,2,1,128,128]{4,3,2,1,0:T(8,128)(2,1)S(1)}, u32[]{:S(2)}, u32[]{:S(2)}) collective-permute-start(bf16[2,2,1,128,128]{4,3,2,1,0:T(8,128)(2,1)S(1)} %copy-done), channel_id=1, source_target_pairs={{0,1},{1,0},{2,3},{3,2},{4,5},{5,4},{6,7},{7,6},{8,9},{9,8},{10,11... | collective-permute-start | bytes 393224 | tf_op jit(solution)/shard_map/ppermute | solution.py:581
  9.7 3.8 %prepare.1 = (f32[128,512]{1,0:T(8,128)S(1)}, f32[128,512]{1,0:T(8,128)S(1)}, f32[8,512]{1,0:T(8,128)S(1)}, f32[128,1536]{1,0:T(8,128)S(1)}, s32[12,128]{1,0:T(8...) custom-call(bf16[2,2,1,128,128]{4,3,2,1,0:T(8,128)(2,1)} %latent_any., ...), custom_call_target="tpu_custom_call" | custom-call | flops 500000000 | tf_op jit(solution)/shard_map/prepare/pallas_call | solution.py:603
  13.5 0.2 collective-permute-start.5
  13.7 0.4 %collective-permute-start.6 = (bf16[3,128,128]{2,1,0:T(8,128)(2,1)S(1)}, bf16[3,128,128]{2,1,0:T(8,128)(2,1)S(1)}, u32[]{:S(2)}, u32[]{:S(2)}) collective-permute-start(bf16[3,128,128]{2,1,0:T(8,128)(2,1)S(1)} %collective-permute-done.2.refs_2_), channel_id=1, source_target_pairs={{0,1},{1,0},{2,3},{3,2},{4,5},{5,4},{6,7},{7,6},{8,9},{9,8},{10,11... | collective-permute-start | bytes 294920 | tf_op jit(solution)/shard_map/ppermute | solution.py:581
  14.1 0.1 collective-permute-start.4
  14.2 1.2 %collective-permute-done.4.refs_4_ = bf16[2,128,128]{2,1,0:T(8,128)(2,1)S(1)} collective-permute-done((bf16[2,128,128]{2,1,0:T(8,128)(2,1)S(1)}, bf16[2,128,128]{2,1,0:T(8,128)(2,1)S(1)}, u32[]{:S(2)}, u32[]{:S(2)}) %collective-permute-start.4) | collective-permute-done | bytes 65568 | tf_op jit(solution)/shard_map/ppermute | solution.py:581
  15.4 3.3 %movers.1 = (bf16[12,128,256]{2,1,0:T(8,128)(2,1)S(1)}, f32[16,128]{1,0:T(8,128)S(1)}) custom-call(bf16[2,2,1,128,128]{4,3,2,1,0:T(8,128)(2,1)S(1)} %copy-done.1, bf16[2,128,128]{2,1,0:T(8,128)(2,1)S(1)} %collective-permute-done.refs_0_, bf16[3,128,128]{2,1,0:T(8,128)(2,1)S(1)} %collective-permute-done.1.refs_1_, ...), custom_call_target="tpu_custom_call" | custom-call | flops 3000000000 | tf_op jit(solution)/shard_map/movers/pallas_call | solution.py:603
  18.7 1.3 %collective-permute-start.7 = (f32[16,128]{1,0:T(8,128)S(1)}, f32[16,128]{1,0:T(8,128)S(1)}, u32[]{:S(2)}, u32[]{:S(2)}) collective-permute-start(f32[16,128]{1,0:T(8,128)S(1)} %get-tuple-element.76), channel_id=1, source_target_pairs={{0,2},{2,0},{1,3},{3,1},{4,6},{6,4},{5,7},{7,5},{8,10},{10,8},{9,1... | collective-permute-start | bytes 24584 | tf_op jit(solution)/shard_map/ppermute | solution.py:581
  20.0 4.7 %edges.2.first_ref = bf16[2,128,128]{2,1,0:T(8,128)(2,1)S(1)} custom-call(s32[2,1,2]{2,1,0:T(1,128)} %bitcast.18, bf16[2,2,1,128,128]{4,3,2,1,0:T(8,128)(2,1)} %latent_any.7, bf16[2,2,1,12,128,128]{5,4,3,2,1,0:T(8,128)(2,1)} %edge_any.5, s32[2,2,12,1,128]{4,3,2,1,0:T(1,128)} %bitcast.14, bf16[12,128,256]{2,1,0:T(8,128)(2,1)S(1)} %get-tuple-element.77.far_ref, ...), custom_call_target="tpu_custom_call" | custom-call | flops 4000000000 | tf_op jit(solution)/shard_map/edges/pallas_call | solution.py:603
  24.8 0.1 collective-permute-start.9
  24.9 3.4 %collective-permute-start.8 = (f32[2,16,128]{2,1,0:T(8,128)S(1)}, f32[2,16,128]{2,1,0:T(8,128)S(1)}, u32[]{:S(2)}, u32[]{:S(2)}) collective-permute-start(f32[2,16,128]{2,1,0:T(8,128)S(1)} %pad_maximum_fusion.2.own_ref), channel_id=1, source_target_pairs={{0,4},{1,5},{4,0},{5,1},{8,12},{9,13},{12,8},{13,9},{2,6},{3,7},{6... | collective-permute-start | bytes 49160 | tf_op jit(solution)/shard_map/ppermute | solution.py:599
  28.2 4.7 %edges.3.second_ref = bf16[2,128,128]{2,1,0:T(8,128)(2,1)S(1)} custom-call(s32[2,1,2]{2,1,0:T(1,128)} %bitcast.19, bf16[2,2,1,128,128]{4,3,2,1,0:T(8,128)(2,1)} %latent_any.7, bf16[2,2,1,12,128,128]{5,4,3,2,1,0:T(8,128)(2,1)} %edge_any.5, s32[2,2,12,1,128]{4,3,2,1,0:T(1,128)} %bitcast.15, bf16[12,128,256]{2,1,0:T(8,128)(2,1)S(1)} %get-tuple-element.77.far_ref, ...), custom_call_target="tpu_custom_call" | custom-call | flops 4000000000 | tf_op jit(solution)/shard_map/edges/pallas_call | solution.py:603
  33.0 0.1 collective-permute-start.10
  33.1 0.5 %collective-permute-start.11 = (f32[2,16,128]{2,1,0:T(8,128)S(1)}, f32[2,16,128]{2,1,0:T(8,128)S(1)}, u32[]{:S(2)}, u32[]{:S(2)}) collective-permute-start(f32[2,16,128]{2,1,0:T(8,128)S(1)} %collective-permute-done.8.even_ref), channel_id=1, source_target_pairs={{0,1},{1,0},{2,3},{3,2},{4,5},{5,4},{6,7},{7,6},{8,9},{9,8},{10,11... | collective-permute-start | bytes 49160 | tf_op jit(solution)/shard_map/ppermute | solution.py:581
  33.6 0.1 collective-permute-start.12
  33.7 2.3 %nodes.1 = (bf16[2,2,1,128,128]{4,3,2,1,0:T(8,128)(2,1)}, f32[9,2,2,1,128]{4,3,2,1,0:T(1,128)}) custom-call(bf16[2,128,128]{2,1,0:T(8,128)(2,1)S(1)} %edges.2.first_ref, bf16[2,128,128]{2,1,0:T(8,128)(2,1)S(1)} %edges.3.second_ref, f32[128,512]{1,0:T(8,128)S(1)} %get-tuple-element.81.node_pre_ref, f32[128,512]{1,0:T(8,128)S(1)} %get-tuple-element.82.latent_t_ref, ...), custom_call_target="tpu_custom_call" | custom-call | flops 2000000000 | tf_op jit(solution)/shard_map/nodes/pallas_call | solution.py:603
  36.0 1.5 %arrive.1 = (bf16[1,1,1,208,128]{4,3,2,1,0:T(8,128)(2,1)}, f32[9,1,1,1,208]{4,3,2,1,0:T(1,128)}) custom-call(f32[2,16,128]{2,1,0:T(8,128)S(1)} %pad_maximum_fusion.2.own_ref, f32[2,16,128]{2,1,0:T(8,128)S(1)} %collective-permute-done.8.even_ref, f32[2,16,128]{2,1,0:T(8,128)S(1)} %collective-permute-done.9.odd_ref, ...), custom_call_target="tpu_custom_call" | custom-call | flops 1000000000 | tf_op jit(solution)/shard_map/arrive/pallas_call | solution.py:603
  (19 shorter events, 0.1 us)
Async XLA Ops:
  0.6 8.6 %copy-start = (bf16[2,2,1,128,128]{4,3,2,1,0:T(8,128)(2,1)S(1)}, bf16[2,2,1,128,128]{4,3,2,1,0:T(8,128)(2,1)}, u32[]{:S(2)}) copy-start(bf16[2,2,1,128,128]{4,3,2,1,0:T(8,128)(2,1)} %latent_any.7) | copy-start | bytes 393220
  1.6 5.9 %collective-permute-start = (bf16[2,128,128]{2,1,0:T(8,128)(2,1)S(1)}, bf16[2,128,128]{2,1,0:T(8,128)(2,1)S(1)}, u32[]{:S(2)}, u32[]{:S(2)}) collective-permute-start(bf16[2,128,128]{2,1,0:T(8,128)(2,1)S(1)} %dynamic-slice_bitcast_fusion.2), channel_id=1, source_target_pairs={{0,2},{2,0},{1,3},{3,1},{4,6},{6,4},{5,7},{7,5},{8,10},{10,8},{9,1... | collective-permute-start | bytes 196616 | tf_op jit(solution)/shard_map/ppermute | solution.py:581
  7.4 7.9 %copy-start.1 = (bf16[2,2,1,128,128]{4,3,2,1,0:T(8,128)(2,1)S(1)}, bf16[2,2,1,128,128]{4,3,2,1,0:T(8,128)(2,1)}, u32[]{:S(2)}) copy-start(bf16[2,2,1,128,128]{4,3,2,1,0:T(8,128)(2,1)} %latent_any.7) | copy-start | bytes 393220
  7.5 6.0 %collective-permute-start.1 = (bf16[3,128,128]{2,1,0:T(8,128)(2,1)S(1)}, bf16[3,128,128]{2,1,0:T(8,128)(2,1)S(1)}, u32[]{:S(2)}, u32[]{:S(2)}) collective-permute-start(bf16[3,128,128]{2,1,0:T(8,128)(2,1)S(1)} %pad_maximum_fusion), channel_id=1, source_target_pairs={{0,4},{1,5},{4,0},{5,1},{8,12},{9,13},{12,8},{13,9},{2,6},{3,7},{6... | collective-permute-start | bytes 294920 | tf_op jit(solution)/shard_map/ppermute | solution.py:599
  9.2 4.4 %collective-permute-start.2 = (bf16[3,128,128]{2,1,0:T(8,128)(2,1)S(1)}, bf16[3,128,128]{2,1,0:T(8,128)(2,1)S(1)}, u32[]{:S(2)}, u32[]{:S(2)}) collective-permute-start(bf16[3,128,128]{2,1,0:T(8,128)(2,1)S(1)} %pad_maximum_fusion.1), channel_id=1, source_target_pairs={{0,1},{1,0},{4,8},{5,9},{8,4},{9,5},{12,13},{13,12},{2,3},{3,2},{6... | collective-permute-start | bytes 294920 | tf_op jit(solution)/shard_map/ppermute | solution.py:599
  9.3 5.0 %collective-permute-start.3 = (bf16[2,2,1,128,128]{4,3,2,1,0:T(8,128)(2,1)S(1)}, bf16[2,2,1,128,128]{4,3,2,1,0:T(8,128)(2,1)S(1)}, u32[]{:S(2)}, u32[]{:S(2)}) collective-permute-start(bf16[2,2,1,128,128]{4,3,2,1,0:T(8,128)(2,1)S(1)} %copy-done), channel_id=1, source_target_pairs={{0,1},{1,0},{2,3},{3,2},{4,5},{5,4},{6,7},{7,6},{8,9},{9,8},{10,11... | collective-permute-start | bytes 393224 | tf_op jit(solution)/shard_map/ppermute | solution.py:581
  13.5 1.8 %collective-permute-start.5 = (bf16[3,128,128]{2,1,0:T(8,128)(2,1)S(1)}, bf16[3,128,128]{2,1,0:T(8,128)(2,1)S(1)}, u32[]{:S(2)}, u32[]{:S(2)}) collective-permute-start(bf16[3,128,128]{2,1,0:T(8,128)(2,1)S(1)} %collective-permute-done.1.refs_1_), channel_id=1, source_target_pairs={{0,1},{1,0},{2,3},{3,2},{4,5},{5,4},{6,7},{7,6},{8,9},{9,8},{10,11... | collective-permute-start | bytes 294920 | tf_op jit(solution)/shard_map/ppermute | solution.py:581
  13.7 1.7 %collective-permute-start.6 = (bf16[3,128,128]{2,1,0:T(8,128)(2,1)S(1)}, bf16[3,128,128]{2,1,0:T(8,128)(2,1)S(1)}, u32[]{:S(2)}, u32[]{:S(2)}) collective-permute-start(bf16[3,128,128]{2,1,0:T(8,128)(2,1)S(1)} %collective-permute-done.2.refs_2_), channel_id=1, source_target_pairs={{0,1},{1,0},{2,3},{3,2},{4,5},{5,4},{6,7},{7,6},{8,9},{9,8},{10,11... | collective-permute-start | bytes 294920 | tf_op jit(solution)/shard_map/ppermute | solution.py:581
  14.1 1.3 %collective-permute-start.4 = (bf16[2,128,128]{2,1,0:T(8,128)(2,1)S(1)}, bf16[2,128,128]{2,1,0:T(8,128)(2,1)S(1)}, u32[]{:S(2)}, u32[]{:S(2)}) collective-permute-start(bf16[2,128,128]{2,1,0:T(8,128)(2,1)S(1)} %collective-permute-done.refs_0_), channel_id=1, source_target_pairs={{0,1},{1,0},{2,3},{3,2},{4,5},{5,4},{6,7},{7,6},{8,9},{9,8},{10,11... | collective-permute-start | bytes 196616 | tf_op jit(solution)/shard_map/ppermute | solution.py:581
  18.7 6.1 %collective-permute-start.7 = (f32[16,128]{1,0:T(8,128)S(1)}, f32[16,128]{1,0:T(8,128)S(1)}, u32[]{:S(2)}, u32[]{:S(2)}) collective-permute-start(f32[16,128]{1,0:T(8,128)S(1)} %get-tuple-element.76), channel_id=1, source_target_pairs={{0,2},{2,0},{1,3},{3,1},{4,6},{6,4},{5,7},{7,5},{8,10},{10,8},{9,1... | collective-permute-start | bytes 24584 | tf_op jit(solution)/shard_map/ppermute | solution.py:581
  24.8 8.3 %collective-permute-start.9 = (f32[2,16,128]{2,1,0:T(8,128)S(1)}, f32[2,16,128]{2,1,0:T(8,128)S(1)}, u32[]{:S(2)}, u32[]{:S(2)}) collective-permute-start(f32[2,16,128]{2,1,0:T(8,128)S(1)} %pad_maximum_fusion.2.own_ref), channel_id=1, source_target_pairs={{0,1},{1,0},{4,8},{5,9},{8,4},{9,5},{12,13},{13,12},{2,3},{3,2},{6... | collective-permute-start | bytes 49160 | tf_op jit(solution)/shard_map/ppermute | solution.py:599
  24.9 8.2 %collective-permute-start.8 = (f32[2,16,128]{2,1,0:T(8,128)S(1)}, f32[2,16,128]{2,1,0:T(8,128)S(1)}, u32[]{:S(2)}, u32[]{:S(2)}) collective-permute-start(f32[2,16,128]{2,1,0:T(8,128)S(1)} %pad_maximum_fusion.2.own_ref), channel_id=1, source_target_pairs={{0,4},{1,5},{4,0},{5,1},{8,12},{9,13},{12,8},{13,9},{2,6},{3,7},{6... | collective-permute-start | bytes 49160 | tf_op jit(solution)/shard_map/ppermute | solution.py:599
  33.0 3.0 %collective-permute-start.10 = (f32[2,16,128]{2,1,0:T(8,128)S(1)}, f32[2,16,128]{2,1,0:T(8,128)S(1)}, u32[]{:S(2)}, u32[]{:S(2)}) collective-permute-start(f32[2,16,128]{2,1,0:T(8,128)S(1)} %pad_maximum_fusion.2.own_ref), channel_id=1, source_target_pairs={{0,1},{1,0},{2,3},{3,2},{4,5},{5,4},{6,7},{7,6},{8,9},{9,8},{10,11... | collective-permute-start | bytes 49160 | tf_op jit(solution)/shard_map/ppermute | solution.py:581
  33.1 2.9 %collective-permute-start.11 = (f32[2,16,128]{2,1,0:T(8,128)S(1)}, f32[2,16,128]{2,1,0:T(8,128)S(1)}, u32[]{:S(2)}, u32[]{:S(2)}) collective-permute-start(f32[2,16,128]{2,1,0:T(8,128)S(1)} %collective-permute-done.8.even_ref), channel_id=1, source_target_pairs={{0,1},{1,0},{2,3},{3,2},{4,5},{5,4},{6,7},{7,6},{8,9},{9,8},{10,11... | collective-permute-start | bytes 49160 | tf_op jit(solution)/shard_map/ppermute | solution.py:581
  33.6 2.4 %collective-permute-start.12 = (f32[2,16,128]{2,1,0:T(8,128)S(1)}, f32[2,16,128]{2,1,0:T(8,128)S(1)}, u32[]{:S(2)}, u32[]{:S(2)}) collective-permute-start(f32[2,16,128]{2,1,0:T(8,128)S(1)} %collective-permute-done.9.odd_ref), channel_id=1, source_target_pairs={{0,1},{1,0},{2,3},{3,2},{4,5},{5,4},{6,7},{7,6},{8,9},{9,8},{10,11... | collective-permute-start | bytes 49160 | tf_op jit(solution)/shard_map/ppermute | solution.py:581

commit v5 on v4

--- a/solution.py
+++ b/solution.py
@@ -167,12 +167,25 @@
     decoder_out_any,
     encoder_in_any,
     encoder_w_any,
+    latent_any,
+    neighbours_any,
+    positions_any,
+    velocity_any,
+    edge_any,
     weights_ref,
     decoder_out_ref,
     inward_ref,
     encoder_w_ref,
     placer_ref,
     masks_ref,
+    alive_ref,
+    latent_ref,
+    neighbours_ref,
+    positions_ref,
+    velocity_ref,
+    edge_ref,
+    first_end_ref,
+    second_end_ref,
     owners_ref,
     edge_w_ref,
     node_in_ref,
@@ -193,16 +206,24 @@
             (decoder_out_any, decoder_out_ref),
             (encoder_in_any, encoder_in_ref),
             (encoder_w_any, encoder_w_ref),
+            (latent_any, latent_ref),
+            (neighbours_any, neighbours_ref),
+            (positions_any, positions_ref),
+            (velocity_any, velocity_ref),
+            (edge_any, edge_ref),
         ],
         sems,
     )
-    for copy in copies:
-        copy.wait()
+    copies[0].wait()
     index_x = lax.axis_index("gx")
     index_y = lax.axis_index("gy")
     index_z = lax.axis_index("gz")
     slots = owners_ref.shape[-1]
     width = node_in_ref.shape[-1]
+    for a, b in CELLS:
+        alive_ref[a, b] = jnp.where(
+            lax.broadcasted_iota(I32, (1, slots), 1) < fill_ref[a, 0, b], 1.0, 0.0
+        )
 
     lane = lax.broadcasted_iota(I32, (1, slots), 1)
     owner = jnp.concatenate([owners_ref[a, b] for a, b in CELLS], axis=1)
@@ -245,6 +266,8 @@
         [stays, moving.astype(F32), jnp.zeros((6, particles), F32)], axis=0
     )
 
+    for copy in copies[1:]:
+        copy.wait()
     for i in range(5):
         weights_ref[i] = flip(edge_w_ref[i])
     weights_ref[NODE_OLD] = flip(node_in_ref[:width])
@@ -255,15 +278,19 @@
     inward = jnp.concatenate([encoder_in_ref[...].astype(F32), jnp.zeros((4, width), F32)], axis=0)
     inward = inward.astype(BF16)
     inward_ref[...] = jnp.concatenate([inward, inward, inward], axis=0)
+    parity = index_x & 1
+    for b in range(2):
+        first_end_ref[b] = latent_ref[1 - parity, b, 0]
+        second_end_ref[b] = latent_ref[parity, b, 0]
 
 
 def prepare_kernel(
     sizes,
-    latent_any,
-    edge_any,
-    positions_any,
-    velocity_any,
-    neighbours_any,
+    latent_ref,
+    edge_ref,
+    positions_ref,
+    velocity_ref,
+    neighbours_ref,
     weights_ref,
     placer_ref,
     masks_ref,
@@ -276,26 +303,8 @@
     mover_node_pre_ref,
     mover_latent_ref,
     mover_state_ref,
-    latent_ref,
-    edge_ref,
-    positions_ref,
-    velocity_ref,
-    neighbours_ref,
-    sems,
 ):
     fold_y = sizes[1] == 2
-    copies = fetch(
-        [
-            (neighbours_any, neighbours_ref),
-            (positions_any, positions_ref),
-            (velocity_any, velocity_ref),
-            (latent_any, latent_ref),
-            (edge_any, edge_ref),
-        ],
-        sems,
-    )
-    for copy in copies[:4]:
-        copy.wait()
     neighbour_count = edge_ref.shape[3]
     placer = placer_ref[...]
     movers, particles = placer.shape
@@ -329,7 +338,6 @@
     place, key = places(ids[:neighbour_count], ids[neighbour_count : 2 * neighbour_count], fold_y)
     mover_place_ref[...] = place
     mover_key_ref[...] = key
-    copies[4].wait()
     for k in range(neighbour_count):
         edges = jnp.concatenate([edge_ref[a, b, 0, k] for a, b in CELLS], axis=0)
         edges = dot(placer, edges).astype(BF16)
@@ -339,10 +347,10 @@
 def movers_kernel(
     sizes,
     side_count,
-    latent_any,
+    own_ref,
     *refs,
 ):
-    count_x, count_y, _ = sizes
+    count_x, count_y, count_z = sizes
     fold_y = count_y == 2
     side_refs, refs = refs[:side_count], refs[side_count:]
     even_ref, odd_ref, own_zed, refs = refs[0], refs[1], refs[2], refs[3:]
@@ -359,22 +367,21 @@
         state_ref,
         far_ref,
         bucket_ref,
-        own_ref,
         hidden_ref,
-        sems,
     ) = refs
-    copies = fetch([(latent_any, own_ref)], sems)
     row_count = 3 if fold_y else 4
     own_rows = (0, 1) if fold_y else (1, 2)
     outer = {2: 0} if fold_y else {0: 0, 3: 1}
-    parity = lax.axis_index("gx") & 1
+    index_x = lax.axis_index("gx")
+    index_y = lax.axis_index("gy")
+    index_z = lax.axis_index("gz")
+    parity = index_x & 1
     far_t = weights_ref[FAR]
 
     def far(at, here, beside):
         pair = jnp.concatenate([here, beside], axis=0)
         far_ref[at] = dot_nt(far_t, pair).astype(BF16)
 
-    copies[0].wait()
     for row in range(row_count):
         for ex in (1, 2):
             if row in own_rows:
@@ -408,41 +415,48 @@
     )
     mask = state_ref[6:7]
     state = moved(state_ref[0:3], state_ref[3:6], acceleration) * mask
-    bucket_ref[...] = jnp.concatenate([state, mask, jnp.zeros((ROWS - 10, movers), F32)], axis=0)
+    rows = jnp.concatenate([state, mask, jnp.zeros((118, movers), F32)], axis=0).T
+    bucket_ref[...] = jnp.zeros_like(bucket_ref)
+    options_y = 2 if fold_y else 3
+    for step_x in (-1, 0, 1):
+        for side_y in range(options_y):
+            for side_z in range(2):
+                if step_x == 0 and side_y == 0 and side_z == 0:
+                    continue
+                to_x = index_x + step_x
+                if side_y == 0:
+                    to_y = index_y
+                elif fold_y:
+                    to_y = 1 - index_y
+                else:
+                    to_y = index_y + (2 * side_y - 3)
+                to_z = index_z if side_z == 0 else 1 - index_z
+                at = (((step_x + 1) * options_y + side_y) * 2 + side_z) * CAP
+
+                @pl.when((to_x >= 0) & (to_x < count_x) & (to_y >= 0) & (to_y < count_y))
+                def _(to=(to_x * count_y + to_y) * count_z + to_z, at=at):
+                    bucket_ref[to] = rows[at : at + CAP]
 
 
 def edges_kernel(
     sizes,
     a,
-    fill_ref,
-    latent_any,
-    edge_any,
-    neighbours_any,
+    alive_ref,
+    latent_ref,
+    edge_ref,
+    neighbours_ref,
     far_ref,
     weights_ref,
     total_ref,
-    latent_ref,
-    edge_ref,
-    neighbours_ref,
     hidden_ref,
-    sems,
 ):
     fold_y = sizes[1] == 2
     row_count = 3 if fold_y else 4
     index_y = lax.axis_index("gy")
-    copies = fetch(
-        [
-            (neighbours_any.at[a], neighbours_ref),
-            (latent_any.at[a], latent_ref),
-            (edge_any.at[a], edge_ref),
-        ],
-        sems,
-    )
-    for copy in copies:
-        copy.wait()
+    alive_ref, latent_ref = alive_ref.at[a], latent_ref.at[a]
+    edge_ref, neighbours_ref = edge_ref.at[a], neighbours_ref.at[a]
     slots, width = latent_ref.shape[-2:]
     neighbour_count = edge_ref.shape[2]
-    lane = lax.broadcasted_iota(I32, (1, slots), 1)
     for bt in range(2):
         if fold_y:
             b = index_y if bt == 0 else 1 - index_y
@@ -471,7 +485,7 @@
             weights_ref[FINAL],
             hidden_ref.at[bt],
         )
-        total = jnp.where(lane < fill_ref[a, 0, b], slot_sum(message, slots), 0.0)
+        total = jnp.where(alive_ref[b] > 0.5, slot_sum(message, slots), 0.0)
         total_ref[b] = total.astype(BF16)
 
 
@@ -507,68 +521,28 @@
 
 def arrive_kernel(
     sizes,
-    own_ref,
-    even_ref,
-    odd_ref,
-    own_zed,
-    even_zed,
-    odd_zed,
+    received_ref,
     inward_ref,
     encoder_w_ref,
     arrived_latent_ref,
     arrived_state_ref,
 ):
     count_x, count_y, count_z = sizes
-    fold_y = count_y == 2
     index_x = lax.axis_index("gx")
     index_y = lax.axis_index("gy")
     index_z = lax.axis_index("gz")
-    options_y = 2 if fold_y else 3
-    lanes = own_ref.shape[-1]
-    group = lax.broadcasted_iota(I32, (ROWS, lanes), 1) >> 3
-    even = (index_x & 1) == 0
-    found = jnp.zeros((ROWS, lanes), F32)
-    for source_x in (-1, 0, 1):
-        for from_y in range(options_y):
-            for from_z in range(2):
-                if source_x == 0 and from_y == 0 and from_z == 0:
-                    continue
-                if from_z == 0:
-                    own, first, second = own_ref, even_ref, odd_ref
-                else:
-                    own, first, second = own_zed, even_zed, odd_zed
-                side_y = from_y if fold_y or from_y == 0 else 3 - from_y
-                target = ((1 - source_x) * options_y + side_y) * 2 + from_z
-                if source_x == 0:
-                    tile = own[from_y]
-                    there = group == target
-                elif source_x == -1:
-                    tile = jnp.where(even, second[from_y], first[from_y])
-                    there = (group == target) & (index_x > 0)
-                else:
-                    tile = jnp.where(even, first[from_y], second[from_y])
-                    there = (group == target) & (index_x < count_x - 1)
-                found = jnp.where(there, tile, found)
-    out_lanes = arrived_state_ref.shape[-1]
-    spread_shape = (lanes, out_lanes)
-    line = lax.broadcasted_iota(I32, spread_shape, 0)
-    from_group = line >> 3
-    plane = from_group >> 1
-    from_x = 1 - ((plane >> 1) if fold_y else ((plane * 43) >> 7))
-    side_y = plane - (1 - from_x) * options_y
-    if fold_y:
-        from_y = jnp.where(side_y == 0, 0, jnp.where(index_y == 0, 1, -1))
-    else:
-        from_y = jnp.where(side_y == 0, 0, jnp.where(side_y == 1, 1, -1))
-    from_z = jnp.where((from_group & 1) == 0, 0, jnp.where(index_z == 0, 1, -1))
-    direction = (from_x + 1) * 9 + (from_y + 1) * 3 + from_z + 1
-    direction = direction - jnp.where(direction > 13, 1, 0)
-    column = direction * CAP + (line & 7)
-    valid = (lax.broadcasted_iota(I32, spread_shape, 1) == column) & (
-        (from_x != 0) | (from_y != 0) | (from_z != 0)
-    )
-    spread = jnp.where(valid, 1.0, 0.0).astype(BF16)
-    arrived = joined(dot(thirds(found), spread))
+    rows = []
+    for direction in range(27):
+        if direction == 13:
+            continue
+        x = index_x + (direction // 9 - 1)
+        y = index_y + (direction // 3 % 3 - 1)
+        z = index_z + (direction % 3 - 1)
+        inside = (x >= 0) & (x < count_x) & (y >= 0) & (y < count_y) & (z >= 0) & (z < count_z)
+        source = jnp.where(inside, (x * count_y + y) * count_z + z, 0)
+        rows.append(jnp.where(inside, received_ref[source], 0.0))
+    rows.append(jnp.zeros((256 - 26 * CAP, 128), F32))
+    arrived = jnp.concatenate(rows, axis=0).T[:ROWS, : 26 * CAP]
     for j in range(9):
         arrived_state_ref[j, 0, 0] = arrived[j : j + 1]
     extent = (2.0 * count_x, 2.0 * count_y, 1.0 * count_z)
@@ -655,10 +629,11 @@
     else:
         sides = [shift(cells[:, 1], "gy", 0), shift(cells[:, 0], "gy", 1)]
 
+    fetched = (node_latent, neighbours, positions, velocity, edge_latent)
     ranked = call(
         functools.partial(ranks_kernel, sizes),
         "ranks",
-        [SMEM] + [ANY] * 8,
+        [SMEM] + [ANY] * 13,
         [
             ((11, width, width), BF16),
             (decoder_out.shape, BF16),
@@ -666,6 +641,10 @@
             (encoder_weights.shape, BF16),
             ((movers, particles), BF16),
             ((8, particles), F32),
+            ((2, 2, 1, slots), F32),
+            *((array.shape, array.dtype) for array in fetched),
+            ((2, slots, width), BF16),
+            ((2, slots, width), BF16),
         ],
         [
             like(owners),
@@ -674,7 +653,7 @@
             like(node_weights),
             like(decoder_weights),
             like(encoder_in),
-            pltpu.SemaphoreType.DMA((8,)),
+            pltpu.SemaphoreType.DMA((13,)),
         ],
         [
             in_hbm(array)
@@ -688,28 +667,26 @@
                 decoder_out,
                 encoder_in,
                 encoder_weights,
+                *fetched,
             )
         ],
         500_000_000,
     )
     sides, ranked = lax.optimization_barrier((sides, ranked))
-    weights, decoder_out, inward, encoder_weights, placer, masks = ranked
-
-    if fold_y:
-        layers = [cells, sides[0][:, None]]
-    else:
-        layers = [sides[0][:, None], cells, sides[1][:, None]]
-
-    def layer(a):
-        return jnp.concatenate(
-            [lax.dynamic_index_in_dim(part, a, 0, keepdims=False) for part in layers], axis=0
-        )
-
-    ends = [swap_x(layer(1 - parity), 0), swap_x(layer(parity), 1)]
+    weights, decoder_out, inward, encoder_weights, placer, masks, alive, *ranked = ranked
+    latent, neighbours, positions, velocity, edge_latent, *own_ends = ranked
+
+    def layer(a, own):
+        outer = [lax.dynamic_index_in_dim(side, a, 0) for side in sides]
+        parts = [own, outer[0]] if fold_y else [outer[0], own, outer[1]]
+        return jnp.concatenate(parts, axis=0)
+
+    ends = [swap_x(layer(1 - parity, own_ends[0]), 0), swap_x(layer(parity, own_ends[1]), 1)]
+    zeds = [swap(part, "gz") for part in [latent, *sides]]
     prepared = call(
         functools.partial(prepare_kernel, sizes),
         "prepare",
-        [ANY] * 5 + [VMEM] * 3,
+        [VMEM] * 8,
         [
             ((width, particles), F32),
             ((width, particles), F32),
@@ -721,22 +698,11 @@
             ((width, movers), F32),
             ((8, movers), F32),
         ],
-        [
-            like(node_latent),
-            like(edge_latent),
-            like(positions),
-            like(velocity),
-            like(neighbours),
-            pltpu.SemaphoreType.DMA((5,)),
-        ],
-        [
-            in_hbm(array)
-            for array in (node_latent, edge_latent, positions, velocity, neighbours)
-        ]
-        + [weights, placer, masks],
+        [],
+        (latent, edge_latent, positions, velocity, neighbours, weights, placer, masks),
         500_000_000,
     )
-    ends, prepared = lax.optimization_barrier((ends, prepared))
+    ends, zeds, prepared = lax.optimization_barrier((ends, zeds, prepared))
     (
         latent_t,
         node_pre,
@@ -748,21 +714,16 @@
         mover_latent,
         mover_state,
     ) = prepared
-    halo = [*sides, *ends]
-    halo = halo + [swap(part, "gz") for part in [node_latent] + halo]
+    halo = [*sides, *ends, *zeds, *(swap(part, "gz") for part in ends)]
 
     far, bucket = call(
         functools.partial(movers_kernel, sizes, len(sides)),
         "movers",
-        [ANY] + [VMEM] * (len(halo) + 8),
-        [((4 * rows, width, 2 * slots), BF16), ((ROWS, movers), F32)],
-        [
-            like(node_latent),
-            pltpu.VMEM((width, neighbour_count * movers), BF16),
-            pltpu.SemaphoreType.DMA((1,)),
-        ],
+        [VMEM] * (len(halo) + 9),
+        [((4 * rows, width, 2 * slots), BF16), ((sizes[0] * sizes[1] * sizes[2], CAP, 128), F32)],
+        [pltpu.VMEM((width, neighbour_count * movers), BF16)],
         (
-            node_latent,
+            latent,
             *halo,
             weights,
             decoder_out,
@@ -780,31 +741,15 @@
         return call(
             functools.partial(edges_kernel, sizes, a),
             "edges",
-            [SMEM] + [ANY] * 3 + [VMEM] * 2,
+            [VMEM] * 6,
             [((2, width, slots), BF16)],
-            [
-                pltpu.VMEM(node_latent.shape[1:], BF16),
-                pltpu.VMEM(edge_latent.shape[1:], BF16),
-                pltpu.VMEM(neighbours.shape[1:], I32),
-                pltpu.VMEM((2, width, neighbour_count * slots), BF16),
-                pltpu.SemaphoreType.DMA((3,)),
-            ],
-            (in_hbm(fill), in_hbm(node_latent), in_hbm(edge_latent), in_hbm(neighbours), far, weights),
+            [pltpu.VMEM((2, width, neighbour_count * slots), BF16)],
+            (alive, latent, edge_latent, neighbours, far, weights),
             4_000_000_000,
         )[0]
 
-    first = edges(0)
-    if fold_y:
-        tiles = [swap(bucket, "gy")]
-    else:
-        tiles = [shift(bucket, "gy", 0), shift(bucket, "gy", 1)]
-    tiles, first = lax.optimization_barrier((tiles, first))
-    tiles = jnp.stack([bucket, *tiles], axis=0)
-    second = edges(1)
-    sided = [swap_x(tiles, 0), swap_x(tiles, 1)]
-    sided, second = lax.optimization_barrier((sided, second))
-    tiles = [tiles, *sided]
-    tiles = tiles + [swap(part, "gz") for part in tiles]
+    received = lax.all_to_all(bucket, ("gx", "gy", "gz"), 0, 0, tiled=True)
+    first, second = edges(0), edges(1)
     kept_latent, kept_state = call(
         functools.partial(nodes_kernel, sizes),
         "nodes",
@@ -827,10 +772,10 @@
     arrived_latent, arrived_state = call(
         functools.partial(arrive_kernel, sizes),
         "arrive",
-        [VMEM] * 8,
+        [VMEM] * 3,
         [((1, 1, 1, 26 * CAP, width), BF16), ((9, 1, 1, 1, 26 * CAP), F32)],
         [],
-        (*tiles, inward, encoder_weights),
+        (received, inward, encoder_weights),
         1_000_000_000,
     )
     return kept_latent, kept_state, arrived_latent, arrived_state

time: 37.9 us -> 38.4 us (1.013)
  waiting for transfers between devices: 1.19 us -> 5.78 us
  Pallas kernels: 22.4 us -> 18.3 us
  starting transfers between devices: 11.2 us -> 12.4 us
  local copies, waits for them, and re-layouts: 1.81 us -> 0.87 us
    all_to_all x0 -> x1, starting transfers between devices: none -> 6.6 us  [body(): received = lax.all_to_all(bucket, ('gx', 'gy', 'gz'), 0, 0, tiled=True)]
    all_to_all x0 -> x1, waiting for transfers between devices: none -> 4.54 us  [body(): received = lax.all_to_all(bucket, ('gx', 'gy', 'gz'), 0, 0, tiled=True)]
    pallas_call x7, Pallas kernels: 22.4 us -> 18.3 us  [call(): pl.pallas_call(kernel, out_shape=tuple((jax.ShapeDtypeStruct(shape, kind)...]
    ppermute x4 -> x2, starting transfers between devices: 5.17 us -> 2.21 us  [swap_x(): return lax.ppermute(values, ('gx', 'gz'), pairs)]
    ppermute x9 -> x5, starting transfers between devices: 6.08 us -> 3.6 us  [swap(): return lax.ppermute(values, axis, [(0, 1), (1, 0)])]
    squeeze x2 -> x0, local copies, waits for them, and re-layouts: 0.9 us -> none  [layer(): lax.dynamic_index_in_dim(part, a, 0, keepdims=False)]
    ppermute x9 -> x5, waiting for transfers between devices: 1.18 us -> 1.23 us  [swap(): return lax.ppermute(values, axis, [(0, 1), (1, 0)])]
  transfers between devices with their start and end apart: 13 -> 8, of which waited for: 1 -> 3; matrix products, arithmetic and copies ran while one was open for 2% -> 0% of each run, Pallas kernels for 47% -> 20%
where the time goes in v5:
time: 38.4 us; the launch traced here: 38.1 us
  Pallas kernels  18.3 us (48%)
  starting transfers between devices  12.4 us (32%)
  waiting for transfers between devices  5.78 us (15%)
  local copies, waits for them, and re-layouts  0.87 us (2%)
  between operations  0.74 us (2%)
    pallas_call x7, Pallas kernels, call(): pl.pallas_call(kernel, out_shape=tuple((jax.ShapeDtypeStruct(shape, kind)...  18.3 us
    all_to_all x1, starting transfers between devices, body(): received = lax.all_to_all(bucket, ('gx', 'gy', 'gz'), 0, 0, tiled=True)  6.6 us
    all_to_all x1, waiting for transfers between devices, body(): received = lax.all_to_all(bucket, ('gx', 'gy', 'gz'), 0, 0, tiled=True)  4.54 us
    ppermute x5, starting transfers between devices, swap(): return lax.ppermute(values, axis, [(0, 1), (1, 0)])  3.6 us
    ppermute x2, starting transfers between devices, swap_x(): return lax.ppermute(values, ('gx', 'gz'), pairs)  2.21 us
    ppermute x5, waiting for transfers between devices, swap(): return lax.ppermute(values, axis, [(0, 1), (1, 0)])  1.23 us
    squeeze x1, local copies, waits for them, and re-layouts, body(): lax.dynamic_index_in_dim(cells, inner, 1, keepdims=False)  0.85 us
  transfers between devices with their start and end apart: 8, of which 3 were waited for; matrix products, arithmetic and copies ran while one was open for 0% of the time, Pallas kernels for 20%

profile of v5, /device:TPU:0, one launch (start us, length us, event | category | flops | bytes accessed | tf_op | source)
XLA Modules:
  0.0 38.1 jit_solution(8623583404113908865)
XLA Ops:
  0.6 0.9 %dynamic-slice_bitcast_fusion = bf16[2,128,128]{2,1,0:T(8,128)(2,1)S(1)} fusion(bf16[2,2,1,128,128]{4,3,2,1,0:T(8,128)(2,1)} %latent_any.1, s32[]{:T(128)S(6)} %select_n.11), kind=kLoop, calls=%fused_computation.2 | loop fusion | bytes 131076 | tf_op jit(solution)/shard_map/jit(dynamic_index_in_dim)/squeeze | solution.py:628
  1.5 2.9 %collective-permute-start = (bf16[2,128,128]{2,1,0:T(8,128)(2,1)S(1)}, bf16[2,128,128]{2,1,0:T(8,128)(2,1)S(1)}, u32[]{:S(2)}, u32[]{:S(2)}) collective-permute-start(bf16[2,128,128]{2,1,0:T(8,128)(2,1)S(1)} %dynamic-slice_bitcast_fusion), channel_id=1, source_target_pairs={{0,2},{2,0},{1,3},{3,1},{4,6},{6,4},{5,7},{7,5},{8,10},{10,8},{9,1... | collective-permute-start | bytes 196616 | tf_op jit(solution)/shard_map/ppermute | solution.py:555
  4.4 2.8 %ranks.1 = (bf16[11,128,128]{2,1,0:T(8,128)(2,1)S(1)}, bf16[3,128]{1,0:T(4,128)(2,1)S(1)}, bf16[48,128]{1,0:T(8,128)(2,1)S(1)}, bf16[2,128,128]{2,1,0:T(8,128)(2...) custom-call(s32[2,1,2]{2,1,0:T(1,128)} %bitcast.7, ...), custom_call_target="tpu_custom_call" | custom-call | flops 500000000 | tf_op jit(solution)/shard_map/ranks/pallas_call | solution.py:577
  7.2 0.0 collective-permute-done.refs_0_
  7.2 1.6 %collective-permute-start.1 = (bf16[3,128,128]{2,1,0:T(8,128)(2,1)S(1)}, bf16[3,128,128]{2,1,0:T(8,128)(2,1)S(1)}, u32[]{:S(2)}, u32[]{:S(2)}) collective-permute-start(bf16[3,128,128]{2,1,0:T(8,128)(2,1)S(1)} %pad_maximum_fusion), channel_id=1, source_target_pairs={{0,4},{1,5},{4,0},{5,1},{8,12},{9,13},{12,8},{13,9},{2,6},{3,7},{6... | collective-permute-start | bytes 294920 | tf_op jit(solution)/shard_map/ppermute | solution.py:573
  8.9 0.0 collective-permute-start.3
  8.9 0.6 %collective-permute-start.2 = (bf16[3,128,128]{2,1,0:T(8,128)(2,1)S(1)}, bf16[3,128,128]{2,1,0:T(8,128)(2,1)S(1)}, u32[]{:S(2)}, u32[]{:S(2)}) collective-permute-start(bf16[3,128,128]{2,1,0:T(8,128)(2,1)S(1)} %pad_maximum_fusion.1), channel_id=1, source_target_pairs={{0,1},{1,0},{4,8},{5,9},{8,4},{9,5},{12,13},{13,12},{2,3},{3,2},{6... | collective-permute-start | bytes 294920 | tf_op jit(solution)/shard_map/ppermute | solution.py:573
  9.5 0.1 collective-permute-start.4
  9.6 2.5 %prepare.1 = (f32[128,512]{1,0:T(8,128)S(1)}, f32[128,512]{1,0:T(8,128)S(1)}, f32[8,512]{1,0:T(8,128)S(1)}, f32[128,1536]{1,0:T(8,128)S(1)}, s32[12,128]{1,0:T(8...) custom-call(bf16[2,2,1,128,128]{4,3,2,1,0:T(8,128)(2,1)S(1)} %get-tup, ...), custom_call_target="tpu_custom_call" | custom-call | flops 500000000 | tf_op jit(solution)/shard_map/prepare/pallas_call | solution.py:577
  12.1 0.0 collective-permute-done.4.refs_4_
  12.1 0.0 collective-permute-done.1.refs_1_
  12.1 0.0 collective-permute-done.2.refs_2_
  12.1 0.0 collective-permute-done.3.refs_3_
  12.1 0.5 %collective-permute-start.5 = (bf16[3,128,128]{2,1,0:T(8,128)(2,1)S(1)}, bf16[3,128,128]{2,1,0:T(8,128)(2,1)S(1)}, u32[]{:S(2)}, u32[]{:S(2)}) collective-permute-start(bf16[3,128,128]{2,1,0:T(8,128)(2,1)S(1)} %collective-permute-done.1.refs_1_), channel_id=1, source_target_pairs={{0,1},{1,0},{2,3},{3,2},{4,5},{5,4},{6,7},{7,6},{8,9},{9,8},{10,11... | collective-permute-start | bytes 294920 | tf_op jit(solution)/shard_map/ppermute | solution.py:555
  12.6 0.1 collective-permute-start.6
  12.7 0.9 %collective-permute-done.5.refs_5_ = bf16[3,128,128]{2,1,0:T(8,128)(2,1)S(1)} collective-permute-done((bf16[3,128,128]{2,1,0:T(8,128)(2,1)S(1)}, bf16[3,128,128]{2,1,0:T(8,128)(2,1)S(1)}, u32[]{:S(2)}, u32[]{:S(2)}) %collective-permute-start.5) | collective-permute-done | bytes 98336 | tf_op jit(solution)/shard_map/ppermute | solution.py:555
  13.6 0.4 collective-permute-done.6.refs_6_
  13.9 3.8 %movers.1 = (bf16[12,128,256]{2,1,0:T(8,128)(2,1)S(1)}, f32[16,8,128]{2,1,0:T(8,128)}) custom-call(bf16[2,2,1,128,128]{4,3,2,1,0:T(8,128)(2,1)S(1)} %get-tuple-element.76.latent_ref.own_ref, bf16[2,128,128]{2,1,0:T(8,128)(2,1)S(1)} %collective-permute-done.refs_0_, bf16[3,128,128]{2,1,0:T(8,128)(2,1)S(1)} %collective-permute-done.1.refs_1_, ...), custom_call_target="tpu_custom_call" | custom-call | flops 3000000000 | tf_op jit(solution)/shard_map/movers/pallas_call | solution.py:577
  17.7 2.7 %edges.3.second_ref = bf16[2,128,128]{2,1,0:T(8,128)(2,1)S(1)} custom-call(f32[2,2,1,128]{3,2,1,0:T(1,128)S(1)} %get-tuple-element.75.alive_ref, bf16[2,2,1,128,128]{4,3,2,1,0:T(8,128)(2,1)S(1)} %get-tuple-element.76.latent_ref.own_ref, bf16[2,2,1,12,128,128]{5,4,3,2,1,0:T(8,128)(2,1)S(1)} %get-tuple-element.77.edge_ref, ...), custom_call_target="tpu_custom_call" | custom-call | flops 4000000000 | tf_op jit(solution)/shard_map/edges/pallas_call | solution.py:577
  20.5 2.8 %edges.2.first_ref = bf16[2,128,128]{2,1,0:T(8,128)(2,1)S(1)} custom-call(f32[2,2,1,128]{3,2,1,0:T(1,128)S(1)} %get-tuple-element.75.alive_ref, bf16[2,2,1,128,128]{4,3,2,1,0:T(8,128)(2,1)S(1)} %get-tuple-element.76.latent_ref.own_ref, bf16[2,2,1,12,128,128]{5,4,3,2,1,0:T(8,128)(2,1)S(1)} %get-tuple-element.77.edge_ref, ...), custom_call_target="tpu_custom_call" | custom-call | flops 4000000000 | tf_op jit(solution)/shard_map/edges/pallas_call | solution.py:577
  23.2 6.6 %all-to-all-start = ((f32[16,8,128]{2,1,0:T(8,128)}), f32[16,8,128]{2,1,0:T(8,128)S(1)}, u32[]{:S(2)}, u32[]{:S(2)}) async-start(f32[16,8,128]{2,1,0:T(8,128)} %get-tuple-element.115), calls=%async_computation | async-start | bytes 131072 | tf_op jit(solution)/shard_map/all_to_all | solution.py:751
  29.8 2.4 %nodes.1 = (bf16[2,2,1,128,128]{4,3,2,1,0:T(8,128)(2,1)}, f32[9,2,2,1,128]{4,3,2,1,0:T(1,128)}) custom-call(bf16[2,128,128]{2,1,0:T(8,128)(2,1)S(1)} %edges.2.first_ref, bf16[2,128,128]{2,1,0:T(8,128)(2,1)S(1)} %edges.3.second_ref, f32[128,512]{1,0:T(8,128)S(1)} %get-tuple-element.108.node_pre_ref, f32[128,512]{1,0:T(8,128)S(1)} %get-tuple-element.109.latent_t_ref, ...), custom_call_target="tpu_custom_call" | custom-call | flops 2000000000 | tf_op jit(solution)/shard_map/nodes/pallas_call | solution.py:577
  32.2 4.5 %all-to-all-done.received_ref = f32[16,8,128]{2,1,0:T(8,128)S(1)} async-done(((f32[16,8,128]{2,1,0:T(8,128)}), f32[16,8,128]{2,1,0:T(8,128)S(1)}, u32[]{:S(2)}, u32[]{:S(2)}) %all-to-all-start) | async-done | bytes 65568 | tf_op jit(solution)/shard_map/all_to_all | solution.py:751
  36.7 1.4 %arrive.1 = (bf16[1,1,1,208,128]{4,3,2,1,0:T(8,128)(2,1)}, f32[9,1,1,1,208]{4,3,2,1,0:T(1,128)}) custom-call(f32[16,8,128]{2,1,0:T(8,128)S(1)} %all-to-all-done.received_ref, bf16[48,128]{1,0:T(8,128)(2,1)S(1)} %get-tuple-element.111.inward_ref, bf16[2,128,128]{2,1,0:T(8,128)(2,1)S(1)} %get-tuple-element.112.encoder_w_ref), custom_call_target="tpu_custom_call" | custom-call | flops 1000000000 | tf_op jit(solution)/shard_map/arrive/pallas_call | solution.py:577
  (3 shorter events, 0.0 us)
Async XLA Ops:
  1.5 5.7 %collective-permute-start = (bf16[2,128,128]{2,1,0:T(8,128)(2,1)S(1)}, bf16[2,128,128]{2,1,0:T(8,128)(2,1)S(1)}, u32[]{:S(2)}, u32[]{:S(2)}) collective-permute-start(bf16[2,128,128]{2,1,0:T(8,128)(2,1)S(1)} %dynamic-slice_bitcast_fusion), channel_id=1, source_target_pairs={{0,2},{2,0},{1,3},{3,1},{4,6},{6,4},{5,7},{7,5},{8,10},{10,8},{9,1... | collective-permute-start | bytes 196616 | tf_op jit(solution)/shard_map/ppermute | solution.py:555
  7.2 4.9 %collective-permute-start.1 = (bf16[3,128,128]{2,1,0:T(8,128)(2,1)S(1)}, bf16[3,128,128]{2,1,0:T(8,128)(2,1)S(1)}, u32[]{:S(2)}, u32[]{:S(2)}) collective-permute-start(bf16[3,128,128]{2,1,0:T(8,128)(2,1)S(1)} %pad_maximum_fusion), channel_id=1, source_target_pairs={{0,4},{1,5},{4,0},{5,1},{8,12},{9,13},{12,8},{13,9},{2,6},{3,7},{6... | collective-permute-start | bytes 294920 | tf_op jit(solution)/shard_map/ppermute | solution.py:573
  8.9 3.2 %collective-permute-start.3 = (bf16[2,2,1,128,128]{4,3,2,1,0:T(8,128)(2,1)S(1)}, bf16[2,2,1,128,128]{4,3,2,1,0:T(8,128)(2,1)S(1)}, u32[]{:S(2)}, u32[]{:S(2)}) collective-permute-start(bf16[2,2,1,128,128]{4,3,2,1,0:T(8,128)(2,1)S(1)} %get-tuple-element.76.latent_ref.own_ref), channel_id=1, source_target_pairs={{0,1},{1,0},{2,3},{3,2},{4,5},{5,4},{6,7},{7,6},{8,9},{9,8},{10,11... | collective-permute-start | bytes 393224 | tf_op jit(solution)/shard_map/ppermute | solution.py:555
  8.9 3.2 %collective-permute-start.2 = (bf16[3,128,128]{2,1,0:T(8,128)(2,1)S(1)}, bf16[3,128,128]{2,1,0:T(8,128)(2,1)S(1)}, u32[]{:S(2)}, u32[]{:S(2)}) collective-permute-start(bf16[3,128,128]{2,1,0:T(8,128)(2,1)S(1)} %pad_maximum_fusion.1), channel_id=1, source_target_pairs={{0,1},{1,0},{4,8},{5,9},{8,4},{9,5},{12,13},{13,12},{2,3},{3,2},{6... | collective-permute-start | bytes 294920 | tf_op jit(solution)/shard_map/ppermute | solution.py:573
  9.5 2.6 %collective-permute-start.4 = (bf16[2,128,128]{2,1,0:T(8,128)(2,1)S(1)}, bf16[2,128,128]{2,1,0:T(8,128)(2,1)S(1)}, u32[]{:S(2)}, u32[]{:S(2)}) collective-permute-start(bf16[2,128,128]{2,1,0:T(8,128)(2,1)S(1)} %collective-permute-done.refs_0_), channel_id=1, source_target_pairs={{0,1},{1,0},{2,3},{3,2},{4,5},{5,4},{6,7},{7,6},{8,9},{9,8},{10,11... | collective-permute-start | bytes 196616 | tf_op jit(solution)/shard_map/ppermute | solution.py:555
  12.1 1.4 %collective-permute-start.5 = (bf16[3,128,128]{2,1,0:T(8,128)(2,1)S(1)}, bf16[3,128,128]{2,1,0:T(8,128)(2,1)S(1)}, u32[]{:S(2)}, u32[]{:S(2)}) collective-permute-start(bf16[3,128,128]{2,1,0:T(8,128)(2,1)S(1)} %collective-permute-done.1.refs_1_), channel_id=1, source_target_pairs={{0,1},{1,0},{2,3},{3,2},{4,5},{5,4},{6,7},{7,6},{8,9},{9,8},{10,11... | collective-permute-start | bytes 294920 | tf_op jit(solution)/shard_map/ppermute | solution.py:555
  12.6 1.3 %collective-permute-start.6 = (bf16[3,128,128]{2,1,0:T(8,128)(2,1)S(1)}, bf16[3,128,128]{2,1,0:T(8,128)(2,1)S(1)}, u32[]{:S(2)}, u32[]{:S(2)}) collective-permute-start(bf16[3,128,128]{2,1,0:T(8,128)(2,1)S(1)} %collective-permute-done.2.refs_2_), channel_id=1, source_target_pairs={{0,1},{1,0},{2,3},{3,2},{4,5},{5,4},{6,7},{7,6},{8,9},{9,8},{10,11... | collective-permute-start | bytes 294920 | tf_op jit(solution)/shard_map/ppermute | solution.py:555
  23.2 13.5 %all-to-all-start = ((f32[16,8,128]{2,1,0:T(8,128)}), f32[16,8,128]{2,1,0:T(8,128)S(1)}, u32[]{:S(2)}, u32[]{:S(2)}) async-start(f32[16,8,128]{2,1,0:T(8,128)} %get-tuple-element.115), calls=%async_computation | async-start | bytes 131072 | tf_op jit(solution)/shard_map/all_to_all | solution.py:751

commit v6 on v5

--- a/solution.py
+++ b/solution.py
@@ -372,10 +372,7 @@
     row_count = 3 if fold_y else 4
     own_rows = (0, 1) if fold_y else (1, 2)
     outer = {2: 0} if fold_y else {0: 0, 3: 1}
-    index_x = lax.axis_index("gx")
-    index_y = lax.axis_index("gy")
-    index_z = lax.axis_index("gz")
-    parity = index_x & 1
+    parity = lax.axis_index("gx") & 1
     far_t = weights_ref[FAR]
 
     def far(at, here, beside):
@@ -415,27 +412,7 @@
     )
     mask = state_ref[6:7]
     state = moved(state_ref[0:3], state_ref[3:6], acceleration) * mask
-    rows = jnp.concatenate([state, mask, jnp.zeros((118, movers), F32)], axis=0).T
-    bucket_ref[...] = jnp.zeros_like(bucket_ref)
-    options_y = 2 if fold_y else 3
-    for step_x in (-1, 0, 1):
-        for side_y in range(options_y):
-            for side_z in range(2):
-                if step_x == 0 and side_y == 0 and side_z == 0:
-                    continue
-                to_x = index_x + step_x
-                if side_y == 0:
-                    to_y = index_y
-                elif fold_y:
-                    to_y = 1 - index_y
-                else:
-                    to_y = index_y + (2 * side_y - 3)
-                to_z = index_z if side_z == 0 else 1 - index_z
-                at = (((step_x + 1) * options_y + side_y) * 2 + side_z) * CAP
-
-                @pl.when((to_x >= 0) & (to_x < count_x) & (to_y >= 0) & (to_y < count_y))
-                def _(to=(to_x * count_y + to_y) * count_z + to_z, at=at):
-                    bucket_ref[to] = rows[at : at + CAP]
+    bucket_ref[...] = jnp.concatenate([state, mask, jnp.zeros((ROWS - 10, movers), F32)], axis=0)
 
 
 def edges_kernel(
@@ -490,7 +467,6 @@
 
 
 def nodes_kernel(
-    sizes,
     first_ref,
     second_ref,
     node_pre_ref,
@@ -498,54 +474,96 @@
     state_ref,
     weights_ref,
     decoder_out_ref,
+    moved_ref,
+):
+    aggregate = jnp.concatenate([first_ref[0], first_ref[1], second_ref[0], second_ref[1]], axis=1)
+    acceleration = advance(
+        node_pre_ref[...], aggregate, latent_t_ref[...], weights_ref, decoder_out_ref[...]
+    )
+    state = moved(state_ref[0:3], state_ref[3:6], acceleration)
+    moved_ref[...] = jnp.concatenate(
+        [state, state_ref[6:7], jnp.zeros((ROWS - 10, state.shape[1]), F32)], axis=0
+    )
+
+
+def finish_kernel(
+    sizes,
+    moved_ref,
+    own_ref,
+    even_ref,
+    odd_ref,
+    own_zed,
+    even_zed,
+    odd_zed,
     inward_ref,
     encoder_w_ref,
     kept_latent_ref,
     kept_state_ref,
+    arrived_latent_ref,
+    arrived_state_ref,
 ):
-    slots = first_ref.shape[-1]
-    aggregate = jnp.concatenate([first_ref[0], first_ref[1], second_ref[0], second_ref[1]], axis=1)
-    acceleration = advance(
-        node_pre_ref[...], aggregate, latent_t_ref[...], weights_ref, decoder_out_ref[...]
-    )
-    stays = state_ref[6:7]
-    state = moved(state_ref[0:3], state_ref[3:6], acceleration)
-    extent = (2.0 * sizes[0], 2.0 * sizes[1], 1.0 * sizes[2])
-    latents = encode(state, stays, inward_ref[...], encoder_w_ref[...], extent)
-    kept = state * stays
+    count_x, count_y, count_z = sizes
+    extent = (2.0 * count_x, 2.0 * count_y, 1.0 * count_z)
+    slots = kept_latent_ref.shape[-2]
+    stays = moved_ref[9:10]
+    kept = moved_ref[:9] * stays
+    latents = encode(moved_ref[:9], stays, inward_ref[...], encoder_w_ref[...], extent)
     for i, (a, b) in enumerate(CELLS):
         kept_latent_ref[a, b, 0] = latents[i * slots : (i + 1) * slots]
         for j in range(9):
             kept_state_ref[j, a, b] = kept[j : j + 1, i * slots : (i + 1) * slots]
-
-
-def arrive_kernel(
-    sizes,
-    received_ref,
-    inward_ref,
-    encoder_w_ref,
-    arrived_latent_ref,
-    arrived_state_ref,
-):
-    count_x, count_y, count_z = sizes
+    fold_y = count_y == 2
     index_x = lax.axis_index("gx")
     index_y = lax.axis_index("gy")
     index_z = lax.axis_index("gz")
-    rows = []
-    for direction in range(27):
-        if direction == 13:
-            continue
-        x = index_x + (direction // 9 - 1)
-        y = index_y + (direction // 3 % 3 - 1)
-        z = index_z + (direction % 3 - 1)
-        inside = (x >= 0) & (x < count_x) & (y >= 0) & (y < count_y) & (z >= 0) & (z < count_z)
-        source = jnp.where(inside, (x * count_y + y) * count_z + z, 0)
-        rows.append(jnp.where(inside, received_ref[source], 0.0))
-    rows.append(jnp.zeros((256 - 26 * CAP, 128), F32))
-    arrived = jnp.concatenate(rows, axis=0).T[:ROWS, : 26 * CAP]
+    options_y = 2 if fold_y else 3
+    lanes = own_ref.shape[-1]
+    group = lax.broadcasted_iota(I32, (ROWS, lanes), 1) >> 3
+    even = (index_x & 1) == 0
+    found = jnp.zeros((ROWS, lanes), F32)
+    for source_x in (-1, 0, 1):
+        for from_y in range(options_y):
+            for from_z in range(2):
+                if source_x == 0 and from_y == 0 and from_z == 0:
+                    continue
+                if from_z == 0:
+                    own, first, second = own_ref, even_ref, odd_ref
+                else:
+                    own, first, second = own_zed, even_zed, odd_zed
+                side_y = from_y if fold_y or from_y == 0 else 3 - from_y
+                target = ((1 - source_x) * options_y + side_y) * 2 + from_z
+                if source_x == 0:
+                    tile = own[from_y]
+                    there = group == target
+                elif source_x == -1:
+                    tile = jnp.where(even, second[from_y], first[from_y])
+                    there = (group == target) & (index_x > 0)
+                else:
+                    tile = jnp.where(even, first[from_y], second[from_y])
+                    there = (group == target) & (index_x < count_x - 1)
+                found = jnp.where(there, tile, found)
+    out_lanes = arrived_state_ref.shape[-1]
+    spread_shape = (lanes, out_lanes)
+    line = lax.broadcasted_iota(I32, spread_shape, 0)
+    from_group = line >> 3
+    plane = from_group >> 1
+    from_x = 1 - ((plane >> 1) if fold_y else ((plane * 43) >> 7))
+    side_y = plane - (1 - from_x) * options_y
+    if fold_y:
+        from_y = jnp.where(side_y == 0, 0, jnp.where(index_y == 0, 1, -1))
+    else:
+        from_y = jnp.where(side_y == 0, 0, jnp.where(side_y == 1, 1, -1))
+    from_z = jnp.where((from_group & 1) == 0, 0, jnp.where(index_z == 0, 1, -1))
+    direction = (from_x + 1) * 9 + (from_y + 1) * 3 + from_z + 1
+    direction = direction - jnp.where(direction > 13, 1, 0)
+    column = direction * CAP + (line & 7)
+    valid = (lax.broadcasted_iota(I32, spread_shape, 1) == column) & (
+        (from_x != 0) | (from_y != 0) | (from_z != 0)
+    )
+    spread = jnp.where(valid, 1.0, 0.0).astype(BF16)
+    arrived = joined(dot(thirds(found), spread))
     for j in range(9):
         arrived_state_ref[j, 0, 0] = arrived[j : j + 1]
-    extent = (2.0 * count_x, 2.0 * count_y, 1.0 * count_z)
     arrived_latent_ref[0, 0, 0] = encode(
         arrived[:9], arrived[9:10], inward_ref[...], encoder_w_ref[...], extent
     )
@@ -720,7 +738,7 @@
         functools.partial(movers_kernel, sizes, len(sides)),
         "movers",
         [VMEM] * (len(halo) + 9),
-        [((4 * rows, width, 2 * slots), BF16), ((sizes[0] * sizes[1] * sizes[2], CAP, 128), F32)],
+        [((4 * rows, width, 2 * slots), BF16), ((ROWS, movers), F32)],
         [pltpu.VMEM((width, neighbour_count * movers), BF16)],
         (
             latent,
@@ -748,37 +766,42 @@
             4_000_000_000,
         )[0]
 
-    received = lax.all_to_all(bucket, ("gx", "gy", "gz"), 0, 0, tiled=True)
-    first, second = edges(0), edges(1)
-    kept_latent, kept_state = call(
-        functools.partial(nodes_kernel, sizes),
+    first = edges(0)
+    if fold_y:
+        tiles = [swap(bucket, "gy")]
+    else:
+        tiles = [shift(bucket, "gy", 0), shift(bucket, "gy", 1)]
+    tiles, first = lax.optimization_barrier((tiles, first))
+    tiles = jnp.stack([bucket, *tiles], axis=0)
+    second = edges(1)
+    sided = [swap_x(tiles, 0), swap_x(tiles, 1)]
+    sided, second = lax.optimization_barrier((sided, second))
+    tiles = [tiles, *sided]
+    zeds = [swap(part, "gz") for part in tiles]
+    state = call(
+        nodes_kernel,
         "nodes",
+        [VMEM] * 7,
+        [((ROWS, particles), F32)],
+        [],
+        (first, second, node_pre, latent_t, state, weights, decoder_out),
+        1_000_000_000,
+    )[0]
+    zeds, state = lax.optimization_barrier((zeds, state))
+    return call(
+        functools.partial(finish_kernel, sizes),
+        "finish",
         [VMEM] * 9,
-        [(node_latent.shape, BF16), ((9,) + node_latent.shape[:4], F32)],
+        [
+            (node_latent.shape, BF16),
+            ((9,) + node_latent.shape[:4], F32),
+            ((1, 1, 1, 26 * CAP, width), BF16),
+            ((9, 1, 1, 1, 26 * CAP), F32),
+        ],
         [],
-        (
-            first,
-            second,
-            node_pre,
-            latent_t,
-            state,
-            weights,
-            decoder_out,
-            inward,
-            encoder_weights,
-        ),
-        2_000_000_000,
-    )
-    arrived_latent, arrived_state = call(
-        functools.partial(arrive_kernel, sizes),
-        "arrive",
-        [VMEM] * 3,
-        [((1, 1, 1, 26 * CAP, width), BF16), ((9, 1, 1, 1, 26 * CAP), F32)],
-        [],
-        (received, inward, encoder_weights),
+        (state, *tiles, *zeds, inward, encoder_weights),
         1_000_000_000,
     )
-    return kept_latent, kept_state, arrived_latent, arrived_state
 
 
 def solution(mesh):

time: 38.4 us -> 32.7 us (0.85)
  waiting for transfers between devices: 5.78 us -> 1.3 us
  Pallas kernels: 18.3 us -> 16.6 us
  starting transfers between devices: 12.4 us -> 12.8 us
    all_to_all x1 -> x0, starting transfers between devices: 6.6 us -> none  [body(): received = lax.all_to_all(bucket, ('gx', 'gy', 'gz'), 0, 0, tiled=True)]
    ppermute x2 -> x4, starting transfers between devices: 2.21 us -> 7.12 us  [swap_x(): return lax.ppermute(values, ('gx', 'gz'), pairs)]
    all_to_all x1 -> x0, waiting for transfers between devices: 4.54 us -> none  [body(): received = lax.all_to_all(bucket, ('gx', 'gy', 'gz'), 0, 0, tiled=True)]
    ppermute x5 -> x9, starting transfers between devices: 3.6 us -> 5.72 us  [swap(): return lax.ppermute(values, axis, [(0, 1), (1, 0)])]
    pallas_call x7, Pallas kernels: 18.3 us -> 16.6 us  [call(): pl.pallas_call(kernel, out_shape=tuple((jax.ShapeDtypeStruct(shape, kind)...]
    ppermute x5 -> x9, waiting for transfers between devices: 1.23 us -> 1.29 us  [swap(): return lax.ppermute(values, axis, [(0, 1), (1, 0)])]
  transfers between devices with their start and end apart: 8 -> 13, of which waited for: 3 -> 3; matrix products, arithmetic and copies ran while one was open for 0% -> 0% of each run, Pallas kernels for 20% -> 36%
where the time goes in v6:
time: 32.7 us; the launch traced here: 32.5 us
  Pallas kernels  16.6 us (51%)
  starting transfers between devices  12.8 us (39%)
  waiting for transfers between devices  1.3 us (4%)
  local copies, waits for them, and re-layouts  0.87 us (3%)
  between operations  0.81 us (2%)
    pallas_call x7, Pallas kernels, call(): pl.pallas_call(kernel, out_shape=tuple((jax.ShapeDtypeStruct(shape, kind)...  16.6 us
    ppermute x4, starting transfers between devices, swap_x(): return lax.ppermute(values, ('gx', 'gz'), pairs)  7.12 us
    ppermute x9, starting transfers between devices, swap(): return lax.ppermute(values, axis, [(0, 1), (1, 0)])  5.72 us
    ppermute x9, waiting for transfers between devices, swap(): return lax.ppermute(values, axis, [(0, 1), (1, 0)])  1.29 us
    squeeze x1, local copies, waits for them, and re-layouts, body(): lax.dynamic_index_in_dim(cells, inner, 1, keepdims=False)  0.85 us
  transfers between devices with their start and end apart: 13, of which 3 were waited for; matrix products, arithmetic and copies ran while one was open for 0% of the time, Pallas kernels for 36%

profile of v6, /device:TPU:0, one launch (start us, length us, event | category | flops | bytes accessed | tf_op | source)
XLA Modules:
  0.0 32.5 jit_solution(16377242798094616882)
XLA Ops:
  0.6 0.9 %dynamic-slice_bitcast_fusion = bf16[2,128,128]{2,1,0:T(8,128)(2,1)S(1)} fusion(bf16[2,2,1,128,128]{4,3,2,1,0:T(8,128)(2,1)} %latent_any.1, s32[]{:T(128)S(6)} %select_n.11), kind=kLoop, calls=%fused_computation.2 | loop fusion | bytes 131076 | tf_op jit(solution)/shard_map/jit(dynamic_index_in_dim)/squeeze | solution.py:646
  1.5 2.9 %collective-permute-start = (bf16[2,128,128]{2,1,0:T(8,128)(2,1)S(1)}, bf16[2,128,128]{2,1,0:T(8,128)(2,1)S(1)}, u32[]{:S(2)}, u32[]{:S(2)}) collective-permute-start(bf16[2,128,128]{2,1,0:T(8,128)(2,1)S(1)} %dynamic-slice_bitcast_fusion), channel_id=1, source_target_pairs={{0,2},{2,0},{1,3},{3,1},{4,6},{6,4},{5,7},{7,5},{8,10},{10,8},{9,1... | collective-permute-start | bytes 196616 | tf_op jit(solution)/shard_map/ppermute | solution.py:573
  4.4 2.8 %ranks.1 = (bf16[11,128,128]{2,1,0:T(8,128)(2,1)S(1)}, bf16[3,128]{1,0:T(4,128)(2,1)S(1)}, bf16[48,128]{1,0:T(8,128)(2,1)S(1)}, bf16[2,128,128]{2,1,0:T(8,128)(2...) custom-call(s32[2,1,2]{2,1,0:T(1,128)} %bitcast.11, ...), custom_call_target="tpu_custom_call" | custom-call | flops 500000000 | tf_op jit(solution)/shard_map/ranks/pallas_call | solution.py:595
  7.2 1.6 %collective-permute-start.1 = (bf16[3,128,128]{2,1,0:T(8,128)(2,1)S(1)}, bf16[3,128,128]{2,1,0:T(8,128)(2,1)S(1)}, u32[]{:S(2)}, u32[]{:S(2)}) collective-permute-start(bf16[3,128,128]{2,1,0:T(8,128)(2,1)S(1)} %pad_maximum_fusion), channel_id=1, source_target_pairs={{0,4},{1,5},{4,0},{5,1},{8,12},{9,13},{12,8},{13,9},{2,6},{3,7},{6... | collective-permute-start | bytes 294920 | tf_op jit(solution)/shard_map/ppermute | solution.py:591
  8.9 0.0 collective-permute-start.3
  8.9 0.6 %collective-permute-start.2 = (bf16[3,128,128]{2,1,0:T(8,128)(2,1)S(1)}, bf16[3,128,128]{2,1,0:T(8,128)(2,1)S(1)}, u32[]{:S(2)}, u32[]{:S(2)}) collective-permute-start(bf16[3,128,128]{2,1,0:T(8,128)(2,1)S(1)} %pad_maximum_fusion.1), channel_id=1, source_target_pairs={{0,1},{1,0},{4,8},{5,9},{8,4},{9,5},{12,13},{13,12},{2,3},{3,2},{6... | collective-permute-start | bytes 294920 | tf_op jit(solution)/shard_map/ppermute | solution.py:591
  9.5 0.1 collective-permute-start.4
  9.6 2.5 %prepare.1 = (f32[128,512]{1,0:T(8,128)S(1)}, f32[128,512]{1,0:T(8,128)S(1)}, f32[8,512]{1,0:T(8,128)S(1)}, f32[128,1536]{1,0:T(8,128)S(1)}, s32[12,128]{1,0:T(8...) custom-call(bf16[2,2,1,128,128]{4,3,2,1,0:T(8,128)(2,1)S(1)} %get-tup, ...), custom_call_target="tpu_custom_call" | custom-call | flops 500000000 | tf_op jit(solution)/shard_map/prepare/pallas_call | solution.py:595
  12.1 0.5 %collective-permute-start.5 = (bf16[3,128,128]{2,1,0:T(8,128)(2,1)S(1)}, bf16[3,128,128]{2,1,0:T(8,128)(2,1)S(1)}, u32[]{:S(2)}, u32[]{:S(2)}) collective-permute-start(bf16[3,128,128]{2,1,0:T(8,128)(2,1)S(1)} %collective-permute-done.1.refs_1_), channel_id=1, source_target_pairs={{0,1},{1,0},{2,3},{3,2},{4,5},{5,4},{6,7},{7,6},{8,9},{9,8},{10,11... | collective-permute-start | bytes 294920 | tf_op jit(solution)/shard_map/ppermute | solution.py:573
  12.6 0.1 collective-permute-start.6
  12.7 0.9 %collective-permute-done.5.refs_5_ = bf16[3,128,128]{2,1,0:T(8,128)(2,1)S(1)} collective-permute-done((bf16[3,128,128]{2,1,0:T(8,128)(2,1)S(1)}, bf16[3,128,128]{2,1,0:T(8,128)(2,1)S(1)}, u32[]{:S(2)}, u32[]{:S(2)}) %collective-permute-start.5) | collective-permute-done | bytes 98336 | tf_op jit(solution)/shard_map/ppermute | solution.py:573
  13.6 0.4 %collective-permute-done.6.refs_6_ = bf16[3,128,128]{2,1,0:T(8,128)(2,1)S(1)} collective-permute-done((bf16[3,128,128]{2,1,0:T(8,128)(2,1)S(1)}, bf16[3,128,128]{2,1,0:T(8,128)(2,1)S(1)}, u32[]{:S(2)}, u32[]{:S(2)}) %collective-permute-start.6) | collective-permute-done | bytes 98336 | tf_op jit(solution)/shard_map/ppermute | solution.py:573
  13.9 3.0 %movers.1 = (bf16[12,128,256]{2,1,0:T(8,128)(2,1)S(1)}, f32[16,128]{1,0:T(8,128)S(1)}) custom-call(bf16[2,2,1,128,128]{4,3,2,1,0:T(8,128)(2,1)S(1)} %get-tuple-element.80.latent_ref.own_ref, bf16[2,128,128]{2,1,0:T(8,128)(2,1)S(1)} %collective-permute-done.refs_0_, bf16[3,128,128]{2,1,0:T(8,128)(2,1)S(1)} %collective-permute-done.1.refs_1_, ...), custom_call_target="tpu_custom_call" | custom-call | flops 3000000000 | tf_op jit(solution)/shard_map/movers/pallas_call | solution.py:595
  17.0 1.5 %collective-permute-start.7 = (f32[16,128]{1,0:T(8,128)S(1)}, f32[16,128]{1,0:T(8,128)S(1)}, u32[]{:S(2)}, u32[]{:S(2)}) collective-permute-start(f32[16,128]{1,0:T(8,128)S(1)} %get-tuple-element.111), channel_id=1, source_target_pairs={{0,2},{2,0},{1,3},{3,1},{4,6},{6,4},{5,7},{7,5},{8,10},{10,8},{9,1... | collective-permute-start | bytes 24584 | tf_op jit(solution)/shard_map/ppermute | solution.py:573
  18.5 2.7 %edges.2.first_ref = bf16[2,128,128]{2,1,0:T(8,128)(2,1)S(1)} custom-call(f32[2,2,1,128]{3,2,1,0:T(1,128)S(1)} %get-tuple-element.112.alive_ref, bf16[2,2,1,128,128]{4,3,2,1,0:T(8,128)(2,1)S(1)} %get-tuple-element.80.latent_ref.own_ref, bf16[2,2,1,12,128,128]{5,4,3,2,1,0:T(8,128)(2,1)S(1)} %get-tuple-element.84.edge_ref, ...), custom_call_target="tpu_custom_call" | custom-call | flops 4000000000 | tf_op jit(solution)/shard_map/edges/pallas_call | solution.py:595
  21.2 0.1 collective-permute-start.10
  21.3 4.8 %collective-permute-start.9 = (f32[2,16,128]{2,1,0:T(8,128)S(1)}, f32[2,16,128]{2,1,0:T(8,128)S(1)}, u32[]{:S(2)}, u32[]{:S(2)}) collective-permute-start(f32[2,16,128]{2,1,0:T(8,128)S(1)} %pad_maximum_fusion.2.own_ref), channel_id=1, source_target_pairs={{0,4},{1,5},{4,0},{5,1},{8,12},{9,13},{12,8},{13,9},{2,6},{3,7},{6... | collective-permute-start | bytes 49160 | tf_op jit(solution)/shard_map/ppermute | solution.py:591
  26.1 2.7 %edges.3.second_ref = bf16[2,128,128]{2,1,0:T(8,128)(2,1)S(1)} custom-call(f32[2,2,1,128]{3,2,1,0:T(1,128)S(1)} %get-tuple-element.112.alive_ref, bf16[2,2,1,128,128]{4,3,2,1,0:T(8,128)(2,1)S(1)} %get-tuple-element.80.latent_ref.own_ref, bf16[2,2,1,12,128,128]{5,4,3,2,1,0:T(8,128)(2,1)S(1)} %get-tuple-element.84.edge_ref, ...), custom_call_target="tpu_custom_call" | custom-call | flops 4000000000 | tf_op jit(solution)/shard_map/edges/pallas_call | solution.py:595
  28.9 0.1 collective-permute-start.8
  29.0 0.5 %collective-permute-start.11 = (f32[2,16,128]{2,1,0:T(8,128)S(1)}, f32[2,16,128]{2,1,0:T(8,128)S(1)}, u32[]{:S(2)}, u32[]{:S(2)}) collective-permute-start(f32[2,16,128]{2,1,0:T(8,128)S(1)} %collective-permute-done.9.even_ref), channel_id=1, source_target_pairs={{0,1},{1,0},{2,3},{3,2},{4,5},{5,4},{6,7},{7,6},{8,9},{9,8},{10,11... | collective-permute-start | bytes 49160 | tf_op jit(solution)/shard_map/ppermute | solution.py:573
  29.5 0.1 collective-permute-start.12
  29.6 1.0 %nodes.1.moved_ref = f32[16,512]{1,0:T(8,128)S(1)} custom-call(bf16[2,128,128]{2,1,0:T(8,128)(2,1)S(1)} %edges.2.first_ref, bf16[2,128,128]{2,1,0:T(8,128)(2,1)S(1)} %edges.3.second_ref, f32[128,512]{1,0:T(8,128)S(1)} %get-tuple-element.119.node_pre_ref, f32[128,512]{1,0:T(8,128)S(1)} %get-tuple-element.120.latent_t_ref, ...), custom_call_target="tpu_custom_call" | custom-call | flops 1000000000 | tf_op jit(solution)/shard_map/nodes/pallas_call | solution.py:595
  30.6 0.1 collective-permute-done.12.odd_zed
  30.7 1.8 %finish.1 = (bf16[2,2,1,128,128]{4,3,2,1,0:T(8,128)(2,1)}, f32[9,2,2,1,128]{4,3,2,1,0:T(1,128)}, bf16[1,1,1,208,128]{4,3,2,1,0:T(8,128)(2,1)}, f32[9,1,1,1,208]{4,3,2,1,0:T(1,128)}) custom-call(f32[16,512]{1,0:T(8,128)S(1)} %nodes.1.moved_ref, f32[2,16,128]{2,1,0:T(8,128)S(1)} %pad_maximum_fusion.2.own_ref, ...), custom_call_target="tpu_custom_call" | custom-call | flops 1000000000 | tf_op jit(solution)/shard_map/finish/pallas_call | solution.py:595
  (14 shorter events, 0.1 us)
Async XLA Ops:
  1.5 5.7 %collective-permute-start = (bf16[2,128,128]{2,1,0:T(8,128)(2,1)S(1)}, bf16[2,128,128]{2,1,0:T(8,128)(2,1)S(1)}, u32[]{:S(2)}, u32[]{:S(2)}) collective-permute-start(bf16[2,128,128]{2,1,0:T(8,128)(2,1)S(1)} %dynamic-slice_bitcast_fusion), channel_id=1, source_target_pairs={{0,2},{2,0},{1,3},{3,1},{4,6},{6,4},{5,7},{7,5},{8,10},{10,8},{9,1... | collective-permute-start | bytes 196616 | tf_op jit(solution)/shard_map/ppermute | solution.py:573
  7.2 4.9 %collective-permute-start.1 = (bf16[3,128,128]{2,1,0:T(8,128)(2,1)S(1)}, bf16[3,128,128]{2,1,0:T(8,128)(2,1)S(1)}, u32[]{:S(2)}, u32[]{:S(2)}) collective-permute-start(bf16[3,128,128]{2,1,0:T(8,128)(2,1)S(1)} %pad_maximum_fusion), channel_id=1, source_target_pairs={{0,4},{1,5},{4,0},{5,1},{8,12},{9,13},{12,8},{13,9},{2,6},{3,7},{6... | collective-permute-start | bytes 294920 | tf_op jit(solution)/shard_map/ppermute | solution.py:591
  8.9 3.2 %collective-permute-start.3 = (bf16[2,2,1,128,128]{4,3,2,1,0:T(8,128)(2,1)S(1)}, bf16[2,2,1,128,128]{4,3,2,1,0:T(8,128)(2,1)S(1)}, u32[]{:S(2)}, u32[]{:S(2)}) collective-permute-start(bf16[2,2,1,128,128]{4,3,2,1,0:T(8,128)(2,1)S(1)} %get-tuple-element.80.latent_ref.own_ref), channel_id=1, source_target_pairs={{0,1},{1,0},{2,3},{3,2},{4,5},{5,4},{6,7},{7,6},{8,9},{9,8},{10,11... | collective-permute-start | bytes 393224 | tf_op jit(solution)/shard_map/ppermute | solution.py:573
  8.9 3.2 %collective-permute-start.2 = (bf16[3,128,128]{2,1,0:T(8,128)(2,1)S(1)}, bf16[3,128,128]{2,1,0:T(8,128)(2,1)S(1)}, u32[]{:S(2)}, u32[]{:S(2)}) collective-permute-start(bf16[3,128,128]{2,1,0:T(8,128)(2,1)S(1)} %pad_maximum_fusion.1), channel_id=1, source_target_pairs={{0,1},{1,0},{4,8},{5,9},{8,4},{9,5},{12,13},{13,12},{2,3},{3,2},{6... | collective-permute-start | bytes 294920 | tf_op jit(solution)/shard_map/ppermute | solution.py:591
  9.5 2.6 %collective-permute-start.4 = (bf16[2,128,128]{2,1,0:T(8,128)(2,1)S(1)}, bf16[2,128,128]{2,1,0:T(8,128)(2,1)S(1)}, u32[]{:S(2)}, u32[]{:S(2)}) collective-permute-start(bf16[2,128,128]{2,1,0:T(8,128)(2,1)S(1)} %collective-permute-done.refs_0_), channel_id=1, source_target_pairs={{0,1},{1,0},{2,3},{3,2},{4,5},{5,4},{6,7},{7,6},{8,9},{9,8},{10,11... | collective-permute-start | bytes 196616 | tf_op jit(solution)/shard_map/ppermute | solution.py:573
  12.1 1.4 %collective-permute-start.5 = (bf16[3,128,128]{2,1,0:T(8,128)(2,1)S(1)}, bf16[3,128,128]{2,1,0:T(8,128)(2,1)S(1)}, u32[]{:S(2)}, u32[]{:S(2)}) collective-permute-start(bf16[3,128,128]{2,1,0:T(8,128)(2,1)S(1)} %collective-permute-done.1.refs_1_), channel_id=1, source_target_pairs={{0,1},{1,0},{2,3},{3,2},{4,5},{5,4},{6,7},{7,6},{8,9},{9,8},{10,11... | collective-permute-start | bytes 294920 | tf_op jit(solution)/shard_map/ppermute | solution.py:573
  12.6 1.3 %collective-permute-start.6 = (bf16[3,128,128]{2,1,0:T(8,128)(2,1)S(1)}, bf16[3,128,128]{2,1,0:T(8,128)(2,1)S(1)}, u32[]{:S(2)}, u32[]{:S(2)}) collective-permute-start(bf16[3,128,128]{2,1,0:T(8,128)(2,1)S(1)} %collective-permute-done.2.refs_2_), channel_id=1, source_target_pairs={{0,1},{1,0},{2,3},{3,2},{4,5},{5,4},{6,7},{7,6},{8,9},{9,8},{10,11... | collective-permute-start | bytes 294920 | tf_op jit(solution)/shard_map/ppermute | solution.py:573
  17.0 4.2 %collective-permute-start.7 = (f32[16,128]{1,0:T(8,128)S(1)}, f32[16,128]{1,0:T(8,128)S(1)}, u32[]{:S(2)}, u32[]{:S(2)}) collective-permute-start(f32[16,128]{1,0:T(8,128)S(1)} %get-tuple-element.111), channel_id=1, source_target_pairs={{0,2},{2,0},{1,3},{3,1},{4,6},{6,4},{5,7},{7,5},{8,10},{10,8},{9,1... | collective-permute-start | bytes 24584 | tf_op jit(solution)/shard_map/ppermute | solution.py:573
  21.2 7.7 %collective-permute-start.10 = (f32[2,16,128]{2,1,0:T(8,128)S(1)}, f32[2,16,128]{2,1,0:T(8,128)S(1)}, u32[]{:S(2)}, u32[]{:S(2)}) collective-permute-start(f32[2,16,128]{2,1,0:T(8,128)S(1)} %pad_maximum_fusion.2.own_ref), channel_id=1, source_target_pairs={{0,1},{1,0},{4,8},{5,9},{8,4},{9,5},{12,13},{13,12},{2,3},{3,2},{6... | collective-permute-start | bytes 49160 | tf_op jit(solution)/shard_map/ppermute | solution.py:591
  21.3 7.7 %collective-permute-start.9 = (f32[2,16,128]{2,1,0:T(8,128)S(1)}, f32[2,16,128]{2,1,0:T(8,128)S(1)}, u32[]{:S(2)}, u32[]{:S(2)}) collective-permute-start(f32[2,16,128]{2,1,0:T(8,128)S(1)} %pad_maximum_fusion.2.own_ref), channel_id=1, source_target_pairs={{0,4},{1,5},{4,0},{5,1},{8,12},{9,13},{12,8},{13,9},{2,6},{3,7},{6... | collective-permute-start | bytes 49160 | tf_op jit(solution)/shard_map/ppermute | solution.py:591
  28.9 1.7 %collective-permute-start.8 = (f32[2,16,128]{2,1,0:T(8,128)S(1)}, f32[2,16,128]{2,1,0:T(8,128)S(1)}, u32[]{:S(2)}, u32[]{:S(2)}) collective-permute-start(f32[2,16,128]{2,1,0:T(8,128)S(1)} %pad_maximum_fusion.2.own_ref), channel_id=1, source_target_pairs={{0,1},{1,0},{2,3},{3,2},{4,5},{5,4},{6,7},{7,6},{8,9},{9,8},{10,11... | collective-permute-start | bytes 49160 | tf_op jit(solution)/shard_map/ppermute | solution.py:573
  29.0 1.6 %collective-permute-start.11 = (f32[2,16,128]{2,1,0:T(8,128)S(1)}, f32[2,16,128]{2,1,0:T(8,128)S(1)}, u32[]{:S(2)}, u32[]{:S(2)}) collective-permute-start(f32[2,16,128]{2,1,0:T(8,128)S(1)} %collective-permute-done.9.even_ref), channel_id=1, source_target_pairs={{0,1},{1,0},{2,3},{3,2},{4,5},{5,4},{6,7},{7,6},{8,9},{9,8},{10,11... | collective-permute-start | bytes 49160 | tf_op jit(solution)/shard_map/ppermute | solution.py:573
  29.5 1.2 %collective-permute-start.12 = (f32[2,16,128]{2,1,0:T(8,128)S(1)}, f32[2,16,128]{2,1,0:T(8,128)S(1)}, u32[]{:S(2)}, u32[]{:S(2)}) collective-permute-start(f32[2,16,128]{2,1,0:T(8,128)S(1)} %collective-permute-done.10.odd_ref), channel_id=1, source_target_pairs={{0,1},{1,0},{2,3},{3,2},{4,5},{5,4},{6,7},{7,6},{8,9},{9,8},{10,11... | collective-permute-start | bytes 49160 | tf_op jit(solution)/shard_map/ppermute | solution.py:573

commit v7 on v6

--- a/solution.py
+++ b/solution.py
@@ -106,33 +106,58 @@
     return ex * 4 + row, ids_low + jnp.where(ez == 1, 0, 128)
 
 
-def messages(far_ref, columns, row_count, place, key, pre, middle_t, final_t, hidden_ref):
-    width = far_ref.shape[1]
+def pick(cells, place, key):
+    width = cells[0][1].shape[0]
     chunk = 32
     window = jnp.concatenate(
-        [
-            far_ref[ex * row_count + row, f : f + chunk]
-            for f in range(0, width, chunk)
-            for ex, row in columns
-        ],
-        axis=0,
+        [ref[f : f + chunk] for f in range(0, width, chunk) for _, ref in cells], axis=0
     )
     key_rows = lax.broadcasted_iota(I32, (TILE, TILE), 0)
-    lanes = place.shape[1]
-    for tile in range(lanes // TILE):
+    picker = jnp.where(key_rows == key, 1.0, 0.0).astype(BF16)
+    found = dot(window, picker).reshape(width // chunk, len(cells), chunk // 8, 8, TILE)
+    where = jnp.broadcast_to(place, (8, TILE))
+    parts = []
+    for f in range(width // chunk):
+        part = jnp.zeros((chunk // 8, 8, TILE), F32)
+        for i, (column, _) in enumerate(cells):
+            part = jnp.where((where == column)[None], found[f, i], part)
+        parts.append(part.reshape(chunk, TILE))
+    return jnp.concatenate(parts, axis=0)
+
+
+def messages(cells, place, key, pre, middle_t, final_t, hidden_ref):
+    for tile in range(place.shape[1] // TILE):
         at = slice(tile * TILE, (tile + 1) * TILE)
-        picker = jnp.where(key_rows == key[:, at], 1.0, 0.0).astype(BF16)
-        found = dot(window, picker).reshape(width // chunk, len(columns), chunk // 8, 8, TILE)
-        where = jnp.broadcast_to(place[:, at], (8, TILE))
-        parts = []
-        for f in range(width // chunk):
-            part = jnp.zeros((chunk // 8, 8, TILE), F32)
-            for i, (ex, row) in enumerate(columns):
-                part = jnp.where((where == ex * 4 + row)[None], found[f, i], part)
-            parts.append(part.reshape(chunk, TILE))
-        hidden_ref[:, at] = relu16(pre(tile) + jnp.concatenate(parts, axis=0))
+        hidden_ref[:, at] = relu16(pre(tile) + pick(cells, place[:, at], key[:, at]))
     hidden = relu16(dot(middle_t, hidden_ref[...]))
     return norm(dot(final_t, hidden), 0)
+
+
+class Window:
+    def __init__(self, fold_y, own_ref=None, rest_ref=None):
+        self.row_count = 3 if fold_y else 4
+        self.own_rows = (0, 1) if fold_y else (1, 2)
+        self.outer_rows = (2,) if fold_y else (0, 3)
+        self.own_ref, self.rest_ref = own_ref, rest_ref
+
+    def own(self, ex, row):
+        return (ex - 1) * 2 + self.own_rows.index(row)
+
+    def side(self, ex, row):
+        count = len(self.outer_rows)
+        return 2 * self.row_count + (ex - 1) * count + self.outer_rows.index(row)
+
+    def cells(self, columns):
+        found = []
+        for ex, row in columns:
+            if ex in (1, 2) and row in self.own_rows:
+                ref = self.own_ref.at[self.own(ex, row)]
+            elif ex in (1, 2):
+                ref = self.rest_ref.at[self.side(ex, row)]
+            else:
+                ref = self.rest_ref.at[(0 if ex == 0 else self.row_count) + row]
+            found.append((ex * 4 + row, ref))
+        return found
 
 
 def slot_sum(message, step):
@@ -186,6 +211,7 @@
     edge_ref,
     first_end_ref,
     second_end_ref,
+    spread_ref,
     owners_ref,
     edge_w_ref,
     node_in_ref,
@@ -266,6 +292,25 @@
         [stays, moving.astype(F32), jnp.zeros((6, particles), F32)], axis=0
     )
 
+    spread_shape = spread_ref.shape
+    line = lax.broadcasted_iota(I32, spread_shape, 0)
+    from_group = line >> 3
+    plane = from_group >> 1
+    from_x = 1 - ((plane >> 1) if fold_y else ((plane * 43) >> 7))
+    side_y = plane - (1 - from_x) * options_y
+    if fold_y:
+        from_y = jnp.where(side_y == 0, 0, jnp.where(index_y == 0, 1, -1))
+    else:
+        from_y = jnp.where(side_y == 0, 0, jnp.where(side_y == 1, 1, -1))
+    from_z = jnp.where((from_group & 1) == 0, 0, jnp.where(index_z == 0, 1, -1))
+    direction = (from_x + 1) * 9 + (from_y + 1) * 3 + from_z + 1
+    direction = direction - jnp.where(direction > 13, 1, 0)
+    column = direction * CAP + (line & 7)
+    valid = (lax.broadcasted_iota(I32, spread_shape, 1) == column) & (
+        (from_x != 0) | (from_y != 0) | (from_z != 0)
+    )
+    spread_ref[...] = jnp.where(valid, 1.0, 0.0).astype(BF16)
+
     for copy in copies[1:]:
         copy.wait()
     for i in range(5):
@@ -287,6 +332,7 @@
 def prepare_kernel(
     sizes,
     latent_ref,
+    own_zed,
     edge_ref,
     positions_ref,
     velocity_ref,
@@ -294,6 +340,7 @@
     weights_ref,
     placer_ref,
     masks_ref,
+    far_ref,
     latent_t_ref,
     node_pre_ref,
     state_ref,
@@ -336,26 +383,41 @@
     ids = jnp.concatenate([ids & 127, ids >> 7, jnp.zeros((8, particles), I32)], axis=0)
     ids = dot_nt(ids.astype(F32).astype(BF16), placer).astype(I32)
     place, key = places(ids[:neighbour_count], ids[neighbour_count : 2 * neighbour_count], fold_y)
+    place = jnp.concatenate([place[k : k + 1] for k in range(neighbour_count)], axis=1)
+    key = jnp.concatenate([key[k : k + 1] for k in range(neighbour_count)], axis=1)
     mover_place_ref[...] = place
     mover_key_ref[...] = key
-    for k in range(neighbour_count):
-        edges = jnp.concatenate([edge_ref[a, b, 0, k] for a, b in CELLS], axis=0)
-        edges = dot(placer, edges).astype(BF16)
-        mover_pre_ref[:, k * movers : (k + 1) * movers] = dot_nt(weights_ref[EDGE], edges) + near
+    window = Window(fold_y, far_ref)
+    columns = [(ex, row) for ex in (1, 2) for row in window.own_rows]
+    for (ex, row), (a, b) in zip(columns, CELLS):
+        pair = jnp.concatenate([latent_ref[a, b, 0], own_zed[a, b, 0]], axis=0)
+        far_ref[window.own(ex, row)] = dot_nt(weights_ref[FAR], pair).astype(BF16)
+    cells = window.cells(columns)
+    step = TILE // movers
+    near = jnp.concatenate([near] * step, axis=1)
+    for tile in range(neighbour_count // step):
+        edges = []
+        for k in range(tile * step, (tile + 1) * step):
+            rows = jnp.concatenate([edge_ref[a, b, 0, k] for a, b in CELLS], axis=0)
+            edges.append(dot(placer, rows).astype(BF16))
+        at = slice(tile * TILE, (tile + 1) * TILE)
+        mover_pre_ref[:, at] = (
+            dot_nt(weights_ref[EDGE], jnp.concatenate(edges, axis=0))
+            + near
+            + pick(cells, place[:, at], key[:, at])
+        )
 
 
 def movers_kernel(
     sizes,
     side_count,
-    own_ref,
     *refs,
 ):
-    count_x, count_y, count_z = sizes
-    fold_y = count_y == 2
+    fold_y = sizes[1] == 2
     side_refs, refs = refs[:side_count], refs[side_count:]
-    even_ref, odd_ref, own_zed, refs = refs[0], refs[1], refs[2], refs[3:]
+    odd_ref, even_ref, refs = refs[0], refs[1], refs[2:]
     side_zeds, refs = refs[:side_count], refs[side_count:]
-    even_zed, odd_zed, refs = refs[0], refs[1], refs[2:]
+    odd_zed, even_zed, refs = refs[0], refs[1], refs[2:]
     (
         weights_ref,
         decoder_out_ref,
@@ -369,9 +431,8 @@
         bucket_ref,
         hidden_ref,
     ) = refs
-    row_count = 3 if fold_y else 4
-    own_rows = (0, 1) if fold_y else (1, 2)
-    outer = {2: 0} if fold_y else {0: 0, 3: 1}
+    window = Window(fold_y, None, far_ref)
+    row_count = window.row_count
     parity = lax.axis_index("gx") & 1
     far_t = weights_ref[FAR]
 
@@ -380,27 +441,19 @@
         far_ref[at] = dot_nt(far_t, pair).astype(BF16)
 
     for row in range(row_count):
+        far((1 - parity) * row_count + row, even_ref[row], even_zed[row])
+        far(parity * row_count + row, odd_ref[row], odd_zed[row])
+    for side, row in enumerate(window.outer_rows):
         for ex in (1, 2):
-            if row in own_rows:
-                b = own_rows.index(row)
-                far(ex * row_count + row, own_ref[ex - 1, b, 0], own_zed[ex - 1, b, 0])
-            else:
-                side = outer[row]
-                far(ex * row_count + row, side_refs[side][ex - 1], side_zeds[side][ex - 1])
-        far(3 * (1 - parity) * row_count + row, even_ref[row], even_zed[row])
-        far(3 * parity * row_count + row, odd_ref[row], odd_zed[row])
+            far(window.side(ex, row), side_refs[side][ex - 1], side_zeds[side][ex - 1])
 
     movers = state_ref.shape[1]
-    neighbour_count = place_ref.shape[0]
-    place = jnp.concatenate([place_ref[k : k + 1] for k in range(neighbour_count)], axis=1)
-    key = jnp.concatenate([key_ref[k : k + 1] for k in range(neighbour_count)], axis=1)
-    columns = [(ex, row) for ex in range(4) for row in range(row_count)]
+    columns = [(ex, row) for ex in (0, 3) for row in range(row_count)]
+    columns += [(ex, row) for ex in (1, 2) for row in window.outer_rows]
     message = messages(
-        far_ref,
-        columns,
-        row_count,
-        place,
-        key,
+        window.cells(columns),
+        place_ref[...],
+        key_ref[...],
         lambda tile: pre_ref[:, tile * TILE : (tile + 1) * TILE],
         weights_ref[MIDDLE],
         weights_ref[FINAL],
@@ -422,13 +475,14 @@
     latent_ref,
     edge_ref,
     neighbours_ref,
-    far_ref,
+    far_own_ref,
+    far_rest_ref,
     weights_ref,
     total_ref,
     hidden_ref,
 ):
     fold_y = sizes[1] == 2
-    row_count = 3 if fold_y else 4
+    window = Window(fold_y, far_own_ref, far_rest_ref)
     index_y = lax.axis_index("gy")
     alive_ref, latent_ref = alive_ref.at[a], latent_ref.at[a]
     edge_ref, neighbours_ref = edge_ref.at[a], neighbours_ref.at[a]
@@ -452,9 +506,7 @@
             return dot_nt(weights_ref[EDGE], edges) + near
 
         message = messages(
-            far_ref,
-            columns,
-            row_count,
+            window.cells(columns),
             place,
             key,
             pre,
@@ -495,6 +547,7 @@
     own_zed,
     even_zed,
     odd_zed,
+    spread_ref,
     inward_ref,
     encoder_w_ref,
     kept_latent_ref,
@@ -514,8 +567,6 @@
             kept_state_ref[j, a, b] = kept[j : j + 1, i * slots : (i + 1) * slots]
     fold_y = count_y == 2
     index_x = lax.axis_index("gx")
-    index_y = lax.axis_index("gy")
-    index_z = lax.axis_index("gz")
     options_y = 2 if fold_y else 3
     lanes = own_ref.shape[-1]
     group = lax.broadcasted_iota(I32, (ROWS, lanes), 1) >> 3
@@ -542,26 +593,7 @@
                     tile = jnp.where(even, first[from_y], second[from_y])
                     there = (group == target) & (index_x < count_x - 1)
                 found = jnp.where(there, tile, found)
-    out_lanes = arrived_state_ref.shape[-1]
-    spread_shape = (lanes, out_lanes)
-    line = lax.broadcasted_iota(I32, spread_shape, 0)
-    from_group = line >> 3
-    plane = from_group >> 1
-    from_x = 1 - ((plane >> 1) if fold_y else ((plane * 43) >> 7))
-    side_y = plane - (1 - from_x) * options_y
-    if fold_y:
-        from_y = jnp.where(side_y == 0, 0, jnp.where(index_y == 0, 1, -1))
-    else:
-        from_y = jnp.where(side_y == 0, 0, jnp.where(side_y == 1, 1, -1))
-    from_z = jnp.where((from_group & 1) == 0, 0, jnp.where(index_z == 0, 1, -1))
-    direction = (from_x + 1) * 9 + (from_y + 1) * 3 + from_z + 1
-    direction = direction - jnp.where(direction > 13, 1, 0)
-    column = direction * CAP + (line & 7)
-    valid = (lax.broadcasted_iota(I32, spread_shape, 1) == column) & (
-        (from_x != 0) | (from_y != 0) | (from_z != 0)
-    )
-    spread = jnp.where(valid, 1.0, 0.0).astype(BF16)
-    arrived = joined(dot(thirds(found), spread))
+    arrived = joined(dot(thirds(found), spread_ref[...]))
     for j in range(9):
         arrived_state_ref[j, 0, 0] = arrived[j : j + 1]
     arrived_latent_ref[0, 0, 0] = encode(
@@ -663,6 +695,7 @@
             *((array.shape, array.dtype) for array in fetched),
             ((2, slots, width), BF16),
             ((2, slots, width), BF16),
+            ((movers, 26 * CAP), BF16),
         ],
         [
             like(owners),
@@ -690,38 +723,41 @@
         ],
         500_000_000,
     )
-    sides, ranked = lax.optimization_barrier((sides, ranked))
+    own_zed = swap(node_latent, "gz")
+    sides, own_zed, ranked = lax.optimization_barrier((sides, own_zed, ranked))
     weights, decoder_out, inward, encoder_weights, placer, masks, alive, *ranked = ranked
-    latent, neighbours, positions, velocity, edge_latent, *own_ends = ranked
+    latent, neighbours, positions, velocity, edge_latent, *own_ends, spread = ranked
 
     def layer(a, own):
         outer = [lax.dynamic_index_in_dim(side, a, 0) for side in sides]
         parts = [own, outer[0]] if fold_y else [outer[0], own, outer[1]]
         return jnp.concatenate(parts, axis=0)
 
-    ends = [swap_x(layer(1 - parity, own_ends[0]), 0), swap_x(layer(parity, own_ends[1]), 1)]
-    zeds = [swap(part, "gz") for part in [latent, *sides]]
+    ends = [swap_x(layer(parity, own_ends[1]), 1), swap_x(layer(1 - parity, own_ends[0]), 0)]
+    zeds = [swap(part, "gz") for part in sides]
     prepared = call(
         functools.partial(prepare_kernel, sizes),
         "prepare",
-        [VMEM] * 8,
+        [VMEM] * 9,
         [
+            ((4, width, 2 * slots), BF16),
             ((width, particles), F32),
             ((width, particles), F32),
             ((8, particles), F32),
             ((width, neighbour_count * movers), F32),
-            ((neighbour_count, movers), I32),
-            ((neighbour_count, movers), I32),
+            ((1, neighbour_count * movers), I32),
+            ((1, neighbour_count * movers), I32),
             ((width, movers), F32),
             ((width, movers), F32),
             ((8, movers), F32),
         ],
         [],
-        (latent, edge_latent, positions, velocity, neighbours, weights, placer, masks),
+        (latent, own_zed, edge_latent, positions, velocity, neighbours, weights, placer, masks),
         500_000_000,
     )
     ends, zeds, prepared = lax.optimization_barrier((ends, zeds, prepared))
     (
+        far_own,
         latent_t,
         node_pre,
         state,
@@ -734,14 +770,13 @@
     ) = prepared
     halo = [*sides, *ends, *zeds, *(swap(part, "gz") for part in ends)]
 
-    far, bucket = call(
+    far_rest, bucket = call(
         functools.partial(movers_kernel, sizes, len(sides)),
         "movers",
-        [VMEM] * (len(halo) + 9),
-        [((4 * rows, width, 2 * slots), BF16), ((ROWS, movers), F32)],
+        [VMEM] * (len(halo) + 8),
+        [((4 * rows - 4, width, 2 * slots), BF16), ((ROWS, movers), F32)],
         [pltpu.VMEM((width, neighbour_count * movers), BF16)],
         (
-            latent,
             *halo,
             weights,
             decoder_out,
@@ -759,10 +794,10 @@
         return call(
             functools.partial(edges_kernel, sizes, a),
             "edges",
-            [VMEM] * 6,
+            [VMEM] * 7,
             [((2, width, slots), BF16)],
             [pltpu.VMEM((2, width, neighbour_count * slots), BF16)],
-            (alive, latent, edge_latent, neighbours, far, weights),
+            (alive, latent, edge_latent, neighbours, far_own, far_rest, weights),
             4_000_000_000,
         )[0]
 
@@ -774,7 +809,8 @@
     tiles, first = lax.optimization_barrier((tiles, first))
     tiles = jnp.stack([bucket, *tiles], axis=0)
     second = edges(1)
-    sided = [swap_x(tiles, 0), swap_x(tiles, 1)]
+    odd = swap_x(tiles, 1)
+    sided = [swap_x(tiles, 0), odd]
     sided, second = lax.optimization_barrier((sided, second))
     tiles = [tiles, *sided]
     zeds = [swap(part, "gz") for part in tiles]
@@ -791,7 +827,7 @@
     return call(
         functools.partial(finish_kernel, sizes),
         "finish",
-        [VMEM] * 9,
+        [VMEM] * 10,
         [
             (node_latent.shape, BF16),
             ((9,) + node_latent.shape[:4], F32),
@@ -799,7 +835,7 @@
             ((9, 1, 1, 1, 26 * CAP), F32),
         ],
         [],
-        (state, *tiles, *zeds, inward, encoder_weights),
+        (state, *tiles, *zeds, spread, inward, encoder_weights),
         1_000_000_000,
     )
 

time: 32.7 us -> 30.8 us (0.942)
  starting transfers between devices: 12.8 us -> 11.5 us
  Pallas kernels: 16.6 us -> 16 us
    ppermute x4, starting transfers between devices: 7.12 us -> 5.79 us  [swap_x(): return lax.ppermute(values, ('gx', 'gz'), pairs)]
    pallas_call x7, Pallas kernels: 16.6 us -> 16 us  [call(): pl.pallas_call(kernel, out_shape=tuple((jax.ShapeDtypeStruct(shape, kind)...]
  transfers between devices with their start and end apart: 13 -> 13, of which waited for: 3 -> 3; matrix products, arithmetic and copies ran while one was open for 0% -> 3% of each run, Pallas kernels for 36% -> 38%
where the time goes in v7:
time: 30.8 us; the launch traced here: 30.6 us
  Pallas kernels  16 us (52%)
  starting transfers between devices  11.5 us (37%)
  waiting for transfers between devices  1.44 us (5%)
  local copies, waits for them, and re-layouts  0.86 us (3%)
  between operations  0.79 us (3%)
    pallas_call x7, Pallas kernels, call(): pl.pallas_call(kernel, out_shape=tuple((jax.ShapeDtypeStruct(shape, kind)...  16 us
    ppermute x4, starting transfers between devices, swap_x(): return lax.ppermute(values, ('gx', 'gz'), pairs)  5.79 us
    ppermute x9, starting transfers between devices, swap(): return lax.ppermute(values, axis, [(0, 1), (1, 0)])  5.69 us
    ppermute x9, waiting for transfers between devices, swap(): return lax.ppermute(values, axis, [(0, 1), (1, 0)])  1.13 us
    squeeze x1, local copies, waits for them, and re-layouts, body(): lax.dynamic_index_in_dim(cells, inner, 1, keepdims=False)  0.84 us
  transfers between devices with their start and end apart: 13, of which 3 were waited for; matrix products, arithmetic and copies ran while one was open for 3% of the time, Pallas kernels for 38%

profile of v7, /device:TPU:0, one launch (start us, length us, event | category | flops | bytes accessed | tf_op | source)
XLA Modules:
  0.0 30.6 jit_solution(16283960329366927021)
XLA Ops:
  0.6 0.5 %collective-permute-start.1 = (bf16[2,2,1,128,128]{4,3,2,1,0:T(8,128)(2,1)}, bf16[2,2,1,128,128]{4,3,2,1,0:T(8,128)(2,1)S(1)}, u32[]{:S(2)}, u32[]{:S(2)}) collective-permute-start(bf16[2,2,1,128,128]{4,3,2,1,0:T(8,128)(2,1)} %latent_any.1), channel_id=1, source_target_pairs={{0,1},{1,0},{2,3},{3,2},{4,5},{5,4},{6,7},{7,6},{8,9},{9,8},{10,11... | collective-permute-start | bytes 393224 | tf_op jit(solution)/shard_map/ppermute | solution.py:605
  1.1 0.8 %dynamic-slice_bitcast_fusion = bf16[2,128,128]{2,1,0:T(8,128)(2,1)S(1)} fusion(bf16[2,2,1,128,128]{4,3,2,1,0:T(8,128)(2,1)} %latent_any.1, s32[]{:T(128)S(6)} %select_n.11), kind=kLoop, calls=%fused_computation.2 | loop fusion | bytes 131076 | tf_op jit(solution)/shard_map/jit(dynamic_index_in_dim)/squeeze | solution.py:678
  2.0 2.5 %collective-permute-start = (bf16[2,128,128]{2,1,0:T(8,128)(2,1)S(1)}, bf16[2,128,128]{2,1,0:T(8,128)(2,1)S(1)}, u32[]{:S(2)}, u32[]{:S(2)}) collective-permute-start(bf16[2,128,128]{2,1,0:T(8,128)(2,1)S(1)} %dynamic-slice_bitcast_fusion), channel_id=1, source_target_pairs={{0,2},{2,0},{1,3},{3,1},{4,6},{6,4},{5,7},{7,5},{8,10},{10,8},{9,1... | collective-permute-start | bytes 196616 | tf_op jit(solution)/shard_map/ppermute | solution.py:605
  4.5 2.8 %ranks.1 = (bf16[11,128,128]{2,1,0:T(8,128)(2,1)S(1)}, bf16[3,128]{1,0:T(4,128)(2,1)S(1)}, bf16[48,128]{1,0:T(8,128)(2,1)S(1)}, bf16[2,128,128]{2,1,0:T(8,128)(2...) custom-call(s32[2,1,2]{2,1,0:T(1,128)} %bitcast.11, ...), custom_call_target="tpu_custom_call" | custom-call | flops 500000000 | tf_op jit(solution)/shard_map/ranks/pallas_call | solution.py:627
  7.3 0.3 collective-permute-start.2
  7.6 3.2 %collective-permute-start.3 = (bf16[3,128,128]{2,1,0:T(8,128)(2,1)S(1)}, bf16[3,128,128]{2,1,0:T(8,128)(2,1)S(1)}, u32[]{:S(2)}, u32[]{:S(2)}) collective-permute-start(bf16[3,128,128]{2,1,0:T(8,128)(2,1)S(1)} %pad_maximum_fusion.1), channel_id=1, source_target_pairs={{0,4},{1,5},{4,0},{5,1},{8,12},{9,13},{12,8},{13,9},{2,6},{3,7},{6... | collective-permute-start | bytes 294920 | tf_op jit(solution)/shard_map/ppermute | solution.py:623
  10.8 2.4 %prepare.1 = (bf16[4,128,256]{2,1,0:T(8,128)(2,1)S(1)}, f32[128,512]{1,0:T(8,128)S(1)}, f32[128,512]{1,0:T(8,128)S(1)}, f32[8,512]{1,0:T(8,128)S(1)}, f32[128,15...) custom-call(bf16[2,2,1,128,128]{4,3,2,1,0:T(8,128)(2,1)S(1)} %get-tu, ...), custom_call_target="tpu_custom_call" | custom-call | flops 500000000 | tf_op jit(solution)/shard_map/prepare/pallas_call | solution.py:627
  13.2 0.3 collective-permute-done.3.refs_2_
  13.5 0.3 collective-permute-start.5
  13.8 0.2 collective-permute-start.6
  14.0 0.8 %collective-permute-done.5.refs_4_ = bf16[3,128,128]{2,1,0:T(8,128)(2,1)S(1)} collective-permute-done((bf16[3,128,128]{2,1,0:T(8,128)(2,1)S(1)}, bf16[3,128,128]{2,1,0:T(8,128)(2,1)S(1)}, u32[]{:S(2)}, u32[]{:S(2)}) %collective-permute-start.5) | collective-permute-done | bytes 98336 | tf_op jit(solution)/shard_map/ppermute | solution.py:605
  14.8 0.3 collective-permute-done.6.refs_5_
  15.1 2.5 %movers.1 = (bf16[8,128,256]{2,1,0:T(8,128)(2,1)S(1)}, f32[16,128]{1,0:T(8,128)S(1)}) custom-call(bf16[2,128,128]{2,1,0:T(8,128)(2,1)S(1)} %collective-permute-done.refs_0_, bf16[3,128,128]{2,1,0:T(8,128)(2,1)S(1)} %collective-permute-done.2.refs_1_, bf16[3,128,128]{2,1,0:T(8,128)(2,1)S(1)} %collective-permute-done.3.refs_2_, ...), custom_call_target="tpu_custom_call" | custom-call | flops 3000000000 | tf_op jit(solution)/shard_map/movers/pallas_call | solution.py:627
  17.6 1.5 %collective-permute-start.7 = (f32[16,128]{1,0:T(8,128)S(1)}, f32[16,128]{1,0:T(8,128)S(1)}, u32[]{:S(2)}, u32[]{:S(2)}) collective-permute-start(f32[16,128]{1,0:T(8,128)S(1)} %get-tuple-element.117), channel_id=1, source_target_pairs={{0,2},{2,0},{1,3},{3,1},{4,6},{6,4},{5,7},{7,5},{8,10},{10,8},{9,1... | collective-permute-start | bytes 24584 | tf_op jit(solution)/shard_map/ppermute | solution.py:605
  19.1 2.8 %edges.2.first_ref = bf16[2,128,128]{2,1,0:T(8,128)(2,1)S(1)} custom-call(f32[2,2,1,128]{3,2,1,0:T(1,128)S(1)} %get-tuple-element.118.alive_ref, bf16[2,2,1,128,128]{4,3,2,1,0:T(8,128)(2,1)S(1)} %get-tuple-element.88.latent_ref, bf16[2,2,1,12,128,128]{5,4,3,2,1,0:T(8,128)(2,1)S(1)} %get-tuple-element.90.edge_ref, ...), custom_call_target="tpu_custom_call" | custom-call | flops 4000000000 | tf_op jit(solution)/shard_map/edges/pallas_call | solution.py:627
  21.9 0.1 collective-permute-start.10
  22.0 2.2 %collective-permute-start.9 = (f32[2,16,128]{2,1,0:T(8,128)S(1)}, f32[2,16,128]{2,1,0:T(8,128)S(1)}, u32[]{:S(2)}, u32[]{:S(2)}) collective-permute-start(f32[2,16,128]{2,1,0:T(8,128)S(1)} %pad_maximum_fusion.2.own_ref), channel_id=1, source_target_pairs={{0,4},{1,5},{4,0},{5,1},{8,12},{9,13},{12,8},{13,9},{2,6},{3,7},{6... | collective-permute-start | bytes 49160 | tf_op jit(solution)/shard_map/ppermute | solution.py:623
  24.3 2.8 %edges.3.second_ref = bf16[2,128,128]{2,1,0:T(8,128)(2,1)S(1)} custom-call(f32[2,2,1,128]{3,2,1,0:T(1,128)S(1)} %get-tuple-element.118.alive_ref, bf16[2,2,1,128,128]{4,3,2,1,0:T(8,128)(2,1)S(1)} %get-tuple-element.88.latent_ref, bf16[2,2,1,12,128,128]{5,4,3,2,1,0:T(8,128)(2,1)S(1)} %get-tuple-element.90.edge_ref, ...), custom_call_target="tpu_custom_call" | custom-call | flops 4000000000 | tf_op jit(solution)/shard_map/edges/pallas_call | solution.py:627
  27.1 0.1 collective-permute-start.8
  27.2 0.5 %collective-permute-start.11 = (f32[2,16,128]{2,1,0:T(8,128)S(1)}, f32[2,16,128]{2,1,0:T(8,128)S(1)}, u32[]{:S(2)}, u32[]{:S(2)}) collective-permute-start(f32[2,16,128]{2,1,0:T(8,128)S(1)} %collective-permute-done.9.even_ref), channel_id=1, source_target_pairs={{0,1},{1,0},{2,3},{3,2},{4,5},{5,4},{6,7},{7,6},{8,9},{9,8},{10,11... | collective-permute-start | bytes 49160 | tf_op jit(solution)/shard_map/ppermute | solution.py:605
  27.6 0.1 collective-permute-start.12
  27.7 1.0 %nodes.1.moved_ref = f32[16,512]{1,0:T(8,128)S(1)} custom-call(bf16[2,128,128]{2,1,0:T(8,128)(2,1)S(1)} %edges.2.first_ref, bf16[2,128,128]{2,1,0:T(8,128)(2,1)S(1)} %edges.3.second_ref, f32[128,512]{1,0:T(8,128)S(1)} %get-tuple-element.126.node_pre_ref, f32[128,512]{1,0:T(8,128)S(1)} %get-tuple-element.127.latent_t_ref, ...), custom_call_target="tpu_custom_call" | custom-call | flops 1000000000 | tf_op jit(solution)/shard_map/nodes/pallas_call | solution.py:627
  28.8 0.0 collective-permute-done.12.odd_zed
  28.8 1.8 %finish.1 = (bf16[2,2,1,128,128]{4,3,2,1,0:T(8,128)(2,1)}, f32[9,2,2,1,128]{4,3,2,1,0:T(1,128)}, bf16[1,1,1,208,128]{4,3,2,1,0:T(8,128)(2,1)}, f32[9,1,1,1,208]{4,3,2,1,0:T(1,128)}) custom-call(f32[16,512]{1,0:T(8,128)S(1)} %nodes.1.moved_ref, f32[2,16,128]{2,1,0:T(8,128)S(1)} %pad_maximum_fusion.2.own_ref, ...), custom_call_target="tpu_custom_call" | custom-call | flops 1000000000 | tf_op jit(solution)/shard_map/finish/pallas_call | solution.py:627
  (14 shorter events, 0.1 us)
Async XLA Ops:
  0.6 6.7 %collective-permute-start.1 = (bf16[2,2,1,128,128]{4,3,2,1,0:T(8,128)(2,1)}, bf16[2,2,1,128,128]{4,3,2,1,0:T(8,128)(2,1)S(1)}, u32[]{:S(2)}, u32[]{:S(2)}) collective-permute-start(bf16[2,2,1,128,128]{4,3,2,1,0:T(8,128)(2,1)} %latent_any.1), channel_id=1, source_target_pairs={{0,1},{1,0},{2,3},{3,2},{4,5},{5,4},{6,7},{7,6},{8,9},{9,8},{10,11... | collective-permute-start | bytes 393224 | tf_op jit(solution)/shard_map/ppermute | solution.py:605
  2.0 5.3 %collective-permute-start = (bf16[2,128,128]{2,1,0:T(8,128)(2,1)S(1)}, bf16[2,128,128]{2,1,0:T(8,128)(2,1)S(1)}, u32[]{:S(2)}, u32[]{:S(2)}) collective-permute-start(bf16[2,128,128]{2,1,0:T(8,128)(2,1)S(1)} %dynamic-slice_bitcast_fusion), channel_id=1, source_target_pairs={{0,2},{2,0},{1,3},{3,1},{4,6},{6,4},{5,7},{7,5},{8,10},{10,8},{9,1... | collective-permute-start | bytes 196616 | tf_op jit(solution)/shard_map/ppermute | solution.py:605
  7.3 5.9 %collective-permute-start.2 = (bf16[3,128,128]{2,1,0:T(8,128)(2,1)S(1)}, bf16[3,128,128]{2,1,0:T(8,128)(2,1)S(1)}, u32[]{:S(2)}, u32[]{:S(2)}) collective-permute-start(bf16[3,128,128]{2,1,0:T(8,128)(2,1)S(1)} %pad_maximum_fusion), channel_id=1, source_target_pairs={{0,1},{1,0},{4,8},{5,9},{8,4},{9,5},{12,13},{13,12},{2,3},{3,2},{6... | collective-permute-start | bytes 294920 | tf_op jit(solution)/shard_map/ppermute | solution.py:623
  7.6 5.9 %collective-permute-start.3 = (bf16[3,128,128]{2,1,0:T(8,128)(2,1)S(1)}, bf16[3,128,128]{2,1,0:T(8,128)(2,1)S(1)}, u32[]{:S(2)}, u32[]{:S(2)}) collective-permute-start(bf16[3,128,128]{2,1,0:T(8,128)(2,1)S(1)} %pad_maximum_fusion.1), channel_id=1, source_target_pairs={{0,4},{1,5},{4,0},{5,1},{8,12},{9,13},{12,8},{13,9},{2,6},{3,7},{6... | collective-permute-start | bytes 294920 | tf_op jit(solution)/shard_map/ppermute | solution.py:623
  10.8 2.4 %collective-permute-start.4 = (bf16[2,128,128]{2,1,0:T(8,128)(2,1)S(1)}, bf16[2,128,128]{2,1,0:T(8,128)(2,1)S(1)}, u32[]{:S(2)}, u32[]{:S(2)}) collective-permute-start(bf16[2,128,128]{2,1,0:T(8,128)(2,1)S(1)} %collective-permute-done.refs_0_), channel_id=1, source_target_pairs={{0,1},{1,0},{2,3},{3,2},{4,5},{5,4},{6,7},{7,6},{8,9},{9,8},{10,11... | collective-permute-start | bytes 196616 | tf_op jit(solution)/shard_map/ppermute | solution.py:605
  13.5 1.3 %collective-permute-start.5 = (bf16[3,128,128]{2,1,0:T(8,128)(2,1)S(1)}, bf16[3,128,128]{2,1,0:T(8,128)(2,1)S(1)}, u32[]{:S(2)}, u32[]{:S(2)}) collective-permute-start(bf16[3,128,128]{2,1,0:T(8,128)(2,1)S(1)} %collective-permute-done.2.refs_1_), channel_id=1, source_target_pairs={{0,1},{1,0},{2,3},{3,2},{4,5},{5,4},{6,7},{7,6},{8,9},{9,8},{10,11... | collective-permute-start | bytes 294920 | tf_op jit(solution)/shard_map/ppermute | solution.py:605
  13.8 1.3 %collective-permute-start.6 = (bf16[3,128,128]{2,1,0:T(8,128)(2,1)S(1)}, bf16[3,128,128]{2,1,0:T(8,128)(2,1)S(1)}, u32[]{:S(2)}, u32[]{:S(2)}) collective-permute-start(bf16[3,128,128]{2,1,0:T(8,128)(2,1)S(1)} %collective-permute-done.3.refs_2_), channel_id=1, source_target_pairs={{0,1},{1,0},{2,3},{3,2},{4,5},{5,4},{6,7},{7,6},{8,9},{9,8},{10,11... | collective-permute-start | bytes 294920 | tf_op jit(solution)/shard_map/ppermute | solution.py:605
  17.6 4.3 %collective-permute-start.7 = (f32[16,128]{1,0:T(8,128)S(1)}, f32[16,128]{1,0:T(8,128)S(1)}, u32[]{:S(2)}, u32[]{:S(2)}) collective-permute-start(f32[16,128]{1,0:T(8,128)S(1)} %get-tuple-element.117), channel_id=1, source_target_pairs={{0,2},{2,0},{1,3},{3,1},{4,6},{6,4},{5,7},{7,5},{8,10},{10,8},{9,1... | collective-permute-start | bytes 24584 | tf_op jit(solution)/shard_map/ppermute | solution.py:605
  21.9 5.2 %collective-permute-start.10 = (f32[2,16,128]{2,1,0:T(8,128)S(1)}, f32[2,16,128]{2,1,0:T(8,128)S(1)}, u32[]{:S(2)}, u32[]{:S(2)}) collective-permute-start(f32[2,16,128]{2,1,0:T(8,128)S(1)} %pad_maximum_fusion.2.own_ref), channel_id=1, source_target_pairs={{0,1},{1,0},{4,8},{5,9},{8,4},{9,5},{12,13},{13,12},{2,3},{3,2},{6... | collective-permute-start | bytes 49160 | tf_op jit(solution)/shard_map/ppermute | solution.py:623
  22.0 5.1 %collective-permute-start.9 = (f32[2,16,128]{2,1,0:T(8,128)S(1)}, f32[2,16,128]{2,1,0:T(8,128)S(1)}, u32[]{:S(2)}, u32[]{:S(2)}) collective-permute-start(f32[2,16,128]{2,1,0:T(8,128)S(1)} %pad_maximum_fusion.2.own_ref), channel_id=1, source_target_pairs={{0,4},{1,5},{4,0},{5,1},{8,12},{9,13},{12,8},{13,9},{2,6},{3,7},{6... | collective-permute-start | bytes 49160 | tf_op jit(solution)/shard_map/ppermute | solution.py:623
  27.1 1.7 %collective-permute-start.8 = (f32[2,16,128]{2,1,0:T(8,128)S(1)}, f32[2,16,128]{2,1,0:T(8,128)S(1)}, u32[]{:S(2)}, u32[]{:S(2)}) collective-permute-start(f32[2,16,128]{2,1,0:T(8,128)S(1)} %pad_maximum_fusion.2.own_ref), channel_id=1, source_target_pairs={{0,1},{1,0},{2,3},{3,2},{4,5},{5,4},{6,7},{7,6},{8,9},{9,8},{10,11... | collective-permute-start | bytes 49160 | tf_op jit(solution)/shard_map/ppermute | solution.py:605
  27.2 1.6 %collective-permute-start.11 = (f32[2,16,128]{2,1,0:T(8,128)S(1)}, f32[2,16,128]{2,1,0:T(8,128)S(1)}, u32[]{:S(2)}, u32[]{:S(2)}) collective-permute-start(f32[2,16,128]{2,1,0:T(8,128)S(1)} %collective-permute-done.9.even_ref), channel_id=1, source_target_pairs={{0,1},{1,0},{2,3},{3,2},{4,5},{5,4},{6,7},{7,6},{8,9},{9,8},{10,11... | collective-permute-start | bytes 49160 | tf_op jit(solution)/shard_map/ppermute | solution.py:605
  27.6 1.2 %collective-permute-start.12 = (f32[2,16,128]{2,1,0:T(8,128)S(1)}, f32[2,16,128]{2,1,0:T(8,128)S(1)}, u32[]{:S(2)}, u32[]{:S(2)}) collective-permute-start(f32[2,16,128]{2,1,0:T(8,128)S(1)} %collective-permute-done.10.odd_ref), channel_id=1, source_target_pairs={{0,1},{1,0},{2,3},{3,2},{4,5},{5,4},{6,7},{7,6},{8,9},{9,8},{10,11... | collective-permute-start | bytes 49160 | tf_op jit(solution)/shard_map/ppermute | solution.py:605

commit v8 on v7

--- a/solution.py
+++ b/solution.py
@@ -181,6 +181,22 @@
     return jnp.concatenate([position + new_velocity, new_velocity, velocity], axis=0)
 
 
+def cut_kernel(fold_y, latent_any, latent_ref, edge_ref, inner_ref, sems):
+    end = 1 - lax.axis_index("gz")
+    inner = 1 - lax.axis_index("gy") if fold_y else 0
+    copies = fetch(
+        [
+            (latent_any, latent_ref),
+            (latent_any.at[end], edge_ref),
+            (latent_any.at[0, inner], inner_ref.at[0]),
+            (latent_any.at[1, inner], inner_ref.at[1]),
+        ],
+        sems,
+    )
+    for copy in copies:
+        copy.wait()
+
+
 def ranks_kernel(
     sizes,
     fill_ref,
@@ -192,11 +208,11 @@
     decoder_out_any,
     encoder_in_any,
     encoder_w_any,
-    latent_any,
     neighbours_any,
     positions_any,
     velocity_any,
     edge_any,
+    _,
     weights_ref,
     decoder_out_ref,
     inward_ref,
@@ -204,13 +220,10 @@
     placer_ref,
     masks_ref,
     alive_ref,
-    latent_ref,
     neighbours_ref,
     positions_ref,
     velocity_ref,
     edge_ref,
-    first_end_ref,
-    second_end_ref,
     spread_ref,
     owners_ref,
     edge_w_ref,
@@ -232,7 +245,6 @@
             (decoder_out_any, decoder_out_ref),
             (encoder_in_any, encoder_in_ref),
             (encoder_w_any, encoder_w_ref),
-            (latent_any, latent_ref),
             (neighbours_any, neighbours_ref),
             (positions_any, positions_ref),
             (velocity_any, velocity_ref),
@@ -323,10 +335,6 @@
     inward = jnp.concatenate([encoder_in_ref[...].astype(F32), jnp.zeros((4, width), F32)], axis=0)
     inward = inward.astype(BF16)
     inward_ref[...] = jnp.concatenate([inward, inward, inward], axis=0)
-    parity = index_x & 1
-    for b in range(2):
-        first_end_ref[b] = latent_ref[1 - parity, b, 0]
-        second_end_ref[b] = latent_ref[parity, b, 0]
 
 
 def prepare_kernel(
@@ -415,9 +423,8 @@
 ):
     fold_y = sizes[1] == 2
     side_refs, refs = refs[:side_count], refs[side_count:]
-    odd_ref, even_ref, refs = refs[0], refs[1], refs[2:]
     side_zeds, refs = refs[:side_count], refs[side_count:]
-    odd_zed, even_zed, refs = refs[0], refs[1], refs[2:]
+    mine_ref, other_ref, refs = refs[0], refs[1], refs[2:]
     (
         weights_ref,
         decoder_out_ref,
@@ -433,7 +440,7 @@
     ) = refs
     window = Window(fold_y, None, far_ref)
     row_count = window.row_count
-    parity = lax.axis_index("gx") & 1
+    core = lax.axis_index("gz")
     far_t = weights_ref[FAR]
 
     def far(at, here, beside):
@@ -441,8 +448,8 @@
         far_ref[at] = dot_nt(far_t, pair).astype(BF16)
 
     for row in range(row_count):
-        far((1 - parity) * row_count + row, even_ref[row], even_zed[row])
-        far(parity * row_count + row, odd_ref[row], odd_zed[row])
+        far((1 - core) * row_count + row, mine_ref[1, row], mine_ref[0, row])
+        far(core * row_count + row, other_ref[0, row], other_ref[1, row])
     for side, row in enumerate(window.outer_rows):
         for ex in (1, 2):
             far(window.side(ex, row), side_refs[side][ex - 1], side_zeds[side][ex - 1])
@@ -623,6 +630,21 @@
     return lax.ppermute(values, ("gx", "gz"), pairs)
 
 
+def swap_chips(values, cross):
+    count_x, count_y, count_z = (lax.axis_size(axis) for axis in ("gx", "gy", "gz"))
+    pairs = []
+    for x in range(count_x):
+        for y in range(count_y):
+            for z in range(count_z):
+                to_x = x + 1 - 2 * z
+                if 0 <= to_x < count_x:
+                    to = (to_x, y ^ 1 if cross else y, 1 - z)
+                else:
+                    to = (x, y ^ 1, z)
+                pairs.append(((x * count_y + y) * count_z + z, (to[0] * count_y + to[1]) * count_z + to[2]))
+    return lax.ppermute(values, ("gx", "gy", "gz"), pairs)
+
+
 def call(kernel, name, in_specs, outs, scratch, operands, flops):
     return pl.pallas_call(
         kernel,
@@ -671,15 +693,38 @@
     fill = jnp.transpose(fill, (0, 2, 1))
     neighbours = neighbours.reshape(2, 2, neighbour_count, 1, slots)
 
-    parity = lax.axis_index("gx") & 1
-    cells = node_latent[:, :, 0]
+    own_zed = swap(node_latent, "gz")
+    latent, end, inner = call(
+        functools.partial(cut_kernel, fold_y),
+        "cut",
+        [ANY],
+        [
+            (node_latent.shape, BF16),
+            (node_latent.shape[1:], BF16),
+            ((2, 1, slots, width), BF16),
+        ],
+        [pltpu.SemaphoreType.DMA((4,))],
+        (in_hbm(node_latent),),
+        1_000_000,
+    )
+    core = lax.axis_index("gz")
     if fold_y:
-        inner = 1 - lax.axis_index("gy")
-        sides = [swap(lax.dynamic_index_in_dim(cells, inner, 1, keepdims=False), "gy")]
+        sides = [swap(inner[:, 0], "gy")]
+        row = 1 - lax.axis_index("gy")
+        both = jnp.stack([end[:, 0], lax.dynamic_index_in_dim(own_zed[:, :, 0], 1 - core, 0, False)])
+        corner = lax.dynamic_slice_in_dim(both, row, 1, axis=1)
+        mine = [swap_chips(both, False), swap_chips(corner, True)]
     else:
-        sides = [shift(cells[:, 1], "gy", 0), shift(cells[:, 0], "gy", 1)]
-
-    fetched = (node_latent, neighbours, positions, velocity, edge_latent)
+        sides = [shift(latent[:, 1, 0], "gy", 0), shift(latent[:, 0, 0], "gy", 1)]
+        side_zeds = [swap(part, "gz") for part in sides]
+        layers = []
+        for middle, outer in ((latent, sides), (own_zed, side_zeds)):
+            parts = [outer[0][:, None], middle[:, :, 0], outer[1][:, None]]
+            parts = [lax.dynamic_index_in_dim(part, 1 - core, 0, False) for part in parts]
+            layers.append(jnp.concatenate(parts, axis=0))
+        mine = [swap_chips(jnp.stack(layers), False)]
+
+    fetched = (neighbours, positions, velocity, edge_latent)
     ranked = call(
         functools.partial(ranks_kernel, sizes),
         "ranks",
@@ -693,8 +738,6 @@
             ((8, particles), F32),
             ((2, 2, 1, slots), F32),
             *((array.shape, array.dtype) for array in fetched),
-            ((2, slots, width), BF16),
-            ((2, slots, width), BF16),
             ((movers, 26 * CAP), BF16),
         ],
         [
@@ -704,7 +747,7 @@
             like(node_weights),
             like(decoder_weights),
             like(encoder_in),
-            pltpu.SemaphoreType.DMA((13,)),
+            pltpu.SemaphoreType.DMA((12,)),
         ],
         [
             in_hbm(array)
@@ -720,21 +763,20 @@
                 encoder_weights,
                 *fetched,
             )
-        ],
+        ]
+        + [own_zed],
         500_000_000,
     )
-    own_zed = swap(node_latent, "gz")
-    sides, own_zed, ranked = lax.optimization_barrier((sides, own_zed, ranked))
+    sides, mine, ranked = lax.optimization_barrier((sides, mine, ranked))
     weights, decoder_out, inward, encoder_weights, placer, masks, alive, *ranked = ranked
-    latent, neighbours, positions, velocity, edge_latent, *own_ends, spread = ranked
-
-    def layer(a, own):
-        outer = [lax.dynamic_index_in_dim(side, a, 0) for side in sides]
-        parts = [own, outer[0]] if fold_y else [outer[0], own, outer[1]]
-        return jnp.concatenate(parts, axis=0)
-
-    ends = [swap_x(layer(parity, own_ends[1]), 1), swap_x(layer(1 - parity, own_ends[0]), 0)]
-    zeds = [swap(part, "gz") for part in sides]
+    neighbours, positions, velocity, edge_latent, spread = ranked
+
+    mine = jnp.concatenate(mine, axis=1)
+    if fold_y:
+        packed = jnp.concatenate([mine.reshape(-1, slots, width), sides[0]], axis=0)
+    else:
+        packed = mine.reshape(-1, slots, width)
+    packed = swap(packed, "gz")
     prepared = call(
         functools.partial(prepare_kernel, sizes),
         "prepare",
@@ -755,7 +797,11 @@
         (latent, own_zed, edge_latent, positions, velocity, neighbours, weights, placer, masks),
         500_000_000,
     )
-    ends, zeds, prepared = lax.optimization_barrier((ends, zeds, prepared))
+    packed, prepared = lax.optimization_barrier((packed, prepared))
+    cells = mine.shape[0] * mine.shape[1]
+    if fold_y:
+        side_zeds = [packed[cells:]]
+    halo = [*sides, *side_zeds, mine, packed[:cells].reshape(mine.shape)]
     (
         far_own,
         latent_t,
@@ -768,8 +814,6 @@
         mover_latent,
         mover_state,
     ) = prepared
-    halo = [*sides, *ends, *zeds, *(swap(part, "gz") for part in ends)]
-
     far_rest, bucket = call(
         functools.partial(movers_kernel, sizes, len(sides)),
         "movers",

time: 30.8 us -> 29.5 us (0.958)
  starting transfers between devices: 11.5 us -> 9.87 us
  Pallas kernels: 16 us -> 16.9 us
  local copies, waits for them, and re-layouts: 0.86 us -> 0.05 us
    ppermute x4 -> x2, starting transfers between devices: 5.79 us -> 3.31 us  [swap_x(): return lax.ppermute(values, ('gx', 'gz'), pairs)]
    ppermute x0 -> x2, starting transfers between devices: none -> 1.82 us  [swap_chips(): return lax.ppermute(values, ('gx', 'gy', 'gz'), pairs)]
    ppermute x0 -> x2, waiting for transfers between devices: none -> 1.61 us  [swap_chips(): return lax.ppermute(values, ('gx', 'gy', 'gz'), pairs)]
    ppermute x9 -> x7, waiting for transfers between devices: 1.13 us -> 0.06 us  [swap(): return lax.ppermute(values, axis, [(0, 1), (1, 0)])]
    ppermute x9 -> x7, starting transfers between devices: 5.69 us -> 4.75 us  [swap(): return lax.ppermute(values, axis, [(0, 1), (1, 0)])]
    pallas_call x7 -> x8, Pallas kernels: 16 us -> 16.9 us  [call(): pl.pallas_call(kernel, out_shape=tuple((jax.ShapeDtypeStruct(shape, kind)...]
    squeeze x1 -> x0, local copies, waits for them, and re-layouts: 0.84 us -> none  [body(): lax.dynamic_index_in_dim(cells, inner, 1, keepdims=False)]
  transfers between devices with their start and end apart: 13 -> 11, of which waited for: 3 -> 1; matrix products, arithmetic and copies ran while one was open for 3% -> 0% of each run, Pallas kernels for 38% -> 43%
where the time goes in v8:
time: 29.5 us; the launch traced here: 29.4 us
  Pallas kernels  16.9 us (57%)
  starting transfers between devices  9.87 us (33%)
  waiting for transfers between devices  1.67 us (6%)
  between operations  0.81 us (3%)
    pallas_call x8, Pallas kernels, call(): pl.pallas_call(kernel, out_shape=tuple((jax.ShapeDtypeStruct(shape, kind)...  16.9 us
    ppermute x7, starting transfers between devices, swap(): return lax.ppermute(values, axis, [(0, 1), (1, 0)])  4.75 us
    ppermute x2, starting transfers between devices, swap_x(): return lax.ppermute(values, ('gx', 'gz'), pairs)  3.31 us
    ppermute x2, starting transfers between devices, swap_chips(): return lax.ppermute(values, ('gx', 'gy', 'gz'), pairs)  1.82 us
    ppermute x2, waiting for transfers between devices, swap_chips(): return lax.ppermute(values, ('gx', 'gy', 'gz'), pairs)  1.61 us
  transfers between devices with their start and end apart: 11, of which 1 were waited for; matrix products, arithmetic and copies ran while one was open for 0% of the time, Pallas kernels for 43%

profile of v8, /device:TPU:0, one launch (start us, length us, event | category | flops | bytes accessed | tf_op | source)
XLA Modules:
  0.0 29.4 jit_solution(496179185177745566)
XLA Ops:
  0.6 0.5 %collective-permute-start.1 = (bf16[2,2,1,128,128]{4,3,2,1,0:T(8,128)(2,1)}, bf16[2,2,1,128,128]{4,3,2,1,0:T(8,128)(2,1)S(1)}, u32[]{:S(2)}, u32[]{:S(2)}) collective-permute-start(bf16[2,2,1,128,128]{4,3,2,1,0:T(8,128)(2,1)} %latent_any.1), channel_id=1, source_target_pairs={{0,1},{1,0},{2,3},{3,2},{4,5},{5,4},{6,7},{7,6},{8,9},{9,8},{10,11... | collective-permute-start | bytes 393224 | tf_op jit(solution)/shard_map/ppermute | solution.py:612
  1.1 1.0 %cut.1 = (bf16[2,2,1,128,128]{4,3,2,1,0:T(8,128)(2,1)S(1)}, bf16[2,1,128,128]{3,2,1,0:T(8,128)(2,1)S(1)}, bf16[2,1,128,128]{3,2,1,0:T(8,128)(2,1)S(1)}) custom-call(bf16[2,2,1,128,128]{4,3,2,1,0:T(8,128)(2,1)} %latent_any.1), custom_call_target="tpu_custom_call" | custom-call | flops 1000000 | tf_op jit(solution)/shard_map/cut/pallas_call | solution.py:649
  2.1 2.6 %collective-permute-start = (bf16[2,128,128]{2,1,0:T(8,128)(2,1)S(1)}, bf16[2,128,128]{2,1,0:T(8,128)(2,1)S(1)}, u32[]{:S(2)}, u32[]{:S(2)}) collective-permute-start(bf16[2,128,128]{2,1,0:T(8,128)(2,1)S(1)} %bitcast.17), channel_id=1, source_target_pairs={{0,2},{2,0},{1,3},{3,1},{4,6},{6,4},{5,7},{7,5},{8,10},{10,8},{9,1... | collective-permute-start | bytes 196616 | tf_op jit(solution)/shard_map/ppermute | solution.py:612
  4.7 0.0 collective-permute-done.1._.own_zed
  4.7 1.5 %collective-permute-start.2 = (bf16[2,2,128,128]{3,2,1,0:T(8,128)(2,1)S(1)}, bf16[2,2,128,128]{3,2,1,0:T(8,128)(2,1)S(1)}, u32[]{:S(2)}, u32[]{:S(2)}) collective-permute-start(bf16[2,2,128,128]{3,2,1,0:T(8,128)(2,1)S(1)} %pad_maximum_fusion.1), channel_id=1, source_target_pairs={{0,5},{1,3},{2,7},{3,1},{4,9},{5,0},{6,11},{7,2},{8,13},{9,4},{10,... | collective-permute-start | bytes 393224 | tf_op jit(solution)/shard_map/ppermute | solution.py:645
  6.2 0.4 %collective-permute-start.3 = (bf16[2,1,128,128]{3,2,1,0:T(8,128)(2,1)S(1)}, bf16[2,1,128,128]{3,2,1,0:T(8,128)(2,1)S(1)}, u32[]{:S(2)}, u32[]{:S(2)}) collective-permute-start(bf16[2,1,128,128]{3,2,1,0:T(8,128)(2,1)S(1)} %fusion), channel_id=1, source_target_pairs={{0,7},{1,3},{2,5},{3,1},{4,11},{5,2},{6,9},{7,0},{8,15},{9,6},{10,... | collective-permute-start | bytes 196616 | tf_op jit(solution)/shard_map/ppermute | solution.py:645
  6.5 2.7 %ranks.1 = (bf16[11,128,128]{2,1,0:T(8,128)(2,1)S(1)}, bf16[3,128]{1,0:T(4,128)(2,1)S(1)}, bf16[48,128]{1,0:T(8,128)(2,1)S(1)}, bf16[2,128,128]{2,1,0:T(8,128)(2...) custom-call(s32[2,1,2]{2,1,0:T(1,128)} %bitcast.20, ...), custom_call_target="tpu_custom_call" | custom-call | flops 500000000 | tf_op jit(solution)/shard_map/ranks/pallas_call | solution.py:649
  9.2 1.6 %collective-permute-done.3 = bf16[2,1,128,128]{3,2,1,0:T(8,128)(2,1)S(1)} collective-permute-done((bf16[2,1,128,128]{3,2,1,0:T(8,128)(2,1)S(1)}, bf16[2,1,128,128]{3,2,1,0:T(8,128)(2,1)S(1)}, u32[]{:S(2)}, u32[]{:S(2)}) %collective-permute-start.3) | collective-permute-done | bytes 65568 | tf_op jit(solution)/shard_map/ppermute | solution.py:645
  10.9 0.1 collective-permute-start.4
  11.0 2.4 %prepare.1 = (bf16[4,128,256]{2,1,0:T(8,128)(2,1)S(1)}, f32[128,512]{1,0:T(8,128)S(1)}, f32[128,512]{1,0:T(8,128)S(1)}, f32[8,512]{1,0:T(8,128)S(1)}, f32[128,15...) custom-call(bf16[2,2,1,128,128]{4,3,2,1,0:T(8,128)(2,1)S(1)} %get-tu, ...), custom_call_target="tpu_custom_call" | custom-call | flops 500000000 | tf_op jit(solution)/shard_map/prepare/pallas_call | solution.py:649
  13.4 2.5 %movers.1 = (bf16[8,128,256]{2,1,0:T(8,128)(2,1)S(1)}, f32[16,128]{1,0:T(8,128)S(1)}) custom-call(bf16[2,128,128]{2,1,0:T(8,128)(2,1)S(1)} %collective-permute-done.refs_0_, bf16[2,128,128]{2,1,0:T(8,128)(2,1)S(1)} %slice.6.refs_1_, bf16[2,3,128,128]{3,2,1,0:T(8,128)(2,1)S(1)} %constant_dynamic-update-slice_fusion.refs_2_, ...), custom_call_target="tpu_custom_call" | custom-call | flops 3000000000 | tf_op jit(solution)/shard_map/movers/pallas_call | solution.py:649
  15.9 0.9 %collective-permute-start.5 = (f32[16,128]{1,0:T(8,128)S(1)}, f32[16,128]{1,0:T(8,128)S(1)}, u32[]{:S(2)}, u32[]{:S(2)}) collective-permute-start(f32[16,128]{1,0:T(8,128)S(1)} %get-tuple-element.109), channel_id=1, source_target_pairs={{0,2},{2,0},{1,3},{3,1},{4,6},{6,4},{5,7},{7,5},{8,10},{10,8},{9,1... | collective-permute-start | bytes 24584 | tf_op jit(solution)/shard_map/ppermute | solution.py:612
  16.9 2.8 %edges.2.first_ref = bf16[2,128,128]{2,1,0:T(8,128)(2,1)S(1)} custom-call(f32[2,2,1,128]{3,2,1,0:T(1,128)S(1)} %get-tuple-element.110.alive_ref, bf16[2,2,1,128,128]{4,3,2,1,0:T(8,128)(2,1)S(1)} %get-tuple-element.83.latent_ref, bf16[2,2,1,12,128,128]{5,4,3,2,1,0:T(8,128)(2,1)S(1)} %get-tuple-element.84.edge_ref, ...), custom_call_target="tpu_custom_call" | custom-call | flops 4000000000 | tf_op jit(solution)/shard_map/edges/pallas_call | solution.py:649
  19.7 0.1 collective-permute-start.8
  19.8 3.2 %collective-permute-start.7 = (f32[2,16,128]{2,1,0:T(8,128)S(1)}, f32[2,16,128]{2,1,0:T(8,128)S(1)}, u32[]{:S(2)}, u32[]{:S(2)}) collective-permute-start(f32[2,16,128]{2,1,0:T(8,128)S(1)} %pad_maximum_fusion.2.own_ref), channel_id=1, source_target_pairs={{0,4},{1,5},{4,0},{5,1},{8,12},{9,13},{12,8},{13,9},{2,6},{3,7},{6... | collective-permute-start | bytes 49160 | tf_op jit(solution)/shard_map/ppermute | solution.py:630
  23.0 2.8 %edges.3.second_ref = bf16[2,128,128]{2,1,0:T(8,128)(2,1)S(1)} custom-call(f32[2,2,1,128]{3,2,1,0:T(1,128)S(1)} %get-tuple-element.110.alive_ref, bf16[2,2,1,128,128]{4,3,2,1,0:T(8,128)(2,1)S(1)} %get-tuple-element.83.latent_ref, bf16[2,2,1,12,128,128]{5,4,3,2,1,0:T(8,128)(2,1)S(1)} %get-tuple-element.84.edge_ref, ...), custom_call_target="tpu_custom_call" | custom-call | flops 4000000000 | tf_op jit(solution)/shard_map/edges/pallas_call | solution.py:649
  25.8 0.1 collective-permute-start.6
  25.9 0.0 collective-permute-done.7.even_ref
  25.9 0.5 %collective-permute-start.9 = (f32[2,16,128]{2,1,0:T(8,128)S(1)}, f32[2,16,128]{2,1,0:T(8,128)S(1)}, u32[]{:S(2)}, u32[]{:S(2)}) collective-permute-start(f32[2,16,128]{2,1,0:T(8,128)S(1)} %collective-permute-done.7.even_ref), channel_id=1, source_target_pairs={{0,1},{1,0},{2,3},{3,2},{4,5},{5,4},{6,7},{7,6},{8,9},{9,8},{10,11... | collective-permute-start | bytes 49160 | tf_op jit(solution)/shard_map/ppermute | solution.py:612
  26.4 0.1 collective-permute-start.10
  26.5 1.0 %nodes.1.moved_ref = f32[16,512]{1,0:T(8,128)S(1)} custom-call(bf16[2,128,128]{2,1,0:T(8,128)(2,1)S(1)} %edges.2.first_ref, bf16[2,128,128]{2,1,0:T(8,128)(2,1)S(1)} %edges.3.second_ref, f32[128,512]{1,0:T(8,128)S(1)} %get-tuple-element.118.node_pre_ref, f32[128,512]{1,0:T(8,128)S(1)} %get-tuple-element.119.latent_t_ref, ...), custom_call_target="tpu_custom_call" | custom-call | flops 1000000000 | tf_op jit(solution)/shard_map/nodes/pallas_call | solution.py:649
  27.5 0.0 collective-permute-done.6.own_zed
  27.5 0.0 collective-permute-done.10.odd_zed
  27.6 1.8 %finish.1 = (bf16[2,2,1,128,128]{4,3,2,1,0:T(8,128)(2,1)}, f32[9,2,2,1,128]{4,3,2,1,0:T(1,128)}, bf16[1,1,1,208,128]{4,3,2,1,0:T(8,128)(2,1)}, f32[9,1,1,1,208]{4,3,2,1,0:T(1,128)}) custom-call(f32[16,512]{1,0:T(8,128)S(1)} %nodes.1.moved_ref, f32[2,16,128]{2,1,0:T(8,128)S(1)} %pad_maximum_fusion.2.own_ref, ...), custom_call_target="tpu_custom_call" | custom-call | flops 1000000000 | tf_op jit(solution)/shard_map/finish/pallas_call | solution.py:649
  (15 shorter events, 0.1 us)
Async XLA Ops:
  0.6 4.0 %collective-permute-start.1 = (bf16[2,2,1,128,128]{4,3,2,1,0:T(8,128)(2,1)}, bf16[2,2,1,128,128]{4,3,2,1,0:T(8,128)(2,1)S(1)}, u32[]{:S(2)}, u32[]{:S(2)}) collective-permute-start(bf16[2,2,1,128,128]{4,3,2,1,0:T(8,128)(2,1)} %latent_any.1), channel_id=1, source_target_pairs={{0,1},{1,0},{2,3},{3,2},{4,5},{5,4},{6,7},{7,6},{8,9},{9,8},{10,11... | collective-permute-start | bytes 393224 | tf_op jit(solution)/shard_map/ppermute | solution.py:612
  2.1 7.1 %collective-permute-start = (bf16[2,128,128]{2,1,0:T(8,128)(2,1)S(1)}, bf16[2,128,128]{2,1,0:T(8,128)(2,1)S(1)}, u32[]{:S(2)}, u32[]{:S(2)}) collective-permute-start(bf16[2,128,128]{2,1,0:T(8,128)(2,1)S(1)} %bitcast.17), channel_id=1, source_target_pairs={{0,2},{2,0},{1,3},{3,1},{4,6},{6,4},{5,7},{7,5},{8,10},{10,8},{9,1... | collective-permute-start | bytes 196616 | tf_op jit(solution)/shard_map/ppermute | solution.py:612
  4.7 6.1 %collective-permute-start.2 = (bf16[2,2,128,128]{3,2,1,0:T(8,128)(2,1)S(1)}, bf16[2,2,128,128]{3,2,1,0:T(8,128)(2,1)S(1)}, u32[]{:S(2)}, u32[]{:S(2)}) collective-permute-start(bf16[2,2,128,128]{3,2,1,0:T(8,128)(2,1)S(1)} %pad_maximum_fusion.1), channel_id=1, source_target_pairs={{0,5},{1,3},{2,7},{3,1},{4,9},{5,0},{6,11},{7,2},{8,13},{9,4},{10,... | collective-permute-start | bytes 393224 | tf_op jit(solution)/shard_map/ppermute | solution.py:645
  6.2 4.7 %collective-permute-start.3 = (bf16[2,1,128,128]{3,2,1,0:T(8,128)(2,1)S(1)}, bf16[2,1,128,128]{3,2,1,0:T(8,128)(2,1)S(1)}, u32[]{:S(2)}, u32[]{:S(2)}) collective-permute-start(bf16[2,1,128,128]{3,2,1,0:T(8,128)(2,1)S(1)} %fusion), channel_id=1, source_target_pairs={{0,7},{1,3},{2,5},{3,1},{4,11},{5,2},{6,9},{7,0},{8,15},{9,6},{10,... | collective-permute-start | bytes 196616 | tf_op jit(solution)/shard_map/ppermute | solution.py:645
  10.9 2.5 %collective-permute-start.4 = (bf16[8,128,128]{2,1,0:T(8,128)(2,1)S(1)}, bf16[8,128,128]{2,1,0:T(8,128)(2,1)S(1)}, u32[]{:S(2)}, u32[]{:S(2)}) collective-permute-start(bf16[8,128,128]{2,1,0:T(8,128)(2,1)S(1)} %pad_maximum_fusion), channel_id=1, source_target_pairs={{0,1},{1,0},{2,3},{3,2},{4,5},{5,4},{6,7},{7,6},{8,9},{9,8},{10,11... | collective-permute-start | bytes 786440 | tf_op jit(solution)/shard_map/ppermute | solution.py:612
  15.9 3.8 %collective-permute-start.5 = (f32[16,128]{1,0:T(8,128)S(1)}, f32[16,128]{1,0:T(8,128)S(1)}, u32[]{:S(2)}, u32[]{:S(2)}) collective-permute-start(f32[16,128]{1,0:T(8,128)S(1)} %get-tuple-element.109), channel_id=1, source_target_pairs={{0,2},{2,0},{1,3},{3,1},{4,6},{6,4},{5,7},{7,5},{8,10},{10,8},{9,1... | collective-permute-start | bytes 24584 | tf_op jit(solution)/shard_map/ppermute | solution.py:612
  19.7 6.2 %collective-permute-start.8 = (f32[2,16,128]{2,1,0:T(8,128)S(1)}, f32[2,16,128]{2,1,0:T(8,128)S(1)}, u32[]{:S(2)}, u32[]{:S(2)}) collective-permute-start(f32[2,16,128]{2,1,0:T(8,128)S(1)} %pad_maximum_fusion.2.own_ref), channel_id=1, source_target_pairs={{0,1},{1,0},{4,8},{5,9},{8,4},{9,5},{12,13},{13,12},{2,3},{3,2},{6... | collective-permute-start | bytes 49160 | tf_op jit(solution)/shard_map/ppermute | solution.py:630
  19.8 6.1 %collective-permute-start.7 = (f32[2,16,128]{2,1,0:T(8,128)S(1)}, f32[2,16,128]{2,1,0:T(8,128)S(1)}, u32[]{:S(2)}, u32[]{:S(2)}) collective-permute-start(f32[2,16,128]{2,1,0:T(8,128)S(1)} %pad_maximum_fusion.2.own_ref), channel_id=1, source_target_pairs={{0,4},{1,5},{4,0},{5,1},{8,12},{9,13},{12,8},{13,9},{2,6},{3,7},{6... | collective-permute-start | bytes 49160 | tf_op jit(solution)/shard_map/ppermute | solution.py:630
  25.8 1.7 %collective-permute-start.6 = (f32[2,16,128]{2,1,0:T(8,128)S(1)}, f32[2,16,128]{2,1,0:T(8,128)S(1)}, u32[]{:S(2)}, u32[]{:S(2)}) collective-permute-start(f32[2,16,128]{2,1,0:T(8,128)S(1)} %pad_maximum_fusion.2.own_ref), channel_id=1, source_target_pairs={{0,1},{1,0},{2,3},{3,2},{4,5},{5,4},{6,7},{7,6},{8,9},{9,8},{10,11... | collective-permute-start | bytes 49160 | tf_op jit(solution)/shard_map/ppermute | solution.py:612
  25.9 1.6 %collective-permute-start.9 = (f32[2,16,128]{2,1,0:T(8,128)S(1)}, f32[2,16,128]{2,1,0:T(8,128)S(1)}, u32[]{:S(2)}, u32[]{:S(2)}) collective-permute-start(f32[2,16,128]{2,1,0:T(8,128)S(1)} %collective-permute-done.7.even_ref), channel_id=1, source_target_pairs={{0,1},{1,0},{2,3},{3,2},{4,5},{5,4},{6,7},{7,6},{8,9},{9,8},{10,11... | collective-permute-start | bytes 49160 | tf_op jit(solution)/shard_map/ppermute | solution.py:612
  26.4 1.2 %collective-permute-start.10 = (f32[2,16,128]{2,1,0:T(8,128)S(1)}, f32[2,16,128]{2,1,0:T(8,128)S(1)}, u32[]{:S(2)}, u32[]{:S(2)}) collective-permute-start(f32[2,16,128]{2,1,0:T(8,128)S(1)} %collective-permute-done.8.odd_ref), channel_id=1, source_target_pairs={{0,1},{1,0},{2,3},{3,2},{4,5},{5,4},{6,7},{7,6},{8,9},{9,8},{10,11... | collective-permute-start | bytes 49160 | tf_op jit(solution)/shard_map/ppermute | solution.py:612

commit v9 on v8

--- a/solution.py
+++ b/solution.py
@@ -212,19 +212,27 @@
     positions_any,
     velocity_any,
     edge_any,
-    _,
+    latent_ref,
     weights_ref,
     decoder_out_ref,
     inward_ref,
     encoder_w_ref,
-    placer_ref,
-    masks_ref,
     alive_ref,
     neighbours_ref,
+    edge_ref,
+    spread_ref,
+    latent_t_ref,
+    node_pre_ref,
+    state_ref,
+    mover_edge_ref,
+    mover_place_ref,
+    mover_key_ref,
+    mover_near_ref,
+    mover_node_pre_ref,
+    mover_latent_ref,
+    mover_state_ref,
     positions_ref,
     velocity_ref,
-    edge_ref,
-    spread_ref,
     owners_ref,
     edge_w_ref,
     node_in_ref,
@@ -296,13 +304,10 @@
     counted = jnp.concatenate(counted, axis=1)
     rank = (jnp.sum(counted * member, axis=0, keepdims=True) - 1.0).astype(I32)
     column = jnp.where(moving == 1, group * CAP + rank, -1)
-    movers = placer_ref.shape[0]
-    placer_ref[...] = jnp.where(
+    movers = mover_state_ref.shape[1]
+    placer = jnp.where(
         lax.broadcasted_iota(I32, (movers, particles), 0) == column, 1.0, 0.0
     ).astype(BF16)
-    masks_ref[...] = jnp.concatenate(
-        [stays, moving.astype(F32), jnp.zeros((6, particles), F32)], axis=0
-    )
 
     spread_shape = spread_ref.shape
     line = lax.broadcasted_iota(I32, spread_shape, 0)
@@ -323,7 +328,7 @@
     )
     spread_ref[...] = jnp.where(valid, 1.0, 0.0).astype(BF16)
 
-    for copy in copies[1:]:
+    for copy in copies[1:-1]:
         copy.wait()
     for i in range(5):
         weights_ref[i] = flip(edge_w_ref[i])
@@ -336,35 +341,6 @@
     inward = inward.astype(BF16)
     inward_ref[...] = jnp.concatenate([inward, inward, inward], axis=0)
 
-
-def prepare_kernel(
-    sizes,
-    latent_ref,
-    own_zed,
-    edge_ref,
-    positions_ref,
-    velocity_ref,
-    neighbours_ref,
-    weights_ref,
-    placer_ref,
-    masks_ref,
-    far_ref,
-    latent_t_ref,
-    node_pre_ref,
-    state_ref,
-    mover_pre_ref,
-    mover_place_ref,
-    mover_key_ref,
-    mover_node_pre_ref,
-    mover_latent_ref,
-    mover_state_ref,
-):
-    fold_y = sizes[1] == 2
-    neighbour_count = edge_ref.shape[3]
-    placer = placer_ref[...]
-    movers, particles = placer.shape
-    stays, moving = masks_ref[0:1], masks_ref[1:2]
-
     latent = jnp.concatenate([latent_ref[a, b, 0] for a, b in CELLS], axis=0)
     latent_t_ref[...] = latent.astype(F32).T
     node_pre_ref[...] = dot_nt(weights_ref[NODE_OLD], latent)
@@ -378,9 +354,10 @@
     mover_latent = dot(placer, latent).astype(BF16)
     mover_latent_ref[...] = mover_latent.astype(F32).T
     mover_node_pre_ref[...] = dot_nt(weights_ref[NODE_OLD], mover_latent)
-    near = dot_nt(weights_ref[NEAR], mover_latent)
-    state = jnp.concatenate(state + [moving, jnp.zeros_like(stays)], axis=0)
+    mover_near_ref[...] = dot_nt(weights_ref[NEAR], mover_latent)
+    state = jnp.concatenate(state + [moving.astype(F32), jnp.zeros_like(stays)], axis=0)
     mover_state_ref[...] = joined(dot_nt(thirds(state), placer))
+    neighbour_count = edge_ref.shape[3]
     ids = jnp.concatenate(
         [
             jnp.concatenate([neighbours_ref[a, b, k] for a, b in CELLS], axis=1)
@@ -391,28 +368,48 @@
     ids = jnp.concatenate([ids & 127, ids >> 7, jnp.zeros((8, particles), I32)], axis=0)
     ids = dot_nt(ids.astype(F32).astype(BF16), placer).astype(I32)
     place, key = places(ids[:neighbour_count], ids[neighbour_count : 2 * neighbour_count], fold_y)
-    place = jnp.concatenate([place[k : k + 1] for k in range(neighbour_count)], axis=1)
-    key = jnp.concatenate([key[k : k + 1] for k in range(neighbour_count)], axis=1)
-    mover_place_ref[...] = place
-    mover_key_ref[...] = key
-    window = Window(fold_y, far_ref)
+    mover_place_ref[...] = jnp.concatenate([place[k : k + 1] for k in range(neighbour_count)], axis=1)
+    mover_key_ref[...] = jnp.concatenate([key[k : k + 1] for k in range(neighbour_count)], axis=1)
+    copies[-1].wait()
+    for k in range(neighbour_count):
+        rows = jnp.concatenate([edge_ref[a, b, 0, k] for a, b in CELLS], axis=0)
+        mover_edge_ref[k] = dot(placer, rows).astype(BF16)
+
+
+def prepare_kernel(
+    sizes,
+    latent_ref,
+    own_zed,
+    mine_ref,
+    weights_ref,
+    edge_ref,
+    place_ref,
+    key_ref,
+    near_ref,
+    far_ref,
+    far_mine_ref,
+    pre_ref,
+):
+    window = Window(sizes[1] == 2, far_ref)
+    core = lax.axis_index("gz")
+    far_t = weights_ref[FAR]
     columns = [(ex, row) for ex in (1, 2) for row in window.own_rows]
     for (ex, row), (a, b) in zip(columns, CELLS):
         pair = jnp.concatenate([latent_ref[a, b, 0], own_zed[a, b, 0]], axis=0)
-        far_ref[window.own(ex, row)] = dot_nt(weights_ref[FAR], pair).astype(BF16)
+        far_ref[window.own(ex, row)] = dot_nt(far_t, pair).astype(BF16)
     cells = window.cells(columns)
+    for row in range(window.row_count):
+        pair = jnp.concatenate([mine_ref[1, row], mine_ref[0, row]], axis=0)
+        far_mine_ref[row] = dot_nt(far_t, pair).astype(BF16)
+        cells.append((12 * (1 - core) + row, far_mine_ref.at[row]))
+    neighbour_count, movers = edge_ref.shape[:2]
     step = TILE // movers
-    near = jnp.concatenate([near] * step, axis=1)
+    near = jnp.concatenate([near_ref[...]] * step, axis=1)
     for tile in range(neighbour_count // step):
-        edges = []
-        for k in range(tile * step, (tile + 1) * step):
-            rows = jnp.concatenate([edge_ref[a, b, 0, k] for a, b in CELLS], axis=0)
-            edges.append(dot(placer, rows).astype(BF16))
+        edges = jnp.concatenate([edge_ref[k] for k in range(tile * step, (tile + 1) * step)], axis=0)
         at = slice(tile * TILE, (tile + 1) * TILE)
-        mover_pre_ref[:, at] = (
-            dot_nt(weights_ref[EDGE], jnp.concatenate(edges, axis=0))
-            + near
-            + pick(cells, place[:, at], key[:, at])
+        pre_ref[:, at] = (
+            dot_nt(weights_ref[EDGE], edges) + near + pick(cells, place_ref[:, at], key_ref[:, at])
         )
 
 
@@ -424,7 +421,7 @@
     fold_y = sizes[1] == 2
     side_refs, refs = refs[:side_count], refs[side_count:]
     side_zeds, refs = refs[:side_count], refs[side_count:]
-    mine_ref, other_ref, refs = refs[0], refs[1], refs[2:]
+    other_ref, far_mine_ref, refs = refs[0], refs[1], refs[2:]
     (
         weights_ref,
         decoder_out_ref,
@@ -448,17 +445,18 @@
         far_ref[at] = dot_nt(far_t, pair).astype(BF16)
 
     for row in range(row_count):
-        far((1 - core) * row_count + row, mine_ref[1, row], mine_ref[0, row])
         far(core * row_count + row, other_ref[0, row], other_ref[1, row])
     for side, row in enumerate(window.outer_rows):
         for ex in (1, 2):
             far(window.side(ex, row), side_refs[side][ex - 1], side_zeds[side][ex - 1])
 
     movers = state_ref.shape[1]
-    columns = [(ex, row) for ex in (0, 3) for row in range(row_count)]
-    columns += [(ex, row) for ex in (1, 2) for row in window.outer_rows]
+    for row in range(row_count):
+        far_ref[(1 - core) * row_count + row] = far_mine_ref[row]
+    cells = [(12 * core + row, far_ref.at[core * row_count + row]) for row in range(row_count)]
+    cells += window.cells([(ex, row) for ex in (1, 2) for row in window.outer_rows])
     message = messages(
-        window.cells(columns),
+        cells,
         place_ref[...],
         key_ref[...],
         lambda tile: pre_ref[:, tile * TILE : (tile + 1) * TILE],
@@ -549,11 +547,11 @@
     sizes,
     moved_ref,
     own_ref,
+    odd_ref,
     even_ref,
-    odd_ref,
     own_zed,
+    odd_zed,
     even_zed,
-    odd_zed,
     spread_ref,
     inward_ref,
     encoder_w_ref,
@@ -709,11 +707,12 @@
     )
     core = lax.axis_index("gz")
     if fold_y:
-        sides = [swap(inner[:, 0], "gy")]
         row = 1 - lax.axis_index("gy")
         both = jnp.stack([end[:, 0], lax.dynamic_index_in_dim(own_zed[:, :, 0], 1 - core, 0, False)])
         corner = lax.dynamic_slice_in_dim(both, row, 1, axis=1)
         mine = [swap_chips(both, False), swap_chips(corner, True)]
+        inner, own_zed = lax.optimization_barrier((inner, own_zed))
+        sides = [swap(inner[:, 0], "gy")]
     else:
         sides = [shift(latent[:, 1, 0], "gy", 0), shift(latent[:, 0, 0], "gy", 1)]
         side_zeds = [swap(part, "gz") for part in sides]
@@ -724,23 +723,33 @@
             layers.append(jnp.concatenate(parts, axis=0))
         mine = [swap_chips(jnp.stack(layers), False)]
 
-    fetched = (neighbours, positions, velocity, edge_latent)
     ranked = call(
         functools.partial(ranks_kernel, sizes),
         "ranks",
-        [SMEM] + [ANY] * 13,
+        [SMEM] + [ANY] * 12 + [VMEM],
         [
             ((11, width, width), BF16),
             (decoder_out.shape, BF16),
             ((48, width), BF16),
             (encoder_weights.shape, BF16),
-            ((movers, particles), BF16),
+            ((2, 2, 1, slots), F32),
+            (neighbours.shape, I32),
+            (edge_latent.shape, BF16),
+            ((movers, 26 * CAP), BF16),
+            ((width, particles), F32),
+            ((width, particles), F32),
             ((8, particles), F32),
-            ((2, 2, 1, slots), F32),
-            *((array.shape, array.dtype) for array in fetched),
-            ((movers, 26 * CAP), BF16),
+            ((neighbour_count, movers, width), BF16),
+            ((1, neighbour_count * movers), I32),
+            ((1, neighbour_count * movers), I32),
+            ((width, movers), F32),
+            ((width, movers), F32),
+            ((width, movers), F32),
+            ((8, movers), F32),
         ],
         [
+            like(positions),
+            like(velocity),
             like(owners),
             like(edge_weights),
             like(node_in),
@@ -761,16 +770,36 @@
                 decoder_out,
                 encoder_in,
                 encoder_weights,
-                *fetched,
+                neighbours,
+                positions,
+                velocity,
+                edge_latent,
             )
         ]
-        + [own_zed],
+        + [latent],
         500_000_000,
     )
     sides, mine, ranked = lax.optimization_barrier((sides, mine, ranked))
-    weights, decoder_out, inward, encoder_weights, placer, masks, alive, *ranked = ranked
-    neighbours, positions, velocity, edge_latent, spread = ranked
-
+    (
+        weights,
+        decoder_out,
+        inward,
+        encoder_weights,
+        alive,
+        neighbours,
+        edge_latent,
+        spread,
+        latent_t,
+        node_pre,
+        state,
+        mover_edges,
+        mover_place,
+        mover_key,
+        mover_near,
+        mover_node_pre,
+        mover_latent,
+        mover_state,
+    ) = ranked
     mine = jnp.concatenate(mine, axis=1)
     if fold_y:
         packed = jnp.concatenate([mine.reshape(-1, slots, width), sides[0]], axis=0)
@@ -780,40 +809,23 @@
     prepared = call(
         functools.partial(prepare_kernel, sizes),
         "prepare",
-        [VMEM] * 9,
+        [VMEM] * 8,
         [
             ((4, width, 2 * slots), BF16),
-            ((width, particles), F32),
-            ((width, particles), F32),
-            ((8, particles), F32),
+            ((rows, width, 2 * slots), BF16),
             ((width, neighbour_count * movers), F32),
-            ((1, neighbour_count * movers), I32),
-            ((1, neighbour_count * movers), I32),
-            ((width, movers), F32),
-            ((width, movers), F32),
-            ((8, movers), F32),
         ],
         [],
-        (latent, own_zed, edge_latent, positions, velocity, neighbours, weights, placer, masks),
+        (latent, own_zed, mine, weights, mover_edges, mover_place, mover_key, mover_near),
         500_000_000,
     )
     packed, prepared = lax.optimization_barrier((packed, prepared))
     cells = mine.shape[0] * mine.shape[1]
     if fold_y:
         side_zeds = [packed[cells:]]
-    halo = [*sides, *side_zeds, mine, packed[:cells].reshape(mine.shape)]
-    (
-        far_own,
-        latent_t,
-        node_pre,
-        state,
-        mover_pre,
-        mover_place,
-        mover_key,
-        mover_node_pre,
-        mover_latent,
-        mover_state,
-    ) = prepared
+    far_own, far_mine, mover_pre = prepared
+    halo = [*sides, *side_zeds, packed[:cells].reshape(mine.shape), far_mine]
+
     far_rest, bucket = call(
         functools.partial(movers_kernel, sizes, len(sides)),
         "movers",
@@ -853,8 +865,7 @@
     tiles, first = lax.optimization_barrier((tiles, first))
     tiles = jnp.stack([bucket, *tiles], axis=0)
     second = edges(1)
-    odd = swap_x(tiles, 1)
-    sided = [swap_x(tiles, 0), odd]
+    sided = [swap_x(tiles, 1), swap_x(tiles, 0)]
     sided, second = lax.optimization_barrier((sided, second))
     tiles = [tiles, *sided]
     zeds = [swap(part, "gz") for part in tiles]

time: 29.5 us -> 29.2 us (0.990)
  Pallas kernels: 16.9 us -> 15.9 us
  starting transfers between devices: 9.87 us -> 10.7 us
    ppermute x2, starting transfers between devices: 1.82 us -> 4.16 us  [swap_chips(): return lax.ppermute(values, ('gx', 'gy', 'gz'), pairs)]
    ppermute x7, starting transfers between devices: 4.75 us -> 2.9 us  [swap(): return lax.ppermute(values, axis, [(0, 1), (1, 0)])]
    ppermute x2, waiting for transfers between devices: 1.61 us -> 0.1 us  [swap_chips(): return lax.ppermute(values, ('gx', 'gy', 'gz'), pairs)]
    ppermute x7, waiting for transfers between devices: 0.06 us -> 1.44 us  [swap(): return lax.ppermute(values, axis, [(0, 1), (1, 0)])]
    pallas_call x8, Pallas kernels: 16.9 us -> 15.9 us  [call(): pl.pallas_call(kernel, out_shape=tuple((jax.ShapeDtypeStruct(shape, kind)...]
    ppermute x2, starting transfers between devices: 3.31 us -> 3.65 us  [swap_x(): return lax.ppermute(values, ('gx', 'gz'), pairs)]
  transfers between devices with their start and end apart: 11 -> 11, of which waited for: 1 -> 5; matrix products, arithmetic and copies ran while one was open for 0% -> 0% of each run, Pallas kernels for 43% -> 41%
where the time goes in v9:
time: 29.2 us; the launch traced here: 29 us
  Pallas kernels  15.9 us (54%)
  starting transfers between devices  10.7 us (37%)
  waiting for transfers between devices  1.54 us (5%)
  between operations  0.79 us (3%)
    pallas_call x8, Pallas kernels, call(): pl.pallas_call(kernel, out_shape=tuple((jax.ShapeDtypeStruct(shape, kind)...  15.9 us
    ppermute x2, starting transfers between devices, swap_chips(): return lax.ppermute(values, ('gx', 'gy', 'gz'), pairs)  4.16 us
    ppermute x2, starting transfers between devices, swap_x(): return lax.ppermute(values, ('gx', 'gz'), pairs)  3.65 us
    ppermute x7, starting transfers between devices, swap(): return lax.ppermute(values, axis, [(0, 1), (1, 0)])  2.9 us
    ppermute x7, waiting for transfers between devices, swap(): return lax.ppermute(values, axis, [(0, 1), (1, 0)])  1.44 us
  transfers between devices with their start and end apart: 11, of which 5 were waited for; matrix products, arithmetic and copies ran while one was open for 0% of the time, Pallas kernels for 41%

profile of v9, /device:TPU:0, one launch (start us, length us, event | category | flops | bytes accessed | tf_op | source)
XLA Modules:
  0.0 29.0 jit_solution(1410925137178564982)
XLA Ops:
  0.6 0.5 %collective-permute-start = (bf16[2,2,1,128,128]{4,3,2,1,0:T(8,128)(2,1)}, bf16[2,2,1,128,128]{4,3,2,1,0:T(8,128)(2,1)S(1)}, u32[]{:S(2)}, u32[]{:S(2)}) collective-permute-start(bf16[2,2,1,128,128]{4,3,2,1,0:T(8,128)(2,1)} %latent_any.1), channel_id=1, source_target_pairs={{0,1},{1,0},{2,3},{3,2},{4,5},{5,4},{6,7},{7,6},{8,9},{9,8},{10,11... | collective-permute-start | bytes 393224 | tf_op jit(solution)/shard_map/ppermute | solution.py:610
  1.1 1.0 %cut.1 = (bf16[2,2,1,128,128]{4,3,2,1,0:T(8,128)(2,1)S(1)}, bf16[2,1,128,128]{3,2,1,0:T(8,128)(2,1)S(1)}, bf16[2,1,128,128]{3,2,1,0:T(8,128)(2,1)S(1)}) custom-call(bf16[2,2,1,128,128]{4,3,2,1,0:T(8,128)(2,1)} %latent_any.1), custom_call_target="tpu_custom_call" | custom-call | flops 1000000 | tf_op jit(solution)/shard_map/cut/pallas_call | solution.py:647
  2.1 0.2 collective-permute-done.own_zed
  2.4 2.8 %collective-permute-start.2 = (bf16[2,2,128,128]{3,2,1,0:T(8,128)(2,1)S(1)}, bf16[2,2,128,128]{3,2,1,0:T(8,128)(2,1)S(1)}, u32[]{:S(2)}, u32[]{:S(2)}) collective-permute-start(bf16[2,2,128,128]{3,2,1,0:T(8,128)(2,1)S(1)} %pad_maximum_fusion.1), channel_id=1, source_target_pairs={{0,5},{1,3},{2,7},{3,1},{4,9},{5,0},{6,11},{7,2},{8,13},{9,4},{10,... | collective-permute-start | bytes 393224 | tf_op jit(solution)/shard_map/ppermute | solution.py:643
  5.1 1.4 %collective-permute-start.3 = (bf16[2,1,128,128]{3,2,1,0:T(8,128)(2,1)S(1)}, bf16[2,1,128,128]{3,2,1,0:T(8,128)(2,1)S(1)}, u32[]{:S(2)}, u32[]{:S(2)}) collective-permute-start(bf16[2,1,128,128]{3,2,1,0:T(8,128)(2,1)S(1)} %fusion), channel_id=1, source_target_pairs={{0,7},{1,3},{2,5},{3,1},{4,11},{5,2},{6,9},{7,0},{8,15},{9,6},{10,... | collective-permute-start | bytes 196616 | tf_op jit(solution)/shard_map/ppermute | solution.py:643
  6.5 0.2 collective-permute-start.1
  6.8 3.1 %ranks.1 = (bf16[11,128,128]{2,1,0:T(8,128)(2,1)S(1)}, bf16[3,128]{1,0:T(4,128)(2,1)S(1)}, bf16[48,128]{1,0:T(8,128)(2,1)S(1)}, bf16[2,128,128]{2,1,0:T(8,128)(2...) custom-call(s32[2,1,2]{2,1,0:T(1,128)} %bitcast.20, ...), custom_call_target="tpu_custom_call" | custom-call | flops 500000000 | tf_op jit(solution)/shard_map/ranks/pallas_call | solution.py:647
  9.8 0.1 collective-permute-done.3
  9.9 0.9 %collective-permute-done.1.refs_0_ = bf16[2,128,128]{2,1,0:T(8,128)(2,1)S(1)} collective-permute-done((bf16[2,128,128]{2,1,0:T(8,128)(2,1)S(1)}, bf16[2,128,128]{2,1,0:T(8,128)(2,1)S(1)}, u32[]{:S(2)}, u32[]{:S(2)}) %collective-permute-start.1) | collective-permute-done | bytes 65568 | tf_op jit(solution)/shard_map/ppermute | solution.py:610
  10.9 0.1 collective-permute-start.4
  10.9 1.3 %prepare.1 = (bf16[4,128,256]{2,1,0:T(8,128)(2,1)S(1)}, bf16[3,128,256]{2,1,0:T(8,128)(2,1)S(1)}, f32[128,1536]{1,0:T(8,128)S(1)}) custom-call(bf16[2,2,1,128,128]{4,3,2,1,0:T(8,128)(2,1)S(1)} %get-tuple-element.69.latent_ref, bf16[2,2,1,128,128]{4,3,2,1,0:T(8,128)(2,1)S(1)} %collective-permute-done.own_zed, ...), custom_call_target="tpu_custom_call" | custom-call | flops 500000000 | tf_op jit(solution)/shard_map/prepare/pallas_call | solution.py:647
  12.2 0.3 collective-permute-done.4
  12.5 2.3 %movers.1 = (bf16[8,128,256]{2,1,0:T(8,128)(2,1)S(1)}, f32[16,128]{1,0:T(8,128)S(1)}) custom-call(bf16[2,128,128]{2,1,0:T(8,128)(2,1)S(1)} %collective-permute-done.1.refs_0_, bf16[2,128,128]{2,1,0:T(8,128)(2,1)S(1)} %slice.6.refs_1_, bf16[2,3,128,128]{3,2,1,0:T(8,128)(2,1)S(1)} %bitcast.15, bf16[3,128,256]{2,1,0:T(8,128)(2,1)S(1)} %get-tuple-element.101.refs_3_, ...), custom_call_target="tpu_custom_call" | custom-call | flops 3000000000 | tf_op jit(solution)/shard_map/movers/pallas_call | solution.py:647
  14.8 1.4 %collective-permute-start.5 = (f32[16,128]{1,0:T(8,128)S(1)}, f32[16,128]{1,0:T(8,128)S(1)}, u32[]{:S(2)}, u32[]{:S(2)}) collective-permute-start(f32[16,128]{1,0:T(8,128)S(1)} %get-tuple-element.107), channel_id=1, source_target_pairs={{0,2},{2,0},{1,3},{3,1},{4,6},{6,4},{5,7},{7,5},{8,10},{10,8},{9,1... | collective-permute-start | bytes 24584 | tf_op jit(solution)/shard_map/ppermute | solution.py:610
  16.2 2.8 %edges.2.first_ref = bf16[2,128,128]{2,1,0:T(8,128)(2,1)S(1)} custom-call(f32[2,2,1,128]{3,2,1,0:T(1,128)S(1)} %get-tuple-element.108.alive_ref, bf16[2,2,1,128,128]{4,3,2,1,0:T(8,128)(2,1)S(1)} %get-tuple-element.69.latent_ref, bf16[2,2,1,12,128,128]{5,4,3,2,1,0:T(8,128)(2,1)S(1)} %get-tuple-element.109.edge_ref, ...), custom_call_target="tpu_custom_call" | custom-call | flops 4000000000 | tf_op jit(solution)/shard_map/edges/pallas_call | solution.py:647
  19.0 0.1 collective-permute-start.7
  19.1 3.6 %collective-permute-start.8 = (f32[2,16,128]{2,1,0:T(8,128)S(1)}, f32[2,16,128]{2,1,0:T(8,128)S(1)}, u32[]{:S(2)}, u32[]{:S(2)}) collective-permute-start(f32[2,16,128]{2,1,0:T(8,128)S(1)} %pad_maximum_fusion.2.own_ref), channel_id=1, source_target_pairs={{0,4},{1,5},{4,0},{5,1},{8,12},{9,13},{12,8},{13,9},{2,6},{3,7},{6... | collective-permute-start | bytes 49160 | tf_op jit(solution)/shard_map/ppermute | solution.py:628
  22.7 2.8 %edges.3.second_ref = bf16[2,128,128]{2,1,0:T(8,128)(2,1)S(1)} custom-call(f32[2,2,1,128]{3,2,1,0:T(1,128)S(1)} %get-tuple-element.108.alive_ref, bf16[2,2,1,128,128]{4,3,2,1,0:T(8,128)(2,1)S(1)} %get-tuple-element.69.latent_ref, bf16[2,2,1,12,128,128]{5,4,3,2,1,0:T(8,128)(2,1)S(1)} %get-tuple-element.109.edge_ref, ...), custom_call_target="tpu_custom_call" | custom-call | flops 4000000000 | tf_op jit(solution)/shard_map/edges/pallas_call | solution.py:647
  25.5 0.1 collective-permute-start.6
  25.6 0.5 %collective-permute-start.10 = (f32[2,16,128]{2,1,0:T(8,128)S(1)}, f32[2,16,128]{2,1,0:T(8,128)S(1)}, u32[]{:S(2)}, u32[]{:S(2)}) collective-permute-start(f32[2,16,128]{2,1,0:T(8,128)S(1)} %collective-permute-done.8.even_ref), channel_id=1, source_target_pairs={{0,1},{1,0},{2,3},{3,2},{4,5},{5,4},{6,7},{7,6},{8,9},{9,8},{10,11... | collective-permute-start | bytes 49160 | tf_op jit(solution)/shard_map/ppermute | solution.py:610
  26.1 0.1 collective-permute-start.9
  26.2 1.0 %nodes.1.moved_ref = f32[16,512]{1,0:T(8,128)S(1)} custom-call(bf16[2,128,128]{2,1,0:T(8,128)(2,1)S(1)} %edges.2.first_ref, bf16[2,128,128]{2,1,0:T(8,128)(2,1)S(1)} %edges.3.second_ref, f32[128,512]{1,0:T(8,128)S(1)} %get-tuple-element.118.node_pre_ref, f32[128,512]{1,0:T(8,128)S(1)} %get-tuple-element.119.latent_t_ref, ...), custom_call_target="tpu_custom_call" | custom-call | flops 1000000000 | tf_op jit(solution)/shard_map/nodes/pallas_call | solution.py:647
  27.2 0.1 collective-permute-done.9.odd_zed
  27.3 1.8 %finish.1 = (bf16[2,2,1,128,128]{4,3,2,1,0:T(8,128)(2,1)}, f32[9,2,2,1,128]{4,3,2,1,0:T(1,128)}, bf16[1,1,1,208,128]{4,3,2,1,0:T(8,128)(2,1)}, f32[9,1,1,1,208]{4,3,2,1,0:T(1,128)}) custom-call(f32[16,512]{1,0:T(8,128)S(1)} %nodes.1.moved_ref, f32[2,16,128]{2,1,0:T(8,128)S(1)} %pad_maximum_fusion.2.own_ref, ...), custom_call_target="tpu_custom_call" | custom-call | flops 1000000000 | tf_op jit(solution)/shard_map/finish/pallas_call | solution.py:647
  (15 shorter events, 0.1 us)
Async XLA Ops:
  0.6 1.7 %collective-permute-start = (bf16[2,2,1,128,128]{4,3,2,1,0:T(8,128)(2,1)}, bf16[2,2,1,128,128]{4,3,2,1,0:T(8,128)(2,1)S(1)}, u32[]{:S(2)}, u32[]{:S(2)}) collective-permute-start(bf16[2,2,1,128,128]{4,3,2,1,0:T(8,128)(2,1)} %latent_any.1), channel_id=1, source_target_pairs={{0,1},{1,0},{2,3},{3,2},{4,5},{5,4},{6,7},{7,6},{8,9},{9,8},{10,11... | collective-permute-start | bytes 393224 | tf_op jit(solution)/shard_map/ppermute | solution.py:610
  2.4 8.4 %collective-permute-start.2 = (bf16[2,2,128,128]{3,2,1,0:T(8,128)(2,1)S(1)}, bf16[2,2,128,128]{3,2,1,0:T(8,128)(2,1)S(1)}, u32[]{:S(2)}, u32[]{:S(2)}) collective-permute-start(bf16[2,2,128,128]{3,2,1,0:T(8,128)(2,1)S(1)} %pad_maximum_fusion.1), channel_id=1, source_target_pairs={{0,5},{1,3},{2,7},{3,1},{4,9},{5,0},{6,11},{7,2},{8,13},{9,4},{10,... | collective-permute-start | bytes 393224 | tf_op jit(solution)/shard_map/ppermute | solution.py:643
  5.1 4.8 %collective-permute-start.3 = (bf16[2,1,128,128]{3,2,1,0:T(8,128)(2,1)S(1)}, bf16[2,1,128,128]{3,2,1,0:T(8,128)(2,1)S(1)}, u32[]{:S(2)}, u32[]{:S(2)}) collective-permute-start(bf16[2,1,128,128]{3,2,1,0:T(8,128)(2,1)S(1)} %fusion), channel_id=1, source_target_pairs={{0,7},{1,3},{2,5},{3,1},{4,11},{5,2},{6,9},{7,0},{8,15},{9,6},{10,... | collective-permute-start | bytes 196616 | tf_op jit(solution)/shard_map/ppermute | solution.py:643
  6.5 4.3 %collective-permute-start.1 = (bf16[2,128,128]{2,1,0:T(8,128)(2,1)S(1)}, bf16[2,128,128]{2,1,0:T(8,128)(2,1)S(1)}, u32[]{:S(2)}, u32[]{:S(2)}) collective-permute-start(bf16[2,128,128]{2,1,0:T(8,128)(2,1)S(1)} %bitcast.17), channel_id=1, source_target_pairs={{0,2},{2,0},{1,3},{3,1},{4,6},{6,4},{5,7},{7,5},{8,10},{10,8},{9,1... | collective-permute-start | bytes 196616 | tf_op jit(solution)/shard_map/ppermute | solution.py:610
  10.9 1.6 %collective-permute-start.4 = (bf16[8,128,128]{2,1,0:T(8,128)(2,1)S(1)}, bf16[8,128,128]{2,1,0:T(8,128)(2,1)S(1)}, u32[]{:S(2)}, u32[]{:S(2)}) collective-permute-start(bf16[8,128,128]{2,1,0:T(8,128)(2,1)S(1)} %pad_maximum_fusion), channel_id=1, source_target_pairs={{0,1},{1,0},{2,3},{3,2},{4,5},{5,4},{6,7},{7,6},{8,9},{9,8},{10,11... | collective-permute-start | bytes 786440 | tf_op jit(solution)/shard_map/ppermute | solution.py:610
  14.8 4.3 %collective-permute-start.5 = (f32[16,128]{1,0:T(8,128)S(1)}, f32[16,128]{1,0:T(8,128)S(1)}, u32[]{:S(2)}, u32[]{:S(2)}) collective-permute-start(f32[16,128]{1,0:T(8,128)S(1)} %get-tuple-element.107), channel_id=1, source_target_pairs={{0,2},{2,0},{1,3},{3,1},{4,6},{6,4},{5,7},{7,5},{8,10},{10,8},{9,1... | collective-permute-start | bytes 24584 | tf_op jit(solution)/shard_map/ppermute | solution.py:610
  19.0 6.6 %collective-permute-start.7 = (f32[2,16,128]{2,1,0:T(8,128)S(1)}, f32[2,16,128]{2,1,0:T(8,128)S(1)}, u32[]{:S(2)}, u32[]{:S(2)}) collective-permute-start(f32[2,16,128]{2,1,0:T(8,128)S(1)} %pad_maximum_fusion.2.own_ref), channel_id=1, source_target_pairs={{0,1},{1,0},{4,8},{5,9},{8,4},{9,5},{12,13},{13,12},{2,3},{3,2},{6... | collective-permute-start | bytes 49160 | tf_op jit(solution)/shard_map/ppermute | solution.py:628
  19.1 6.5 %collective-permute-start.8 = (f32[2,16,128]{2,1,0:T(8,128)S(1)}, f32[2,16,128]{2,1,0:T(8,128)S(1)}, u32[]{:S(2)}, u32[]{:S(2)}) collective-permute-start(f32[2,16,128]{2,1,0:T(8,128)S(1)} %pad_maximum_fusion.2.own_ref), channel_id=1, source_target_pairs={{0,4},{1,5},{4,0},{5,1},{8,12},{9,13},{12,8},{13,9},{2,6},{3,7},{6... | collective-permute-start | bytes 49160 | tf_op jit(solution)/shard_map/ppermute | solution.py:628
  25.5 1.7 %collective-permute-start.6 = (f32[2,16,128]{2,1,0:T(8,128)S(1)}, f32[2,16,128]{2,1,0:T(8,128)S(1)}, u32[]{:S(2)}, u32[]{:S(2)}) collective-permute-start(f32[2,16,128]{2,1,0:T(8,128)S(1)} %pad_maximum_fusion.2.own_ref), channel_id=1, source_target_pairs={{0,1},{1,0},{2,3},{3,2},{4,5},{5,4},{6,7},{7,6},{8,9},{9,8},{10,11... | collective-permute-start | bytes 49160 | tf_op jit(solution)/shard_map/ppermute | solution.py:610
  25.6 1.6 %collective-permute-start.10 = (f32[2,16,128]{2,1,0:T(8,128)S(1)}, f32[2,16,128]{2,1,0:T(8,128)S(1)}, u32[]{:S(2)}, u32[]{:S(2)}) collective-permute-start(f32[2,16,128]{2,1,0:T(8,128)S(1)} %collective-permute-done.8.even_ref), channel_id=1, source_target_pairs={{0,1},{1,0},{2,3},{3,2},{4,5},{5,4},{6,7},{7,6},{8,9},{9,8},{10,11... | collective-permute-start | bytes 49160 | tf_op jit(solution)/shard_map/ppermute | solution.py:610
  26.1 1.2 %collective-permute-start.9 = (f32[2,16,128]{2,1,0:T(8,128)S(1)}, f32[2,16,128]{2,1,0:T(8,128)S(1)}, u32[]{:S(2)}, u32[]{:S(2)}) collective-permute-start(f32[2,16,128]{2,1,0:T(8,128)S(1)} %collective-permute-done.7.odd_ref), channel_id=1, source_target_pairs={{0,1},{1,0},{2,3},{3,2},{4,5},{5,4},{6,7},{7,6},{8,9},{9,8},{10,11... | collective-permute-start | bytes 49160 | tf_op jit(solution)/shard_map/ppermute | solution.py:610

commit v10 on v9

--- a/solution.py
+++ b/solution.py
@@ -112,8 +112,10 @@
     window = jnp.concatenate(
         [ref[f : f + chunk] for f in range(0, width, chunk) for _, ref in cells], axis=0
     )
-    key_rows = lax.broadcasted_iota(I32, (TILE, TILE), 0)
-    picker = jnp.where(key_rows == key, 1.0, 0.0).astype(BF16)
+    key_rows = lax.broadcasted_iota(I32, (TILE, TILE), 0).astype(F32).astype(BF16)
+    key = jnp.broadcast_to(key.astype(F32), (16, TILE)).astype(BF16)
+    same = key_rows.reshape(TILE // 16, 16, TILE) == key[None]
+    picker = jnp.where(same, jnp.ones((), BF16), jnp.zeros((), BF16)).reshape(TILE, TILE)
     found = dot(window, picker).reshape(width // chunk, len(cells), chunk // 8, 8, TILE)
     where = jnp.broadcast_to(place, (8, TILE))
     parts = []
@@ -708,11 +710,14 @@
     core = lax.axis_index("gz")
     if fold_y:
         row = 1 - lax.axis_index("gy")
-        both = jnp.stack([end[:, 0], lax.dynamic_index_in_dim(own_zed[:, :, 0], 1 - core, 0, False)])
-        corner = lax.dynamic_slice_in_dim(both, row, 1, axis=1)
-        mine = [swap_chips(both, False), swap_chips(corner, True)]
-        inner, own_zed = lax.optimization_barrier((inner, own_zed))
         sides = [swap(inner[:, 0], "gy")]
+        beside = lax.dynamic_index_in_dim(own_zed[:, :, 0], 1 - core, 0, False)
+        corner = jnp.concatenate(
+            [lax.dynamic_slice_in_dim(part, row, 1, 0) for part in (end[:, 0], beside)], axis=0
+        )
+        both = jnp.stack([end[:, 0], beside])
+        corner = corner[:, None]
+        mine = [swap_chips(corner, True), swap_chips(both, False)]
     else:
         sides = [shift(latent[:, 1, 0], "gy", 0), shift(latent[:, 0, 0], "gy", 1)]
         side_zeds = [swap(part, "gz") for part in sides]
@@ -777,7 +782,7 @@
             )
         ]
         + [latent],
-        500_000_000,
+        5_000_000_000,
     )
     sides, mine, ranked = lax.optimization_barrier((sides, mine, ranked))
     (
@@ -800,7 +805,7 @@
         mover_latent,
         mover_state,
     ) = ranked
-    mine = jnp.concatenate(mine, axis=1)
+    mine = jnp.concatenate(mine[::-1], axis=1)
     if fold_y:
         packed = jnp.concatenate([mine.reshape(-1, slots, width), sides[0]], axis=0)
     else:
@@ -817,7 +822,7 @@
         ],
         [],
         (latent, own_zed, mine, weights, mover_edges, mover_place, mover_key, mover_near),
-        500_000_000,
+        5_000_000_000,
     )
     packed, prepared = lax.optimization_barrier((packed, prepared))
     cells = mine.shape[0] * mine.shape[1]

time: 29.2 us -> 28.5 us (0.976)
  starting transfers between devices: 10.7 us -> 10.3 us
    ppermute x7, starting transfers between devices: 2.9 us -> 5.29 us  [swap(): return lax.ppermute(values, axis, [(0, 1), (1, 0)])]
    ppermute x2, starting transfers between devices: 4.16 us -> 1.82 us  [swap_chips(): return lax.ppermute(values, ('gx', 'gy', 'gz'), pairs)]
    ppermute x7, waiting for transfers between devices: 1.44 us -> 0.43 us  [swap(): return lax.ppermute(values, axis, [(0, 1), (1, 0)])]
    ppermute x2, waiting for transfers between devices: 0.1 us -> 0.99 us  [swap_chips(): return lax.ppermute(values, ('gx', 'gy', 'gz'), pairs)]
    ppermute x2, starting transfers between devices: 3.65 us -> 3.21 us  [swap_x(): return lax.ppermute(values, ('gx', 'gz'), pairs)]
  transfers between devices with their start and end apart: 11 -> 11, of which waited for: 5 -> 3; matrix products, arithmetic and copies ran while one was open for 0% -> 0% of each run, Pallas kernels for 41% -> 41%
where the time goes in v10:
time: 28.5 us; the launch traced here: 28.3 us
  Pallas kernels  15.7 us (55%)
  starting transfers between devices  10.3 us (36%)
  waiting for transfers between devices  1.42 us (5%)
  between operations  0.81 us (3%)
    pallas_call x8, Pallas kernels, call(): pl.pallas_call(kernel, out_shape=tuple((jax.ShapeDtypeStruct(shape, kind)...  15.7 us
    ppermute x7, starting transfers between devices, swap(): return lax.ppermute(values, axis, [(0, 1), (1, 0)])  5.29 us
    ppermute x2, starting transfers between devices, swap_x(): return lax.ppermute(values, ('gx', 'gz'), pairs)  3.21 us
    ppermute x2, starting transfers between devices, swap_chips(): return lax.ppermute(values, ('gx', 'gy', 'gz'), pairs)  1.82 us
    ppermute x2, waiting for transfers between devices, swap_chips(): return lax.ppermute(values, ('gx', 'gy', 'gz'), pairs)  0.99 us
  transfers between devices with their start and end apart: 11, of which 3 were waited for; matrix products, arithmetic and copies ran while one was open for 0% of the time, Pallas kernels for 41%

profile of v10, /device:TPU:0, one launch (start us, length us, event | category | flops | bytes accessed | tf_op | source)
XLA Modules:
  0.0 28.3 jit_solution(18197716082128306343)
XLA Ops:
  0.6 0.5 %collective-permute-start.1 = (bf16[2,2,1,128,128]{4,3,2,1,0:T(8,128)(2,1)}, bf16[2,2,1,128,128]{4,3,2,1,0:T(8,128)(2,1)S(1)}, u32[]{:S(2)}, u32[]{:S(2)}) collective-permute-start(bf16[2,2,1,128,128]{4,3,2,1,0:T(8,128)(2,1)} %latent_any.1), channel_id=1, source_target_pairs={{0,1},{1,0},{2,3},{3,2},{4,5},{5,4},{6,7},{7,6},{8,9},{9,8},{10,11... | collective-permute-start | bytes 393224 | tf_op jit(solution)/shard_map/ppermute | solution.py:612
  1.1 1.0 %cut.1 = (bf16[2,2,1,128,128]{4,3,2,1,0:T(8,128)(2,1)S(1)}, bf16[2,1,128,128]{3,2,1,0:T(8,128)(2,1)S(1)}, bf16[2,1,128,128]{3,2,1,0:T(8,128)(2,1)S(1)}) custom-call(bf16[2,2,1,128,128]{4,3,2,1,0:T(8,128)(2,1)} %latent_any.1), custom_call_target="tpu_custom_call" | custom-call | flops 1000000 | tf_op jit(solution)/shard_map/cut/pallas_call | solution.py:649
  2.1 2.6 %collective-permute-start = (bf16[2,128,128]{2,1,0:T(8,128)(2,1)S(1)}, bf16[2,128,128]{2,1,0:T(8,128)(2,1)S(1)}, u32[]{:S(2)}, u32[]{:S(2)}) collective-permute-start(bf16[2,128,128]{2,1,0:T(8,128)(2,1)S(1)} %bitcast.22), channel_id=1, source_target_pairs={{0,2},{2,0},{1,3},{3,1},{4,6},{6,4},{5,7},{7,5},{8,10},{10,8},{9,1... | collective-permute-start | bytes 196616 | tf_op jit(solution)/shard_map/ppermute | solution.py:612
  4.7 1.4 %collective-permute-start.2 = (bf16[2,1,128,128]{3,2,1,0:T(8,128)(2,1)S(1)}, bf16[2,1,128,128]{3,2,1,0:T(8,128)(2,1)S(1)}, u32[]{:S(2)}, u32[]{:S(2)}) collective-permute-start(bf16[2,1,128,128]{3,2,1,0:T(8,128)(2,1)S(1)} %maximum_bitcast_fusion), channel_id=1, source_target_pairs={{0,7},{1,3},{2,5},{3,1},{4,11},{5,2},{6,9},{7,0},{8,15},{9,6},{10,... | collective-permute-start | bytes 196616 | tf_op jit(solution)/shard_map/ppermute | solution.py:645
  6.2 0.4 %collective-permute-start.3 = (bf16[2,2,128,128]{3,2,1,0:T(8,128)(2,1)S(1)}, bf16[2,2,128,128]{3,2,1,0:T(8,128)(2,1)S(1)}, u32[]{:S(2)}, u32[]{:S(2)}) collective-permute-start(bf16[2,2,128,128]{3,2,1,0:T(8,128)(2,1)S(1)} %pad_maximum_fusion.1), channel_id=1, source_target_pairs={{0,5},{1,3},{2,7},{3,1},{4,9},{5,0},{6,11},{7,2},{8,13},{9,4},{10,... | collective-permute-start | bytes 393224 | tf_op jit(solution)/shard_map/ppermute | solution.py:645
  6.5 3.1 %ranks.1 = (bf16[11,128,128]{2,1,0:T(8,128)(2,1)S(1)}, bf16[3,128]{1,0:T(4,128)(2,1)S(1)}, bf16[48,128]{1,0:T(8,128)(2,1)S(1)}, bf16[2,128,128]{2,1,0:T(8,128)(2...) custom-call(s32[2,1,2]{2,1,0:T(1,128)} %bitcast.25, ...), custom_call_target="tpu_custom_call" | custom-call | flops 5000000000 | tf_op jit(solution)/shard_map/ranks/pallas_call | solution.py:649
  9.6 0.0 collective-permute-done.refs_0_
  9.6 1.0 %collective-permute-done.3 = bf16[2,2,128,128]{3,2,1,0:T(8,128)(2,1)S(1)} collective-permute-done((bf16[2,2,128,128]{3,2,1,0:T(8,128)(2,1)S(1)}, bf16[2,2,128,128]{3,2,1,0:T(8,128)(2,1)S(1)}, u32[]{:S(2)}, u32[]{:S(2)}) %collective-permute-start.3) | collective-permute-done | bytes 131104 | tf_op jit(solution)/shard_map/ppermute | solution.py:645
  10.7 0.1 collective-permute-start.4
  10.8 1.2 %prepare.1 = (bf16[4,128,256]{2,1,0:T(8,128)(2,1)S(1)}, bf16[3,128,256]{2,1,0:T(8,128)(2,1)S(1)}, f32[128,1536]{1,0:T(8,128)S(1)}) custom-call(bf16[2,2,1,128,128]{4,3,2,1,0:T(8,128)(2,1)S(1)} %get-tuple-element.66.latent_ref, bf16[2,2,1,128,128]{4,3,2,1,0:T(8,128)(2,1)S(1)} %collective-permute-done.1.own_zed, ...), custom_call_target="tpu_custom_call" | custom-call | flops 5000000000 | tf_op jit(solution)/shard_map/prepare/pallas_call | solution.py:649
  11.9 0.4 %collective-permute-done.4 = bf16[8,128,128]{2,1,0:T(8,128)(2,1)S(1)} collective-permute-done((bf16[8,128,128]{2,1,0:T(8,128)(2,1)S(1)}, bf16[8,128,128]{2,1,0:T(8,128)(2,1)S(1)}, u32[]{:S(2)}, u32[]{:S(2)}) %collective-permute-start.4) | collective-permute-done | bytes 262176 | tf_op jit(solution)/shard_map/ppermute | solution.py:612
  12.3 2.2 %movers.1 = (bf16[8,128,256]{2,1,0:T(8,128)(2,1)S(1)}, f32[16,128]{1,0:T(8,128)S(1)}) custom-call(bf16[2,128,128]{2,1,0:T(8,128)(2,1)S(1)} %collective-permute-done.refs_0_, bf16[2,128,128]{2,1,0:T(8,128)(2,1)S(1)} %slice.6.refs_1_, bf16[2,3,128,128]{3,2,1,0:T(8,128)(2,1)S(1)} %bitcast.19, bf16[3,128,256]{2,1,0:T(8,128)(2,1)S(1)} %get-tuple-element.97.refs_3_, ...), custom_call_target="tpu_custom_call" | custom-call | flops 3000000000 | tf_op jit(solution)/shard_map/movers/pallas_call | solution.py:649
  14.5 1.5 %collective-permute-start.5 = (f32[16,128]{1,0:T(8,128)S(1)}, f32[16,128]{1,0:T(8,128)S(1)}, u32[]{:S(2)}, u32[]{:S(2)}) collective-permute-start(f32[16,128]{1,0:T(8,128)S(1)} %get-tuple-element.103), channel_id=1, source_target_pairs={{0,2},{2,0},{1,3},{3,1},{4,6},{6,4},{5,7},{7,5},{8,10},{10,8},{9,1... | collective-permute-start | bytes 24584 | tf_op jit(solution)/shard_map/ppermute | solution.py:612
  16.0 2.8 %edges.2.first_ref = bf16[2,128,128]{2,1,0:T(8,128)(2,1)S(1)} custom-call(f32[2,2,1,128]{3,2,1,0:T(1,128)S(1)} %get-tuple-element.104.alive_ref, bf16[2,2,1,128,128]{4,3,2,1,0:T(8,128)(2,1)S(1)} %get-tuple-element.66.latent_ref, bf16[2,2,1,12,128,128]{5,4,3,2,1,0:T(8,128)(2,1)S(1)} %get-tuple-element.105.edge_ref, ...), custom_call_target="tpu_custom_call" | custom-call | flops 4000000000 | tf_op jit(solution)/shard_map/edges/pallas_call | solution.py:649
  18.8 0.1 collective-permute-start.7
  18.9 3.1 %collective-permute-start.8 = (f32[2,16,128]{2,1,0:T(8,128)S(1)}, f32[2,16,128]{2,1,0:T(8,128)S(1)}, u32[]{:S(2)}, u32[]{:S(2)}) collective-permute-start(f32[2,16,128]{2,1,0:T(8,128)S(1)} %pad_maximum_fusion.2.own_ref), channel_id=1, source_target_pairs={{0,4},{1,5},{4,0},{5,1},{8,12},{9,13},{12,8},{13,9},{2,6},{3,7},{6... | collective-permute-start | bytes 49160 | tf_op jit(solution)/shard_map/ppermute | solution.py:630
  22.0 2.8 %edges.3.second_ref = bf16[2,128,128]{2,1,0:T(8,128)(2,1)S(1)} custom-call(f32[2,2,1,128]{3,2,1,0:T(1,128)S(1)} %get-tuple-element.104.alive_ref, bf16[2,2,1,128,128]{4,3,2,1,0:T(8,128)(2,1)S(1)} %get-tuple-element.66.latent_ref, bf16[2,2,1,12,128,128]{5,4,3,2,1,0:T(8,128)(2,1)S(1)} %get-tuple-element.105.edge_ref, ...), custom_call_target="tpu_custom_call" | custom-call | flops 4000000000 | tf_op jit(solution)/shard_map/edges/pallas_call | solution.py:649
  24.8 0.1 collective-permute-start.6
  24.9 0.0 collective-permute-done.8.even_ref
  24.9 0.5 %collective-permute-start.10 = (f32[2,16,128]{2,1,0:T(8,128)S(1)}, f32[2,16,128]{2,1,0:T(8,128)S(1)}, u32[]{:S(2)}, u32[]{:S(2)}) collective-permute-start(f32[2,16,128]{2,1,0:T(8,128)S(1)} %collective-permute-done.8.even_ref), channel_id=1, source_target_pairs={{0,1},{1,0},{2,3},{3,2},{4,5},{5,4},{6,7},{7,6},{8,9},{9,8},{10,11... | collective-permute-start | bytes 49160 | tf_op jit(solution)/shard_map/ppermute | solution.py:612
  25.4 0.1 collective-permute-start.9
  25.5 1.0 %nodes.1.moved_ref = f32[16,512]{1,0:T(8,128)S(1)} custom-call(bf16[2,128,128]{2,1,0:T(8,128)(2,1)S(1)} %edges.2.first_ref, bf16[2,128,128]{2,1,0:T(8,128)(2,1)S(1)} %edges.3.second_ref, f32[128,512]{1,0:T(8,128)S(1)} %get-tuple-element.114.node_pre_ref, f32[128,512]{1,0:T(8,128)S(1)} %get-tuple-element.115.latent_t_ref, ...), custom_call_target="tpu_custom_call" | custom-call | flops 1000000000 | tf_op jit(solution)/shard_map/nodes/pallas_call | solution.py:649
  26.5 0.1 collective-permute-done.9.odd_zed
  26.6 1.8 %finish.1 = (bf16[2,2,1,128,128]{4,3,2,1,0:T(8,128)(2,1)}, f32[9,2,2,1,128]{4,3,2,1,0:T(1,128)}, bf16[1,1,1,208,128]{4,3,2,1,0:T(8,128)(2,1)}, f32[9,1,1,1,208]{4,3,2,1,0:T(1,128)}) custom-call(f32[16,512]{1,0:T(8,128)S(1)} %nodes.1.moved_ref, f32[2,16,128]{2,1,0:T(8,128)S(1)} %pad_maximum_fusion.2.own_ref, ...), custom_call_target="tpu_custom_call" | custom-call | flops 1000000000 | tf_op jit(solution)/shard_map/finish/pallas_call | solution.py:649
  (17 shorter events, 0.1 us)
Async XLA Ops:
  0.6 4.1 %collective-permute-start.1 = (bf16[2,2,1,128,128]{4,3,2,1,0:T(8,128)(2,1)}, bf16[2,2,1,128,128]{4,3,2,1,0:T(8,128)(2,1)S(1)}, u32[]{:S(2)}, u32[]{:S(2)}) collective-permute-start(bf16[2,2,1,128,128]{4,3,2,1,0:T(8,128)(2,1)} %latent_any.1), channel_id=1, source_target_pairs={{0,1},{1,0},{2,3},{3,2},{4,5},{5,4},{6,7},{7,6},{8,9},{9,8},{10,11... | collective-permute-start | bytes 393224 | tf_op jit(solution)/shard_map/ppermute | solution.py:612
  2.1 7.5 %collective-permute-start = (bf16[2,128,128]{2,1,0:T(8,128)(2,1)S(1)}, bf16[2,128,128]{2,1,0:T(8,128)(2,1)S(1)}, u32[]{:S(2)}, u32[]{:S(2)}) collective-permute-start(bf16[2,128,128]{2,1,0:T(8,128)(2,1)S(1)} %bitcast.22), channel_id=1, source_target_pairs={{0,2},{2,0},{1,3},{3,1},{4,6},{6,4},{5,7},{7,5},{8,10},{10,8},{9,1... | collective-permute-start | bytes 196616 | tf_op jit(solution)/shard_map/ppermute | solution.py:612
  4.7 4.9 %collective-permute-start.2 = (bf16[2,1,128,128]{3,2,1,0:T(8,128)(2,1)S(1)}, bf16[2,1,128,128]{3,2,1,0:T(8,128)(2,1)S(1)}, u32[]{:S(2)}, u32[]{:S(2)}) collective-permute-start(bf16[2,1,128,128]{3,2,1,0:T(8,128)(2,1)S(1)} %maximum_bitcast_fusion), channel_id=1, source_target_pairs={{0,7},{1,3},{2,5},{3,1},{4,11},{5,2},{6,9},{7,0},{8,15},{9,6},{10,... | collective-permute-start | bytes 196616 | tf_op jit(solution)/shard_map/ppermute | solution.py:645
  6.2 4.5 %collective-permute-start.3 = (bf16[2,2,128,128]{3,2,1,0:T(8,128)(2,1)S(1)}, bf16[2,2,128,128]{3,2,1,0:T(8,128)(2,1)S(1)}, u32[]{:S(2)}, u32[]{:S(2)}) collective-permute-start(bf16[2,2,128,128]{3,2,1,0:T(8,128)(2,1)S(1)} %pad_maximum_fusion.1), channel_id=1, source_target_pairs={{0,5},{1,3},{2,7},{3,1},{4,9},{5,0},{6,11},{7,2},{8,13},{9,4},{10,... | collective-permute-start | bytes 393224 | tf_op jit(solution)/shard_map/ppermute | solution.py:645
  10.7 1.6 %collective-permute-start.4 = (bf16[8,128,128]{2,1,0:T(8,128)(2,1)S(1)}, bf16[8,128,128]{2,1,0:T(8,128)(2,1)S(1)}, u32[]{:S(2)}, u32[]{:S(2)}) collective-permute-start(bf16[8,128,128]{2,1,0:T(8,128)(2,1)S(1)} %pad_maximum_fusion), channel_id=1, source_target_pairs={{0,1},{1,0},{2,3},{3,2},{4,5},{5,4},{6,7},{7,6},{8,9},{9,8},{10,11... | collective-permute-start | bytes 786440 | tf_op jit(solution)/shard_map/ppermute | solution.py:612
  14.5 4.3 %collective-permute-start.5 = (f32[16,128]{1,0:T(8,128)S(1)}, f32[16,128]{1,0:T(8,128)S(1)}, u32[]{:S(2)}, u32[]{:S(2)}) collective-permute-start(f32[16,128]{1,0:T(8,128)S(1)} %get-tuple-element.103), channel_id=1, source_target_pairs={{0,2},{2,0},{1,3},{3,1},{4,6},{6,4},{5,7},{7,5},{8,10},{10,8},{9,1... | collective-permute-start | bytes 24584 | tf_op jit(solution)/shard_map/ppermute | solution.py:612
  18.8 6.1 %collective-permute-start.7 = (f32[2,16,128]{2,1,0:T(8,128)S(1)}, f32[2,16,128]{2,1,0:T(8,128)S(1)}, u32[]{:S(2)}, u32[]{:S(2)}) collective-permute-start(f32[2,16,128]{2,1,0:T(8,128)S(1)} %pad_maximum_fusion.2.own_ref), channel_id=1, source_target_pairs={{0,1},{1,0},{4,8},{5,9},{8,4},{9,5},{12,13},{13,12},{2,3},{3,2},{6... | collective-permute-start | bytes 49160 | tf_op jit(solution)/shard_map/ppermute | solution.py:630
  18.9 6.0 %collective-permute-start.8 = (f32[2,16,128]{2,1,0:T(8,128)S(1)}, f32[2,16,128]{2,1,0:T(8,128)S(1)}, u32[]{:S(2)}, u32[]{:S(2)}) collective-permute-start(f32[2,16,128]{2,1,0:T(8,128)S(1)} %pad_maximum_fusion.2.own_ref), channel_id=1, source_target_pairs={{0,4},{1,5},{4,0},{5,1},{8,12},{9,13},{12,8},{13,9},{2,6},{3,7},{6... | collective-permute-start | bytes 49160 | tf_op jit(solution)/shard_map/ppermute | solution.py:630
  24.8 1.7 %collective-permute-start.6 = (f32[2,16,128]{2,1,0:T(8,128)S(1)}, f32[2,16,128]{2,1,0:T(8,128)S(1)}, u32[]{:S(2)}, u32[]{:S(2)}) collective-permute-start(f32[2,16,128]{2,1,0:T(8,128)S(1)} %pad_maximum_fusion.2.own_ref), channel_id=1, source_target_pairs={{0,1},{1,0},{2,3},{3,2},{4,5},{5,4},{6,7},{7,6},{8,9},{9,8},{10,11... | collective-permute-start | bytes 49160 | tf_op jit(solution)/shard_map/ppermute | solution.py:612
  24.9 1.6 %collective-permute-start.10 = (f32[2,16,128]{2,1,0:T(8,128)S(1)}, f32[2,16,128]{2,1,0:T(8,128)S(1)}, u32[]{:S(2)}, u32[]{:S(2)}) collective-permute-start(f32[2,16,128]{2,1,0:T(8,128)S(1)} %collective-permute-done.8.even_ref), channel_id=1, source_target_pairs={{0,1},{1,0},{2,3},{3,2},{4,5},{5,4},{6,7},{7,6},{8,9},{9,8},{10,11... | collective-permute-start | bytes 49160 | tf_op jit(solution)/shard_map/ppermute | solution.py:612
  25.4 1.2 %collective-permute-start.9 = (f32[2,16,128]{2,1,0:T(8,128)S(1)}, f32[2,16,128]{2,1,0:T(8,128)S(1)}, u32[]{:S(2)}, u32[]{:S(2)}) collective-permute-start(f32[2,16,128]{2,1,0:T(8,128)S(1)} %collective-permute-done.7.odd_ref), channel_id=1, source_target_pairs={{0,1},{1,0},{2,3},{3,2},{4,5},{5,4},{6,7},{7,6},{8,9},{9,8},{10,11... | collective-permute-start | bytes 49160 | tf_op jit(solution)/shard_map/ppermute | solution.py:612

commit v11 on v10

--- a/solution.py
+++ b/solution.py
@@ -311,24 +311,22 @@
         lax.broadcasted_iota(I32, (movers, particles), 0) == column, 1.0, 0.0
     ).astype(BF16)
 
-    spread_shape = spread_ref.shape
-    line = lax.broadcasted_iota(I32, spread_shape, 0)
-    from_group = line >> 3
-    plane = from_group >> 1
-    from_x = 1 - ((plane >> 1) if fold_y else ((plane * 43) >> 7))
-    side_y = plane - (1 - from_x) * options_y
+    line = lax.broadcasted_iota(I32, spread_ref.shape, 1)
+    direction = line >> 3
+    direction = direction + jnp.where(direction > 12, 1, 0)
+    plane = (direction * 57) >> 9
+    from_z = direction - 3 * ((direction * 43) >> 7) - 1
+    from_y = ((direction * 43) >> 7) - 3 * plane - 1
     if fold_y:
-        from_y = jnp.where(side_y == 0, 0, jnp.where(index_y == 0, 1, -1))
+        side_y = jnp.where(from_y == 0, 0, 1)
+        valid = (from_y == 0) | (from_y == 1 - 2 * index_y)
     else:
-        from_y = jnp.where(side_y == 0, 0, jnp.where(side_y == 1, 1, -1))
-    from_z = jnp.where((from_group & 1) == 0, 0, jnp.where(index_z == 0, 1, -1))
-    direction = (from_x + 1) * 9 + (from_y + 1) * 3 + from_z + 1
-    direction = direction - jnp.where(direction > 13, 1, 0)
-    column = direction * CAP + (line & 7)
-    valid = (lax.broadcasted_iota(I32, spread_shape, 1) == column) & (
-        (from_x != 0) | (from_y != 0) | (from_z != 0)
-    )
-    spread_ref[...] = jnp.where(valid, 1.0, 0.0).astype(BF16)
+        side_y = jnp.where(from_y < 0, 2, from_y)
+        valid = from_y < 2
+    side_z = jnp.where(from_z == 0, 0, 1)
+    valid = valid & ((from_z == 0) | (from_z == 1 - 2 * index_z)) & (line < 26 * CAP)
+    target = ((2 - plane) * options_y + side_y) * 2 + side_z
+    spread_ref[...] = jnp.where(valid, target * CAP + (line & 7), -1)
 
     for copy in copies[1:-1]:
         copy.wait()
@@ -548,12 +546,8 @@
 def finish_kernel(
     sizes,
     moved_ref,
-    own_ref,
-    odd_ref,
-    even_ref,
-    own_zed,
-    odd_zed,
-    even_zed,
+    tiles_ref,
+    zeds_ref,
     spread_ref,
     inward_ref,
     encoder_w_ref,
@@ -575,7 +569,7 @@
     fold_y = count_y == 2
     index_x = lax.axis_index("gx")
     options_y = 2 if fold_y else 3
-    lanes = own_ref.shape[-1]
+    lanes = tiles_ref.shape[-1]
     group = lax.broadcasted_iota(I32, (ROWS, lanes), 1) >> 3
     even = (index_x & 1) == 0
     found = jnp.zeros((ROWS, lanes), F32)
@@ -584,10 +578,8 @@
             for from_z in range(2):
                 if source_x == 0 and from_y == 0 and from_z == 0:
                     continue
-                if from_z == 0:
-                    own, first, second = own_ref, even_ref, odd_ref
-                else:
-                    own, first, second = own_zed, even_zed, odd_zed
+                ref = tiles_ref if from_z == 0 else zeds_ref
+                own, second, first = ref.at[0], ref.at[1], ref.at[2]
                 side_y = from_y if fold_y or from_y == 0 else 3 - from_y
                 target = ((1 - source_x) * options_y + side_y) * 2 + from_z
                 if source_x == 0:
@@ -600,7 +592,17 @@
                     tile = jnp.where(even, first[from_y], second[from_y])
                     there = (group == target) & (index_x < count_x - 1)
                 found = jnp.where(there, tile, found)
-    arrived = joined(dot(thirds(found), spread_ref[...]))
+    halves = []
+    for at in range(0, spread_ref.shape[1], 128):
+        lane = jnp.broadcast_to(spread_ref[0:1, at : at + 128], (ROWS, 128))
+        half = jnp.zeros((ROWS, 128), F32)
+        for base in range(0, lanes, 128):
+            index = jnp.clip(lane - base, 0, 127)
+            there = (lane >= base) & (lane < base + 128)
+            part = jnp.take_along_axis(found[:, base : base + 128], index, axis=1)
+            half = jnp.where(there, part, half)
+        halves.append(half)
+    arrived = jnp.concatenate(halves, axis=1)[:, : 26 * CAP]
     for j in range(9):
         arrived_state_ref[j, 0, 0] = arrived[j : j + 1]
     arrived_latent_ref[0, 0, 0] = encode(
@@ -710,14 +712,15 @@
     core = lax.axis_index("gz")
     if fold_y:
         row = 1 - lax.axis_index("gy")
-        sides = [swap(inner[:, 0], "gy")]
         beside = lax.dynamic_index_in_dim(own_zed[:, :, 0], 1 - core, 0, False)
         corner = jnp.concatenate(
             [lax.dynamic_slice_in_dim(part, row, 1, 0) for part in (end[:, 0], beside)], axis=0
         )
         both = jnp.stack([end[:, 0], beside])
-        corner = corner[:, None]
-        mine = [swap_chips(corner, True), swap_chips(both, False)]
+        corner, inner = lax.optimization_barrier((corner, inner))
+        mine = [swap_chips(corner[:, None], True)]
+        sides = [swap(inner[:, 0], "gy")]
+        mine.append(swap_chips(both, False))
     else:
         sides = [shift(latent[:, 1, 0], "gy", 0), shift(latent[:, 0, 0], "gy", 1)]
         side_zeds = [swap(part, "gz") for part in sides]
@@ -740,7 +743,7 @@
             ((2, 2, 1, slots), F32),
             (neighbours.shape, I32),
             (edge_latent.shape, BF16),
-            ((movers, 26 * CAP), BF16),
+            ((8, 256), I32),
             ((width, particles), F32),
             ((width, particles), F32),
             ((8, particles), F32),
@@ -784,7 +787,7 @@
         + [latent],
         5_000_000_000,
     )
-    sides, mine, ranked = lax.optimization_barrier((sides, mine, ranked))
+    mine, sides, ranked = lax.optimization_barrier((mine, sides, ranked))
     (
         weights,
         decoder_out,
@@ -872,8 +875,8 @@
     second = edges(1)
     sided = [swap_x(tiles, 1), swap_x(tiles, 0)]
     sided, second = lax.optimization_barrier((sided, second))
-    tiles = [tiles, *sided]
-    zeds = [swap(part, "gz") for part in tiles]
+    tiles = jnp.stack([tiles, *sided], axis=0)
+    zeds = swap(tiles, "gz")
     state = call(
         nodes_kernel,
         "nodes",
@@ -887,7 +890,7 @@
     return call(
         functools.partial(finish_kernel, sizes),
         "finish",
-        [VMEM] * 10,
+        [VMEM] * 6,
         [
             (node_latent.shape, BF16),
             ((9,) + node_latent.shape[:4], F32),
@@ -895,7 +898,7 @@
             ((9, 1, 1, 1, 26 * CAP), F32),
         ],
         [],
-        (state, *tiles, *zeds, spread, inward, encoder_weights),
+        (state, tiles, zeds, spread, inward, encoder_weights),
         1_000_000_000,
     )
 

time: 28.5 us -> 28.3 us (level)
  starting transfers between devices: 10.3 us -> 9.65 us
  waiting for transfers between devices: 1.42 us -> 2 us
    ppermute x7 -> x5, starting transfers between devices: 5.29 us -> 2.69 us  [swap(): return lax.ppermute(values, axis, [(0, 1), (1, 0)])]
    ppermute x2, starting transfers between devices: 1.82 us -> 3.75 us  [swap_chips(): return lax.ppermute(values, ('gx', 'gy', 'gz'), pairs)]
    ppermute x7 -> x5, waiting for transfers between devices: 0.43 us -> 1.73 us  [swap(): return lax.ppermute(values, axis, [(0, 1), (1, 0)])]
    ppermute x2, waiting for transfers between devices: 0.99 us -> 0.26 us  [swap_chips(): return lax.ppermute(values, ('gx', 'gy', 'gz'), pairs)]
  transfers between devices with their start and end apart: 11 -> 9, of which waited for: 3 -> 5; matrix products, arithmetic and copies ran while one was open for 0% -> 0% of each run, Pallas kernels for 41% -> 42%
where the time goes in v11:
time: 28.3 us; the launch traced here: 28.1 us
  Pallas kernels  15.5 us (55%)
  starting transfers between devices  9.65 us (34%)
  waiting for transfers between devices  2 us (7%)
  between operations  0.8 us (3%)
    pallas_call x8, Pallas kernels, call(): pl.pallas_call(kernel, out_shape=tuple((jax.ShapeDtypeStruct(shape, kind)...  15.5 us
    ppermute x2, starting transfers between devices, swap_chips(): return lax.ppermute(values, ('gx', 'gy', 'gz'), pairs)  3.75 us
    ppermute x2, starting transfers between devices, swap_x(): return lax.ppermute(values, ('gx', 'gz'), pairs)  3.21 us
    ppermute x5, starting transfers between devices, swap(): return lax.ppermute(values, axis, [(0, 1), (1, 0)])  2.69 us
    ppermute x5, waiting for transfers between devices, swap(): return lax.ppermute(values, axis, [(0, 1), (1, 0)])  1.73 us
  transfers between devices with their start and end apart: 9, of which 5 were waited for; matrix products, arithmetic and copies ran while one was open for 0% of the time, Pallas kernels for 42%

profile of v11, /device:TPU:0, one launch (start us, length us, event | category | flops | bytes accessed | tf_op | source)
XLA Modules:
  0.0 28.1 jit_solution(15899697785878625659)
XLA Ops:
  0.6 0.5 %collective-permute-start = (bf16[2,2,1,128,128]{4,3,2,1,0:T(8,128)(2,1)}, bf16[2,2,1,128,128]{4,3,2,1,0:T(8,128)(2,1)S(1)}, u32[]{:S(2)}, u32[]{:S(2)}) collective-permute-start(bf16[2,2,1,128,128]{4,3,2,1,0:T(8,128)(2,1)} %latent_any.1), channel_id=1, source_target_pairs={{0,1},{1,0},{2,3},{3,2},{4,5},{5,4},{6,7},{7,6},{8,9},{9,8},{10,11... | collective-permute-start | bytes 393224 | tf_op jit(solution)/shard_map/ppermute | solution.py:614
  1.1 1.0 %cut.1 = (bf16[2,2,1,128,128]{4,3,2,1,0:T(8,128)(2,1)S(1)}, bf16[2,1,128,128]{3,2,1,0:T(8,128)(2,1)S(1)}, bf16[2,1,128,128]{3,2,1,0:T(8,128)(2,1)S(1)}) custom-call(bf16[2,2,1,128,128]{4,3,2,1,0:T(8,128)(2,1)} %latent_any.1), custom_call_target="tpu_custom_call" | custom-call | flops 1000000 | tf_op jit(solution)/shard_map/cut/pallas_call | solution.py:651
  2.1 0.2 collective-permute-done.own_zed
  2.4 3.7 %collective-permute-start.1 = (bf16[2,1,128,128]{3,2,1,0:T(8,128)(2,1)S(1)}, bf16[2,1,128,128]{3,2,1,0:T(8,128)(2,1)S(1)}, u32[]{:S(2)}, u32[]{:S(2)}) collective-permute-start(bf16[2,1,128,128]{3,2,1,0:T(8,128)(2,1)S(1)} %bitcast.26), channel_id=1, source_target_pairs={{0,7},{1,3},{2,5},{3,1},{4,11},{5,2},{6,9},{7,0},{8,15},{9,6},{10,... | collective-permute-start | bytes 196616 | tf_op jit(solution)/shard_map/ppermute | solution.py:647
  6.0 0.5 %collective-permute-start.3 = (bf16[2,128,128]{2,1,0:T(8,128)(2,1)S(1)}, bf16[2,128,128]{2,1,0:T(8,128)(2,1)S(1)}, u32[]{:S(2)}, u32[]{:S(2)}) collective-permute-start(bf16[2,128,128]{2,1,0:T(8,128)(2,1)S(1)} %bitcast.25), channel_id=1, source_target_pairs={{0,2},{2,0},{1,3},{3,1},{4,6},{6,4},{5,7},{7,5},{8,10},{10,8},{9,1... | collective-permute-start | bytes 196616 | tf_op jit(solution)/shard_map/ppermute | solution.py:614
  6.6 0.1 collective-permute-start.2
  6.7 3.1 %ranks.1 = (bf16[11,128,128]{2,1,0:T(8,128)(2,1)S(1)}, bf16[3,128]{1,0:T(4,128)(2,1)S(1)}, bf16[48,128]{1,0:T(8,128)(2,1)S(1)}, bf16[2,128,128]{2,1,0:T(8,128)(2...) custom-call(s32[2,1,2]{2,1,0:T(1,128)} %bitcast.31, ...), custom_call_target="tpu_custom_call" | custom-call | flops 5000000000 | tf_op jit(solution)/shard_map/ranks/pallas_call | solution.py:651
  9.8 0.0 collective-permute-done.1
  9.8 1.0 %collective-permute-done.3.refs_0_ = bf16[2,128,128]{2,1,0:T(8,128)(2,1)S(1)} collective-permute-done((bf16[2,128,128]{2,1,0:T(8,128)(2,1)S(1)}, bf16[2,128,128]{2,1,0:T(8,128)(2,1)S(1)}, u32[]{:S(2)}, u32[]{:S(2)}) %collective-permute-start.3) | collective-permute-done | bytes 65568 | tf_op jit(solution)/shard_map/ppermute | solution.py:614
  10.8 0.3 collective-permute-done.2
  11.1 0.1 collective-permute-start.4
  11.2 1.2 %prepare.1 = (bf16[4,128,256]{2,1,0:T(8,128)(2,1)S(1)}, bf16[3,128,256]{2,1,0:T(8,128)(2,1)S(1)}, f32[128,1536]{1,0:T(8,128)S(1)}) custom-call(bf16[2,2,1,128,128]{4,3,2,1,0:T(8,128)(2,1)S(1)} %get-tuple-element.68.latent_ref, bf16[2,2,1,128,128]{4,3,2,1,0:T(8,128)(2,1)S(1)} %collective-permute-done.own_zed, ...), custom_call_target="tpu_custom_call" | custom-call | flops 5000000000 | tf_op jit(solution)/shard_map/prepare/pallas_call | solution.py:651
  12.4 0.4 %collective-permute-done.4 = bf16[8,128,128]{2,1,0:T(8,128)(2,1)S(1)} collective-permute-done((bf16[8,128,128]{2,1,0:T(8,128)(2,1)S(1)}, bf16[8,128,128]{2,1,0:T(8,128)(2,1)S(1)}, u32[]{:S(2)}, u32[]{:S(2)}) %collective-permute-start.4) | collective-permute-done | bytes 262176 | tf_op jit(solution)/shard_map/ppermute | solution.py:614
  12.8 2.2 %movers.1 = (bf16[8,128,256]{2,1,0:T(8,128)(2,1)S(1)}, f32[16,128]{1,0:T(8,128)S(1)}) custom-call(bf16[2,128,128]{2,1,0:T(8,128)(2,1)S(1)} %collective-permute-done.3.refs_0_, bf16[2,128,128]{2,1,0:T(8,128)(2,1)S(1)} %slice.6.refs_1_, bf16[2,3,128,128]{3,2,1,0:T(8,128)(2,1)S(1)} %bitcast.22, bf16[3,128,256]{2,1,0:T(8,128)(2,1)S(1)} %get-tuple-element.99.refs_3_, ...), custom_call_target="tpu_custom_call" | custom-call | flops 3000000000 | tf_op jit(solution)/shard_map/movers/pallas_call | solution.py:651
  14.9 1.5 %collective-permute-start.5 = (f32[16,128]{1,0:T(8,128)S(1)}, f32[16,128]{1,0:T(8,128)S(1)}, u32[]{:S(2)}, u32[]{:S(2)}) collective-permute-start(f32[16,128]{1,0:T(8,128)S(1)} %get-tuple-element.105), channel_id=1, source_target_pairs={{0,2},{2,0},{1,3},{3,1},{4,6},{6,4},{5,7},{7,5},{8,10},{10,8},{9,1... | collective-permute-start | bytes 24584 | tf_op jit(solution)/shard_map/ppermute | solution.py:614
  16.4 2.8 %edges.2.first_ref = bf16[2,128,128]{2,1,0:T(8,128)(2,1)S(1)} custom-call(f32[2,2,1,128]{3,2,1,0:T(1,128)S(1)} %get-tuple-element.106.alive_ref, bf16[2,2,1,128,128]{4,3,2,1,0:T(8,128)(2,1)S(1)} %get-tuple-element.68.latent_ref, bf16[2,2,1,12,128,128]{5,4,3,2,1,0:T(8,128)(2,1)S(1)} %get-tuple-element.107.edge_ref, ...), custom_call_target="tpu_custom_call" | custom-call | flops 4000000000 | tf_op jit(solution)/shard_map/edges/pallas_call | solution.py:651
  19.3 0.1 collective-permute-start.6
  19.3 3.1 %collective-permute-start.7 = (f32[2,16,128]{2,1,0:T(8,128)S(1)}, f32[2,16,128]{2,1,0:T(8,128)S(1)}, u32[]{:S(2)}, u32[]{:S(2)}) collective-permute-start(f32[2,16,128]{2,1,0:T(8,128)S(1)} %get-tuple-element.125), channel_id=1, source_target_pairs={{0,4},{1,5},{4,0},{5,1},{8,12},{9,13},{12,8},{13,9},{2,6},{3,7},{6... | collective-permute-start | bytes 49160 | tf_op jit(solution)/shard_map/ppermute | solution.py:632
  22.5 2.8 %edges.3.second_ref = bf16[2,128,128]{2,1,0:T(8,128)(2,1)S(1)} custom-call(f32[2,2,1,128]{3,2,1,0:T(1,128)S(1)} %get-tuple-element.106.alive_ref, bf16[2,2,1,128,128]{4,3,2,1,0:T(8,128)(2,1)S(1)} %get-tuple-element.68.latent_ref, bf16[2,2,1,12,128,128]{5,4,3,2,1,0:T(8,128)(2,1)S(1)} %get-tuple-element.107.edge_ref, ...), custom_call_target="tpu_custom_call" | custom-call | flops 4000000000 | tf_op jit(solution)/shard_map/edges/pallas_call | solution.py:651
  25.3 0.0 collective-permute-done.6
  25.3 0.1 collective-permute-start.8
  25.4 1.0 %nodes.1.moved_ref = f32[16,512]{1,0:T(8,128)S(1)} custom-call(bf16[2,128,128]{2,1,0:T(8,128)(2,1)S(1)} %edges.2.first_ref, bf16[2,128,128]{2,1,0:T(8,128)(2,1)S(1)} %edges.3.second_ref, f32[128,512]{1,0:T(8,128)S(1)} %get-tuple-element.116.node_pre_ref, f32[128,512]{1,0:T(8,128)S(1)} %get-tuple-element.117.latent_t_ref, ...), custom_call_target="tpu_custom_call" | custom-call | flops 1000000000 | tf_op jit(solution)/shard_map/nodes/pallas_call | solution.py:651
  26.4 0.2 collective-permute-done.8.zeds_ref
  26.6 1.5 %finish.1 = (bf16[2,2,1,128,128]{4,3,2,1,0:T(8,128)(2,1)}, f32[9,2,2,1,128]{4,3,2,1,0:T(1,128)}, bf16[1,1,1,208,128]{4,3,2,1,0:T(8,128)(2,1)}, f32[9,1,1,1,208]{4,3,2,1,0:T(1,128)}) custom-call(f32[16,512]{1,0:T(8,128)S(1)} %nodes.1.moved_ref, f32[3,2,16,128]{3,2,1,0:T(8,128)S(1)} %pad_maximum_fusion.3.tiles_ref, ...), custom_call_target="tpu_custom_call" | custom-call | flops 1000000000 | tf_op jit(solution)/shard_map/finish/pallas_call | solution.py:651
  (14 shorter events, 0.1 us)
Async XLA Ops:
  0.6 1.7 %collective-permute-start = (bf16[2,2,1,128,128]{4,3,2,1,0:T(8,128)(2,1)}, bf16[2,2,1,128,128]{4,3,2,1,0:T(8,128)(2,1)S(1)}, u32[]{:S(2)}, u32[]{:S(2)}) collective-permute-start(bf16[2,2,1,128,128]{4,3,2,1,0:T(8,128)(2,1)} %latent_any.1), channel_id=1, source_target_pairs={{0,1},{1,0},{2,3},{3,2},{4,5},{5,4},{6,7},{7,6},{8,9},{9,8},{10,11... | collective-permute-start | bytes 393224 | tf_op jit(solution)/shard_map/ppermute | solution.py:614
  2.4 7.5 %collective-permute-start.1 = (bf16[2,1,128,128]{3,2,1,0:T(8,128)(2,1)S(1)}, bf16[2,1,128,128]{3,2,1,0:T(8,128)(2,1)S(1)}, u32[]{:S(2)}, u32[]{:S(2)}) collective-permute-start(bf16[2,1,128,128]{3,2,1,0:T(8,128)(2,1)S(1)} %bitcast.26), channel_id=1, source_target_pairs={{0,7},{1,3},{2,5},{3,1},{4,11},{5,2},{6,9},{7,0},{8,15},{9,6},{10,... | collective-permute-start | bytes 196616 | tf_op jit(solution)/shard_map/ppermute | solution.py:647
  6.0 4.8 %collective-permute-start.3 = (bf16[2,128,128]{2,1,0:T(8,128)(2,1)S(1)}, bf16[2,128,128]{2,1,0:T(8,128)(2,1)S(1)}, u32[]{:S(2)}, u32[]{:S(2)}) collective-permute-start(bf16[2,128,128]{2,1,0:T(8,128)(2,1)S(1)} %bitcast.25), channel_id=1, source_target_pairs={{0,2},{2,0},{1,3},{3,1},{4,6},{6,4},{5,7},{7,5},{8,10},{10,8},{9,1... | collective-permute-start | bytes 196616 | tf_op jit(solution)/shard_map/ppermute | solution.py:614
  6.6 4.5 %collective-permute-start.2 = (bf16[2,2,128,128]{3,2,1,0:T(8,128)(2,1)S(1)}, bf16[2,2,128,128]{3,2,1,0:T(8,128)(2,1)S(1)}, u32[]{:S(2)}, u32[]{:S(2)}) collective-permute-start(bf16[2,2,128,128]{3,2,1,0:T(8,128)(2,1)S(1)} %pad_maximum_fusion.1), channel_id=1, source_target_pairs={{0,5},{1,3},{2,7},{3,1},{4,9},{5,0},{6,11},{7,2},{8,13},{9,4},{10,... | collective-permute-start | bytes 393224 | tf_op jit(solution)/shard_map/ppermute | solution.py:647
  11.1 1.6 %collective-permute-start.4 = (bf16[8,128,128]{2,1,0:T(8,128)(2,1)S(1)}, bf16[8,128,128]{2,1,0:T(8,128)(2,1)S(1)}, u32[]{:S(2)}, u32[]{:S(2)}) collective-permute-start(bf16[8,128,128]{2,1,0:T(8,128)(2,1)S(1)} %pad_maximum_fusion), channel_id=1, source_target_pairs={{0,1},{1,0},{2,3},{3,2},{4,5},{5,4},{6,7},{7,6},{8,9},{9,8},{10,11... | collective-permute-start | bytes 786440 | tf_op jit(solution)/shard_map/ppermute | solution.py:614
  14.9 4.3 %collective-permute-start.5 = (f32[16,128]{1,0:T(8,128)S(1)}, f32[16,128]{1,0:T(8,128)S(1)}, u32[]{:S(2)}, u32[]{:S(2)}) collective-permute-start(f32[16,128]{1,0:T(8,128)S(1)} %get-tuple-element.105), channel_id=1, source_target_pairs={{0,2},{2,0},{1,3},{3,1},{4,6},{6,4},{5,7},{7,5},{8,10},{10,8},{9,1... | collective-permute-start | bytes 24584 | tf_op jit(solution)/shard_map/ppermute | solution.py:614
  19.3 6.0 %collective-permute-start.6 = (f32[2,16,128]{2,1,0:T(8,128)S(1)}, f32[2,16,128]{2,1,0:T(8,128)S(1)}, u32[]{:S(2)}, u32[]{:S(2)}) collective-permute-start(f32[2,16,128]{2,1,0:T(8,128)S(1)} %get-tuple-element.125), channel_id=1, source_target_pairs={{0,1},{1,0},{4,8},{5,9},{8,4},{9,5},{12,13},{13,12},{2,3},{3,2},{6... | collective-permute-start | bytes 49160 | tf_op jit(solution)/shard_map/ppermute | solution.py:632
  19.3 5.9 %collective-permute-start.7 = (f32[2,16,128]{2,1,0:T(8,128)S(1)}, f32[2,16,128]{2,1,0:T(8,128)S(1)}, u32[]{:S(2)}, u32[]{:S(2)}) collective-permute-start(f32[2,16,128]{2,1,0:T(8,128)S(1)} %get-tuple-element.125), channel_id=1, source_target_pairs={{0,4},{1,5},{4,0},{5,1},{8,12},{9,13},{12,8},{13,9},{2,6},{3,7},{6... | collective-permute-start | bytes 49160 | tf_op jit(solution)/shard_map/ppermute | solution.py:632
  25.3 1.3 %collective-permute-start.8 = (f32[3,2,16,128]{3,2,1,0:T(8,128)S(1)}, f32[3,2,16,128]{3,2,1,0:T(8,128)S(1)}, u32[]{:S(2)}, u32[]{:S(2)}) collective-permute-start(f32[3,2,16,128]{3,2,1,0:T(8,128)S(1)} %pad_maximum_fusion.3.tiles_ref), channel_id=1, source_target_pairs={{0,1},{1,0},{2,3},{3,2},{4,5},{5,4},{6,7},{7,6},{8,9},{9,8},{10,11... | collective-permute-start | bytes 147464 | tf_op jit(solution)/shard_map/ppermute | solution.py:614

commit v12 on v11

--- a/solution.py
+++ b/solution.py
@@ -142,6 +142,9 @@
         self.outer_rows = (2,) if fold_y else (0, 3)
         self.own_ref, self.rest_ref = own_ref, rest_ref
 
+    def own_columns(self):
+        return [(ex, row) for ex in (1, 2) for row in self.own_rows]
+
     def own(self, ex, row):
         return (ex - 1) * 2 + self.own_rows.index(row)
 
@@ -183,18 +186,9 @@
     return jnp.concatenate([position + new_velocity, new_velocity, velocity], axis=0)
 
 
-def cut_kernel(fold_y, latent_any, latent_ref, edge_ref, inner_ref, sems):
+def cut_kernel(latent_any, latent_ref, edge_ref, sems):
     end = 1 - lax.axis_index("gz")
-    inner = 1 - lax.axis_index("gy") if fold_y else 0
-    copies = fetch(
-        [
-            (latent_any, latent_ref),
-            (latent_any.at[end], edge_ref),
-            (latent_any.at[0, inner], inner_ref.at[0]),
-            (latent_any.at[1, inner], inner_ref.at[1]),
-        ],
-        sems,
-    )
+    copies = fetch([(latent_any, latent_ref), (latent_any.at[end], edge_ref)], sems)
     for copy in copies:
         copy.wait()
 
@@ -215,6 +209,7 @@
     velocity_any,
     edge_any,
     latent_ref,
+    own_zed,
     weights_ref,
     decoder_out_ref,
     inward_ref,
@@ -233,6 +228,8 @@
     mover_node_pre_ref,
     mover_latent_ref,
     mover_state_ref,
+    far_ref,
+    early_ref,
     positions_ref,
     velocity_ref,
     owners_ref,
@@ -370,6 +367,20 @@
     place, key = places(ids[:neighbour_count], ids[neighbour_count : 2 * neighbour_count], fold_y)
     mover_place_ref[...] = jnp.concatenate([place[k : k + 1] for k in range(neighbour_count)], axis=1)
     mover_key_ref[...] = jnp.concatenate([key[k : k + 1] for k in range(neighbour_count)], axis=1)
+
+    window = Window(fold_y, far_ref)
+    for (ex, row), (a, b) in zip(window.own_columns(), CELLS):
+        pair = jnp.concatenate([latent_ref[a, b, 0], own_zed[a, b, 0]], axis=0)
+        far_ref[window.own(ex, row)] = dot_nt(weights_ref[FAR], pair).astype(BF16)
+    cells = window.cells(window.own_columns())
+    for a in range(2):
+        b = 1 - index_y if fold_y else 1
+        ids = jnp.concatenate([neighbours_ref[a, b, k] for k in range(neighbour_count)], axis=1)
+        place, key = places(ids & 127, ids >> 7, fold_y)
+        for tile in range(ids.shape[1] // TILE):
+            at = slice(tile * TILE, (tile + 1) * TILE)
+            early_ref[a, :, at] = pick(cells, place[:, at], key[:, at]).astype(BF16)
+
     copies[-1].wait()
     for k in range(neighbour_count):
         rows = jnp.concatenate([edge_ref[a, b, 0, k] for a, b in CELLS], axis=0)
@@ -378,26 +389,20 @@
 
 def prepare_kernel(
     sizes,
-    latent_ref,
-    own_zed,
+    far_ref,
     mine_ref,
     weights_ref,
     edge_ref,
     place_ref,
     key_ref,
     near_ref,
-    far_ref,
     far_mine_ref,
     pre_ref,
 ):
     window = Window(sizes[1] == 2, far_ref)
     core = lax.axis_index("gz")
     far_t = weights_ref[FAR]
-    columns = [(ex, row) for ex in (1, 2) for row in window.own_rows]
-    for (ex, row), (a, b) in zip(columns, CELLS):
-        pair = jnp.concatenate([latent_ref[a, b, 0], own_zed[a, b, 0]], axis=0)
-        far_ref[window.own(ex, row)] = dot_nt(far_t, pair).astype(BF16)
-    cells = window.cells(columns)
+    cells = window.cells(window.own_columns())
     for row in range(window.row_count):
         pair = jnp.concatenate([mine_ref[1, row], mine_ref[0, row]], axis=0)
         far_mine_ref[row] = dot_nt(far_t, pair).astype(BF16)
@@ -482,6 +487,7 @@
     neighbours_ref,
     far_own_ref,
     far_rest_ref,
+    early_ref,
     weights_ref,
     total_ref,
     hidden_ref,
@@ -501,14 +507,19 @@
             b = bt
             rows = (bt, bt + 1, bt + 2)
         columns = [(ex, row) for ex in range(a, a + 3) for row in rows]
+        if bt == 1:
+            columns = [column for column in columns if column not in window.own_columns()]
         near = dot_nt(weights_ref[NEAR], latent_ref[b, 0])
         near = jnp.concatenate([near, near], axis=1)
         ids = jnp.concatenate([neighbours_ref[b, k] for k in range(neighbour_count)], axis=1)
         place, key = places(ids & 127, ids >> 7, fold_y)
 
-        def pre(tile, b=b, near=near):
+        def pre(tile, b=b, bt=bt, near=near):
             edges = jnp.concatenate([edge_ref[b, 0, 2 * tile], edge_ref[b, 0, 2 * tile + 1]], axis=0)
-            return dot_nt(weights_ref[EDGE], edges) + near
+            terms = dot_nt(weights_ref[EDGE], edges) + near
+            if bt == 1:
+                terms = terms + early_ref[a, :, tile * TILE : (tile + 1) * TILE].astype(F32)
+            return terms
 
         message = messages(
             window.cells(columns),
@@ -696,16 +707,14 @@
     neighbours = neighbours.reshape(2, 2, neighbour_count, 1, slots)
 
     own_zed = swap(node_latent, "gz")
-    latent, end, inner = call(
-        functools.partial(cut_kernel, fold_y),
+    if fold_y:
+        sides = [swap(node_latent, "gy")]
+    latent, end = call(
+        cut_kernel,
         "cut",
         [ANY],
-        [
-            (node_latent.shape, BF16),
-            (node_latent.shape[1:], BF16),
-            ((2, 1, slots, width), BF16),
-        ],
-        [pltpu.SemaphoreType.DMA((4,))],
+        [(node_latent.shape, BF16), (node_latent.shape[1:], BF16)],
+        [pltpu.SemaphoreType.DMA((2,))],
         (in_hbm(node_latent),),
         1_000_000,
     )
@@ -717,10 +726,7 @@
             [lax.dynamic_slice_in_dim(part, row, 1, 0) for part in (end[:, 0], beside)], axis=0
         )
         both = jnp.stack([end[:, 0], beside])
-        corner, inner = lax.optimization_barrier((corner, inner))
-        mine = [swap_chips(corner[:, None], True)]
-        sides = [swap(inner[:, 0], "gy")]
-        mine.append(swap_chips(both, False))
+        mine = [swap_chips(corner[:, None], True), swap_chips(both, False)]
     else:
         sides = [shift(latent[:, 1, 0], "gy", 0), shift(latent[:, 0, 0], "gy", 1)]
         side_zeds = [swap(part, "gz") for part in sides]
@@ -734,7 +740,7 @@
     ranked = call(
         functools.partial(ranks_kernel, sizes),
         "ranks",
-        [SMEM] + [ANY] * 12 + [VMEM],
+        [SMEM] + [ANY] * 12 + [VMEM] * 2,
         [
             ((11, width, width), BF16),
             (decoder_out.shape, BF16),
@@ -754,6 +760,8 @@
             ((width, movers), F32),
             ((width, movers), F32),
             ((8, movers), F32),
+            ((4, width, 2 * slots), BF16),
+            ((2, width, neighbour_count * slots), BF16),
         ],
         [
             like(positions),
@@ -784,7 +792,7 @@
                 edge_latent,
             )
         ]
-        + [latent],
+        + [latent, own_zed],
         5_000_000_000,
     )
     mine, sides, ranked = lax.optimization_barrier((mine, sides, ranked))
@@ -807,9 +815,12 @@
         mover_node_pre,
         mover_latent,
         mover_state,
+        far_own,
+        early,
     ) = ranked
     mine = jnp.concatenate(mine[::-1], axis=1)
     if fold_y:
+        sides = [lax.dynamic_index_in_dim(sides[0][:, :, 0], lax.axis_index("gy"), 1, False)]
         packed = jnp.concatenate([mine.reshape(-1, slots, width), sides[0]], axis=0)
     else:
         packed = mine.reshape(-1, slots, width)
@@ -817,21 +828,17 @@
     prepared = call(
         functools.partial(prepare_kernel, sizes),
         "prepare",
-        [VMEM] * 8,
-        [
-            ((4, width, 2 * slots), BF16),
-            ((rows, width, 2 * slots), BF16),
-            ((width, neighbour_count * movers), F32),
-        ],
+        [VMEM] * 7,
+        [((rows, width, 2 * slots), BF16), ((width, neighbour_count * movers), F32)],
         [],
-        (latent, own_zed, mine, weights, mover_edges, mover_place, mover_key, mover_near),
+        (far_own, mine, weights, mover_edges, mover_place, mover_key, mover_near),
         5_000_000_000,
     )
     packed, prepared = lax.optimization_barrier((packed, prepared))
     cells = mine.shape[0] * mine.shape[1]
     if fold_y:
         side_zeds = [packed[cells:]]
-    far_own, far_mine, mover_pre = prepared
+    far_mine, mover_pre = prepared
     halo = [*sides, *side_zeds, packed[:cells].reshape(mine.shape), far_mine]
 
     far_rest, bucket = call(
@@ -858,10 +865,10 @@
         return call(
             functools.partial(edges_kernel, sizes, a),
             "edges",
-            [VMEM] * 7,
+            [VMEM] * 8,
             [((2, width, slots), BF16)],
             [pltpu.VMEM((2, width, neighbour_count * slots), BF16)],
-            (alive, latent, edge_latent, neighbours, far_own, far_rest, weights),
+            (alive, latent, edge_latent, neighbours, far_own, far_rest, early, weights),
             4_000_000_000,
         )[0]
 

time: 28.3 us -> 27.1 us (0.958)
  waiting for transfers between devices: 2 us -> 0.62 us
    ppermute x5, starting transfers between devices: 2.69 us -> 4.86 us  [swap(): return lax.ppermute(values, axis, [(0, 1), (1, 0)])]
    ppermute x2, starting transfers between devices: 3.75 us -> 1.78 us  [swap_chips(): return lax.ppermute(values, ('gx', 'gy', 'gz'), pairs)]
    ppermute x5, waiting for transfers between devices: 1.73 us -> 0.54 us  [swap(): return lax.ppermute(values, axis, [(0, 1), (1, 0)])]
  transfers between devices with their start and end apart: 9 -> 9, of which waited for: 5 -> 3; matrix products, arithmetic and copies ran while one was open for 0% -> 0% of each run, Pallas kernels for 42% -> 44%
where the time goes in v12:
time: 27.1 us; the launch traced here: 26.9 us
  Pallas kernels  15.5 us (57%)
  starting transfers between devices  9.84 us (36%)
  between operations  0.82 us (3%)
  waiting for transfers between devices  0.62 us (2%)
    pallas_call x8, Pallas kernels, call(): pl.pallas_call(kernel, out_shape=tuple((jax.ShapeDtypeStruct(shape, kind)...  15.5 us
    ppermute x5, starting transfers between devices, swap(): return lax.ppermute(values, axis, [(0, 1), (1, 0)])  4.86 us
    ppermute x2, starting transfers between devices, swap_x(): return lax.ppermute(values, ('gx', 'gz'), pairs)  3.2 us
    ppermute x2, starting transfers between devices, swap_chips(): return lax.ppermute(values, ('gx', 'gy', 'gz'), pairs)  1.78 us
  transfers between devices with their start and end apart: 9, of which 3 were waited for; matrix products, arithmetic and copies ran while one was open for 0% of the time, Pallas kernels for 44%

profile of v12, /device:TPU:0, one launch (start us, length us, event | category | flops | bytes accessed | tf_op | source)
XLA Modules:
  0.0 26.9 jit_solution(1888619657427417387)
XLA Ops:
  0.6 0.5 %collective-permute-start = (bf16[2,2,1,128,128]{4,3,2,1,0:T(8,128)(2,1)}, bf16[2,2,1,128,128]{4,3,2,1,0:T(8,128)(2,1)S(1)}, u32[]{:S(2)}, u32[]{:S(2)}) collective-permute-start(bf16[2,2,1,128,128]{4,3,2,1,0:T(8,128)(2,1)} %latent_any.1), channel_id=1, source_target_pairs={{0,1},{1,0},{2,3},{3,2},{4,5},{5,4},{6,7},{7,6},{8,9},{9,8},{10,11... | collective-permute-start | bytes 393224 | tf_op jit(solution)/shard_map/ppermute | solution.py:625
  1.1 2.6 %collective-permute-start.3 = (bf16[2,2,1,128,128]{4,3,2,1,0:T(8,128)(2,1)}, bf16[2,2,1,128,128]{4,3,2,1,0:T(8,128)(2,1)S(1)}, u32[]{:S(2)}, u32[]{:S(2)}) collective-permute-start(bf16[2,2,1,128,128]{4,3,2,1,0:T(8,128)(2,1)} %latent_any.1), channel_id=1, source_target_pairs={{0,2},{2,0},{1,3},{3,1},{4,6},{6,4},{5,7},{7,5},{8,10},{10,8},{9,1... | collective-permute-start | bytes 393224 | tf_op jit(solution)/shard_map/ppermute | solution.py:625
  3.7 1.0 %cut.1 = (bf16[2,2,1,128,128]{4,3,2,1,0:T(8,128)(2,1)S(1)}, bf16[2,1,128,128]{3,2,1,0:T(8,128)(2,1)S(1)}) custom-call(bf16[2,2,1,128,128]{4,3,2,1,0:T(8,128)(2,1)} %latent_any.1), custom_call_target="tpu_custom_call" | custom-call | flops 1000000 | tf_op jit(solution)/shard_map/cut/pallas_call | solution.py:662
  4.7 0.0 collective-permute-done.own_zed
  4.7 1.4 %collective-permute-start.1 = (bf16[2,1,128,128]{3,2,1,0:T(8,128)(2,1)S(1)}, bf16[2,1,128,128]{3,2,1,0:T(8,128)(2,1)S(1)}, u32[]{:S(2)}, u32[]{:S(2)}) collective-permute-start(bf16[2,1,128,128]{3,2,1,0:T(8,128)(2,1)S(1)} %maximum_bitcast_fusion), channel_id=1, source_target_pairs={{0,7},{1,3},{2,5},{3,1},{4,11},{5,2},{6,9},{7,0},{8,15},{9,6},{10,... | collective-permute-start | bytes 196616 | tf_op jit(solution)/shard_map/ppermute | solution.py:658
  6.2 0.4 %collective-permute-start.2 = (bf16[2,2,128,128]{3,2,1,0:T(8,128)(2,1)S(1)}, bf16[2,2,128,128]{3,2,1,0:T(8,128)(2,1)S(1)}, u32[]{:S(2)}, u32[]{:S(2)}) collective-permute-start(bf16[2,2,128,128]{3,2,1,0:T(8,128)(2,1)S(1)} %pad_maximum_fusion.1), channel_id=1, source_target_pairs={{0,5},{1,3},{2,7},{3,1},{4,9},{5,0},{6,11},{7,2},{8,13},{9,4},{10,... | collective-permute-start | bytes 393224 | tf_op jit(solution)/shard_map/ppermute | solution.py:658
  6.5 4.0 %ranks.1 = (bf16[11,128,128]{2,1,0:T(8,128)(2,1)S(1)}, bf16[3,128]{1,0:T(4,128)(2,1)S(1)}, bf16[48,128]{1,0:T(8,128)(2,1)S(1)}, bf16[2,128,128]{2,1,0:T(8,128)(2...) custom-call(s32[2,1,2]{2,1,0:T(1,128)} %bitcast.31, ...), custom_call_target="tpu_custom_call" | custom-call | flops 5000000000 | tf_op jit(solution)/shard_map/ranks/pallas_call | solution.py:662
  10.5 0.0 collective-permute-done.3
  10.5 0.0 collective-permute-done.1
  10.5 0.1 collective-permute-done.2
  10.7 0.2 collective-permute-start.4
  10.9 1.1 %prepare.1 = (bf16[3,128,256]{2,1,0:T(8,128)(2,1)S(1)}, f32[128,1536]{1,0:T(8,128)S(1)}) custom-call(bf16[4,128,256]{2,1,0:T(8,128)(2,1)S(1)} %get-tuple-element.88.far_ref.far_own_ref, bf16[2,3,128,128]{3,2,1,0:T(8,128)(2,1)S(1)} %constant_dynamic-update-slice_fusion.mine_ref, bf16[11,128,128]{2,1,0:T(8,128)(2,1)S(1)} %get-tuple-element.89.weights_ref.refs_4_, ...), custom_call_target="tpu_custom_call" | custom-call | flops 5000000000 | tf_op jit(solution)/shard_map/prepare/pallas_call | solution.py:662
  12.0 0.3 %collective-permute-done.4 = bf16[8,128,128]{2,1,0:T(8,128)(2,1)S(1)} collective-permute-done((bf16[8,128,128]{2,1,0:T(8,128)(2,1)S(1)}, bf16[8,128,128]{2,1,0:T(8,128)(2,1)S(1)}, u32[]{:S(2)}, u32[]{:S(2)}) %collective-permute-start.4) | collective-permute-done | bytes 262176 | tf_op jit(solution)/shard_map/ppermute | solution.py:625
  12.3 2.2 %movers.1 = (bf16[8,128,256]{2,1,0:T(8,128)(2,1)S(1)}, f32[16,128]{1,0:T(8,128)S(1)}) custom-call(bf16[2,128,128]{2,1,0:T(8,128)(2,1)S(1)} %dynamic-slice_bitcast_fusion.refs_0_, bf16[2,128,128]{2,1,0:T(8,128)(2,1)S(1)} %slice.6.refs_1_, bf16[2,3,128,128]{3,2,1,0:T(8,128)(2,1)S(1)} %bitcast.24, bf16[3,128,256]{2,1,0:T(8,128)(2,1)S(1)} %get-tuple-element.97.refs_3_, ...), custom_call_target="tpu_custom_call" | custom-call | flops 3000000000 | tf_op jit(solution)/shard_map/movers/pallas_call | solution.py:662
  14.5 1.5 %collective-permute-start.5 = (f32[16,128]{1,0:T(8,128)S(1)}, f32[16,128]{1,0:T(8,128)S(1)}, u32[]{:S(2)}, u32[]{:S(2)}) collective-permute-start(f32[16,128]{1,0:T(8,128)S(1)} %get-tuple-element.103), channel_id=1, source_target_pairs={{0,2},{2,0},{1,3},{3,1},{4,6},{6,4},{5,7},{7,5},{8,10},{10,8},{9,1... | collective-permute-start | bytes 24584 | tf_op jit(solution)/shard_map/ppermute | solution.py:625
  16.0 2.4 %edges.2.first_ref = bf16[2,128,128]{2,1,0:T(8,128)(2,1)S(1)} custom-call(f32[2,2,1,128]{3,2,1,0:T(1,128)S(1)} %get-tuple-element.104.alive_ref, bf16[2,2,1,128,128]{4,3,2,1,0:T(8,128)(2,1)S(1)} %get-tuple-element.64.latent_ref, bf16[2,2,1,12,128,128]{5,4,3,2,1,0:T(8,128)(2,1)S(1)} %get-tuple-element.105.edge_ref, ...), custom_call_target="tpu_custom_call" | custom-call | flops 4000000000 | tf_op jit(solution)/shard_map/edges/pallas_call | solution.py:662
  18.4 0.1 collective-permute-start.6
  18.5 3.1 %collective-permute-start.7 = (f32[2,16,128]{2,1,0:T(8,128)S(1)}, f32[2,16,128]{2,1,0:T(8,128)S(1)}, u32[]{:S(2)}, u32[]{:S(2)}) collective-permute-start(f32[2,16,128]{2,1,0:T(8,128)S(1)} %get-tuple-element.123), channel_id=1, source_target_pairs={{0,4},{1,5},{4,0},{5,1},{8,12},{9,13},{12,8},{13,9},{2,6},{3,7},{6... | collective-permute-start | bytes 49160 | tf_op jit(solution)/shard_map/ppermute | solution.py:643
  21.7 2.4 %edges.3.second_ref = bf16[2,128,128]{2,1,0:T(8,128)(2,1)S(1)} custom-call(f32[2,2,1,128]{3,2,1,0:T(1,128)S(1)} %get-tuple-element.104.alive_ref, bf16[2,2,1,128,128]{4,3,2,1,0:T(8,128)(2,1)S(1)} %get-tuple-element.64.latent_ref, bf16[2,2,1,12,128,128]{5,4,3,2,1,0:T(8,128)(2,1)S(1)} %get-tuple-element.105.edge_ref, ...), custom_call_target="tpu_custom_call" | custom-call | flops 4000000000 | tf_op jit(solution)/shard_map/edges/pallas_call | solution.py:662
  24.0 0.0 collective-permute-done.6
  24.1 0.1 collective-permute-start.8
  24.1 1.0 %nodes.1.moved_ref = f32[16,512]{1,0:T(8,128)S(1)} custom-call(bf16[2,128,128]{2,1,0:T(8,128)(2,1)S(1)} %edges.2.first_ref, bf16[2,128,128]{2,1,0:T(8,128)(2,1)S(1)} %edges.3.second_ref, f32[128,512]{1,0:T(8,128)S(1)} %get-tuple-element.114.node_pre_ref, f32[128,512]{1,0:T(8,128)S(1)} %get-tuple-element.115.latent_t_ref, ...), custom_call_target="tpu_custom_call" | custom-call | flops 1000000000 | tf_op jit(solution)/shard_map/nodes/pallas_call | solution.py:662
  25.2 0.2 collective-permute-done.8.zeds_ref
  25.4 1.5 %finish.1 = (bf16[2,2,1,128,128]{4,3,2,1,0:T(8,128)(2,1)}, f32[9,2,2,1,128]{4,3,2,1,0:T(1,128)}, bf16[1,1,1,208,128]{4,3,2,1,0:T(8,128)(2,1)}, f32[9,1,1,1,208]{4,3,2,1,0:T(1,128)}) custom-call(f32[16,512]{1,0:T(8,128)S(1)} %nodes.1.moved_ref, f32[3,2,16,128]{3,2,1,0:T(8,128)S(1)} %pad_maximum_fusion.2.tiles_ref, ...), custom_call_target="tpu_custom_call" | custom-call | flops 1000000000 | tf_op jit(solution)/shard_map/finish/pallas_call | solution.py:662
  (15 shorter events, 0.2 us)
Async XLA Ops:
  0.6 4.1 %collective-permute-start = (bf16[2,2,1,128,128]{4,3,2,1,0:T(8,128)(2,1)}, bf16[2,2,1,128,128]{4,3,2,1,0:T(8,128)(2,1)S(1)}, u32[]{:S(2)}, u32[]{:S(2)}) collective-permute-start(bf16[2,2,1,128,128]{4,3,2,1,0:T(8,128)(2,1)} %latent_any.1), channel_id=1, source_target_pairs={{0,1},{1,0},{2,3},{3,2},{4,5},{5,4},{6,7},{7,6},{8,9},{9,8},{10,11... | collective-permute-start | bytes 393224 | tf_op jit(solution)/shard_map/ppermute | solution.py:625
  1.1 9.4 %collective-permute-start.3 = (bf16[2,2,1,128,128]{4,3,2,1,0:T(8,128)(2,1)}, bf16[2,2,1,128,128]{4,3,2,1,0:T(8,128)(2,1)S(1)}, u32[]{:S(2)}, u32[]{:S(2)}) collective-permute-start(bf16[2,2,1,128,128]{4,3,2,1,0:T(8,128)(2,1)} %latent_any.1), channel_id=1, source_target_pairs={{0,2},{2,0},{1,3},{3,1},{4,6},{6,4},{5,7},{7,5},{8,10},{10,8},{9,1... | collective-permute-start | bytes 393224 | tf_op jit(solution)/shard_map/ppermute | solution.py:625
  4.7 5.8 %collective-permute-start.1 = (bf16[2,1,128,128]{3,2,1,0:T(8,128)(2,1)S(1)}, bf16[2,1,128,128]{3,2,1,0:T(8,128)(2,1)S(1)}, u32[]{:S(2)}, u32[]{:S(2)}) collective-permute-start(bf16[2,1,128,128]{3,2,1,0:T(8,128)(2,1)S(1)} %maximum_bitcast_fusion), channel_id=1, source_target_pairs={{0,7},{1,3},{2,5},{3,1},{4,11},{5,2},{6,9},{7,0},{8,15},{9,6},{10,... | collective-permute-start | bytes 196616 | tf_op jit(solution)/shard_map/ppermute | solution.py:658
  6.2 4.5 %collective-permute-start.2 = (bf16[2,2,128,128]{3,2,1,0:T(8,128)(2,1)S(1)}, bf16[2,2,128,128]{3,2,1,0:T(8,128)(2,1)S(1)}, u32[]{:S(2)}, u32[]{:S(2)}) collective-permute-start(bf16[2,2,128,128]{3,2,1,0:T(8,128)(2,1)S(1)} %pad_maximum_fusion.1), channel_id=1, source_target_pairs={{0,5},{1,3},{2,7},{3,1},{4,9},{5,0},{6,11},{7,2},{8,13},{9,4},{10,... | collective-permute-start | bytes 393224 | tf_op jit(solution)/shard_map/ppermute | solution.py:658
  10.7 1.6 %collective-permute-start.4 = (bf16[8,128,128]{2,1,0:T(8,128)(2,1)S(1)}, bf16[8,128,128]{2,1,0:T(8,128)(2,1)S(1)}, u32[]{:S(2)}, u32[]{:S(2)}) collective-permute-start(bf16[8,128,128]{2,1,0:T(8,128)(2,1)S(1)} %pad_maximum_fusion), channel_id=1, source_target_pairs={{0,1},{1,0},{2,3},{3,2},{4,5},{5,4},{6,7},{7,6},{8,9},{9,8},{10,11... | collective-permute-start | bytes 786440 | tf_op jit(solution)/shard_map/ppermute | solution.py:625
  14.5 3.9 %collective-permute-start.5 = (f32[16,128]{1,0:T(8,128)S(1)}, f32[16,128]{1,0:T(8,128)S(1)}, u32[]{:S(2)}, u32[]{:S(2)}) collective-permute-start(f32[16,128]{1,0:T(8,128)S(1)} %get-tuple-element.103), channel_id=1, source_target_pairs={{0,2},{2,0},{1,3},{3,1},{4,6},{6,4},{5,7},{7,5},{8,10},{10,8},{9,1... | collective-permute-start | bytes 24584 | tf_op jit(solution)/shard_map/ppermute | solution.py:625
  18.4 5.6 %collective-permute-start.6 = (f32[2,16,128]{2,1,0:T(8,128)S(1)}, f32[2,16,128]{2,1,0:T(8,128)S(1)}, u32[]{:S(2)}, u32[]{:S(2)}) collective-permute-start(f32[2,16,128]{2,1,0:T(8,128)S(1)} %get-tuple-element.123), channel_id=1, source_target_pairs={{0,1},{1,0},{4,8},{5,9},{8,4},{9,5},{12,13},{13,12},{2,3},{3,2},{6... | collective-permute-start | bytes 49160 | tf_op jit(solution)/shard_map/ppermute | solution.py:643
  18.5 5.5 %collective-permute-start.7 = (f32[2,16,128]{2,1,0:T(8,128)S(1)}, f32[2,16,128]{2,1,0:T(8,128)S(1)}, u32[]{:S(2)}, u32[]{:S(2)}) collective-permute-start(f32[2,16,128]{2,1,0:T(8,128)S(1)} %get-tuple-element.123), channel_id=1, source_target_pairs={{0,4},{1,5},{4,0},{5,1},{8,12},{9,13},{12,8},{13,9},{2,6},{3,7},{6... | collective-permute-start | bytes 49160 | tf_op jit(solution)/shard_map/ppermute | solution.py:643
  24.1 1.3 %collective-permute-start.8 = (f32[3,2,16,128]{3,2,1,0:T(8,128)S(1)}, f32[3,2,16,128]{3,2,1,0:T(8,128)S(1)}, u32[]{:S(2)}, u32[]{:S(2)}) collective-permute-start(f32[3,2,16,128]{3,2,1,0:T(8,128)S(1)} %pad_maximum_fusion.2.tiles_ref), channel_id=1, source_target_pairs={{0,1},{1,0},{2,3},{3,2},{4,5},{5,4},{6,7},{7,6},{8,9},{9,8},{10,11... | collective-permute-start | bytes 147464 | tf_op jit(solution)/shard_map/ppermute | solution.py:625

commit v13 on v12

--- a/solution.py
+++ b/solution.py
@@ -186,36 +186,38 @@
     return jnp.concatenate([position + new_velocity, new_velocity, velocity], axis=0)
 
 
-def cut_kernel(latent_any, latent_ref, edge_ref, sems):
+def cut_kernel(count, fill_any, *refs):
+    sources, refs = refs[:count], refs[count:]
+    copied, (end_ref, alive_ref, fill_ref, sems) = refs[:count], refs[count:]
     end = 1 - lax.axis_index("gz")
-    copies = fetch([(latent_any, latent_ref), (latent_any.at[end], edge_ref)], sems)
-    for copy in copies:
+    copies = fetch(
+        [(fill_any, fill_ref), (sources[0].at[end], end_ref), *zip(sources, copied)], sems
+    )
+    copies[0].wait()
+    lane = lax.broadcasted_iota(I32, alive_ref.shape[2:], 1)
+    for a, b in CELLS:
+        alive_ref[a, b] = jnp.where(lane < fill_ref[a, 0, b], 1.0, 0.0)
+    for copy in copies[1:]:
         copy.wait()
 
 
 def ranks_kernel(
     sizes,
-    fill_ref,
-    owners_any,
-    edge_w_any,
-    node_in_any,
-    node_w_any,
-    decoder_w_any,
-    decoder_out_any,
-    encoder_in_any,
-    encoder_w_any,
-    neighbours_any,
-    positions_any,
-    velocity_any,
     edge_any,
     latent_ref,
     own_zed,
+    alive_ref,
+    owners_ref,
+    edge_w_ref,
+    node_in_ref,
+    node_w_ref,
+    decoder_w_ref,
+    encoder_in_ref,
+    neighbours_ref,
+    positions_ref,
+    velocity_ref,
     weights_ref,
-    decoder_out_ref,
     inward_ref,
-    encoder_w_ref,
-    alive_ref,
-    neighbours_ref,
     edge_ref,
     spread_ref,
     latent_t_ref,
@@ -230,52 +232,21 @@
     mover_state_ref,
     far_ref,
     early_ref,
-    positions_ref,
-    velocity_ref,
-    owners_ref,
-    edge_w_ref,
-    node_in_ref,
-    node_w_ref,
-    decoder_w_ref,
-    encoder_in_ref,
     sems,
 ):
     count_x, count_y, count_z = sizes
     fold_y = count_y == 2
-    copies = fetch(
-        [
-            (owners_any, owners_ref),
-            (edge_w_any, edge_w_ref),
-            (node_in_any, node_in_ref),
-            (node_w_any, node_w_ref),
-            (decoder_w_any, decoder_w_ref),
-            (decoder_out_any, decoder_out_ref),
-            (encoder_in_any, encoder_in_ref),
-            (encoder_w_any, encoder_w_ref),
-            (neighbours_any, neighbours_ref),
-            (positions_any, positions_ref),
-            (velocity_any, velocity_ref),
-            (edge_any, edge_ref),
-        ],
-        sems,
-    )
-    copies[0].wait()
+    copies = fetch([(edge_any, edge_ref)], sems)
     index_x = lax.axis_index("gx")
     index_y = lax.axis_index("gy")
     index_z = lax.axis_index("gz")
     slots = owners_ref.shape[-1]
     width = node_in_ref.shape[-1]
-    for a, b in CELLS:
-        alive_ref[a, b] = jnp.where(
-            lax.broadcasted_iota(I32, (1, slots), 1) < fill_ref[a, 0, b], 1.0, 0.0
-        )
-
-    lane = lax.broadcasted_iota(I32, (1, slots), 1)
     owner = jnp.concatenate([owners_ref[a, b] for a, b in CELLS], axis=1)
-    alive = jnp.concatenate([jnp.where(lane < fill_ref[a, 0, b], 1, 0) for a, b in CELLS], axis=1)
+    alive = jnp.concatenate([alive_ref[a, b] for a, b in CELLS], axis=1)
     own_block = (index_x * count_y + index_y) * count_z + index_z
-    stays = jnp.where((alive == 1) & (owner == own_block), 1.0, 0.0)
-    moving = jnp.where((alive == 1) & (owner != own_block), 1, 0)
+    stays = jnp.where((alive > 0.5) & (owner == own_block), 1.0, 0.0)
+    moving = jnp.where((alive > 0.5) & (owner != own_block), 1, 0)
     owner_x = quotient(owner, count_y * count_z)
     rest = owner - owner_x * (count_y * count_z)
     owner_y = quotient(rest, count_z)
@@ -325,8 +296,6 @@
     target = ((2 - plane) * options_y + side_y) * 2 + side_z
     spread_ref[...] = jnp.where(valid, target * CAP + (line & 7), -1)
 
-    for copy in copies[1:-1]:
-        copy.wait()
     for i in range(5):
         weights_ref[i] = flip(edge_w_ref[i])
     weights_ref[NODE_OLD] = flip(node_in_ref[:width])
@@ -554,20 +523,42 @@
     )
 
 
-def finish_kernel(
-    sizes,
-    moved_ref,
-    tiles_ref,
-    zeds_ref,
-    spread_ref,
-    inward_ref,
-    encoder_w_ref,
-    kept_latent_ref,
-    kept_state_ref,
-    arrived_latent_ref,
-    arrived_state_ref,
-):
+def finish_kernel(sizes, moved_ref, zed_ref, *refs):
     count_x, count_y, count_z = sizes
+    fold_y = count_y == 2
+    options_y = 2 if fold_y else 3
+    side_refs, refs = refs[: options_y - 1], refs[options_y - 1 :]
+    if fold_y:
+        cross_ref, end_ref, *refs = refs
+    else:
+        end_ref, *refs = refs
+    (
+        packed_ref,
+        spread_ref,
+        inward_ref,
+        encoder_w_ref,
+        kept_latent_ref,
+        kept_state_ref,
+        arrived_latent_ref,
+        arrived_state_ref,
+    ) = refs
+    core = lax.axis_index("gz")
+
+    def tile(source_x, from_y, from_z):
+        if source_x == 0:
+            if from_y == 0:
+                return zed_ref[...]
+            if fold_y:
+                return packed_ref[4] if from_z else side_refs[0][...]
+            return side_refs[from_y - 1][from_z]
+        if fold_y:
+            mine = (cross_ref if from_y else end_ref)[1 - from_z]
+            other = packed_ref[(0 if from_y else 2) + from_z]
+        else:
+            mine = end_ref[1 - from_z, from_y]
+            other = packed_ref[from_z, from_y]
+        return jnp.where(core == (1 - source_x) // 2, mine, other)
+
     extent = (2.0 * count_x, 2.0 * count_y, 1.0 * count_z)
     slots = kept_latent_ref.shape[-2]
     stays = moved_ref[9:10]
@@ -579,30 +570,21 @@
             kept_state_ref[j, a, b] = kept[j : j + 1, i * slots : (i + 1) * slots]
     fold_y = count_y == 2
     index_x = lax.axis_index("gx")
-    options_y = 2 if fold_y else 3
-    lanes = tiles_ref.shape[-1]
+    lanes = zed_ref.shape[-1]
     group = lax.broadcasted_iota(I32, (ROWS, lanes), 1) >> 3
-    even = (index_x & 1) == 0
     found = jnp.zeros((ROWS, lanes), F32)
     for source_x in (-1, 0, 1):
         for from_y in range(options_y):
             for from_z in range(2):
                 if source_x == 0 and from_y == 0 and from_z == 0:
                     continue
-                ref = tiles_ref if from_z == 0 else zeds_ref
-                own, second, first = ref.at[0], ref.at[1], ref.at[2]
                 side_y = from_y if fold_y or from_y == 0 else 3 - from_y
-                target = ((1 - source_x) * options_y + side_y) * 2 + from_z
-                if source_x == 0:
-                    tile = own[from_y]
-                    there = group == target
-                elif source_x == -1:
-                    tile = jnp.where(even, second[from_y], first[from_y])
-                    there = (group == target) & (index_x > 0)
-                else:
-                    tile = jnp.where(even, first[from_y], second[from_y])
-                    there = (group == target) & (index_x < count_x - 1)
-                found = jnp.where(there, tile, found)
+                there = group == ((1 - source_x) * options_y + side_y) * 2 + from_z
+                if source_x == -1:
+                    there = there & (index_x > 0)
+                elif source_x == 1:
+                    there = there & (index_x < count_x - 1)
+                found = jnp.where(there, tile(source_x, from_y, from_z), found)
     halves = []
     for at in range(0, spread_ref.shape[1], 128):
         lane = jnp.broadcast_to(spread_ref[0:1, at : at + 128], (ROWS, 128))
@@ -628,19 +610,6 @@
 def shift(values, axis, way):
     pairs = [(i, i + 1) for i in range(lax.axis_size(axis) - 1)]
     return lax.ppermute(values, axis, [(j, i) for i, j in pairs] if way else pairs)
-
-
-def swap_x(values, first):
-    count = lax.axis_size("gx")
-    pairs = []
-    for x in range(count):
-        partner = x + 1 if (x - first) % 2 == 0 else x - 1
-        for z in range(2):
-            if 0 <= partner < count:
-                pairs.append((x * 2 + z, partner * 2 + z))
-            else:
-                pairs.append((x * 2 + z, x * 2 + 1 - z))
-    return lax.ppermute(values, ("gx", "gz"), pairs)
 
 
 def swap_chips(values, cross):
@@ -709,15 +678,32 @@
     own_zed = swap(node_latent, "gz")
     if fold_y:
         sides = [swap(node_latent, "gy")]
-    latent, end = call(
-        cut_kernel,
+    small = (
+        node_latent,
+        owners,
+        edge_weights,
+        node_in,
+        node_weights,
+        decoder_weights,
+        encoder_in,
+        neighbours,
+        positions,
+        velocity,
+        decoder_out,
+        encoder_weights,
+    )
+    *copied, end, alive = call(
+        functools.partial(cut_kernel, len(small)),
         "cut",
-        [ANY],
-        [(node_latent.shape, BF16), (node_latent.shape[1:], BF16)],
-        [pltpu.SemaphoreType.DMA((2,))],
-        (in_hbm(node_latent),),
+        [ANY] * (len(small) + 1),
+        [(array.shape, array.dtype) for array in small]
+        + [(node_latent.shape[1:], BF16), ((2, 2, 1, slots), F32)],
+        [pltpu.SMEM(fill.shape, I32), pltpu.SemaphoreType.DMA((len(small) + 2,))],
+        [in_hbm(array) for array in (fill, *small)],
         1_000_000,
     )
+    latent, *copied, decoder_out, encoder_weights = copied
+    neighbours = copied[6]
     core = lax.axis_index("gz")
     if fold_y:
         row = 1 - lax.axis_index("gy")
@@ -740,14 +726,10 @@
     ranked = call(
         functools.partial(ranks_kernel, sizes),
         "ranks",
-        [SMEM] + [ANY] * 12 + [VMEM] * 2,
+        [ANY] + [VMEM] * 12,
         [
             ((11, width, width), BF16),
-            (decoder_out.shape, BF16),
             ((48, width), BF16),
-            (encoder_weights.shape, BF16),
-            ((2, 2, 1, slots), F32),
-            (neighbours.shape, I32),
             (edge_latent.shape, BF16),
             ((8, 256), I32),
             ((width, particles), F32),
@@ -763,46 +745,14 @@
             ((4, width, 2 * slots), BF16),
             ((2, width, neighbour_count * slots), BF16),
         ],
-        [
-            like(positions),
-            like(velocity),
-            like(owners),
-            like(edge_weights),
-            like(node_in),
-            like(node_weights),
-            like(decoder_weights),
-            like(encoder_in),
-            pltpu.SemaphoreType.DMA((12,)),
-        ],
-        [
-            in_hbm(array)
-            for array in (
-                fill,
-                owners,
-                edge_weights,
-                node_in,
-                node_weights,
-                decoder_weights,
-                decoder_out,
-                encoder_in,
-                encoder_weights,
-                neighbours,
-                positions,
-                velocity,
-                edge_latent,
-            )
-        ]
-        + [latent, own_zed],
+        [pltpu.SemaphoreType.DMA((1,))],
+        (in_hbm(edge_latent), latent, own_zed, alive, *copied),
         5_000_000_000,
     )
     mine, sides, ranked = lax.optimization_barrier((mine, sides, ranked))
     (
         weights,
-        decoder_out,
         inward,
-        encoder_weights,
-        alive,
-        neighbours,
         edge_latent,
         spread,
         latent_t,
@@ -872,18 +822,22 @@
             4_000_000_000,
         )[0]
 
-    first = edges(0)
+    zed = swap(bucket, "gz")
     if fold_y:
-        tiles = [swap(bucket, "gy")]
+        sides = [swap(bucket, "gy")]
+        zed, far_rest = lax.optimization_barrier((zed, far_rest))
+        both = jnp.stack([bucket, zed])
+        ends = [swap_chips(both, True), swap_chips(both, False)]
     else:
-        tiles = [shift(bucket, "gy", 0), shift(bucket, "gy", 1)]
-    tiles, first = lax.optimization_barrier((tiles, first))
-    tiles = jnp.stack([bucket, *tiles], axis=0)
-    second = edges(1)
-    sided = [swap_x(tiles, 1), swap_x(tiles, 0)]
-    sided, second = lax.optimization_barrier((sided, second))
-    tiles = jnp.stack([tiles, *sided], axis=0)
-    zeds = swap(tiles, "gz")
+        both = jnp.stack([bucket, zed])
+        sides = [shift(both, "gy", 0), shift(both, "gy", 1)]
+        ends = [swap_chips(jnp.stack([both, *sides], axis=1), False)]
+    first, second = edges(0), edges(1)
+    sides, ends, first, second = lax.optimization_barrier((sides, ends, first, second))
+    if fold_y:
+        packed = swap(jnp.concatenate([*ends, sides[0][None]], axis=0), "gz")
+    else:
+        packed = swap(ends[0], "gz")
     state = call(
         nodes_kernel,
         "nodes",
@@ -893,11 +847,11 @@
         (first, second, node_pre, latent_t, state, weights, decoder_out),
         1_000_000_000,
     )[0]
-    zeds, state = lax.optimization_barrier((zeds, state))
+    packed, state = lax.optimization_barrier((packed, state))
     return call(
         functools.partial(finish_kernel, sizes),
         "finish",
-        [VMEM] * 6,
+        [VMEM] * (len(sides) + len(ends) + 6),
         [
             (node_latent.shape, BF16),
             ((9,) + node_latent.shape[:4], F32),
@@ -905,7 +859,7 @@
             ((9, 1, 1, 1, 26 * CAP), F32),
         ],
         [],
-        (state, tiles, zeds, spread, inward, encoder_weights),
+        (state, zed, *sides, *ends, packed, spread, inward, encoder_weights),
         1_000_000_000,
     )
 

time: 27.1 us -> 26.5 us (0.978)
  waiting for transfers between devices: 0.62 us -> 2.4 us
  starting transfers between devices: 9.84 us -> 8.58 us
  Pallas kernels: 15.5 us -> 14.4 us
    ppermute x2 -> x0, starting transfers between devices: 3.2 us -> none  [swap_x(): return lax.ppermute(values, ('gx', 'gz'), pairs)]
    ppermute x2 -> x4, starting transfers between devices: 1.78 us -> 3.71 us  [swap_chips(): return lax.ppermute(values, ('gx', 'gy', 'gz'), pairs)]
    ppermute x2 -> x4, waiting for transfers between devices: 0.07 us -> 1.79 us  [swap_chips(): return lax.ppermute(values, ('gx', 'gy', 'gz'), pairs)]
    pallas_call x8, Pallas kernels: 15.5 us -> 14.4 us  [call(): pl.pallas_call(kernel, out_shape=tuple((jax.ShapeDtypeStruct(shape, kind)...]
    ppermute x5 -> x6, waiting for transfers between devices: 0.54 us -> 0.61 us  [swap(): return lax.ppermute(values, axis, [(0, 1), (1, 0)])]
    ppermute x5 -> x6, starting transfers between devices: 4.86 us -> 4.87 us  [swap(): return lax.ppermute(values, axis, [(0, 1), (1, 0)])]
  transfers between devices with their start and end apart: 9 -> 10, of which waited for: 3 -> 4; matrix products, arithmetic and copies ran while one was open for 0% -> 0% of each run, Pallas kernels for 44% -> 41%
where the time goes in v13:
time: 26.5 us; the launch traced here: 26.3 us
  Pallas kernels  14.4 us (54%)
  starting transfers between devices  8.58 us (32%)
  waiting for transfers between devices  2.4 us (9%)
  between operations  0.82 us (3%)
    pallas_call x8, Pallas kernels, call(): pl.pallas_call(kernel, out_shape=tuple((jax.ShapeDtypeStruct(shape, kind)...  14.4 us
    ppermute x6, starting transfers between devices, swap(): return lax.ppermute(values, axis, [(0, 1), (1, 0)])  4.87 us
    ppermute x4, starting transfers between devices, swap_chips(): return lax.ppermute(values, ('gx', 'gy', 'gz'), pairs)  3.71 us
    ppermute x4, waiting for transfers between devices, swap_chips(): return lax.ppermute(values, ('gx', 'gy', 'gz'), pairs)  1.79 us
    ppermute x6, waiting for transfers between devices, swap(): return lax.ppermute(values, axis, [(0, 1), (1, 0)])  0.61 us
  transfers between devices with their start and end apart: 10, of which 4 were waited for; matrix products, arithmetic and copies ran while one was open for 0% of the time, Pallas kernels for 41%

profile of v13, /device:TPU:0, one launch (start us, length us, event | category | flops | bytes accessed | tf_op | source)
XLA Modules:
  0.0 26.3 jit_solution(4879238605710985561)
XLA Ops:
  0.6 0.5 %collective-permute-start = (bf16[2,2,1,128,128]{4,3,2,1,0:T(8,128)(2,1)}, bf16[2,2,1,128,128]{4,3,2,1,0:T(8,128)(2,1)S(1)}, u32[]{:S(2)}, u32[]{:S(2)}) collective-permute-start(bf16[2,2,1,128,128]{4,3,2,1,0:T(8,128)(2,1)} %refs_0_.1), channel_id=1, source_target_pairs={{0,1},{1,0},{2,3},{3,2},{4,5},{5,4},{6,7},{7,6},{8,9},{9,8},{10,11... | collective-permute-start | bytes 393224 | tf_op jit(solution)/shard_map/ppermute | solution.py:607
  1.2 2.6 %collective-permute-start.3 = (bf16[2,2,1,128,128]{4,3,2,1,0:T(8,128)(2,1)}, bf16[2,2,1,128,128]{4,3,2,1,0:T(8,128)(2,1)S(1)}, u32[]{:S(2)}, u32[]{:S(2)}) collective-permute-start(bf16[2,2,1,128,128]{4,3,2,1,0:T(8,128)(2,1)} %refs_0_.1), channel_id=1, source_target_pairs={{0,2},{2,0},{1,3},{3,1},{4,6},{6,4},{5,7},{7,5},{8,10},{10,8},{9,1... | collective-permute-start | bytes 393224 | tf_op jit(solution)/shard_map/ppermute | solution.py:607
  3.7 1.3 %cut.1 = (bf16[2,2,1,128,128]{4,3,2,1,0:T(8,128)(2,1)S(1)}, s32[2,2,1,128]{3,2,1,0:T(1,128)S(1)}, bf16[5,128,128]{2,1,0:T(8,128)(2,1)S(1)}, bf16[256,128]{1,0:T(...) custom-call(s32[2,1,2]{2,1,0:T(1,128)} %bitcast.27, ...), custom_call_target="tpu_custom_call" | custom-call | flops 1000000 | tf_op jit(solution)/shard_map/cut/pallas_call | solution.py:631
  5.1 1.4 %collective-permute-start.1 = (bf16[2,1,128,128]{3,2,1,0:T(8,128)(2,1)S(1)}, bf16[2,1,128,128]{3,2,1,0:T(8,128)(2,1)S(1)}, u32[]{:S(2)}, u32[]{:S(2)}) collective-permute-start(bf16[2,1,128,128]{3,2,1,0:T(8,128)(2,1)S(1)} %maximum_bitcast_fusion), channel_id=1, source_target_pairs={{0,7},{1,3},{2,5},{3,1},{4,11},{5,2},{6,9},{7,0},{8,15},{9,6},{10,... | collective-permute-start | bytes 196616 | tf_op jit(solution)/shard_map/ppermute | solution.py:627
  6.5 0.1 collective-permute-start.2
  6.6 2.5 %ranks.1 = (bf16[11,128,128]{2,1,0:T(8,128)(2,1)S(1)}, bf16[48,128]{1,0:T(8,128)(2,1)S(1)}, bf16[2,2,1,12,128,128]{5,4,3,2,1,0:T(8,128)(2,1)S(1)}, s32[8,256]{1,...) custom-call(bf16[2,2,1,12,128,128]{5,4,3,2,1,0:T(8,128)(2,1)} %edge_, ...), custom_call_target="tpu_custom_call" | custom-call | flops 5000000000 | tf_op jit(solution)/shard_map/ranks/pallas_call | solution.py:631
  9.1 0.0 collective-permute-done.3
  9.2 0.7 %collective-permute-done.1 = bf16[2,1,128,128]{3,2,1,0:T(8,128)(2,1)S(1)} collective-permute-done((bf16[2,1,128,128]{3,2,1,0:T(8,128)(2,1)S(1)}, bf16[2,1,128,128]{3,2,1,0:T(8,128)(2,1)S(1)}, u32[]{:S(2)}, u32[]{:S(2)}) %collective-permute-start.1) | collective-permute-done | bytes 65568 | tf_op jit(solution)/shard_map/ppermute | solution.py:627
  9.8 1.1 %collective-permute-done.2 = bf16[2,2,128,128]{3,2,1,0:T(8,128)(2,1)S(1)} collective-permute-done((bf16[2,2,128,128]{3,2,1,0:T(8,128)(2,1)S(1)}, bf16[2,2,128,128]{3,2,1,0:T(8,128)(2,1)S(1)}, u32[]{:S(2)}, u32[]{:S(2)}) %collective-permute-start.2) | collective-permute-done | bytes 131104 | tf_op jit(solution)/shard_map/ppermute | solution.py:627
  11.0 0.1 collective-permute-start.4
  11.1 1.1 %prepare.1 = (bf16[3,128,256]{2,1,0:T(8,128)(2,1)S(1)}, f32[128,1536]{1,0:T(8,128)S(1)}) custom-call(bf16[4,128,256]{2,1,0:T(8,128)(2,1)S(1)} %get-tuple-element.100.far_ref.far_own_ref, bf16[2,3,128,128]{3,2,1,0:T(8,128)(2,1)S(1)} %constant_dynamic-update-slice_fusion.mine_ref, bf16[11,128,128]{2,1,0:T(8,128)(2,1)S(1)} %get-tuple-element.101.weights_ref.refs_4_, ...), custom_call_target="tpu_custom_call" | custom-call | flops 5000000000 | tf_op jit(solution)/shard_map/prepare/pallas_call | solution.py:631
  12.2 0.4 %collective-permute-done.4 = bf16[8,128,128]{2,1,0:T(8,128)(2,1)S(1)} collective-permute-done((bf16[8,128,128]{2,1,0:T(8,128)(2,1)S(1)}, bf16[8,128,128]{2,1,0:T(8,128)(2,1)S(1)}, u32[]{:S(2)}, u32[]{:S(2)}) %collective-permute-start.4) | collective-permute-done | bytes 262176 | tf_op jit(solution)/shard_map/ppermute | solution.py:607
  12.7 2.2 %movers.1 = (bf16[8,128,256]{2,1,0:T(8,128)(2,1)S(1)}, f32[16,128]{1,0:T(8,128)S(1)}) custom-call(bf16[2,128,128]{2,1,0:T(8,128)(2,1)S(1)} %dynamic-slice_bitcast_fusion.refs_0_, bf16[2,128,128]{2,1,0:T(8,128)(2,1)S(1)} %slice.6.refs_1_, bf16[2,3,128,128]{3,2,1,0:T(8,128)(2,1)S(1)} %bitcast.21, bf16[3,128,256]{2,1,0:T(8,128)(2,1)S(1)} %get-tuple-element.109.refs_3_, ...), custom_call_target="tpu_custom_call" | custom-call | flops 3000000000 | tf_op jit(solution)/shard_map/movers/pallas_call | solution.py:631
  14.8 0.1 collective-permute-start.6
  15.0 1.5 %collective-permute-start.5 = (f32[16,128]{1,0:T(8,128)S(1)}, f32[16,128]{1,0:T(8,128)S(1)}, u32[]{:S(2)}, u32[]{:S(2)}) collective-permute-start(f32[16,128]{1,0:T(8,128)S(1)} %get-tuple-element.115), channel_id=1, source_target_pairs={{0,2},{2,0},{1,3},{3,1},{4,6},{6,4},{5,7},{7,5},{8,10},{10,8},{9,1... | collective-permute-start | bytes 24584 | tf_op jit(solution)/shard_map/ppermute | solution.py:607
  16.5 0.0 collective-permute-done.6.zed_ref
  16.5 1.8 %collective-permute-start.7 = (f32[2,16,128]{2,1,0:T(8,128)S(1)}, f32[2,16,128]{2,1,0:T(8,128)S(1)}, u32[]{:S(2)}, u32[]{:S(2)}) collective-permute-start(f32[2,16,128]{2,1,0:T(8,128)S(1)} %pad_maximum_fusion.3), channel_id=1, source_target_pairs={{0,7},{1,3},{2,5},{3,1},{4,11},{5,2},{6,9},{7,0},{8,15},{9,6},{10,... | collective-permute-start | bytes 49160 | tf_op jit(solution)/shard_map/ppermute | solution.py:627
  18.3 0.4 %collective-permute-start.8 = (f32[2,16,128]{2,1,0:T(8,128)S(1)}, f32[2,16,128]{2,1,0:T(8,128)S(1)}, u32[]{:S(2)}, u32[]{:S(2)}) collective-permute-start(f32[2,16,128]{2,1,0:T(8,128)S(1)} %pad_maximum_fusion.3), channel_id=1, source_target_pairs={{0,5},{1,3},{2,7},{3,1},{4,9},{5,0},{6,11},{7,2},{8,13},{9,4},{10,... | collective-permute-start | bytes 49160 | tf_op jit(solution)/shard_map/ppermute | solution.py:627
  18.7 2.4 %edges.3.second_ref = bf16[2,128,128]{2,1,0:T(8,128)(2,1)S(1)} custom-call(f32[2,2,1,128]{3,2,1,0:T(1,128)S(1)} %get-tuple-element.71.alive_ref, bf16[2,2,1,128,128]{4,3,2,1,0:T(8,128)(2,1)S(1)} %get-tuple-element.70.latent_ref, bf16[2,2,1,12,128,128]{5,4,3,2,1,0:T(8,128)(2,1)S(1)} %get-tuple-element.118.edge_ref, ...), custom_call_target="tpu_custom_call" | custom-call | flops 4000000000 | tf_op jit(solution)/shard_map/edges/pallas_call | solution.py:631
  21.1 2.4 %edges.2.first_ref = bf16[2,128,128]{2,1,0:T(8,128)(2,1)S(1)} custom-call(f32[2,2,1,128]{3,2,1,0:T(1,128)S(1)} %get-tuple-element.71.alive_ref, bf16[2,2,1,128,128]{4,3,2,1,0:T(8,128)(2,1)S(1)} %get-tuple-element.70.latent_ref, bf16[2,2,1,12,128,128]{5,4,3,2,1,0:T(8,128)(2,1)S(1)} %get-tuple-element.118.edge_ref, ...), custom_call_target="tpu_custom_call" | custom-call | flops 4000000000 | tf_op jit(solution)/shard_map/edges/pallas_call | solution.py:631
  23.5 0.1 collective-permute-start.9
  23.6 1.0 %nodes.1.moved_ref = f32[16,512]{1,0:T(8,128)S(1)} custom-call(bf16[2,128,128]{2,1,0:T(8,128)(2,1)S(1)} %edges.2.first_ref, bf16[2,128,128]{2,1,0:T(8,128)(2,1)S(1)} %edges.3.second_ref, f32[128,512]{1,0:T(8,128)S(1)} %get-tuple-element.126.node_pre_ref, f32[128,512]{1,0:T(8,128)S(1)} %get-tuple-element.127.latent_t_ref, ...), custom_call_target="tpu_custom_call" | custom-call | flops 1000000000 | tf_op jit(solution)/shard_map/nodes/pallas_call | solution.py:631
  24.6 0.2 collective-permute-done.9.refs_3_
  24.8 1.5 %finish.1 = (bf16[2,2,1,128,128]{4,3,2,1,0:T(8,128)(2,1)}, f32[9,2,2,1,128]{4,3,2,1,0:T(1,128)}, bf16[1,1,1,208,128]{4,3,2,1,0:T(8,128)(2,1)}, f32[9,1,1,1,208]{4,3,2,1,0:T(1,128)}) custom-call(f32[16,512]{1,0:T(8,128)S(1)} %nodes.1.moved_ref, f32[16,128]{1,0:T(8,128)S(1)} %collective-permute-done.6.zed_ref, f32[16,128]{1,0:T(8,128)S(1)} %collective-permute-done.5.refs_0_, ...), custom_call_target="tpu_custom_call" | custom-call | flops 1000000000 | tf_op jit(solution)/shard_map/finish/pallas_call | solution.py:631
  (17 shorter events, 0.2 us)
Async XLA Ops:
  0.6 4.4 %collective-permute-start = (bf16[2,2,1,128,128]{4,3,2,1,0:T(8,128)(2,1)}, bf16[2,2,1,128,128]{4,3,2,1,0:T(8,128)(2,1)S(1)}, u32[]{:S(2)}, u32[]{:S(2)}) collective-permute-start(bf16[2,2,1,128,128]{4,3,2,1,0:T(8,128)(2,1)} %refs_0_.1), channel_id=1, source_target_pairs={{0,1},{1,0},{2,3},{3,2},{4,5},{5,4},{6,7},{7,6},{8,9},{9,8},{10,11... | collective-permute-start | bytes 393224 | tf_op jit(solution)/shard_map/ppermute | solution.py:607
  1.2 8.0 %collective-permute-start.3 = (bf16[2,2,1,128,128]{4,3,2,1,0:T(8,128)(2,1)}, bf16[2,2,1,128,128]{4,3,2,1,0:T(8,128)(2,1)S(1)}, u32[]{:S(2)}, u32[]{:S(2)}) collective-permute-start(bf16[2,2,1,128,128]{4,3,2,1,0:T(8,128)(2,1)} %refs_0_.1), channel_id=1, source_target_pairs={{0,2},{2,0},{1,3},{3,1},{4,6},{6,4},{5,7},{7,5},{8,10},{10,8},{9,1... | collective-permute-start | bytes 393224 | tf_op jit(solution)/shard_map/ppermute | solution.py:607
  5.1 4.8 %collective-permute-start.1 = (bf16[2,1,128,128]{3,2,1,0:T(8,128)(2,1)S(1)}, bf16[2,1,128,128]{3,2,1,0:T(8,128)(2,1)S(1)}, u32[]{:S(2)}, u32[]{:S(2)}) collective-permute-start(bf16[2,1,128,128]{3,2,1,0:T(8,128)(2,1)S(1)} %maximum_bitcast_fusion), channel_id=1, source_target_pairs={{0,7},{1,3},{2,5},{3,1},{4,11},{5,2},{6,9},{7,0},{8,15},{9,6},{10,... | collective-permute-start | bytes 196616 | tf_op jit(solution)/shard_map/ppermute | solution.py:627
  6.5 4.5 %collective-permute-start.2 = (bf16[2,2,128,128]{3,2,1,0:T(8,128)(2,1)S(1)}, bf16[2,2,128,128]{3,2,1,0:T(8,128)(2,1)S(1)}, u32[]{:S(2)}, u32[]{:S(2)}) collective-permute-start(bf16[2,2,128,128]{3,2,1,0:T(8,128)(2,1)S(1)} %pad_maximum_fusion.1), channel_id=1, source_target_pairs={{0,5},{1,3},{2,7},{3,1},{4,9},{5,0},{6,11},{7,2},{8,13},{9,4},{10,... | collective-permute-start | bytes 393224 | tf_op jit(solution)/shard_map/ppermute | solution.py:627
  11.0 1.6 %collective-permute-start.4 = (bf16[8,128,128]{2,1,0:T(8,128)(2,1)S(1)}, bf16[8,128,128]{2,1,0:T(8,128)(2,1)S(1)}, u32[]{:S(2)}, u32[]{:S(2)}) collective-permute-start(bf16[8,128,128]{2,1,0:T(8,128)(2,1)S(1)} %pad_maximum_fusion), channel_id=1, source_target_pairs={{0,1},{1,0},{2,3},{3,2},{4,5},{5,4},{6,7},{7,6},{8,9},{9,8},{10,11... | collective-permute-start | bytes 786440 | tf_op jit(solution)/shard_map/ppermute | solution.py:607
  14.8 1.7 %collective-permute-start.6 = (f32[16,128]{1,0:T(8,128)S(1)}, f32[16,128]{1,0:T(8,128)S(1)}, u32[]{:S(2)}, u32[]{:S(2)}) collective-permute-start(f32[16,128]{1,0:T(8,128)S(1)} %get-tuple-element.115), channel_id=1, source_target_pairs={{0,1},{1,0},{2,3},{3,2},{4,5},{5,4},{6,7},{7,6},{8,9},{9,8},{10,11... | collective-permute-start | bytes 24584 | tf_op jit(solution)/shard_map/ppermute | solution.py:607
  15.0 8.5 %collective-permute-start.5 = (f32[16,128]{1,0:T(8,128)S(1)}, f32[16,128]{1,0:T(8,128)S(1)}, u32[]{:S(2)}, u32[]{:S(2)}) collective-permute-start(f32[16,128]{1,0:T(8,128)S(1)} %get-tuple-element.115), channel_id=1, source_target_pairs={{0,2},{2,0},{1,3},{3,1},{4,6},{6,4},{5,7},{7,5},{8,10},{10,8},{9,1... | collective-permute-start | bytes 24584 | tf_op jit(solution)/shard_map/ppermute | solution.py:607
  16.5 7.0 %collective-permute-start.7 = (f32[2,16,128]{2,1,0:T(8,128)S(1)}, f32[2,16,128]{2,1,0:T(8,128)S(1)}, u32[]{:S(2)}, u32[]{:S(2)}) collective-permute-start(f32[2,16,128]{2,1,0:T(8,128)S(1)} %pad_maximum_fusion.3), channel_id=1, source_target_pairs={{0,7},{1,3},{2,5},{3,1},{4,11},{5,2},{6,9},{7,0},{8,15},{9,6},{10,... | collective-permute-start | bytes 49160 | tf_op jit(solution)/shard_map/ppermute | solution.py:627
  18.3 5.2 %collective-permute-start.8 = (f32[2,16,128]{2,1,0:T(8,128)S(1)}, f32[2,16,128]{2,1,0:T(8,128)S(1)}, u32[]{:S(2)}, u32[]{:S(2)}) collective-permute-start(f32[2,16,128]{2,1,0:T(8,128)S(1)} %pad_maximum_fusion.3), channel_id=1, source_target_pairs={{0,5},{1,3},{2,7},{3,1},{4,9},{5,0},{6,11},{7,2},{8,13},{9,4},{10,... | collective-permute-start | bytes 49160 | tf_op jit(solution)/shard_map/ppermute | solution.py:627
  23.5 1.3 %collective-permute-start.9 = (f32[5,16,128]{2,1,0:T(8,128)S(1)}, f32[5,16,128]{2,1,0:T(8,128)S(1)}, u32[]{:S(2)}, u32[]{:S(2)}) collective-permute-start(f32[5,16,128]{2,1,0:T(8,128)S(1)} %pad_maximum_fusion.2), channel_id=1, source_target_pairs={{0,1},{1,0},{2,3},{3,2},{4,5},{5,4},{6,7},{7,6},{8,9},{9,8},{10,11... | collective-permute-start | bytes 122888 | tf_op jit(solution)/shard_map/ppermute | solution.py:607

commit v14 on v13

--- a/solution.py
+++ b/solution.py
@@ -342,13 +342,13 @@
         pair = jnp.concatenate([latent_ref[a, b, 0], own_zed[a, b, 0]], axis=0)
         far_ref[window.own(ex, row)] = dot_nt(weights_ref[FAR], pair).astype(BF16)
     cells = window.cells(window.own_columns())
-    for a in range(2):
-        b = 1 - index_y if fold_y else 1
+    for a, bt in CELLS:
+        b = (index_y if bt == 0 else 1 - index_y) if fold_y else bt
         ids = jnp.concatenate([neighbours_ref[a, b, k] for k in range(neighbour_count)], axis=1)
         place, key = places(ids & 127, ids >> 7, fold_y)
         for tile in range(ids.shape[1] // TILE):
             at = slice(tile * TILE, (tile + 1) * TILE)
-            early_ref[a, :, at] = pick(cells, place[:, at], key[:, at]).astype(BF16)
+            early_ref[2 * a + bt, :, at] = pick(cells, place[:, at], key[:, at]).astype(BF16)
 
     copies[-1].wait()
     for k in range(neighbour_count):
@@ -476,8 +476,7 @@
             b = bt
             rows = (bt, bt + 1, bt + 2)
         columns = [(ex, row) for ex in range(a, a + 3) for row in rows]
-        if bt == 1:
-            columns = [column for column in columns if column not in window.own_columns()]
+        columns = [column for column in columns if column not in window.own_columns()]
         near = dot_nt(weights_ref[NEAR], latent_ref[b, 0])
         near = jnp.concatenate([near, near], axis=1)
         ids = jnp.concatenate([neighbours_ref[b, k] for k in range(neighbour_count)], axis=1)
@@ -485,10 +484,8 @@
 
         def pre(tile, b=b, bt=bt, near=near):
             edges = jnp.concatenate([edge_ref[b, 0, 2 * tile], edge_ref[b, 0, 2 * tile + 1]], axis=0)
-            terms = dot_nt(weights_ref[EDGE], edges) + near
-            if bt == 1:
-                terms = terms + early_ref[a, :, tile * TILE : (tile + 1) * TILE].astype(F32)
-            return terms
+            early = early_ref[2 * a + bt, :, tile * TILE : (tile + 1) * TILE]
+            return dot_nt(weights_ref[EDGE], edges) + near + early.astype(F32)
 
         message = messages(
             window.cells(columns),
@@ -678,20 +675,7 @@
     own_zed = swap(node_latent, "gz")
     if fold_y:
         sides = [swap(node_latent, "gy")]
-    small = (
-        node_latent,
-        owners,
-        edge_weights,
-        node_in,
-        node_weights,
-        decoder_weights,
-        encoder_in,
-        neighbours,
-        positions,
-        velocity,
-        decoder_out,
-        encoder_weights,
-    )
+    small = (node_latent,)
     *copied, end, alive = call(
         functools.partial(cut_kernel, len(small)),
         "cut",
@@ -700,10 +684,9 @@
         + [(node_latent.shape[1:], BF16), ((2, 2, 1, slots), F32)],
         [pltpu.SMEM(fill.shape, I32), pltpu.SemaphoreType.DMA((len(small) + 2,))],
         [in_hbm(array) for array in (fill, *small)],
-        1_000_000,
-    )
-    latent, *copied, decoder_out, encoder_weights = copied
-    neighbours = copied[6]
+        5_000_000_000,
+    )
+    latent = copied[0]
     core = lax.axis_index("gz")
     if fold_y:
         row = 1 - lax.axis_index("gy")
@@ -743,10 +726,10 @@
             ((width, movers), F32),
             ((8, movers), F32),
             ((4, width, 2 * slots), BF16),
-            ((2, width, neighbour_count * slots), BF16),
+            ((4, width, neighbour_count * slots), BF16),
         ],
         [pltpu.SemaphoreType.DMA((1,))],
-        (in_hbm(edge_latent), latent, own_zed, alive, *copied),
+        (in_hbm(edge_latent), latent, own_zed, alive, owners, edge_weights, node_in, node_weights, decoder_weights, encoder_in, neighbours, positions, velocity),
         5_000_000_000,
     )
     mine, sides, ranked = lax.optimization_barrier((mine, sides, ranked))

time: 26.5 us -> 25.6 us (0.966)
  waiting for transfers between devices: 2.4 us -> 1.68 us
  Pallas kernels: 14.4 us -> 13.9 us
    ppermute x4, waiting for transfers between devices: 1.79 us -> 1.16 us  [swap_chips(): return lax.ppermute(values, ('gx', 'gy', 'gz'), pairs)]
    pallas_call x8, Pallas kernels: 14.4 us -> 13.9 us  [call(): pl.pallas_call(kernel, out_shape=tuple((jax.ShapeDtypeStruct(shape, kind)...]
  transfers between devices with their start and end apart: 10 -> 10, of which waited for: 4 -> 4; matrix products, arithmetic and copies ran while one was open for 0% -> 0% of each run, Pallas kernels for 41% -> 40%
where the time goes in v14:
time: 25.6 us; the launch traced here: 25.4 us
  Pallas kernels  13.9 us (54%)
  starting transfers between devices  8.77 us (34%)
  waiting for transfers between devices  1.68 us (7%)
  between operations  0.93 us (4%)
    pallas_call x8, Pallas kernels, call(): pl.pallas_call(kernel, out_shape=tuple((jax.ShapeDtypeStruct(shape, kind)...  13.9 us
    ppermute x6, starting transfers between devices, swap(): return lax.ppermute(values, axis, [(0, 1), (1, 0)])  4.98 us
    ppermute x4, starting transfers between devices, swap_chips(): return lax.ppermute(values, ('gx', 'gy', 'gz'), pairs)  3.79 us
    ppermute x4, waiting for transfers between devices, swap_chips(): return lax.ppermute(values, ('gx', 'gy', 'gz'), pairs)  1.16 us
    ppermute x6, waiting for transfers between devices, swap(): return lax.ppermute(values, axis, [(0, 1), (1, 0)])  0.53 us
  transfers between devices with their start and end apart: 10, of which 4 were waited for; matrix products, arithmetic and copies ran while one was open for 0% of the time, Pallas kernels for 40%

profile of v14, /device:TPU:0, one launch (start us, length us, event | category | flops | bytes accessed | tf_op | source)
XLA Modules:
  0.0 25.4 jit_solution(18320628719599722254)
XLA Ops:
  0.6 0.5 %collective-permute-start = (bf16[2,2,1,128,128]{4,3,2,1,0:T(8,128)(2,1)}, bf16[2,2,1,128,128]{4,3,2,1,0:T(8,128)(2,1)S(1)}, u32[]{:S(2)}, u32[]{:S(2)}) collective-permute-start(bf16[2,2,1,128,128]{4,3,2,1,0:T(8,128)(2,1)} %refs_0_.1), channel_id=1, source_target_pairs={{0,1},{1,0},{2,3},{3,2},{4,5},{5,4},{6,7},{7,6},{8,9},{9,8},{10,11... | collective-permute-start | bytes 393224 | tf_op jit(solution)/shard_map/ppermute | solution.py:604
  1.2 2.6 %collective-permute-start.3 = (bf16[2,2,1,128,128]{4,3,2,1,0:T(8,128)(2,1)}, bf16[2,2,1,128,128]{4,3,2,1,0:T(8,128)(2,1)S(1)}, u32[]{:S(2)}, u32[]{:S(2)}) collective-permute-start(bf16[2,2,1,128,128]{4,3,2,1,0:T(8,128)(2,1)} %refs_0_.1), channel_id=1, source_target_pairs={{0,2},{2,0},{1,3},{3,1},{4,6},{6,4},{5,7},{7,5},{8,10},{10,8},{9,1... | collective-permute-start | bytes 393224 | tf_op jit(solution)/shard_map/ppermute | solution.py:604
  3.8 1.1 %cut.1 = (bf16[2,2,1,128,128]{4,3,2,1,0:T(8,128)(2,1)S(1)}, bf16[2,1,128,128]{3,2,1,0:T(8,128)(2,1)S(1)}, f32[2,2,1,128]{3,2,1,0:T(1,128)S(1)}) custom-call(s32[2,1,2]{2,1,0:T(1,128)} %bitcast.29, bf16[2,2,1,128,128]{4,3,2,1,0:T(8,128)(2,1)} %refs_0_.1), custom_call_target="tpu_custom_call" | custom-call | flops 5000000000 | tf_op jit(solution)/shard_map/cut/pallas_call | solution.py:628
  4.9 1.4 %collective-permute-start.1 = (bf16[2,1,128,128]{3,2,1,0:T(8,128)(2,1)S(1)}, bf16[2,1,128,128]{3,2,1,0:T(8,128)(2,1)S(1)}, u32[]{:S(2)}, u32[]{:S(2)}) collective-permute-start(bf16[2,1,128,128]{3,2,1,0:T(8,128)(2,1)S(1)} %maximum_bitcast_fusion), channel_id=1, source_target_pairs={{0,7},{1,3},{2,5},{3,1},{4,11},{5,2},{6,9},{7,0},{8,15},{9,6},{10,... | collective-permute-start | bytes 196616 | tf_op jit(solution)/shard_map/ppermute | solution.py:624
  6.3 0.2 collective-permute-start.2
  6.6 3.0 %ranks.1 = (bf16[11,128,128]{2,1,0:T(8,128)(2,1)S(1)}, bf16[48,128]{1,0:T(8,128)(2,1)S(1)}, bf16[2,2,1,12,128,128]{5,4,3,2,1,0:T(8,128)(2,1)S(1)}, s32[8,256]{1,...) custom-call(bf16[2,2,1,12,128,128]{5,4,3,2,1,0:T(8,128)(2,1)} %edge_, ...), custom_call_target="tpu_custom_call" | custom-call | flops 5000000000 | tf_op jit(solution)/shard_map/ranks/pallas_call | solution.py:628
  9.7 0.1 collective-permute-done.1
  9.7 1.1 %collective-permute-done.2 = bf16[2,2,128,128]{3,2,1,0:T(8,128)(2,1)S(1)} collective-permute-done((bf16[2,2,128,128]{3,2,1,0:T(8,128)(2,1)S(1)}, bf16[2,2,128,128]{3,2,1,0:T(8,128)(2,1)S(1)}, u32[]{:S(2)}, u32[]{:S(2)}) %collective-permute-start.2) | collective-permute-done | bytes 131104 | tf_op jit(solution)/shard_map/ppermute | solution.py:624
  10.9 0.0 copy-start.10
  10.9 0.2 collective-permute-start.4
  11.1 1.1 %prepare.1 = (bf16[3,128,256]{2,1,0:T(8,128)(2,1)S(1)}, f32[128,1536]{1,0:T(8,128)S(1)}) custom-call(bf16[4,128,256]{2,1,0:T(8,128)(2,1)S(1)} %get-tuple-element.80.far_ref.far_own_ref, bf16[2,3,128,128]{3,2,1,0:T(8,128)(2,1)S(1)} %constant_dynamic-update-slice_fusion.mine_ref, bf16[11,128,128]{2,1,0:T(8,128)(2,1)S(1)} %get-tuple-element.81.weights_ref.refs_4_, ...), custom_call_target="tpu_custom_call" | custom-call | flops 5000000000 | tf_op jit(solution)/shard_map/prepare/pallas_call | solution.py:628
  12.2 0.3 %collective-permute-done.4 = bf16[8,128,128]{2,1,0:T(8,128)(2,1)S(1)} collective-permute-done((bf16[8,128,128]{2,1,0:T(8,128)(2,1)S(1)}, bf16[8,128,128]{2,1,0:T(8,128)(2,1)S(1)}, u32[]{:S(2)}, u32[]{:S(2)}) %collective-permute-start.4) | collective-permute-done | bytes 262176 | tf_op jit(solution)/shard_map/ppermute | solution.py:604
  12.5 2.2 %movers.1 = (bf16[8,128,256]{2,1,0:T(8,128)(2,1)S(1)}, f32[16,128]{1,0:T(8,128)S(1)}) custom-call(bf16[2,128,128]{2,1,0:T(8,128)(2,1)S(1)} %dynamic-slice_bitcast_fusion.refs_0_, bf16[2,128,128]{2,1,0:T(8,128)(2,1)S(1)} %slice.6.refs_1_, bf16[2,3,128,128]{3,2,1,0:T(8,128)(2,1)S(1)} %bitcast.21, bf16[3,128,256]{2,1,0:T(8,128)(2,1)S(1)} %get-tuple-element.89.refs_3_, ...), custom_call_target="tpu_custom_call" | custom-call | flops 3000000000 | tf_op jit(solution)/shard_map/movers/pallas_call | solution.py:628
  14.7 0.1 collective-permute-start.6
  14.9 1.5 %collective-permute-start.5 = (f32[16,128]{1,0:T(8,128)S(1)}, f32[16,128]{1,0:T(8,128)S(1)}, u32[]{:S(2)}, u32[]{:S(2)}) collective-permute-start(f32[16,128]{1,0:T(8,128)S(1)} %get-tuple-element.94), channel_id=1, source_target_pairs={{0,2},{2,0},{1,3},{3,1},{4,6},{6,4},{5,7},{7,5},{8,10},{10,8},{9,1... | collective-permute-start | bytes 24584 | tf_op jit(solution)/shard_map/ppermute | solution.py:604
  16.4 1.8 %collective-permute-start.7 = (f32[2,16,128]{2,1,0:T(8,128)S(1)}, f32[2,16,128]{2,1,0:T(8,128)S(1)}, u32[]{:S(2)}, u32[]{:S(2)}) collective-permute-start(f32[2,16,128]{2,1,0:T(8,128)S(1)} %pad_maximum_fusion.3), channel_id=1, source_target_pairs={{0,7},{1,3},{2,5},{3,1},{4,11},{5,2},{6,9},{7,0},{8,15},{9,6},{10,... | collective-permute-start | bytes 49160 | tf_op jit(solution)/shard_map/ppermute | solution.py:624
  18.2 0.4 %collective-permute-start.8 = (f32[2,16,128]{2,1,0:T(8,128)S(1)}, f32[2,16,128]{2,1,0:T(8,128)S(1)}, u32[]{:S(2)}, u32[]{:S(2)}) collective-permute-start(f32[2,16,128]{2,1,0:T(8,128)S(1)} %pad_maximum_fusion.3), channel_id=1, source_target_pairs={{0,5},{1,3},{2,7},{3,1},{4,9},{5,0},{6,11},{7,2},{8,13},{9,4},{10,... | collective-permute-start | bytes 49160 | tf_op jit(solution)/shard_map/ppermute | solution.py:624
  18.6 2.0 %edges.3.second_ref = bf16[2,128,128]{2,1,0:T(8,128)(2,1)S(1)} custom-call(f32[2,2,1,128]{3,2,1,0:T(1,128)S(1)} %get-tuple-element.60.alive_ref, bf16[2,2,1,128,128]{4,3,2,1,0:T(8,128)(2,1)S(1)} %get-tuple-element.59.latent_ref, bf16[2,2,1,12,128,128]{5,4,3,2,1,0:T(8,128)(2,1)S(1)} %get-tuple-element.97.edge_ref, s32[2,2,12,1,128]{4,3,2,1,0:T(1,128)S(1)} %bitcast.27, ...), custom_call_target="tpu_custom_call" | custom-call | flops 4000000000 | tf_op jit(solution)/shard_map/edges/pallas_call | solution.py:628
  20.6 2.0 %edges.2.first_ref = bf16[2,128,128]{2,1,0:T(8,128)(2,1)S(1)} custom-call(f32[2,2,1,128]{3,2,1,0:T(1,128)S(1)} %get-tuple-element.60.alive_ref, bf16[2,2,1,128,128]{4,3,2,1,0:T(8,128)(2,1)S(1)} %get-tuple-element.59.latent_ref, bf16[2,2,1,12,128,128]{5,4,3,2,1,0:T(8,128)(2,1)S(1)} %get-tuple-element.97.edge_ref, s32[2,2,12,1,128]{4,3,2,1,0:T(1,128)S(1)} %bitcast.28, ...), custom_call_target="tpu_custom_call" | custom-call | flops 4000000000 | tf_op jit(solution)/shard_map/edges/pallas_call | solution.py:628
  22.6 0.0 copy-start.4
  22.6 0.1 collective-permute-start.9
  22.7 1.0 %nodes.1.moved_ref = f32[16,512]{1,0:T(8,128)S(1)} custom-call(bf16[2,128,128]{2,1,0:T(8,128)(2,1)S(1)} %edges.2.first_ref, bf16[2,128,128]{2,1,0:T(8,128)(2,1)S(1)} %edges.3.second_ref, f32[128,512]{1,0:T(8,128)S(1)} %get-tuple-element.105.node_pre_ref, f32[128,512]{1,0:T(8,128)S(1)} %get-tuple-element.106.latent_t_ref, ...), custom_call_target="tpu_custom_call" | custom-call | flops 1000000000 | tf_op jit(solution)/shard_map/nodes/pallas_call | solution.py:628
  23.7 0.2 collective-permute-done.9.refs_3_
  23.9 1.5 %finish.1 = (bf16[2,2,1,128,128]{4,3,2,1,0:T(8,128)(2,1)}, f32[9,2,2,1,128]{4,3,2,1,0:T(1,128)}, bf16[1,1,1,208,128]{4,3,2,1,0:T(8,128)(2,1)}, f32[9,1,1,1,208]{4,3,2,1,0:T(1,128)}) custom-call(f32[16,512]{1,0:T(8,128)S(1)} %nodes.1.moved_ref, f32[16,128]{1,0:T(8,128)S(1)} %collective-permute-done.6.zed_ref, f32[16,128]{1,0:T(8,128)S(1)} %collective-permute-done.5.refs_0_, ...), custom_call_target="tpu_custom_call" | custom-call | flops 1000000000 | tf_op jit(solution)/shard_map/finish/pallas_call | solution.py:628
  (39 shorter events, 0.2 us)
Async XLA Ops:
  0.6 4.3 %collective-permute-start = (bf16[2,2,1,128,128]{4,3,2,1,0:T(8,128)(2,1)}, bf16[2,2,1,128,128]{4,3,2,1,0:T(8,128)(2,1)S(1)}, u32[]{:S(2)}, u32[]{:S(2)}) collective-permute-start(bf16[2,2,1,128,128]{4,3,2,1,0:T(8,128)(2,1)} %refs_0_.1), channel_id=1, source_target_pairs={{0,1},{1,0},{2,3},{3,2},{4,5},{5,4},{6,7},{7,6},{8,9},{9,8},{10,11... | collective-permute-start | bytes 393224 | tf_op jit(solution)/shard_map/ppermute | solution.py:604
  1.2 8.5 %collective-permute-start.3 = (bf16[2,2,1,128,128]{4,3,2,1,0:T(8,128)(2,1)}, bf16[2,2,1,128,128]{4,3,2,1,0:T(8,128)(2,1)S(1)}, u32[]{:S(2)}, u32[]{:S(2)}) collective-permute-start(bf16[2,2,1,128,128]{4,3,2,1,0:T(8,128)(2,1)} %refs_0_.1), channel_id=1, source_target_pairs={{0,2},{2,0},{1,3},{3,1},{4,6},{6,4},{5,7},{7,5},{8,10},{10,8},{9,1... | collective-permute-start | bytes 393224 | tf_op jit(solution)/shard_map/ppermute | solution.py:604
  3.7 2.8 %copy-start = (bf16[5,128,128]{2,1,0:T(8,128)(2,1)S(1)}, bf16[5,128,128]{2,1,0:T(8,128)(2,1)}, u32[]{:S(2)}) copy-start(bf16[5,128,128]{2,1,0:T(8,128)(2,1)} %edge_w_ref.1) | copy-start | bytes 491524
  3.7 2.8 %copy-start.1 = (bf16[256,128]{1,0:T(8,128)(2,1)S(1)}, bf16[256,128]{1,0:T(8,128)(2,1)}, u32[]{:S(2)}) copy-start(bf16[256,128]{1,0:T(8,128)(2,1)} %node_in_ref.1) | copy-start | bytes 196612
  3.7 2.8 %copy-start.2 = (bf16[2,128,128]{2,1,0:T(8,128)(2,1)S(1)}, bf16[2,128,128]{2,1,0:T(8,128)(2,1)}, u32[]{:S(2)}) copy-start(bf16[2,128,128]{2,1,0:T(8,128)(2,1)} %node_w_ref.1) | copy-start | bytes 196612
  3.7 2.8 %copy-start.3 = (bf16[2,128,128]{2,1,0:T(8,128)(2,1)S(1)}, bf16[2,128,128]{2,1,0:T(8,128)(2,1)}, u32[]{:S(2)}) copy-start(bf16[2,128,128]{2,1,0:T(8,128)(2,1)} %decoder_w_ref.1) | copy-start | bytes 196612
  3.7 2.8 %copy-start.5 = (s32[2,2,1,12,128]{4,2,3,1,0:T(1,128)S(1)}, s32[2,2,1,12,128]{4,2,3,1,0:T(1,128)}, u32[]{:S(2)}) copy-start(s32[2,2,1,12,128]{4,2,3,1,0:T(1,128)} %param.19) | copy-start | bytes 73732
  3.7 2.8 %copy-start.6 = (f32[3,2,2,1,128]{4,3,2,1,0:T(1,128)S(1)}, f32[3,2,2,1,128]{4,3,2,1,0:T(1,128)}, u32[]{:S(2)}) copy-start(f32[3,2,2,1,128]{4,3,2,1,0:T(1,128)} %positions_ref.1) | copy-start | bytes 18436
  3.7 2.8 %copy-start.7 = (f32[3,2,2,1,128]{4,3,2,1,0:T(1,128)S(1)}, f32[3,2,2,1,128]{4,3,2,1,0:T(1,128)}, u32[]{:S(2)}) copy-start(f32[3,2,2,1,128]{4,3,2,1,0:T(1,128)} %velocity_ref.1) | copy-start | bytes 18436
  3.8 2.8 %copy-start.8 = (bf16[12,128]{1,0:T(8,128)(2,1)S(1)}, bf16[12,128]{1,0:T(8,128)(2,1)}, u32[]{:S(2)}) copy-start(bf16[12,128]{1,0:T(8,128)(2,1)} %encoder_in_ref.1) | copy-start | bytes 9220
  3.8 2.8 %copy-start.9 = (s32[2,2,1,128]{3,2,1,0:T(1,128)S(1)}, s32[2,2,1,128]{3,2,1,0:T(1,128)}, u32[]{:S(2)}) copy-start(s32[2,2,1,128]{3,2,1,0:T(1,128)} %owners_ref.1) | copy-start | bytes 6148
  4.9 4.8 %collective-permute-start.1 = (bf16[2,1,128,128]{3,2,1,0:T(8,128)(2,1)S(1)}, bf16[2,1,128,128]{3,2,1,0:T(8,128)(2,1)S(1)}, u32[]{:S(2)}, u32[]{:S(2)}) collective-permute-start(bf16[2,1,128,128]{3,2,1,0:T(8,128)(2,1)S(1)} %maximum_bitcast_fusion), channel_id=1, source_target_pairs={{0,7},{1,3},{2,5},{3,1},{4,11},{5,2},{6,9},{7,0},{8,15},{9,6},{10,... | collective-permute-start | bytes 196616 | tf_op jit(solution)/shard_map/ppermute | solution.py:624
  6.3 4.5 %collective-permute-start.2 = (bf16[2,2,128,128]{3,2,1,0:T(8,128)(2,1)S(1)}, bf16[2,2,128,128]{3,2,1,0:T(8,128)(2,1)S(1)}, u32[]{:S(2)}, u32[]{:S(2)}) collective-permute-start(bf16[2,2,128,128]{3,2,1,0:T(8,128)(2,1)S(1)} %pad_maximum_fusion.1), channel_id=1, source_target_pairs={{0,5},{1,3},{2,7},{3,1},{4,9},{5,0},{6,11},{7,2},{8,13},{9,4},{10,... | collective-permute-start | bytes 393224 | tf_op jit(solution)/shard_map/ppermute | solution.py:624
  10.9 1.6 %copy-start.10 = (bf16[3,128]{1,0:T(4,128)(2,1)S(1)}, bf16[3,128]{1,0:T(4,128)(2,1)}, u32[]{:S(2)}) copy-start(bf16[3,128]{1,0:T(4,128)(2,1)} %decoder_out_ref.1) | copy-start | bytes 2308
  10.9 1.6 %collective-permute-start.4 = (bf16[8,128,128]{2,1,0:T(8,128)(2,1)S(1)}, bf16[8,128,128]{2,1,0:T(8,128)(2,1)S(1)}, u32[]{:S(2)}, u32[]{:S(2)}) collective-permute-start(bf16[8,128,128]{2,1,0:T(8,128)(2,1)S(1)} %pad_maximum_fusion), channel_id=1, source_target_pairs={{0,1},{1,0},{2,3},{3,2},{4,5},{5,4},{6,7},{7,6},{8,9},{9,8},{10,11... | collective-permute-start | bytes 786440 | tf_op jit(solution)/shard_map/ppermute | solution.py:604
  14.7 1.6 %collective-permute-start.6 = (f32[16,128]{1,0:T(8,128)S(1)}, f32[16,128]{1,0:T(8,128)S(1)}, u32[]{:S(2)}, u32[]{:S(2)}) collective-permute-start(f32[16,128]{1,0:T(8,128)S(1)} %get-tuple-element.94), channel_id=1, source_target_pairs={{0,1},{1,0},{2,3},{3,2},{4,5},{5,4},{6,7},{7,6},{8,9},{9,8},{10,11... | collective-permute-start | bytes 24584 | tf_op jit(solution)/shard_map/ppermute | solution.py:604
  14.9 7.7 %collective-permute-start.5 = (f32[16,128]{1,0:T(8,128)S(1)}, f32[16,128]{1,0:T(8,128)S(1)}, u32[]{:S(2)}, u32[]{:S(2)}) collective-permute-start(f32[16,128]{1,0:T(8,128)S(1)} %get-tuple-element.94), channel_id=1, source_target_pairs={{0,2},{2,0},{1,3},{3,1},{4,6},{6,4},{5,7},{7,5},{8,10},{10,8},{9,1... | collective-permute-start | bytes 24584 | tf_op jit(solution)/shard_map/ppermute | solution.py:604
  16.4 6.2 %collective-permute-start.7 = (f32[2,16,128]{2,1,0:T(8,128)S(1)}, f32[2,16,128]{2,1,0:T(8,128)S(1)}, u32[]{:S(2)}, u32[]{:S(2)}) collective-permute-start(f32[2,16,128]{2,1,0:T(8,128)S(1)} %pad_maximum_fusion.3), channel_id=1, source_target_pairs={{0,7},{1,3},{2,5},{3,1},{4,11},{5,2},{6,9},{7,0},{8,15},{9,6},{10,... | collective-permute-start | bytes 49160 | tf_op jit(solution)/shard_map/ppermute | solution.py:624
  18.2 4.4 %collective-permute-start.8 = (f32[2,16,128]{2,1,0:T(8,128)S(1)}, f32[2,16,128]{2,1,0:T(8,128)S(1)}, u32[]{:S(2)}, u32[]{:S(2)}) collective-permute-start(f32[2,16,128]{2,1,0:T(8,128)S(1)} %pad_maximum_fusion.3), channel_id=1, source_target_pairs={{0,5},{1,3},{2,7},{3,1},{4,9},{5,0},{6,11},{7,2},{8,13},{9,4},{10,... | collective-permute-start | bytes 49160 | tf_op jit(solution)/shard_map/ppermute | solution.py:624
  22.6 1.3 %copy-start.4 = (bf16[2,128,128]{2,1,0:T(8,128)(2,1)S(1)}, bf16[2,128,128]{2,1,0:T(8,128)(2,1)}, u32[]{:S(2)}) copy-start(bf16[2,128,128]{2,1,0:T(8,128)(2,1)} %refs_6_.1) | copy-start | bytes 196612
  22.6 1.3 %collective-permute-start.9 = (f32[5,16,128]{2,1,0:T(8,128)S(1)}, f32[5,16,128]{2,1,0:T(8,128)S(1)}, u32[]{:S(2)}, u32[]{:S(2)}) collective-permute-start(f32[5,16,128]{2,1,0:T(8,128)S(1)} %pad_maximum_fusion.2), channel_id=1, source_target_pairs={{0,1},{1,0},{2,3},{3,2},{4,5},{5,4},{6,7},{7,6},{8,9},{9,8},{10,11... | collective-permute-start | bytes 122888 | tf_op jit(solution)/shard_map/ppermute | solution.py:604

commit v15 on v14

--- a/solution.py
+++ b/solution.py
@@ -203,7 +203,7 @@
 
 def ranks_kernel(
     sizes,
-    edge_any,
+    edge_ref,
     latent_ref,
     own_zed,
     alive_ref,
@@ -218,7 +218,6 @@
     velocity_ref,
     weights_ref,
     inward_ref,
-    edge_ref,
     spread_ref,
     latent_t_ref,
     node_pre_ref,
@@ -231,12 +230,10 @@
     mover_latent_ref,
     mover_state_ref,
     far_ref,
-    early_ref,
-    sems,
+    pre_ref,
 ):
     count_x, count_y, count_z = sizes
     fold_y = count_y == 2
-    copies = fetch([(edge_any, edge_ref)], sems)
     index_x = lax.axis_index("gx")
     index_y = lax.axis_index("gy")
     index_z = lax.axis_index("gz")
@@ -346,11 +343,16 @@
         b = (index_y if bt == 0 else 1 - index_y) if fold_y else bt
         ids = jnp.concatenate([neighbours_ref[a, b, k] for k in range(neighbour_count)], axis=1)
         place, key = places(ids & 127, ids >> 7, fold_y)
+        near = dot_nt(weights_ref[NEAR], latent_ref[a, b, 0])
+        near = jnp.concatenate([near, near], axis=1)
         for tile in range(ids.shape[1] // TILE):
             at = slice(tile * TILE, (tile + 1) * TILE)
-            early_ref[2 * a + bt, :, at] = pick(cells, place[:, at], key[:, at]).astype(BF16)
-
-    copies[-1].wait()
+            edges = [edge_ref[a, b, 0, k] for k in (2 * tile, 2 * tile + 1)]
+            pre_ref[2 * a + bt, :, at] = (
+                dot_nt(weights_ref[EDGE], jnp.concatenate(edges, axis=0))
+                + near
+                + pick(cells, place[:, at], key[:, at])
+            )
     for k in range(neighbour_count):
         rows = jnp.concatenate([edge_ref[a, b, 0, k] for a, b in CELLS], axis=0)
         mover_edge_ref[k] = dot(placer, rows).astype(BF16)
@@ -451,23 +453,19 @@
     sizes,
     a,
     alive_ref,
-    latent_ref,
-    edge_ref,
     neighbours_ref,
-    far_own_ref,
-    far_rest_ref,
-    early_ref,
+    far_ref,
+    pre_ref,
     weights_ref,
     total_ref,
     hidden_ref,
 ):
     fold_y = sizes[1] == 2
-    window = Window(fold_y, far_own_ref, far_rest_ref)
+    window = Window(fold_y, None, far_ref)
     index_y = lax.axis_index("gy")
-    alive_ref, latent_ref = alive_ref.at[a], latent_ref.at[a]
-    edge_ref, neighbours_ref = edge_ref.at[a], neighbours_ref.at[a]
-    slots, width = latent_ref.shape[-2:]
-    neighbour_count = edge_ref.shape[2]
+    alive_ref, neighbours_ref = alive_ref.at[a], neighbours_ref.at[a]
+    slots = alive_ref.shape[-1]
+    neighbour_count = neighbours_ref.shape[1]
     for bt in range(2):
         if fold_y:
             b = index_y if bt == 0 else 1 - index_y
@@ -477,21 +475,14 @@
             rows = (bt, bt + 1, bt + 2)
         columns = [(ex, row) for ex in range(a, a + 3) for row in rows]
         columns = [column for column in columns if column not in window.own_columns()]
-        near = dot_nt(weights_ref[NEAR], latent_ref[b, 0])
-        near = jnp.concatenate([near, near], axis=1)
         ids = jnp.concatenate([neighbours_ref[b, k] for k in range(neighbour_count)], axis=1)
         place, key = places(ids & 127, ids >> 7, fold_y)
-
-        def pre(tile, b=b, bt=bt, near=near):
-            edges = jnp.concatenate([edge_ref[b, 0, 2 * tile], edge_ref[b, 0, 2 * tile + 1]], axis=0)
-            early = early_ref[2 * a + bt, :, tile * TILE : (tile + 1) * TILE]
-            return dot_nt(weights_ref[EDGE], edges) + near + early.astype(F32)
 
         message = messages(
             window.cells(columns),
             place,
             key,
-            pre,
+            lambda tile, i=2 * a + bt: pre_ref[i, :, tile * TILE : (tile + 1) * TILE],
             weights_ref[MIDDLE],
             weights_ref[FINAL],
             hidden_ref.at[bt],
@@ -691,11 +682,11 @@
     if fold_y:
         row = 1 - lax.axis_index("gy")
         beside = lax.dynamic_index_in_dim(own_zed[:, :, 0], 1 - core, 0, False)
-        corner = jnp.concatenate(
-            [lax.dynamic_slice_in_dim(part, row, 1, 0) for part in (end[:, 0], beside)], axis=0
-        )
         both = jnp.stack([end[:, 0], beside])
-        mine = [swap_chips(corner[:, None], True), swap_chips(both, False)]
+        corner = lax.dynamic_slice_in_dim(both, row, 1, axis=1)
+        mine = [swap_chips(both, False)]
+        corner, both = lax.optimization_barrier((corner, both))
+        mine.append(swap_chips(corner, True))
     else:
         sides = [shift(latent[:, 1, 0], "gy", 0), shift(latent[:, 0, 0], "gy", 1)]
         side_zeds = [swap(part, "gz") for part in sides]
@@ -709,11 +700,10 @@
     ranked = call(
         functools.partial(ranks_kernel, sizes),
         "ranks",
-        [ANY] + [VMEM] * 12,
+        [VMEM] * 13,
         [
             ((11, width, width), BF16),
             ((48, width), BF16),
-            (edge_latent.shape, BF16),
             ((8, 256), I32),
             ((width, particles), F32),
             ((width, particles), F32),
@@ -726,17 +716,16 @@
             ((width, movers), F32),
             ((8, movers), F32),
             ((4, width, 2 * slots), BF16),
-            ((4, width, neighbour_count * slots), BF16),
+            ((4, width, neighbour_count * slots), F32),
         ],
-        [pltpu.SemaphoreType.DMA((1,))],
-        (in_hbm(edge_latent), latent, own_zed, alive, owners, edge_weights, node_in, node_weights, decoder_weights, encoder_in, neighbours, positions, velocity),
+        [],
+        (edge_latent, latent, own_zed, alive, owners, edge_weights, node_in, node_weights, decoder_weights, encoder_in, neighbours, positions, velocity),
         5_000_000_000,
     )
     mine, sides, ranked = lax.optimization_barrier((mine, sides, ranked))
     (
         weights,
         inward,
-        edge_latent,
         spread,
         latent_t,
         node_pre,
@@ -749,9 +738,9 @@
         mover_latent,
         mover_state,
         far_own,
-        early,
+        edge_pre,
     ) = ranked
-    mine = jnp.concatenate(mine[::-1], axis=1)
+    mine = jnp.concatenate(mine, axis=1)
     if fold_y:
         sides = [lax.dynamic_index_in_dim(sides[0][:, :, 0], lax.axis_index("gy"), 1, False)]
         packed = jnp.concatenate([mine.reshape(-1, slots, width), sides[0]], axis=0)
@@ -798,10 +787,10 @@
         return call(
             functools.partial(edges_kernel, sizes, a),
             "edges",
-            [VMEM] * 8,
+            [VMEM] * 5,
             [((2, width, slots), BF16)],
             [pltpu.VMEM((2, width, neighbour_count * slots), BF16)],
-            (alive, latent, edge_latent, neighbours, far_own, far_rest, early, weights),
+            (alive, neighbours, far_rest, edge_pre, weights),
             4_000_000_000,
         )[0]
 

time: 25.6 us -> 25.1 us (0.980)
  starting transfers between devices: 8.77 us -> 8.16 us
    ppermute x6, starting transfers between devices: 4.98 us -> 4.65 us  [swap(): return lax.ppermute(values, axis, [(0, 1), (1, 0)])]
    ppermute x4, starting transfers between devices: 3.79 us -> 3.52 us  [swap_chips(): return lax.ppermute(values, ('gx', 'gy', 'gz'), pairs)]
  transfers between devices with their start and end apart: 10 -> 10, of which waited for: 4 -> 3; matrix products, arithmetic and copies ran while one was open for 0% -> 0% of each run, Pallas kernels for 40% -> 41%
where the time goes in v15:
time: 25.1 us; the launch traced here: 25 us
  Pallas kernels  14 us (56%)
  starting transfers between devices  8.16 us (33%)
  waiting for transfers between devices  1.71 us (7%)
  between operations  0.95 us (4%)
    pallas_call x8, Pallas kernels, call(): pl.pallas_call(kernel, out_shape=tuple((jax.ShapeDtypeStruct(shape, kind)...  14 us
    ppermute x6, starting transfers between devices, swap(): return lax.ppermute(values, axis, [(0, 1), (1, 0)])  4.65 us
    ppermute x4, starting transfers between devices, swap_chips(): return lax.ppermute(values, ('gx', 'gy', 'gz'), pairs)  3.52 us
    ppermute x4, waiting for transfers between devices, swap_chips(): return lax.ppermute(values, ('gx', 'gy', 'gz'), pairs)  1.08 us
    ppermute x6, waiting for transfers between devices, swap(): return lax.ppermute(values, axis, [(0, 1), (1, 0)])  0.63 us
  transfers between devices with their start and end apart: 10, of which 3 were waited for; matrix products, arithmetic and copies ran while one was open for 0% of the time, Pallas kernels for 41%

profile of v15, /device:TPU:0, one launch (start us, length us, event | category | flops | bytes accessed | tf_op | source)
XLA Modules:
  0.0 25.0 jit_solution(13583874309494603630)
XLA Ops:
  0.6 0.5 %collective-permute-start = (bf16[2,2,1,128,128]{4,3,2,1,0:T(8,128)(2,1)}, bf16[2,2,1,128,128]{4,3,2,1,0:T(8,128)(2,1)S(1)}, u32[]{:S(2)}, u32[]{:S(2)}) collective-permute-start(bf16[2,2,1,128,128]{4,3,2,1,0:T(8,128)(2,1)} %refs_0_.1), channel_id=1, source_target_pairs={{0,1},{1,0},{2,3},{3,2},{4,5},{5,4},{6,7},{7,6},{8,9},{9,8},{10,11... | collective-permute-start | bytes 393224 | tf_op jit(solution)/shard_map/ppermute | solution.py:595
  1.2 2.6 %collective-permute-start.3 = (bf16[2,2,1,128,128]{4,3,2,1,0:T(8,128)(2,1)}, bf16[2,2,1,128,128]{4,3,2,1,0:T(8,128)(2,1)S(1)}, u32[]{:S(2)}, u32[]{:S(2)}) collective-permute-start(bf16[2,2,1,128,128]{4,3,2,1,0:T(8,128)(2,1)} %refs_0_.1), channel_id=1, source_target_pairs={{0,2},{2,0},{1,3},{3,1},{4,6},{6,4},{5,7},{7,5},{8,10},{10,8},{9,1... | collective-permute-start | bytes 393224 | tf_op jit(solution)/shard_map/ppermute | solution.py:595
  3.8 0.0 copy-start.10
  3.8 1.1 %cut.1 = (bf16[2,2,1,128,128]{4,3,2,1,0:T(8,128)(2,1)S(1)}, bf16[2,1,128,128]{3,2,1,0:T(8,128)(2,1)S(1)}, f32[2,2,1,128]{3,2,1,0:T(1,128)S(1)}) custom-call(s32[2,1,2]{2,1,0:T(1,128)} %bitcast.24, bf16[2,2,1,128,128]{4,3,2,1,0:T(8,128)(2,1)} %refs_0_.1), custom_call_target="tpu_custom_call" | custom-call | flops 5000000000 | tf_op jit(solution)/shard_map/cut/pallas_call | solution.py:619
  5.0 1.4 %collective-permute-start.1 = (bf16[2,2,128,128]{3,2,1,0:T(8,128)(2,1)S(1)}, bf16[2,2,128,128]{3,2,1,0:T(8,128)(2,1)S(1)}, u32[]{:S(2)}, u32[]{:S(2)}) collective-permute-start(bf16[2,2,128,128]{3,2,1,0:T(8,128)(2,1)S(1)} %pad_maximum_fusion.1), channel_id=1, source_target_pairs={{0,5},{1,3},{2,7},{3,1},{4,9},{5,0},{6,11},{7,2},{8,13},{9,4},{10,... | collective-permute-start | bytes 393224 | tf_op jit(solution)/shard_map/ppermute | solution.py:615
  6.4 0.1 collective-permute-start.2
  6.6 3.3 %ranks.1 = (bf16[11,128,128]{2,1,0:T(8,128)(2,1)S(1)}, bf16[48,128]{1,0:T(8,128)(2,1)S(1)}, s32[8,256]{1,0:T(8,128)S(1)}, f32[128,512]{1,0:T(8,128)S(1)}, f32[12...) custom-call(bf16[2,2,1,12,128,128]{5,4,3,2,1,0:T(8,128)(2,1)S(1)} %c, ...), custom_call_target="tpu_custom_call" | custom-call | flops 5000000000 | tf_op jit(solution)/shard_map/ranks/pallas_call | solution.py:619
  9.9 1.1 %collective-permute-done.2 = bf16[2,1,128,128]{3,2,1,0:T(8,128)(2,1)S(1)} collective-permute-done((bf16[2,1,128,128]{3,2,1,0:T(8,128)(2,1)S(1)}, bf16[2,1,128,128]{3,2,1,0:T(8,128)(2,1)S(1)}, u32[]{:S(2)}, u32[]{:S(2)}) %collective-permute-start.2) | collective-permute-done | bytes 65568 | tf_op jit(solution)/shard_map/ppermute | solution.py:615
  11.1 0.0 copy-start.11
  11.1 0.1 collective-permute-start.4
  11.2 1.1 %prepare.1 = (bf16[3,128,256]{2,1,0:T(8,128)(2,1)S(1)}, f32[128,1536]{1,0:T(8,128)S(1)}) custom-call(bf16[4,128,256]{2,1,0:T(8,128)(2,1)S(1)} %get-tuple-element.79.far_ref, bf16[2,3,128,128]{3,2,1,0:T(8,128)(2,1)S(1)} %constant_dynamic-update-slice_fusion.mine_ref, bf16[11,128,128]{2,1,0:T(8,128)(2,1)S(1)} %get-tuple-element.80.weights_ref.refs_4_, ...), custom_call_target="tpu_custom_call" | custom-call | flops 5000000000 | tf_op jit(solution)/shard_map/prepare/pallas_call | solution.py:619
  12.3 0.4 %collective-permute-done.4 = bf16[8,128,128]{2,1,0:T(8,128)(2,1)S(1)} collective-permute-done((bf16[8,128,128]{2,1,0:T(8,128)(2,1)S(1)}, bf16[8,128,128]{2,1,0:T(8,128)(2,1)S(1)}, u32[]{:S(2)}, u32[]{:S(2)}) %collective-permute-start.4) | collective-permute-done | bytes 262176 | tf_op jit(solution)/shard_map/ppermute | solution.py:595
  12.7 2.2 %movers.1 = (bf16[8,128,256]{2,1,0:T(8,128)(2,1)S(1)}, f32[16,128]{1,0:T(8,128)S(1)}) custom-call(bf16[2,128,128]{2,1,0:T(8,128)(2,1)S(1)} %dynamic-slice_bitcast_fusion.refs_0_, bf16[2,128,128]{2,1,0:T(8,128)(2,1)S(1)} %slice.6.refs_1_, bf16[2,3,128,128]{3,2,1,0:T(8,128)(2,1)S(1)} %bitcast.17, bf16[3,128,256]{2,1,0:T(8,128)(2,1)S(1)} %get-tuple-element.88.refs_3_, ...), custom_call_target="tpu_custom_call" | custom-call | flops 3000000000 | tf_op jit(solution)/shard_map/movers/pallas_call | solution.py:619
  14.9 0.1 collective-permute-start.6
  15.1 1.3 %collective-permute-start.5 = (f32[16,128]{1,0:T(8,128)S(1)}, f32[16,128]{1,0:T(8,128)S(1)}, u32[]{:S(2)}, u32[]{:S(2)}) collective-permute-start(f32[16,128]{1,0:T(8,128)S(1)} %get-tuple-element.93), channel_id=1, source_target_pairs={{0,2},{2,0},{1,3},{3,1},{4,6},{6,4},{5,7},{7,5},{8,10},{10,8},{9,1... | collective-permute-start | bytes 24584 | tf_op jit(solution)/shard_map/ppermute | solution.py:595
  16.4 1.6 %collective-permute-start.7 = (f32[2,16,128]{2,1,0:T(8,128)S(1)}, f32[2,16,128]{2,1,0:T(8,128)S(1)}, u32[]{:S(2)}, u32[]{:S(2)}) collective-permute-start(f32[2,16,128]{2,1,0:T(8,128)S(1)} %pad_maximum_fusion.3), channel_id=1, source_target_pairs={{0,7},{1,3},{2,5},{3,1},{4,11},{5,2},{6,9},{7,0},{8,15},{9,6},{10,... | collective-permute-start | bytes 49160 | tf_op jit(solution)/shard_map/ppermute | solution.py:615
  18.0 0.4 %collective-permute-start.8 = (f32[2,16,128]{2,1,0:T(8,128)S(1)}, f32[2,16,128]{2,1,0:T(8,128)S(1)}, u32[]{:S(2)}, u32[]{:S(2)}) collective-permute-start(f32[2,16,128]{2,1,0:T(8,128)S(1)} %pad_maximum_fusion.3), channel_id=1, source_target_pairs={{0,5},{1,3},{2,7},{3,1},{4,9},{5,0},{6,11},{7,2},{8,13},{9,4},{10,... | collective-permute-start | bytes 49160 | tf_op jit(solution)/shard_map/ppermute | solution.py:615
  18.4 1.9 %edges.3.second_ref = bf16[2,128,128]{2,1,0:T(8,128)(2,1)S(1)} custom-call(f32[2,2,1,128]{3,2,1,0:T(1,128)S(1)} %get-tuple-element.60.alive_ref, s32[2,2,12,1,128]{4,3,2,1,0:T(1,128)S(1)} %bitcast.22, bf16[8,128,256]{2,1,0:T(8,128)(2,1)S(1)} %get-tuple-element.96.far_ref, f32[4,128,1536]{2,1,0:T(8,128)S(1)} %get-tuple-element.97.pre_ref, ...), custom_call_target="tpu_custom_call" | custom-call | flops 4000000000 | tf_op jit(solution)/shard_map/edges/pallas_call | solution.py:619
  20.2 1.9 %edges.2.first_ref = bf16[2,128,128]{2,1,0:T(8,128)(2,1)S(1)} custom-call(f32[2,2,1,128]{3,2,1,0:T(1,128)S(1)} %get-tuple-element.60.alive_ref, s32[2,2,12,1,128]{4,3,2,1,0:T(1,128)S(1)} %bitcast.23, bf16[8,128,256]{2,1,0:T(8,128)(2,1)S(1)} %get-tuple-element.96.far_ref, f32[4,128,1536]{2,1,0:T(8,128)S(1)} %get-tuple-element.97.pre_ref, ...), custom_call_target="tpu_custom_call" | custom-call | flops 4000000000 | tf_op jit(solution)/shard_map/edges/pallas_call | solution.py:619
  22.1 0.0 copy-start.5
  22.2 0.1 collective-permute-start.9
  22.3 1.0 %nodes.1.moved_ref = f32[16,512]{1,0:T(8,128)S(1)} custom-call(bf16[2,128,128]{2,1,0:T(8,128)(2,1)S(1)} %edges.2.first_ref, bf16[2,128,128]{2,1,0:T(8,128)(2,1)S(1)} %edges.3.second_ref, f32[128,512]{1,0:T(8,128)S(1)} %get-tuple-element.103.node_pre_ref, f32[128,512]{1,0:T(8,128)S(1)} %get-tuple-element.104.latent_t_ref, ...), custom_call_target="tpu_custom_call" | custom-call | flops 1000000000 | tf_op jit(solution)/shard_map/nodes/pallas_call | solution.py:619
  23.3 0.2 collective-permute-done.9.refs_3_
  23.5 1.5 %finish.1 = (bf16[2,2,1,128,128]{4,3,2,1,0:T(8,128)(2,1)}, f32[9,2,2,1,128]{4,3,2,1,0:T(1,128)}, bf16[1,1,1,208,128]{4,3,2,1,0:T(8,128)(2,1)}, f32[9,1,1,1,208]{4,3,2,1,0:T(1,128)}) custom-call(f32[16,512]{1,0:T(8,128)S(1)} %nodes.1.moved_ref, f32[16,128]{1,0:T(8,128)S(1)} %collective-permute-done.6.zed_ref, f32[16,128]{1,0:T(8,128)S(1)} %collective-permute-done.5.refs_0_, ...), custom_call_target="tpu_custom_call" | custom-call | flops 1000000000 | tf_op jit(solution)/shard_map/finish/pallas_call | solution.py:619
  (39 shorter events, 0.2 us)
Async XLA Ops:
  0.6 4.3 %collective-permute-start = (bf16[2,2,1,128,128]{4,3,2,1,0:T(8,128)(2,1)}, bf16[2,2,1,128,128]{4,3,2,1,0:T(8,128)(2,1)S(1)}, u32[]{:S(2)}, u32[]{:S(2)}) collective-permute-start(bf16[2,2,1,128,128]{4,3,2,1,0:T(8,128)(2,1)} %refs_0_.1), channel_id=1, source_target_pairs={{0,1},{1,0},{2,3},{3,2},{4,5},{5,4},{6,7},{7,6},{8,9},{9,8},{10,11... | collective-permute-start | bytes 393224 | tf_op jit(solution)/shard_map/ppermute | solution.py:595
  1.2 8.8 %collective-permute-start.3 = (bf16[2,2,1,128,128]{4,3,2,1,0:T(8,128)(2,1)}, bf16[2,2,1,128,128]{4,3,2,1,0:T(8,128)(2,1)S(1)}, u32[]{:S(2)}, u32[]{:S(2)}) collective-permute-start(bf16[2,2,1,128,128]{4,3,2,1,0:T(8,128)(2,1)} %refs_0_.1), channel_id=1, source_target_pairs={{0,2},{2,0},{1,3},{3,1},{4,6},{6,4},{5,7},{7,5},{8,10},{10,8},{9,1... | collective-permute-start | bytes 393224 | tf_op jit(solution)/shard_map/ppermute | solution.py:595
  3.7 2.8 %copy-start = (bf16[2,2,1,12,128,128]{5,4,3,2,1,0:T(8,128)(2,1)S(1)}, bf16[2,2,1,12,128,128]{5,4,3,2,1,0:T(8,128)(2,1)}, u32[]{:S(2)}) copy-start(bf16[2,2,1,12,128,128]{5,4,3,2,1,0:T(8,128)(2,1)} %edge_ref.1) | copy-start | bytes 4718596
  3.7 2.8 %copy-start.1 = (bf16[5,128,128]{2,1,0:T(8,128)(2,1)S(1)}, bf16[5,128,128]{2,1,0:T(8,128)(2,1)}, u32[]{:S(2)}) copy-start(bf16[5,128,128]{2,1,0:T(8,128)(2,1)} %edge_w_ref.1) | copy-start | bytes 491524
  3.7 2.8 %copy-start.2 = (bf16[256,128]{1,0:T(8,128)(2,1)S(1)}, bf16[256,128]{1,0:T(8,128)(2,1)}, u32[]{:S(2)}) copy-start(bf16[256,128]{1,0:T(8,128)(2,1)} %node_in_ref.1) | copy-start | bytes 196612
  3.7 2.8 %copy-start.3 = (bf16[2,128,128]{2,1,0:T(8,128)(2,1)S(1)}, bf16[2,128,128]{2,1,0:T(8,128)(2,1)}, u32[]{:S(2)}) copy-start(bf16[2,128,128]{2,1,0:T(8,128)(2,1)} %node_w_ref.1) | copy-start | bytes 196612
  3.7 2.8 %copy-start.4 = (bf16[2,128,128]{2,1,0:T(8,128)(2,1)S(1)}, bf16[2,128,128]{2,1,0:T(8,128)(2,1)}, u32[]{:S(2)}) copy-start(bf16[2,128,128]{2,1,0:T(8,128)(2,1)} %decoder_w_ref.1) | copy-start | bytes 196612
  3.7 2.8 %copy-start.6 = (s32[2,2,1,12,128]{4,2,3,1,0:T(1,128)S(1)}, s32[2,2,1,12,128]{4,2,3,1,0:T(1,128)}, u32[]{:S(2)}) copy-start(s32[2,2,1,12,128]{4,2,3,1,0:T(1,128)} %param.19) | copy-start | bytes 73732
  3.7 2.8 %copy-start.7 = (f32[3,2,2,1,128]{4,3,2,1,0:T(1,128)S(1)}, f32[3,2,2,1,128]{4,3,2,1,0:T(1,128)}, u32[]{:S(2)}) copy-start(f32[3,2,2,1,128]{4,3,2,1,0:T(1,128)} %positions_ref.1) | copy-start | bytes 18436
  3.8 2.8 %copy-start.8 = (f32[3,2,2,1,128]{4,3,2,1,0:T(1,128)S(1)}, f32[3,2,2,1,128]{4,3,2,1,0:T(1,128)}, u32[]{:S(2)}) copy-start(f32[3,2,2,1,128]{4,3,2,1,0:T(1,128)} %velocity_ref.1) | copy-start | bytes 18436
  3.8 2.8 %copy-start.9 = (bf16[12,128]{1,0:T(8,128)(2,1)S(1)}, bf16[12,128]{1,0:T(8,128)(2,1)}, u32[]{:S(2)}) copy-start(bf16[12,128]{1,0:T(8,128)(2,1)} %encoder_in_ref.1) | copy-start | bytes 9220
  3.8 2.8 %copy-start.10 = (s32[2,2,1,128]{3,2,1,0:T(1,128)S(1)}, s32[2,2,1,128]{3,2,1,0:T(1,128)}, u32[]{:S(2)}) copy-start(s32[2,2,1,128]{3,2,1,0:T(1,128)} %owners_ref.1) | copy-start | bytes 6148
  5.0 6.0 %collective-permute-start.1 = (bf16[2,2,128,128]{3,2,1,0:T(8,128)(2,1)S(1)}, bf16[2,2,128,128]{3,2,1,0:T(8,128)(2,1)S(1)}, u32[]{:S(2)}, u32[]{:S(2)}) collective-permute-start(bf16[2,2,128,128]{3,2,1,0:T(8,128)(2,1)S(1)} %pad_maximum_fusion.1), channel_id=1, source_target_pairs={{0,5},{1,3},{2,7},{3,1},{4,9},{5,0},{6,11},{7,2},{8,13},{9,4},{10,... | collective-permute-start | bytes 393224 | tf_op jit(solution)/shard_map/ppermute | solution.py:615
  6.4 4.6 %collective-permute-start.2 = (bf16[2,1,128,128]{3,2,1,0:T(8,128)(2,1)S(1)}, bf16[2,1,128,128]{3,2,1,0:T(8,128)(2,1)S(1)}, u32[]{:S(2)}, u32[]{:S(2)}) collective-permute-start(bf16[2,1,128,128]{3,2,1,0:T(8,128)(2,1)S(1)} %fusion), channel_id=1, source_target_pairs={{0,7},{1,3},{2,5},{3,1},{4,11},{5,2},{6,9},{7,0},{8,15},{9,6},{10,... | collective-permute-start | bytes 196616 | tf_op jit(solution)/shard_map/ppermute | solution.py:615
  11.1 1.6 %copy-start.11 = (bf16[3,128]{1,0:T(4,128)(2,1)S(1)}, bf16[3,128]{1,0:T(4,128)(2,1)}, u32[]{:S(2)}) copy-start(bf16[3,128]{1,0:T(4,128)(2,1)} %decoder_out_ref.1) | copy-start | bytes 2308
  11.1 1.6 %collective-permute-start.4 = (bf16[8,128,128]{2,1,0:T(8,128)(2,1)S(1)}, bf16[8,128,128]{2,1,0:T(8,128)(2,1)S(1)}, u32[]{:S(2)}, u32[]{:S(2)}) collective-permute-start(bf16[8,128,128]{2,1,0:T(8,128)(2,1)S(1)} %pad_maximum_fusion), channel_id=1, source_target_pairs={{0,1},{1,0},{2,3},{3,2},{4,5},{5,4},{6,7},{7,6},{8,9},{9,8},{10,11... | collective-permute-start | bytes 786440 | tf_op jit(solution)/shard_map/ppermute | solution.py:595
  14.9 1.4 %collective-permute-start.6 = (f32[16,128]{1,0:T(8,128)S(1)}, f32[16,128]{1,0:T(8,128)S(1)}, u32[]{:S(2)}, u32[]{:S(2)}) collective-permute-start(f32[16,128]{1,0:T(8,128)S(1)} %get-tuple-element.93), channel_id=1, source_target_pairs={{0,1},{1,0},{2,3},{3,2},{4,5},{5,4},{6,7},{7,6},{8,9},{9,8},{10,11... | collective-permute-start | bytes 24584 | tf_op jit(solution)/shard_map/ppermute | solution.py:595
  15.1 7.1 %collective-permute-start.5 = (f32[16,128]{1,0:T(8,128)S(1)}, f32[16,128]{1,0:T(8,128)S(1)}, u32[]{:S(2)}, u32[]{:S(2)}) collective-permute-start(f32[16,128]{1,0:T(8,128)S(1)} %get-tuple-element.93), channel_id=1, source_target_pairs={{0,2},{2,0},{1,3},{3,1},{4,6},{6,4},{5,7},{7,5},{8,10},{10,8},{9,1... | collective-permute-start | bytes 24584 | tf_op jit(solution)/shard_map/ppermute | solution.py:595
  16.4 5.8 %collective-permute-start.7 = (f32[2,16,128]{2,1,0:T(8,128)S(1)}, f32[2,16,128]{2,1,0:T(8,128)S(1)}, u32[]{:S(2)}, u32[]{:S(2)}) collective-permute-start(f32[2,16,128]{2,1,0:T(8,128)S(1)} %pad_maximum_fusion.3), channel_id=1, source_target_pairs={{0,7},{1,3},{2,5},{3,1},{4,11},{5,2},{6,9},{7,0},{8,15},{9,6},{10,... | collective-permute-start | bytes 49160 | tf_op jit(solution)/shard_map/ppermute | solution.py:615
  18.0 4.2 %collective-permute-start.8 = (f32[2,16,128]{2,1,0:T(8,128)S(1)}, f32[2,16,128]{2,1,0:T(8,128)S(1)}, u32[]{:S(2)}, u32[]{:S(2)}) collective-permute-start(f32[2,16,128]{2,1,0:T(8,128)S(1)} %pad_maximum_fusion.3), channel_id=1, source_target_pairs={{0,5},{1,3},{2,7},{3,1},{4,9},{5,0},{6,11},{7,2},{8,13},{9,4},{10,... | collective-permute-start | bytes 49160 | tf_op jit(solution)/shard_map/ppermute | solution.py:615
  22.1 1.3 %copy-start.5 = (bf16[2,128,128]{2,1,0:T(8,128)(2,1)S(1)}, bf16[2,128,128]{2,1,0:T(8,128)(2,1)}, u32[]{:S(2)}) copy-start(bf16[2,128,128]{2,1,0:T(8,128)(2,1)} %refs_6_.1) | copy-start | bytes 196612
  22.2 1.3 %collective-permute-start.9 = (f32[5,16,128]{2,1,0:T(8,128)S(1)}, f32[5,16,128]{2,1,0:T(8,128)S(1)}, u32[]{:S(2)}, u32[]{:S(2)}) collective-permute-start(f32[5,16,128]{2,1,0:T(8,128)S(1)} %pad_maximum_fusion.2), channel_id=1, source_target_pairs={{0,1},{1,0},{2,3},{3,2},{4,5},{5,4},{6,7},{7,6},{8,9},{9,8},{10,11... | collective-permute-start | bytes 122888 | tf_op jit(solution)/shard_map/ppermute | solution.py:595

commit v16 on v15

--- a/solution.py
+++ b/solution.py
@@ -186,19 +186,26 @@
     return jnp.concatenate([position + new_velocity, new_velocity, velocity], axis=0)
 
 
-def cut_kernel(count, fill_any, *refs):
-    sources, refs = refs[:count], refs[count:]
-    copied, (end_ref, alive_ref, fill_ref, sems) = refs[:count], refs[count:]
-    end = 1 - lax.axis_index("gz")
-    copies = fetch(
-        [(fill_any, fill_ref), (sources[0].at[end], end_ref), *zip(sources, copied)], sems
-    )
-    copies[0].wait()
-    lane = lax.broadcasted_iota(I32, alive_ref.shape[2:], 1)
-    for a, b in CELLS:
-        alive_ref[a, b] = jnp.where(lane < fill_ref[a, 0, b], 1.0, 0.0)
-    for copy in copies[1:]:
-        copy.wait()
+def tables_kernel(fold_y, spread_ref):
+    index_y = lax.axis_index("gy")
+    index_z = lax.axis_index("gz")
+    options_y = 2 if fold_y else 3
+    line = lax.broadcasted_iota(I32, spread_ref.shape, 1)
+    direction = line >> 3
+    direction = direction + jnp.where(direction > 12, 1, 0)
+    plane = (direction * 57) >> 9
+    from_z = direction - 3 * ((direction * 43) >> 7) - 1
+    from_y = ((direction * 43) >> 7) - 3 * plane - 1
+    if fold_y:
+        side_y = jnp.where(from_y == 0, 0, 1)
+        valid = (from_y == 0) | (from_y == 1 - 2 * index_y)
+    else:
+        side_y = jnp.where(from_y < 0, 2, from_y)
+        valid = from_y < 2
+    side_z = jnp.where(from_z == 0, 0, 1)
+    valid = valid & ((from_z == 0) | (from_z == 1 - 2 * index_z)) & (line < 26 * CAP)
+    target = ((2 - plane) * options_y + side_y) * 2 + side_z
+    spread_ref[...] = jnp.where(valid, target * CAP + (line & 7), -1)
 
 
 def ranks_kernel(
@@ -206,7 +213,7 @@
     edge_ref,
     latent_ref,
     own_zed,
-    alive_ref,
+    fill_ref,
     owners_ref,
     edge_w_ref,
     node_in_ref,
@@ -218,7 +225,7 @@
     velocity_ref,
     weights_ref,
     inward_ref,
-    spread_ref,
+    alive_ref,
     latent_t_ref,
     node_pre_ref,
     state_ref,
@@ -239,6 +246,11 @@
     index_z = lax.axis_index("gz")
     slots = owners_ref.shape[-1]
     width = node_in_ref.shape[-1]
+    lane = lax.broadcasted_iota(I32, (1, slots), 1)
+    for a, b in CELLS:
+        fill = jnp.broadcast_to(fill_ref[a, :, b : b + 1], (1, slots))
+        alive_ref[a, b] = jnp.where(lane < fill, 1.0, 0.0)
+
     owner = jnp.concatenate([owners_ref[a, b] for a, b in CELLS], axis=1)
     alive = jnp.concatenate([alive_ref[a, b] for a, b in CELLS], axis=1)
     own_block = (index_x * count_y + index_y) * count_z + index_z
@@ -275,23 +287,6 @@
     placer = jnp.where(
         lax.broadcasted_iota(I32, (movers, particles), 0) == column, 1.0, 0.0
     ).astype(BF16)
-
-    line = lax.broadcasted_iota(I32, spread_ref.shape, 1)
-    direction = line >> 3
-    direction = direction + jnp.where(direction > 12, 1, 0)
-    plane = (direction * 57) >> 9
-    from_z = direction - 3 * ((direction * 43) >> 7) - 1
-    from_y = ((direction * 43) >> 7) - 3 * plane - 1
-    if fold_y:
-        side_y = jnp.where(from_y == 0, 0, 1)
-        valid = (from_y == 0) | (from_y == 1 - 2 * index_y)
-    else:
-        side_y = jnp.where(from_y < 0, 2, from_y)
-        valid = from_y < 2
-    side_z = jnp.where(from_z == 0, 0, 1)
-    valid = valid & ((from_z == 0) | (from_z == 1 - 2 * index_z)) & (line < 26 * CAP)
-    target = ((2 - plane) * options_y + side_y) * 2 + side_z
-    spread_ref[...] = jnp.where(valid, target * CAP + (line & 7), -1)
 
     for i in range(5):
         weights_ref[i] = flip(edge_w_ref[i])
@@ -666,23 +661,22 @@
     own_zed = swap(node_latent, "gz")
     if fold_y:
         sides = [swap(node_latent, "gy")]
-    small = (node_latent,)
-    *copied, end, alive = call(
-        functools.partial(cut_kernel, len(small)),
-        "cut",
-        [ANY] * (len(small) + 1),
-        [(array.shape, array.dtype) for array in small]
-        + [(node_latent.shape[1:], BF16), ((2, 2, 1, slots), F32)],
-        [pltpu.SMEM(fill.shape, I32), pltpu.SemaphoreType.DMA((len(small) + 2,))],
-        [in_hbm(array) for array in (fill, *small)],
+    spread = call(
+        functools.partial(tables_kernel, fold_y),
+        "tables",
+        [],
+        [((8, 256), I32)],
+        [],
+        [],
         5_000_000_000,
-    )
-    latent = copied[0]
+    )[0]
+    latent, spread = lax.optimization_barrier((node_latent, spread))
     core = lax.axis_index("gz")
     if fold_y:
         row = 1 - lax.axis_index("gy")
+        end = lax.dynamic_index_in_dim(latent[:, :, 0], 1 - core, 0, False)
         beside = lax.dynamic_index_in_dim(own_zed[:, :, 0], 1 - core, 0, False)
-        both = jnp.stack([end[:, 0], beside])
+        both = jnp.stack([end, beside])
         corner = lax.dynamic_slice_in_dim(both, row, 1, axis=1)
         mine = [swap_chips(both, False)]
         corner, both = lax.optimization_barrier((corner, both))
@@ -704,7 +698,7 @@
         [
             ((11, width, width), BF16),
             ((48, width), BF16),
-            ((8, 256), I32),
+            ((2, 2, 1, slots), F32),
             ((width, particles), F32),
             ((width, particles), F32),
             ((8, particles), F32),
@@ -719,14 +713,14 @@
             ((4, width, neighbour_count * slots), F32),
         ],
         [],
-        (edge_latent, latent, own_zed, alive, owners, edge_weights, node_in, node_weights, decoder_weights, encoder_in, neighbours, positions, velocity),
+        (edge_latent, latent, own_zed, fill, owners, edge_weights, node_in, node_weights, decoder_weights, encoder_in, neighbours, positions, velocity),
         5_000_000_000,
     )
     mine, sides, ranked = lax.optimization_barrier((mine, sides, ranked))
     (
         weights,
         inward,
-        spread,
+        alive,
         latent_t,
         node_pre,
         state,

time: 25.1 us -> 25.3 us (level)
  starting transfers between devices: 8.16 us -> 10.7 us
  waiting for transfers between devices: 1.71 us -> 0.32 us
  Pallas kernels: 14 us -> 12.9 us
    ppermute x6, starting transfers between devices: 4.65 us -> 6.04 us  [swap(): return lax.ppermute(values, axis, [(0, 1), (1, 0)])]
    ppermute x4, starting transfers between devices: 3.52 us -> 4.64 us  [swap_chips(): return lax.ppermute(values, ('gx', 'gy', 'gz'), pairs)]
    pallas_call x8, Pallas kernels: 14 us -> 12.9 us  [call(): pl.pallas_call(kernel, out_shape=tuple((jax.ShapeDtypeStruct(shape, kind)...]
    ppermute x4, waiting for transfers between devices: 1.08 us -> 0.04 us  [swap_chips(): return lax.ppermute(values, ('gx', 'gy', 'gz'), pairs)]
    ppermute x6, waiting for transfers between devices: 0.63 us -> 0.28 us  [swap(): return lax.ppermute(values, axis, [(0, 1), (1, 0)])]
  transfers between devices with their start and end apart: 10 -> 10, of which waited for: 3 -> 2; matrix products, arithmetic and copies ran while one was open for 0% -> 0% of each run, Pallas kernels for 41% -> 37%
where the time goes in v16:
time: 25.3 us; the launch traced here: 25.1 us
  Pallas kernels  12.9 us (51%)
  starting transfers between devices  10.7 us (42%)
  between operations  1 us (4%)
  waiting for transfers between devices  0.32 us (1%)
    pallas_call x8, Pallas kernels, call(): pl.pallas_call(kernel, out_shape=tuple((jax.ShapeDtypeStruct(shape, kind)...  12.9 us
    ppermute x6, starting transfers between devices, swap(): return lax.ppermute(values, axis, [(0, 1), (1, 0)])  6.04 us
    ppermute x4, starting transfers between devices, swap_chips(): return lax.ppermute(values, ('gx', 'gy', 'gz'), pairs)  4.64 us
  transfers between devices with their start and end apart: 10, of which 2 were waited for; matrix products, arithmetic and copies ran while one was open for 0% of the time, Pallas kernels for 37%

profile of v16, /device:TPU:0, one launch (start us, length us, event | category | flops | bytes accessed | tf_op | source)
XLA Modules:
  0.0 25.1 jit_solution(13845166352252285382)
XLA Ops:
  0.8 0.5 %collective-permute-start = (bf16[2,2,1,128,128]{4,3,2,1,0:T(8,128)(2,1)}, bf16[2,2,1,128,128]{4,3,2,1,0:T(8,128)(2,1)S(1)}, u32[]{:S(2)}, u32[]{:S(2)}) collective-permute-start(bf16[2,2,1,128,128]{4,3,2,1,0:T(8,128)(2,1)} %latent_ref), channel_id=1, source_target_pairs={{0,1},{1,0},{2,3},{3,2},{4,5},{5,4},{6,7},{7,6},{8,9},{9,8},{10,11... | collective-permute-start | bytes 393224 | tf_op jit(solution)/shard_map/ppermute | solution.py:590
  1.3 2.6 %collective-permute-start.3 = (bf16[2,2,1,128,128]{4,3,2,1,0:T(8,128)(2,1)}, bf16[2,2,1,128,128]{4,3,2,1,0:T(8,128)(2,1)S(1)}, u32[]{:S(2)}, u32[]{:S(2)}) collective-permute-start(bf16[2,2,1,128,128]{4,3,2,1,0:T(8,128)(2,1)} %latent_ref), channel_id=1, source_target_pairs={{0,2},{2,0},{1,3},{3,1},{4,6},{6,4},{5,7},{7,5},{8,10},{10,8},{9,1... | collective-permute-start | bytes 393224 | tf_op jit(solution)/shard_map/ppermute | solution.py:590
  3.9 0.0 collective-permute-done.own_zed
  4.0 1.4 %collective-permute-start.1 = (bf16[2,2,128,128]{3,2,1,0:T(8,128)(2,1)S(1)}, bf16[2,2,128,128]{3,2,1,0:T(8,128)(2,1)S(1)}, u32[]{:S(2)}, u32[]{:S(2)}) collective-permute-start(bf16[2,2,128,128]{3,2,1,0:T(8,128)(2,1)S(1)} %pad_maximum_fusion.1), channel_id=1, source_target_pairs={{0,5},{1,3},{2,7},{3,1},{4,9},{5,0},{6,11},{7,2},{8,13},{9,4},{10,... | collective-permute-start | bytes 393224 | tf_op jit(solution)/shard_map/ppermute | solution.py:610
  5.4 1.2 %collective-permute-start.2 = (bf16[2,1,128,128]{3,2,1,0:T(8,128)(2,1)S(1)}, bf16[2,1,128,128]{3,2,1,0:T(8,128)(2,1)S(1)}, u32[]{:S(2)}, u32[]{:S(2)}) collective-permute-start(bf16[2,1,128,128]{3,2,1,0:T(8,128)(2,1)S(1)} %fusion), channel_id=1, source_target_pairs={{0,7},{1,3},{2,5},{3,1},{4,11},{5,2},{6,9},{7,0},{8,15},{9,6},{10,... | collective-permute-start | bytes 196616 | tf_op jit(solution)/shard_map/ppermute | solution.py:610
  6.7 3.3 %ranks.1 = (bf16[11,128,128]{2,1,0:T(8,128)(2,1)S(1)}, bf16[48,128]{1,0:T(8,128)(2,1)S(1)}, f32[2,2,1,128]{3,2,1,0:T(1,128)S(1)}, f32[128,512]{1,0:T(8,128)S(1)}...) custom-call(bf16[2,2,1,12,128,128]{5,4,3,2,1,0:T(8,128)(2,1)S(1)} %c, ...), custom_call_target="tpu_custom_call" | custom-call | flops 5000000000 | tf_op jit(solution)/shard_map/ranks/pallas_call | solution.py:614
  10.0 0.0 collective-permute-done.3
  10.1 0.0 collective-permute-done.2
  10.2 0.0 copy-start.13
  10.2 0.7 %collective-permute-start.4 = (bf16[8,128,128]{2,1,0:T(8,128)(2,1)S(1)}, bf16[8,128,128]{2,1,0:T(8,128)(2,1)S(1)}, u32[]{:S(2)}, u32[]{:S(2)}) collective-permute-start(bf16[8,128,128]{2,1,0:T(8,128)(2,1)S(1)} %pad_maximum_fusion), channel_id=1, source_target_pairs={{0,1},{1,0},{2,3},{3,2},{4,5},{5,4},{6,7},{7,6},{8,9},{9,8},{10,11... | collective-permute-start | bytes 786440 | tf_op jit(solution)/shard_map/ppermute | solution.py:590
  10.9 1.1 %prepare.1 = (bf16[3,128,256]{2,1,0:T(8,128)(2,1)S(1)}, f32[128,1536]{1,0:T(8,128)S(1)}) custom-call(bf16[4,128,256]{2,1,0:T(8,128)(2,1)S(1)} %get-tuple-element.76.far_ref, bf16[2,3,128,128]{3,2,1,0:T(8,128)(2,1)S(1)} %constant_dynamic-update-slice_fusion.mine_ref, bf16[11,128,128]{2,1,0:T(8,128)(2,1)S(1)} %get-tuple-element.77.weights_ref.refs_4_, ...), custom_call_target="tpu_custom_call" | custom-call | flops 5000000000 | tf_op jit(solution)/shard_map/prepare/pallas_call | solution.py:614
  12.0 0.1 collective-permute-done.4
  12.1 2.2 %movers.1 = (bf16[8,128,256]{2,1,0:T(8,128)(2,1)S(1)}, f32[16,128]{1,0:T(8,128)S(1)}) custom-call(bf16[2,128,128]{2,1,0:T(8,128)(2,1)S(1)} %dynamic-slice_bitcast_fusion.refs_0_, bf16[2,128,128]{2,1,0:T(8,128)(2,1)S(1)} %slice.6.refs_1_, bf16[2,3,128,128]{3,2,1,0:T(8,128)(2,1)S(1)} %bitcast.16, bf16[3,128,256]{2,1,0:T(8,128)(2,1)S(1)} %get-tuple-element.85.refs_3_, ...), custom_call_target="tpu_custom_call" | custom-call | flops 3000000000 | tf_op jit(solution)/shard_map/movers/pallas_call | solution.py:614
  14.3 0.4 %collective-permute-start.6 = (f32[16,128]{1,0:T(8,128)S(1)}, f32[16,128]{1,0:T(8,128)S(1)}, u32[]{:S(2)}, u32[]{:S(2)}) collective-permute-start(f32[16,128]{1,0:T(8,128)S(1)} %get-tuple-element.90), channel_id=1, source_target_pairs={{0,1},{1,0},{2,3},{3,2},{4,5},{5,4},{6,7},{7,6},{8,9},{9,8},{10,11... | collective-permute-start | bytes 24584 | tf_op jit(solution)/shard_map/ppermute | solution.py:590
  14.7 1.8 %collective-permute-start.5 = (f32[16,128]{1,0:T(8,128)S(1)}, f32[16,128]{1,0:T(8,128)S(1)}, u32[]{:S(2)}, u32[]{:S(2)}) collective-permute-start(f32[16,128]{1,0:T(8,128)S(1)} %get-tuple-element.90), channel_id=1, source_target_pairs={{0,2},{2,0},{1,3},{3,1},{4,6},{6,4},{5,7},{7,5},{8,10},{10,8},{9,1... | collective-permute-start | bytes 24584 | tf_op jit(solution)/shard_map/ppermute | solution.py:590
  16.5 1.1 %collective-permute-start.7 = (f32[2,16,128]{2,1,0:T(8,128)S(1)}, f32[2,16,128]{2,1,0:T(8,128)S(1)}, u32[]{:S(2)}, u32[]{:S(2)}) collective-permute-start(f32[2,16,128]{2,1,0:T(8,128)S(1)} %pad_maximum_fusion.3), channel_id=1, source_target_pairs={{0,7},{1,3},{2,5},{3,1},{4,11},{5,2},{6,9},{7,0},{8,15},{9,6},{10,... | collective-permute-start | bytes 49160 | tf_op jit(solution)/shard_map/ppermute | solution.py:610
  17.6 0.9 %collective-permute-start.8 = (f32[2,16,128]{2,1,0:T(8,128)S(1)}, f32[2,16,128]{2,1,0:T(8,128)S(1)}, u32[]{:S(2)}, u32[]{:S(2)}) collective-permute-start(f32[2,16,128]{2,1,0:T(8,128)S(1)} %pad_maximum_fusion.3), channel_id=1, source_target_pairs={{0,5},{1,3},{2,7},{3,1},{4,9},{5,0},{6,11},{7,2},{8,13},{9,4},{10,... | collective-permute-start | bytes 49160 | tf_op jit(solution)/shard_map/ppermute | solution.py:610
  18.5 1.9 %edges.3.second_ref = bf16[2,128,128]{2,1,0:T(8,128)(2,1)S(1)} custom-call(f32[2,2,1,128]{3,2,1,0:T(1,128)S(1)} %get-tuple-element.93.alive_ref, s32[2,2,12,1,128]{4,3,2,1,0:T(1,128)S(1)} %bitcast.21, bf16[8,128,256]{2,1,0:T(8,128)(2,1)S(1)} %get-tuple-element.94.far_ref, f32[4,128,1536]{2,1,0:T(8,128)S(1)} %get-tuple-element.95.pre_ref, ...), custom_call_target="tpu_custom_call" | custom-call | flops 4000000000 | tf_op jit(solution)/shard_map/edges/pallas_call | solution.py:614
  20.4 1.9 %edges.2.first_ref = bf16[2,128,128]{2,1,0:T(8,128)(2,1)S(1)} custom-call(f32[2,2,1,128]{3,2,1,0:T(1,128)S(1)} %get-tuple-element.93.alive_ref, s32[2,2,12,1,128]{4,3,2,1,0:T(1,128)S(1)} %bitcast.22, bf16[8,128,256]{2,1,0:T(8,128)(2,1)S(1)} %get-tuple-element.94.far_ref, f32[4,128,1536]{2,1,0:T(8,128)S(1)} %get-tuple-element.95.pre_ref, ...), custom_call_target="tpu_custom_call" | custom-call | flops 4000000000 | tf_op jit(solution)/shard_map/edges/pallas_call | solution.py:614
  22.3 0.0 copy-start.6
  22.3 0.1 collective-permute-start.9
  22.4 1.0 %nodes.1.moved_ref = f32[16,512]{1,0:T(8,128)S(1)} custom-call(bf16[2,128,128]{2,1,0:T(8,128)(2,1)S(1)} %edges.2.first_ref, bf16[2,128,128]{2,1,0:T(8,128)(2,1)S(1)} %edges.3.second_ref, f32[128,512]{1,0:T(8,128)S(1)} %get-tuple-element.101.node_pre_ref, f32[128,512]{1,0:T(8,128)S(1)} %get-tuple-element.102.latent_t_ref, ...), custom_call_target="tpu_custom_call" | custom-call | flops 1000000000 | tf_op jit(solution)/shard_map/nodes/pallas_call | solution.py:614
  23.4 0.2 collective-permute-done.9.refs_3_
  23.6 1.5 %finish.1 = (bf16[2,2,1,128,128]{4,3,2,1,0:T(8,128)(2,1)}, f32[9,2,2,1,128]{4,3,2,1,0:T(1,128)}, bf16[1,1,1,208,128]{4,3,2,1,0:T(8,128)(2,1)}, f32[9,1,1,1,208]{4,3,2,1,0:T(1,128)}) custom-call(f32[16,512]{1,0:T(8,128)S(1)} %nodes.1.moved_ref, f32[16,128]{1,0:T(8,128)S(1)} %collective-permute-done.6.zed_ref, f32[16,128]{1,0:T(8,128)S(1)} %collective-permute-done.5.refs_0_, ...), custom_call_target="tpu_custom_call" | custom-call | flops 1000000000 | tf_op jit(solution)/shard_map/finish/pallas_call | solution.py:614
  (44 shorter events, 0.2 us)
Async XLA Ops:
  0.6 3.2 %copy-start = (bf16[2,2,1,128,128]{4,3,2,1,0:T(8,128)(2,1)S(1)}, bf16[2,2,1,128,128]{4,3,2,1,0:T(8,128)(2,1)}, u32[]{:S(2)}) copy-start(bf16[2,2,1,128,128]{4,3,2,1,0:T(8,128)(2,1)} %latent_ref) | copy-start | bytes 393220
  0.6 6.0 %copy-start.7 = (s32[2,2,1,12,128]{4,2,3,1,0:T(1,128)S(1)}, s32[2,2,1,12,128]{4,2,3,1,0:T(1,128)}, u32[]{:S(2)}) copy-start(s32[2,2,1,12,128]{4,2,3,1,0:T(1,128)} %param.19) | copy-start | bytes 73732
  0.7 6.0 %copy-start.12 = (s32[2,2,1]{1,2,0:T(1,128)S(1)}, s32[2,2,1]{1,2,0:T(1,128)}, u32[]{:S(2)}) copy-start(s32[2,2,1]{1,2,0:T(1,128)} %param.18) | copy-start | bytes 52
  0.7 6.0 %copy-start.1 = (bf16[2,2,1,12,128,128]{5,4,3,2,1,0:T(8,128)(2,1)S(1)}, bf16[2,2,1,12,128,128]{5,4,3,2,1,0:T(8,128)(2,1)}, u32[]{:S(2)}) copy-start(bf16[2,2,1,12,128,128]{5,4,3,2,1,0:T(8,128)(2,1)} %edge_ref.1) | copy-start | bytes 4718596
  0.7 5.9 %copy-start.8 = (f32[3,2,2,1,128]{4,3,2,1,0:T(1,128)S(1)}, f32[3,2,2,1,128]{4,3,2,1,0:T(1,128)}, u32[]{:S(2)}) copy-start(f32[3,2,2,1,128]{4,3,2,1,0:T(1,128)} %positions_ref.1) | copy-start | bytes 18436
  0.7 5.9 %copy-start.9 = (f32[3,2,2,1,128]{4,3,2,1,0:T(1,128)S(1)}, f32[3,2,2,1,128]{4,3,2,1,0:T(1,128)}, u32[]{:S(2)}) copy-start(f32[3,2,2,1,128]{4,3,2,1,0:T(1,128)} %velocity_ref.1) | copy-start | bytes 18436
  0.7 5.9 %copy-start.11 = (s32[2,2,1,128]{3,2,1,0:T(1,128)S(1)}, s32[2,2,1,128]{3,2,1,0:T(1,128)}, u32[]{:S(2)}) copy-start(s32[2,2,1,128]{3,2,1,0:T(1,128)} %owners_ref.1) | copy-start | bytes 6148
  0.7 5.9 %copy-start.2 = (bf16[5,128,128]{2,1,0:T(8,128)(2,1)S(1)}, bf16[5,128,128]{2,1,0:T(8,128)(2,1)}, u32[]{:S(2)}) copy-start(bf16[5,128,128]{2,1,0:T(8,128)(2,1)} %edge_w_ref.1) | copy-start | bytes 491524
  0.7 5.9 %copy-start.3 = (bf16[256,128]{1,0:T(8,128)(2,1)S(1)}, bf16[256,128]{1,0:T(8,128)(2,1)}, u32[]{:S(2)}) copy-start(bf16[256,128]{1,0:T(8,128)(2,1)} %node_in_ref.1) | copy-start | bytes 196612
  0.7 5.9 %copy-start.4 = (bf16[2,128,128]{2,1,0:T(8,128)(2,1)S(1)}, bf16[2,128,128]{2,1,0:T(8,128)(2,1)}, u32[]{:S(2)}) copy-start(bf16[2,128,128]{2,1,0:T(8,128)(2,1)} %node_w_ref.1) | copy-start | bytes 196612
  0.7 5.9 %copy-start.5 = (bf16[2,128,128]{2,1,0:T(8,128)(2,1)S(1)}, bf16[2,128,128]{2,1,0:T(8,128)(2,1)}, u32[]{:S(2)}) copy-start(bf16[2,128,128]{2,1,0:T(8,128)(2,1)} %decoder_w_ref.1) | copy-start | bytes 196612
  0.7 5.9 %copy-start.10 = (bf16[12,128]{1,0:T(8,128)(2,1)S(1)}, bf16[12,128]{1,0:T(8,128)(2,1)}, u32[]{:S(2)}) copy-start(bf16[12,128]{1,0:T(8,128)(2,1)} %encoder_in_ref.1) | copy-start | bytes 9220
  0.8 3.1 %collective-permute-start = (bf16[2,2,1,128,128]{4,3,2,1,0:T(8,128)(2,1)}, bf16[2,2,1,128,128]{4,3,2,1,0:T(8,128)(2,1)S(1)}, u32[]{:S(2)}, u32[]{:S(2)}) collective-permute-start(bf16[2,2,1,128,128]{4,3,2,1,0:T(8,128)(2,1)} %latent_ref), channel_id=1, source_target_pairs={{0,1},{1,0},{2,3},{3,2},{4,5},{5,4},{6,7},{7,6},{8,9},{9,8},{10,11... | collective-permute-start | bytes 393224 | tf_op jit(solution)/shard_map/ppermute | solution.py:590
  1.3 8.8 %collective-permute-start.3 = (bf16[2,2,1,128,128]{4,3,2,1,0:T(8,128)(2,1)}, bf16[2,2,1,128,128]{4,3,2,1,0:T(8,128)(2,1)S(1)}, u32[]{:S(2)}, u32[]{:S(2)}) collective-permute-start(bf16[2,2,1,128,128]{4,3,2,1,0:T(8,128)(2,1)} %latent_ref), channel_id=1, source_target_pairs={{0,2},{2,0},{1,3},{3,1},{4,6},{6,4},{5,7},{7,5},{8,10},{10,8},{9,1... | collective-permute-start | bytes 393224 | tf_op jit(solution)/shard_map/ppermute | solution.py:590
  4.0 6.1 %collective-permute-start.1 = (bf16[2,2,128,128]{3,2,1,0:T(8,128)(2,1)S(1)}, bf16[2,2,128,128]{3,2,1,0:T(8,128)(2,1)S(1)}, u32[]{:S(2)}, u32[]{:S(2)}) collective-permute-start(bf16[2,2,128,128]{3,2,1,0:T(8,128)(2,1)S(1)} %pad_maximum_fusion.1), channel_id=1, source_target_pairs={{0,5},{1,3},{2,7},{3,1},{4,9},{5,0},{6,11},{7,2},{8,13},{9,4},{10,... | collective-permute-start | bytes 393224 | tf_op jit(solution)/shard_map/ppermute | solution.py:610
  5.4 4.7 %collective-permute-start.2 = (bf16[2,1,128,128]{3,2,1,0:T(8,128)(2,1)S(1)}, bf16[2,1,128,128]{3,2,1,0:T(8,128)(2,1)S(1)}, u32[]{:S(2)}, u32[]{:S(2)}) collective-permute-start(bf16[2,1,128,128]{3,2,1,0:T(8,128)(2,1)S(1)} %fusion), channel_id=1, source_target_pairs={{0,7},{1,3},{2,5},{3,1},{4,11},{5,2},{6,9},{7,0},{8,15},{9,6},{10,... | collective-permute-start | bytes 196616 | tf_op jit(solution)/shard_map/ppermute | solution.py:610
  10.2 1.9 %copy-start.13 = (bf16[3,128]{1,0:T(4,128)(2,1)S(1)}, bf16[3,128]{1,0:T(4,128)(2,1)}, u32[]{:S(2)}) copy-start(bf16[3,128]{1,0:T(4,128)(2,1)} %decoder_out_ref.1) | copy-start | bytes 2308
  10.2 1.9 %collective-permute-start.4 = (bf16[8,128,128]{2,1,0:T(8,128)(2,1)S(1)}, bf16[8,128,128]{2,1,0:T(8,128)(2,1)S(1)}, u32[]{:S(2)}, u32[]{:S(2)}) collective-permute-start(bf16[8,128,128]{2,1,0:T(8,128)(2,1)S(1)} %pad_maximum_fusion), channel_id=1, source_target_pairs={{0,1},{1,0},{2,3},{3,2},{4,5},{5,4},{6,7},{7,6},{8,9},{9,8},{10,11... | collective-permute-start | bytes 786440 | tf_op jit(solution)/shard_map/ppermute | solution.py:590
  14.3 2.2 %collective-permute-start.6 = (f32[16,128]{1,0:T(8,128)S(1)}, f32[16,128]{1,0:T(8,128)S(1)}, u32[]{:S(2)}, u32[]{:S(2)}) collective-permute-start(f32[16,128]{1,0:T(8,128)S(1)} %get-tuple-element.90), channel_id=1, source_target_pairs={{0,1},{1,0},{2,3},{3,2},{4,5},{5,4},{6,7},{7,6},{8,9},{9,8},{10,11... | collective-permute-start | bytes 24584 | tf_op jit(solution)/shard_map/ppermute | solution.py:590
  14.7 7.6 %collective-permute-start.5 = (f32[16,128]{1,0:T(8,128)S(1)}, f32[16,128]{1,0:T(8,128)S(1)}, u32[]{:S(2)}, u32[]{:S(2)}) collective-permute-start(f32[16,128]{1,0:T(8,128)S(1)} %get-tuple-element.90), channel_id=1, source_target_pairs={{0,2},{2,0},{1,3},{3,1},{4,6},{6,4},{5,7},{7,5},{8,10},{10,8},{9,1... | collective-permute-start | bytes 24584 | tf_op jit(solution)/shard_map/ppermute | solution.py:590
  16.5 5.8 %collective-permute-start.7 = (f32[2,16,128]{2,1,0:T(8,128)S(1)}, f32[2,16,128]{2,1,0:T(8,128)S(1)}, u32[]{:S(2)}, u32[]{:S(2)}) collective-permute-start(f32[2,16,128]{2,1,0:T(8,128)S(1)} %pad_maximum_fusion.3), channel_id=1, source_target_pairs={{0,7},{1,3},{2,5},{3,1},{4,11},{5,2},{6,9},{7,0},{8,15},{9,6},{10,... | collective-permute-start | bytes 49160 | tf_op jit(solution)/shard_map/ppermute | solution.py:610
  17.6 4.8 %collective-permute-start.8 = (f32[2,16,128]{2,1,0:T(8,128)S(1)}, f32[2,16,128]{2,1,0:T(8,128)S(1)}, u32[]{:S(2)}, u32[]{:S(2)}) collective-permute-start(f32[2,16,128]{2,1,0:T(8,128)S(1)} %pad_maximum_fusion.3), channel_id=1, source_target_pairs={{0,5},{1,3},{2,7},{3,1},{4,9},{5,0},{6,11},{7,2},{8,13},{9,4},{10,... | collective-permute-start | bytes 49160 | tf_op jit(solution)/shard_map/ppermute | solution.py:610
  22.3 1.3 %copy-start.6 = (bf16[2,128,128]{2,1,0:T(8,128)(2,1)S(1)}, bf16[2,128,128]{2,1,0:T(8,128)(2,1)}, u32[]{:S(2)}) copy-start(bf16[2,128,128]{2,1,0:T(8,128)(2,1)} %refs_6_.1) | copy-start | bytes 196612
  22.3 1.3 %collective-permute-start.9 = (f32[5,16,128]{2,1,0:T(8,128)S(1)}, f32[5,16,128]{2,1,0:T(8,128)S(1)}, u32[]{:S(2)}, u32[]{:S(2)}) collective-permute-start(f32[5,16,128]{2,1,0:T(8,128)S(1)} %pad_maximum_fusion.2), channel_id=1, source_target_pairs={{0,1},{1,0},{2,3},{3,2},{4,5},{5,4},{6,7},{7,6},{8,9},{9,8},{10,11... | collective-permute-start | bytes 122888 | tf_op jit(solution)/shard_map/ppermute | solution.py:590

commit v17 on v16

--- a/solution.py
+++ b/solution.py
@@ -605,7 +605,7 @@
                 if 0 <= to_x < count_x:
                     to = (to_x, y ^ 1 if cross else y, 1 - z)
                 else:
-                    to = (x, y ^ 1, z)
+                    to = (x, y, z)
                 pairs.append(((x * count_y + y) * count_z + z, (to[0] * count_y + to[1]) * count_z + to[2]))
     return lax.ppermute(values, ("gx", "gy", "gz"), pairs)
 

time: 25.3 us -> 32.1 us (1.27)
  starting transfers between devices: 10.7 us -> 17 us
    ppermute x4, starting transfers between devices: 4.64 us -> 12.4 us  [swap_chips(): return lax.ppermute(values, ('gx', 'gy', 'gz'), pairs)]
    ppermute x6, starting transfers between devices: 6.04 us -> 4.59 us  [swap(): return lax.ppermute(values, axis, [(0, 1), (1, 0)])]
    ppermute x6, waiting for transfers between devices: 0.28 us -> 0.63 us  [swap(): return lax.ppermute(values, axis, [(0, 1), (1, 0)])]
  transfers between devices with their start and end apart: 10 -> 10, of which waited for: 2 -> 2; matrix products, arithmetic and copies ran while one was open for 0% -> 0% of each run, Pallas kernels for 37% -> 29%
where the time goes in v17:
time: 32.1 us; the launch traced here: 31.9 us
  starting transfers between devices  17 us (53%)
  Pallas kernels  12.9 us (40%)
  between operations  1.08 us (3%)
  waiting for transfers between devices  0.64 us (2%)
    pallas_call x8, Pallas kernels, call(): pl.pallas_call(kernel, out_shape=tuple((jax.ShapeDtypeStruct(shape, kind)...  12.9 us
    ppermute x4, starting transfers between devices, swap_chips(): return lax.ppermute(values, ('gx', 'gy', 'gz'), pairs)  12.4 us
    ppermute x6, starting transfers between devices, swap(): return lax.ppermute(values, axis, [(0, 1), (1, 0)])  4.59 us
  transfers between devices with their start and end apart: 10, of which 2 were waited for; matrix products, arithmetic and copies ran while one was open for 0% of the time, Pallas kernels for 29%

profile of v17, /device:TPU:0, one launch (start us, length us, event | category | flops | bytes accessed | tf_op | source)
XLA Modules:
  0.0 31.9 jit_solution(10819080942554092047)
XLA Ops:
  0.8 0.5 %collective-permute-start = (bf16[2,2,1,128,128]{4,3,2,1,0:T(8,128)(2,1)}, bf16[2,2,1,128,128]{4,3,2,1,0:T(8,128)(2,1)S(1)}, u32[]{:S(2)}, u32[]{:S(2)}) collective-permute-start(bf16[2,2,1,128,128]{4,3,2,1,0:T(8,128)(2,1)} %latent_ref), channel_id=1, source_target_pairs={{0,1},{1,0},{2,3},{3,2},{4,5},{5,4},{6,7},{7,6},{8,9},{9,8},{10,11... | collective-permute-start | bytes 393224 | tf_op jit(solution)/shard_map/ppermute | solution.py:590
  1.3 2.6 %collective-permute-start.3 = (bf16[2,2,1,128,128]{4,3,2,1,0:T(8,128)(2,1)}, bf16[2,2,1,128,128]{4,3,2,1,0:T(8,128)(2,1)S(1)}, u32[]{:S(2)}, u32[]{:S(2)}) collective-permute-start(bf16[2,2,1,128,128]{4,3,2,1,0:T(8,128)(2,1)} %latent_ref), channel_id=1, source_target_pairs={{0,2},{2,0},{1,3},{3,1},{4,6},{6,4},{5,7},{7,5},{8,10},{10,8},{9,1... | collective-permute-start | bytes 393224 | tf_op jit(solution)/shard_map/ppermute | solution.py:590
  3.9 0.0 collective-permute-done.own_zed
  4.0 3.3 %collective-permute-start.1 = (bf16[2,2,128,128]{3,2,1,0:T(8,128)(2,1)S(1)}, bf16[2,2,128,128]{3,2,1,0:T(8,128)(2,1)S(1)}, u32[]{:S(2)}, u32[]{:S(2)}) collective-permute-start(bf16[2,2,128,128]{3,2,1,0:T(8,128)(2,1)S(1)} %pad_maximum_fusion.1), channel_id=1, source_target_pairs={{0,5},{1,1},{2,7},{3,3},{4,9},{5,0},{6,11},{7,2},{8,13},{9,4},{10,... | collective-permute-start | bytes 393224 | tf_op jit(solution)/shard_map/ppermute | solution.py:610
  7.2 3.1 %collective-permute-start.2 = (bf16[2,1,128,128]{3,2,1,0:T(8,128)(2,1)S(1)}, bf16[2,1,128,128]{3,2,1,0:T(8,128)(2,1)S(1)}, u32[]{:S(2)}, u32[]{:S(2)}) collective-permute-start(bf16[2,1,128,128]{3,2,1,0:T(8,128)(2,1)S(1)} %fusion), channel_id=1, source_target_pairs={{0,7},{1,1},{2,5},{3,3},{4,11},{5,2},{6,9},{7,0},{8,15},{9,6},{10,... | collective-permute-start | bytes 196616 | tf_op jit(solution)/shard_map/ppermute | solution.py:610
  10.5 3.4 %ranks.1 = (bf16[11,128,128]{2,1,0:T(8,128)(2,1)S(1)}, bf16[48,128]{1,0:T(8,128)(2,1)S(1)}, f32[2,2,1,128]{3,2,1,0:T(1,128)S(1)}, f32[128,512]{1,0:T(8,128)S(1)}...) custom-call(bf16[2,2,1,12,128,128]{5,4,3,2,1,0:T(8,128)(2,1)S(1)} %c, ...), custom_call_target="tpu_custom_call" | custom-call | flops 5000000000 | tf_op jit(solution)/shard_map/ranks/pallas_call | solution.py:614
  13.9 0.0 collective-permute-done.3
  13.9 0.0 collective-permute-done.2
  14.0 0.0 copy-start.13
  14.0 0.1 collective-permute-start.4
  14.1 1.1 %prepare.1 = (bf16[3,128,256]{2,1,0:T(8,128)(2,1)S(1)}, f32[128,1536]{1,0:T(8,128)S(1)}) custom-call(bf16[4,128,256]{2,1,0:T(8,128)(2,1)S(1)} %get-tuple-element.76.far_ref, bf16[2,3,128,128]{3,2,1,0:T(8,128)(2,1)S(1)} %constant_dynamic-update-slice_fusion.mine_ref, bf16[11,128,128]{2,1,0:T(8,128)(2,1)S(1)} %get-tuple-element.77.weights_ref.refs_4_, ...), custom_call_target="tpu_custom_call" | custom-call | flops 5000000000 | tf_op jit(solution)/shard_map/prepare/pallas_call | solution.py:614
  15.2 0.4 %collective-permute-done.4 = bf16[8,128,128]{2,1,0:T(8,128)(2,1)S(1)} collective-permute-done((bf16[8,128,128]{2,1,0:T(8,128)(2,1)S(1)}, bf16[8,128,128]{2,1,0:T(8,128)(2,1)S(1)}, u32[]{:S(2)}, u32[]{:S(2)}) %collective-permute-start.4) | collective-permute-done | bytes 262176 | tf_op jit(solution)/shard_map/ppermute | solution.py:590
  15.6 2.2 %movers.1 = (bf16[8,128,256]{2,1,0:T(8,128)(2,1)S(1)}, f32[16,128]{1,0:T(8,128)S(1)}) custom-call(bf16[2,128,128]{2,1,0:T(8,128)(2,1)S(1)} %dynamic-slice_bitcast_fusion.refs_0_, bf16[2,128,128]{2,1,0:T(8,128)(2,1)S(1)} %slice.6.refs_1_, bf16[2,3,128,128]{3,2,1,0:T(8,128)(2,1)S(1)} %bitcast.16, bf16[3,128,256]{2,1,0:T(8,128)(2,1)S(1)} %get-tuple-element.85.refs_3_, ...), custom_call_target="tpu_custom_call" | custom-call | flops 3000000000 | tf_op jit(solution)/shard_map/movers/pallas_call | solution.py:614
  17.8 0.1 collective-permute-start.6
  18.0 1.2 %collective-permute-start.5 = (f32[16,128]{1,0:T(8,128)S(1)}, f32[16,128]{1,0:T(8,128)S(1)}, u32[]{:S(2)}, u32[]{:S(2)}) collective-permute-start(f32[16,128]{1,0:T(8,128)S(1)} %get-tuple-element.90), channel_id=1, source_target_pairs={{0,2},{2,0},{1,3},{3,1},{4,6},{6,4},{5,7},{7,5},{8,10},{10,8},{9,1... | collective-permute-start | bytes 24584 | tf_op jit(solution)/shard_map/ppermute | solution.py:590
  19.2 3.8 %collective-permute-start.7 = (f32[2,16,128]{2,1,0:T(8,128)S(1)}, f32[2,16,128]{2,1,0:T(8,128)S(1)}, u32[]{:S(2)}, u32[]{:S(2)}) collective-permute-start(f32[2,16,128]{2,1,0:T(8,128)S(1)} %pad_maximum_fusion.3), channel_id=1, source_target_pairs={{0,7},{1,1},{2,5},{3,3},{4,11},{5,2},{6,9},{7,0},{8,15},{9,6},{10,... | collective-permute-start | bytes 49160 | tf_op jit(solution)/shard_map/ppermute | solution.py:610
  23.0 2.2 %collective-permute-start.8 = (f32[2,16,128]{2,1,0:T(8,128)S(1)}, f32[2,16,128]{2,1,0:T(8,128)S(1)}, u32[]{:S(2)}, u32[]{:S(2)}) collective-permute-start(f32[2,16,128]{2,1,0:T(8,128)S(1)} %pad_maximum_fusion.3), channel_id=1, source_target_pairs={{0,5},{1,1},{2,7},{3,3},{4,9},{5,0},{6,11},{7,2},{8,13},{9,4},{10,... | collective-permute-start | bytes 49160 | tf_op jit(solution)/shard_map/ppermute | solution.py:610
  25.2 1.9 %edges.3.second_ref = bf16[2,128,128]{2,1,0:T(8,128)(2,1)S(1)} custom-call(f32[2,2,1,128]{3,2,1,0:T(1,128)S(1)} %get-tuple-element.93.alive_ref, s32[2,2,12,1,128]{4,3,2,1,0:T(1,128)S(1)} %bitcast.21, bf16[8,128,256]{2,1,0:T(8,128)(2,1)S(1)} %get-tuple-element.94.far_ref, f32[4,128,1536]{2,1,0:T(8,128)S(1)} %get-tuple-element.95.pre_ref, ...), custom_call_target="tpu_custom_call" | custom-call | flops 4000000000 | tf_op jit(solution)/shard_map/edges/pallas_call | solution.py:614
  27.1 1.9 %edges.2.first_ref = bf16[2,128,128]{2,1,0:T(8,128)(2,1)S(1)} custom-call(f32[2,2,1,128]{3,2,1,0:T(1,128)S(1)} %get-tuple-element.93.alive_ref, s32[2,2,12,1,128]{4,3,2,1,0:T(1,128)S(1)} %bitcast.22, bf16[8,128,256]{2,1,0:T(8,128)(2,1)S(1)} %get-tuple-element.94.far_ref, f32[4,128,1536]{2,1,0:T(8,128)S(1)} %get-tuple-element.95.pre_ref, ...), custom_call_target="tpu_custom_call" | custom-call | flops 4000000000 | tf_op jit(solution)/shard_map/edges/pallas_call | solution.py:614
  29.0 0.0 copy-start.6
  29.1 0.1 collective-permute-start.9
  29.1 1.0 %nodes.1.moved_ref = f32[16,512]{1,0:T(8,128)S(1)} custom-call(bf16[2,128,128]{2,1,0:T(8,128)(2,1)S(1)} %edges.2.first_ref, bf16[2,128,128]{2,1,0:T(8,128)(2,1)S(1)} %edges.3.second_ref, f32[128,512]{1,0:T(8,128)S(1)} %get-tuple-element.101.node_pre_ref, f32[128,512]{1,0:T(8,128)S(1)} %get-tuple-element.102.latent_t_ref, ...), custom_call_target="tpu_custom_call" | custom-call | flops 1000000000 | tf_op jit(solution)/shard_map/nodes/pallas_call | solution.py:614
  30.2 0.2 collective-permute-done.9.refs_3_
  30.3 1.5 %finish.1 = (bf16[2,2,1,128,128]{4,3,2,1,0:T(8,128)(2,1)}, f32[9,2,2,1,128]{4,3,2,1,0:T(1,128)}, bf16[1,1,1,208,128]{4,3,2,1,0:T(8,128)(2,1)}, f32[9,1,1,1,208]{4,3,2,1,0:T(1,128)}) custom-call(f32[16,512]{1,0:T(8,128)S(1)} %nodes.1.moved_ref, f32[16,128]{1,0:T(8,128)S(1)} %collective-permute-done.6.zed_ref, f32[16,128]{1,0:T(8,128)S(1)} %collective-permute-done.5.refs_0_, ...), custom_call_target="tpu_custom_call" | custom-call | flops 1000000000 | tf_op jit(solution)/shard_map/finish/pallas_call | solution.py:614
  (44 shorter events, 0.2 us)
Async XLA Ops:
  0.6 3.2 %copy-start = (bf16[2,2,1,128,128]{4,3,2,1,0:T(8,128)(2,1)S(1)}, bf16[2,2,1,128,128]{4,3,2,1,0:T(8,128)(2,1)}, u32[]{:S(2)}) copy-start(bf16[2,2,1,128,128]{4,3,2,1,0:T(8,128)(2,1)} %latent_ref) | copy-start | bytes 393220
  0.6 9.7 %copy-start.7 = (s32[2,2,1,12,128]{4,2,3,1,0:T(1,128)S(1)}, s32[2,2,1,12,128]{4,2,3,1,0:T(1,128)}, u32[]{:S(2)}) copy-start(s32[2,2,1,12,128]{4,2,3,1,0:T(1,128)} %param.19) | copy-start | bytes 73732
  0.7 9.7 %copy-start.12 = (s32[2,2,1]{1,2,0:T(1,128)S(1)}, s32[2,2,1]{1,2,0:T(1,128)}, u32[]{:S(2)}) copy-start(s32[2,2,1]{1,2,0:T(1,128)} %param.18) | copy-start | bytes 52
  0.7 9.7 %copy-start.1 = (bf16[2,2,1,12,128,128]{5,4,3,2,1,0:T(8,128)(2,1)S(1)}, bf16[2,2,1,12,128,128]{5,4,3,2,1,0:T(8,128)(2,1)}, u32[]{:S(2)}) copy-start(bf16[2,2,1,12,128,128]{5,4,3,2,1,0:T(8,128)(2,1)} %edge_ref.1) | copy-start | bytes 4718596
  0.7 9.7 %copy-start.8 = (f32[3,2,2,1,128]{4,3,2,1,0:T(1,128)S(1)}, f32[3,2,2,1,128]{4,3,2,1,0:T(1,128)}, u32[]{:S(2)}) copy-start(f32[3,2,2,1,128]{4,3,2,1,0:T(1,128)} %positions_ref.1) | copy-start | bytes 18436
  0.7 9.7 %copy-start.9 = (f32[3,2,2,1,128]{4,3,2,1,0:T(1,128)S(1)}, f32[3,2,2,1,128]{4,3,2,1,0:T(1,128)}, u32[]{:S(2)}) copy-start(f32[3,2,2,1,128]{4,3,2,1,0:T(1,128)} %velocity_ref.1) | copy-start | bytes 18436
  0.7 9.7 %copy-start.11 = (s32[2,2,1,128]{3,2,1,0:T(1,128)S(1)}, s32[2,2,1,128]{3,2,1,0:T(1,128)}, u32[]{:S(2)}) copy-start(s32[2,2,1,128]{3,2,1,0:T(1,128)} %owners_ref.1) | copy-start | bytes 6148
  0.7 9.7 %copy-start.2 = (bf16[5,128,128]{2,1,0:T(8,128)(2,1)S(1)}, bf16[5,128,128]{2,1,0:T(8,128)(2,1)}, u32[]{:S(2)}) copy-start(bf16[5,128,128]{2,1,0:T(8,128)(2,1)} %edge_w_ref.1) | copy-start | bytes 491524
  0.7 9.7 %copy-start.3 = (bf16[256,128]{1,0:T(8,128)(2,1)S(1)}, bf16[256,128]{1,0:T(8,128)(2,1)}, u32[]{:S(2)}) copy-start(bf16[256,128]{1,0:T(8,128)(2,1)} %node_in_ref.1) | copy-start | bytes 196612
  0.7 9.7 %copy-start.4 = (bf16[2,128,128]{2,1,0:T(8,128)(2,1)S(1)}, bf16[2,128,128]{2,1,0:T(8,128)(2,1)}, u32[]{:S(2)}) copy-start(bf16[2,128,128]{2,1,0:T(8,128)(2,1)} %node_w_ref.1) | copy-start | bytes 196612
  0.7 9.7 %copy-start.5 = (bf16[2,128,128]{2,1,0:T(8,128)(2,1)S(1)}, bf16[2,128,128]{2,1,0:T(8,128)(2,1)}, u32[]{:S(2)}) copy-start(bf16[2,128,128]{2,1,0:T(8,128)(2,1)} %decoder_w_ref.1) | copy-start | bytes 196612
  0.7 9.7 %copy-start.10 = (bf16[12,128]{1,0:T(8,128)(2,1)S(1)}, bf16[12,128]{1,0:T(8,128)(2,1)}, u32[]{:S(2)}) copy-start(bf16[12,128]{1,0:T(8,128)(2,1)} %encoder_in_ref.1) | copy-start | bytes 9220
  0.8 3.1 %collective-permute-start = (bf16[2,2,1,128,128]{4,3,2,1,0:T(8,128)(2,1)}, bf16[2,2,1,128,128]{4,3,2,1,0:T(8,128)(2,1)S(1)}, u32[]{:S(2)}, u32[]{:S(2)}) collective-permute-start(bf16[2,2,1,128,128]{4,3,2,1,0:T(8,128)(2,1)} %latent_ref), channel_id=1, source_target_pairs={{0,1},{1,0},{2,3},{3,2},{4,5},{5,4},{6,7},{7,6},{8,9},{9,8},{10,11... | collective-permute-start | bytes 393224 | tf_op jit(solution)/shard_map/ppermute | solution.py:590
  1.3 12.6 %collective-permute-start.3 = (bf16[2,2,1,128,128]{4,3,2,1,0:T(8,128)(2,1)}, bf16[2,2,1,128,128]{4,3,2,1,0:T(8,128)(2,1)S(1)}, u32[]{:S(2)}, u32[]{:S(2)}) collective-permute-start(bf16[2,2,1,128,128]{4,3,2,1,0:T(8,128)(2,1)} %latent_ref), channel_id=1, source_target_pairs={{0,2},{2,0},{1,3},{3,1},{4,6},{6,4},{5,7},{7,5},{8,10},{10,8},{9,1... | collective-permute-start | bytes 393224 | tf_op jit(solution)/shard_map/ppermute | solution.py:590
  4.0 9.9 %collective-permute-start.1 = (bf16[2,2,128,128]{3,2,1,0:T(8,128)(2,1)S(1)}, bf16[2,2,128,128]{3,2,1,0:T(8,128)(2,1)S(1)}, u32[]{:S(2)}, u32[]{:S(2)}) collective-permute-start(bf16[2,2,128,128]{3,2,1,0:T(8,128)(2,1)S(1)} %pad_maximum_fusion.1), channel_id=1, source_target_pairs={{0,5},{1,1},{2,7},{3,3},{4,9},{5,0},{6,11},{7,2},{8,13},{9,4},{10,... | collective-permute-start | bytes 393224 | tf_op jit(solution)/shard_map/ppermute | solution.py:610
  7.2 6.6 %collective-permute-start.2 = (bf16[2,1,128,128]{3,2,1,0:T(8,128)(2,1)S(1)}, bf16[2,1,128,128]{3,2,1,0:T(8,128)(2,1)S(1)}, u32[]{:S(2)}, u32[]{:S(2)}) collective-permute-start(bf16[2,1,128,128]{3,2,1,0:T(8,128)(2,1)S(1)} %fusion), channel_id=1, source_target_pairs={{0,7},{1,1},{2,5},{3,3},{4,11},{5,2},{6,9},{7,0},{8,15},{9,6},{10,... | collective-permute-start | bytes 196616 | tf_op jit(solution)/shard_map/ppermute | solution.py:610
  14.0 1.6 %copy-start.13 = (bf16[3,128]{1,0:T(4,128)(2,1)S(1)}, bf16[3,128]{1,0:T(4,128)(2,1)}, u32[]{:S(2)}) copy-start(bf16[3,128]{1,0:T(4,128)(2,1)} %decoder_out_ref.1) | copy-start | bytes 2308
  14.0 1.6 %collective-permute-start.4 = (bf16[8,128,128]{2,1,0:T(8,128)(2,1)S(1)}, bf16[8,128,128]{2,1,0:T(8,128)(2,1)S(1)}, u32[]{:S(2)}, u32[]{:S(2)}) collective-permute-start(bf16[8,128,128]{2,1,0:T(8,128)(2,1)S(1)} %pad_maximum_fusion), channel_id=1, source_target_pairs={{0,1},{1,0},{2,3},{3,2},{4,5},{5,4},{6,7},{7,6},{8,9},{9,8},{10,11... | collective-permute-start | bytes 786440 | tf_op jit(solution)/shard_map/ppermute | solution.py:590
  17.8 1.4 %collective-permute-start.6 = (f32[16,128]{1,0:T(8,128)S(1)}, f32[16,128]{1,0:T(8,128)S(1)}, u32[]{:S(2)}, u32[]{:S(2)}) collective-permute-start(f32[16,128]{1,0:T(8,128)S(1)} %get-tuple-element.90), channel_id=1, source_target_pairs={{0,1},{1,0},{2,3},{3,2},{4,5},{5,4},{6,7},{7,6},{8,9},{9,8},{10,11... | collective-permute-start | bytes 24584 | tf_op jit(solution)/shard_map/ppermute | solution.py:590
  18.0 11.0 %collective-permute-start.5 = (f32[16,128]{1,0:T(8,128)S(1)}, f32[16,128]{1,0:T(8,128)S(1)}, u32[]{:S(2)}, u32[]{:S(2)}) collective-permute-start(f32[16,128]{1,0:T(8,128)S(1)} %get-tuple-element.90), channel_id=1, source_target_pairs={{0,2},{2,0},{1,3},{3,1},{4,6},{6,4},{5,7},{7,5},{8,10},{10,8},{9,1... | collective-permute-start | bytes 24584 | tf_op jit(solution)/shard_map/ppermute | solution.py:590
  19.2 9.8 %collective-permute-start.7 = (f32[2,16,128]{2,1,0:T(8,128)S(1)}, f32[2,16,128]{2,1,0:T(8,128)S(1)}, u32[]{:S(2)}, u32[]{:S(2)}) collective-permute-start(f32[2,16,128]{2,1,0:T(8,128)S(1)} %pad_maximum_fusion.3), channel_id=1, source_target_pairs={{0,7},{1,1},{2,5},{3,3},{4,11},{5,2},{6,9},{7,0},{8,15},{9,6},{10,... | collective-permute-start | bytes 49160 | tf_op jit(solution)/shard_map/ppermute | solution.py:610
  23.0 6.0 %collective-permute-start.8 = (f32[2,16,128]{2,1,0:T(8,128)S(1)}, f32[2,16,128]{2,1,0:T(8,128)S(1)}, u32[]{:S(2)}, u32[]{:S(2)}) collective-permute-start(f32[2,16,128]{2,1,0:T(8,128)S(1)} %pad_maximum_fusion.3), channel_id=1, source_target_pairs={{0,5},{1,1},{2,7},{3,3},{4,9},{5,0},{6,11},{7,2},{8,13},{9,4},{10,... | collective-permute-start | bytes 49160 | tf_op jit(solution)/shard_map/ppermute | solution.py:610
  29.0 1.3 %copy-start.6 = (bf16[2,128,128]{2,1,0:T(8,128)(2,1)S(1)}, bf16[2,128,128]{2,1,0:T(8,128)(2,1)}, u32[]{:S(2)}) copy-start(bf16[2,128,128]{2,1,0:T(8,128)(2,1)} %refs_6_.1) | copy-start | bytes 196612
  29.1 1.3 %collective-permute-start.9 = (f32[5,16,128]{2,1,0:T(8,128)S(1)}, f32[5,16,128]{2,1,0:T(8,128)S(1)}, u32[]{:S(2)}, u32[]{:S(2)}) collective-permute-start(f32[5,16,128]{2,1,0:T(8,128)S(1)} %pad_maximum_fusion.2), channel_id=1, source_target_pairs={{0,1},{1,0},{2,3},{3,2},{4,5},{5,4},{6,7},{7,6},{8,9},{9,8},{10,11... | collective-permute-start | bytes 122888 | tf_op jit(solution)/shard_map/ppermute | solution.py:590

commit v18 on v17

--- a/solution.py
+++ b/solution.py
@@ -1,4 +1,5 @@
 import functools
+import itertools
 
 import jax
 import jax.numpy as jnp
@@ -596,18 +597,25 @@
 
 
 def swap_chips(values, cross):
-    count_x, count_y, count_z = (lax.axis_size(axis) for axis in ("gx", "gy", "gz"))
+    axes = ("group", "gx", "gy", "gz")
+    counts = tuple(lax.axis_size(axis) for axis in axes)
+
+    def number(place):
+        total = 0
+        for count, index in zip(counts, place):
+            total = total * count + index
+        return total
+
     pairs = []
-    for x in range(count_x):
-        for y in range(count_y):
-            for z in range(count_z):
-                to_x = x + 1 - 2 * z
-                if 0 <= to_x < count_x:
-                    to = (to_x, y ^ 1 if cross else y, 1 - z)
-                else:
-                    to = (x, y, z)
-                pairs.append(((x * count_y + y) * count_z + z, (to[0] * count_y + to[1]) * count_z + to[2]))
-    return lax.ppermute(values, ("gx", "gy", "gz"), pairs)
+    for place in itertools.product(*(range(count) for count in counts)):
+        group, x, y, z = place
+        to_x = x + 1 - 2 * z
+        if 0 <= to_x < counts[1]:
+            to = (group, to_x, y ^ 1 if cross else y, 1 - z)
+        else:
+            to = (group ^ 1, x, y, z)
+        pairs.append((number(place), number(to)))
+    return lax.ppermute(values, axes, pairs)
 
 
 def call(kernel, name, in_specs, outs, scratch, operands, flops):

time: 32.1 us -> 24.4 us (0.76)
  starting transfers between devices: 17 us -> 9.49 us
    ppermute x4, starting transfers between devices: 12.4 us -> 4.83 us  [swap_chips(): return lax.ppermute(values, axes, pairs)]
  transfers between devices with their start and end apart: 10 -> 10, of which waited for: 2 -> 2; matrix products, arithmetic and copies ran while one was open for 0% -> 0% of each run, Pallas kernels for 29% -> 38%
where the time goes in v18:
time: 24.4 us; the launch traced here: 24.3 us
  Pallas kernels  12.9 us (53%)
  starting transfers between devices  9.49 us (39%)
  between operations  1.03 us (4%)
  waiting for transfers between devices  0.64 us (3%)
    pallas_call x8, Pallas kernels, call(): pl.pallas_call(kernel, out_shape=tuple((jax.ShapeDtypeStruct(shape, kind)...  12.9 us
    ppermute x4, starting transfers between devices, swap_chips(): return lax.ppermute(values, axes, pairs)  4.83 us
    ppermute x6, starting transfers between devices, swap(): return lax.ppermute(values, axis, [(0, 1), (1, 0)])  4.65 us
    ppermute x6, waiting for transfers between devices, swap(): return lax.ppermute(values, axis, [(0, 1), (1, 0)])  0.63 us
  transfers between devices with their start and end apart: 10, of which 2 were waited for; matrix products, arithmetic and copies ran while one was open for 0% of the time, Pallas kernels for 38%

profile of v18, /device:TPU:0, one launch (start us, length us, event | category | flops | bytes accessed | tf_op | source)
XLA Modules:
  0.0 24.3 jit_solution(10552540049190817184)
XLA Ops:
  0.8 0.5 %collective-permute-start = (bf16[2,2,1,128,128]{4,3,2,1,0:T(8,128)(2,1)}, bf16[2,2,1,128,128]{4,3,2,1,0:T(8,128)(2,1)S(1)}, u32[]{:S(2)}, u32[]{:S(2)}) collective-permute-start(bf16[2,2,1,128,128]{4,3,2,1,0:T(8,128)(2,1)} %latent_ref), channel_id=1, source_target_pairs={{0,1},{1,0},{2,3},{3,2},{4,5},{5,4},{6,7},{7,6},{8,9},{9,8},{10,11... | collective-permute-start | bytes 393224 | tf_op jit(solution)/shard_map/ppermute | solution.py:591
  1.3 2.6 %collective-permute-start.3 = (bf16[2,2,1,128,128]{4,3,2,1,0:T(8,128)(2,1)}, bf16[2,2,1,128,128]{4,3,2,1,0:T(8,128)(2,1)S(1)}, u32[]{:S(2)}, u32[]{:S(2)}) collective-permute-start(bf16[2,2,1,128,128]{4,3,2,1,0:T(8,128)(2,1)} %latent_ref), channel_id=1, source_target_pairs={{0,2},{2,0},{1,3},{3,1},{4,6},{6,4},{5,7},{7,5},{8,10},{10,8},{9,1... | collective-permute-start | bytes 393224 | tf_op jit(solution)/shard_map/ppermute | solution.py:591
  3.9 0.0 collective-permute-done.own_zed
  4.0 1.4 %collective-permute-start.1 = (bf16[2,2,128,128]{3,2,1,0:T(8,128)(2,1)S(1)}, bf16[2,2,128,128]{3,2,1,0:T(8,128)(2,1)S(1)}, u32[]{:S(2)}, u32[]{:S(2)}) collective-permute-start(bf16[2,2,128,128]{3,2,1,0:T(8,128)(2,1)S(1)} %pad_maximum_fusion.1), channel_id=1, source_target_pairs={{0,5},{1,17},{2,7},{3,19},{4,9},{5,0},{6,11},{7,2},{8,13},{9,4},{1... | collective-permute-start | bytes 393224 | tf_op jit(solution)/shard_map/ppermute | solution.py:618
  5.4 1.2 %collective-permute-start.2 = (bf16[2,1,128,128]{3,2,1,0:T(8,128)(2,1)S(1)}, bf16[2,1,128,128]{3,2,1,0:T(8,128)(2,1)S(1)}, u32[]{:S(2)}, u32[]{:S(2)}) collective-permute-start(bf16[2,1,128,128]{3,2,1,0:T(8,128)(2,1)S(1)} %fusion), channel_id=1, source_target_pairs={{0,7},{1,17},{2,5},{3,19},{4,11},{5,2},{6,9},{7,0},{8,15},{9,6},{1... | collective-permute-start | bytes 196616 | tf_op jit(solution)/shard_map/ppermute | solution.py:618
  6.7 3.3 %ranks.1 = (bf16[11,128,128]{2,1,0:T(8,128)(2,1)S(1)}, bf16[48,128]{1,0:T(8,128)(2,1)S(1)}, f32[2,2,1,128]{3,2,1,0:T(1,128)S(1)}, f32[128,512]{1,0:T(8,128)S(1)}...) custom-call(bf16[2,2,1,12,128,128]{5,4,3,2,1,0:T(8,128)(2,1)S(1)} %c, ...), custom_call_target="tpu_custom_call" | custom-call | flops 5000000000 | tf_op jit(solution)/shard_map/ranks/pallas_call | solution.py:622
  10.1 0.0 collective-permute-done.2
  10.2 0.0 copy-start.13
  10.2 0.1 collective-permute-start.4
  10.3 1.1 %prepare.1 = (bf16[3,128,256]{2,1,0:T(8,128)(2,1)S(1)}, f32[128,1536]{1,0:T(8,128)S(1)}) custom-call(bf16[4,128,256]{2,1,0:T(8,128)(2,1)S(1)} %get-tuple-element.76.far_ref, bf16[2,3,128,128]{3,2,1,0:T(8,128)(2,1)S(1)} %constant_dynamic-update-slice_fusion.mine_ref, bf16[11,128,128]{2,1,0:T(8,128)(2,1)S(1)} %get-tuple-element.77.weights_ref.refs_4_, ...), custom_call_target="tpu_custom_call" | custom-call | flops 5000000000 | tf_op jit(solution)/shard_map/prepare/pallas_call | solution.py:622
  11.3 0.4 %collective-permute-done.4 = bf16[8,128,128]{2,1,0:T(8,128)(2,1)S(1)} collective-permute-done((bf16[8,128,128]{2,1,0:T(8,128)(2,1)S(1)}, bf16[8,128,128]{2,1,0:T(8,128)(2,1)S(1)}, u32[]{:S(2)}, u32[]{:S(2)}) %collective-permute-start.4) | collective-permute-done | bytes 262176 | tf_op jit(solution)/shard_map/ppermute | solution.py:591
  11.8 2.2 %movers.1 = (bf16[8,128,256]{2,1,0:T(8,128)(2,1)S(1)}, f32[16,128]{1,0:T(8,128)S(1)}) custom-call(bf16[2,128,128]{2,1,0:T(8,128)(2,1)S(1)} %dynamic-slice_bitcast_fusion.refs_0_, bf16[2,128,128]{2,1,0:T(8,128)(2,1)S(1)} %slice.6.refs_1_, bf16[2,3,128,128]{3,2,1,0:T(8,128)(2,1)S(1)} %bitcast.16, bf16[3,128,256]{2,1,0:T(8,128)(2,1)S(1)} %get-tuple-element.85.refs_3_, ...), custom_call_target="tpu_custom_call" | custom-call | flops 3000000000 | tf_op jit(solution)/shard_map/movers/pallas_call | solution.py:622
  14.0 0.1 collective-permute-start.6
  14.2 1.3 %collective-permute-start.5 = (f32[16,128]{1,0:T(8,128)S(1)}, f32[16,128]{1,0:T(8,128)S(1)}, u32[]{:S(2)}, u32[]{:S(2)}) collective-permute-start(f32[16,128]{1,0:T(8,128)S(1)} %get-tuple-element.90), channel_id=1, source_target_pairs={{0,2},{2,0},{1,3},{3,1},{4,6},{6,4},{5,7},{7,5},{8,10},{10,8},{9,1... | collective-permute-start | bytes 24584 | tf_op jit(solution)/shard_map/ppermute | solution.py:591
  15.4 0.0 collective-permute-done.6.zed_ref
  15.4 2.1 %collective-permute-start.7 = (f32[2,16,128]{2,1,0:T(8,128)S(1)}, f32[2,16,128]{2,1,0:T(8,128)S(1)}, u32[]{:S(2)}, u32[]{:S(2)}) collective-permute-start(f32[2,16,128]{2,1,0:T(8,128)S(1)} %pad_maximum_fusion.3), channel_id=1, source_target_pairs={{0,7},{1,17},{2,5},{3,19},{4,11},{5,2},{6,9},{7,0},{8,15},{9,6},{1... | collective-permute-start | bytes 49160 | tf_op jit(solution)/shard_map/ppermute | solution.py:618
  17.6 0.1 collective-permute-start.8
  17.7 1.9 %edges.3.second_ref = bf16[2,128,128]{2,1,0:T(8,128)(2,1)S(1)} custom-call(f32[2,2,1,128]{3,2,1,0:T(1,128)S(1)} %get-tuple-element.93.alive_ref, s32[2,2,12,1,128]{4,3,2,1,0:T(1,128)S(1)} %bitcast.21, bf16[8,128,256]{2,1,0:T(8,128)(2,1)S(1)} %get-tuple-element.94.far_ref, f32[4,128,1536]{2,1,0:T(8,128)S(1)} %get-tuple-element.95.pre_ref, ...), custom_call_target="tpu_custom_call" | custom-call | flops 4000000000 | tf_op jit(solution)/shard_map/edges/pallas_call | solution.py:622
  19.5 1.9 %edges.2.first_ref = bf16[2,128,128]{2,1,0:T(8,128)(2,1)S(1)} custom-call(f32[2,2,1,128]{3,2,1,0:T(1,128)S(1)} %get-tuple-element.93.alive_ref, s32[2,2,12,1,128]{4,3,2,1,0:T(1,128)S(1)} %bitcast.22, bf16[8,128,256]{2,1,0:T(8,128)(2,1)S(1)} %get-tuple-element.94.far_ref, f32[4,128,1536]{2,1,0:T(8,128)S(1)} %get-tuple-element.95.pre_ref, ...), custom_call_target="tpu_custom_call" | custom-call | flops 4000000000 | tf_op jit(solution)/shard_map/edges/pallas_call | solution.py:622
  21.4 0.0 copy-start.6
  21.5 0.1 collective-permute-start.9
  21.6 1.0 %nodes.1.moved_ref = f32[16,512]{1,0:T(8,128)S(1)} custom-call(bf16[2,128,128]{2,1,0:T(8,128)(2,1)S(1)} %edges.2.first_ref, bf16[2,128,128]{2,1,0:T(8,128)(2,1)S(1)} %edges.3.second_ref, f32[128,512]{1,0:T(8,128)S(1)} %get-tuple-element.101.node_pre_ref, f32[128,512]{1,0:T(8,128)S(1)} %get-tuple-element.102.latent_t_ref, ...), custom_call_target="tpu_custom_call" | custom-call | flops 1000000000 | tf_op jit(solution)/shard_map/nodes/pallas_call | solution.py:622
  22.6 0.2 collective-permute-done.9.refs_3_
  22.8 1.5 %finish.1 = (bf16[2,2,1,128,128]{4,3,2,1,0:T(8,128)(2,1)}, f32[9,2,2,1,128]{4,3,2,1,0:T(1,128)}, bf16[1,1,1,208,128]{4,3,2,1,0:T(8,128)(2,1)}, f32[9,1,1,1,208]{4,3,2,1,0:T(1,128)}) custom-call(f32[16,512]{1,0:T(8,128)S(1)} %nodes.1.moved_ref, f32[16,128]{1,0:T(8,128)S(1)} %collective-permute-done.6.zed_ref, f32[16,128]{1,0:T(8,128)S(1)} %collective-permute-done.5.refs_0_, ...), custom_call_target="tpu_custom_call" | custom-call | flops 1000000000 | tf_op jit(solution)/shard_map/finish/pallas_call | solution.py:622
  (44 shorter events, 0.2 us)
Async XLA Ops:
  0.6 3.2 %copy-start = (bf16[2,2,1,128,128]{4,3,2,1,0:T(8,128)(2,1)S(1)}, bf16[2,2,1,128,128]{4,3,2,1,0:T(8,128)(2,1)}, u32[]{:S(2)}) copy-start(bf16[2,2,1,128,128]{4,3,2,1,0:T(8,128)(2,1)} %latent_ref) | copy-start | bytes 393220
  0.6 6.0 %copy-start.7 = (s32[2,2,1,12,128]{4,2,3,1,0:T(1,128)S(1)}, s32[2,2,1,12,128]{4,2,3,1,0:T(1,128)}, u32[]{:S(2)}) copy-start(s32[2,2,1,12,128]{4,2,3,1,0:T(1,128)} %param.19) | copy-start | bytes 73732
  0.7 6.0 %copy-start.12 = (s32[2,2,1]{1,2,0:T(1,128)S(1)}, s32[2,2,1]{1,2,0:T(1,128)}, u32[]{:S(2)}) copy-start(s32[2,2,1]{1,2,0:T(1,128)} %param.18) | copy-start | bytes 52
  0.7 6.0 %copy-start.1 = (bf16[2,2,1,12,128,128]{5,4,3,2,1,0:T(8,128)(2,1)S(1)}, bf16[2,2,1,12,128,128]{5,4,3,2,1,0:T(8,128)(2,1)}, u32[]{:S(2)}) copy-start(bf16[2,2,1,12,128,128]{5,4,3,2,1,0:T(8,128)(2,1)} %edge_ref.1) | copy-start | bytes 4718596
  0.7 5.9 %copy-start.8 = (f32[3,2,2,1,128]{4,3,2,1,0:T(1,128)S(1)}, f32[3,2,2,1,128]{4,3,2,1,0:T(1,128)}, u32[]{:S(2)}) copy-start(f32[3,2,2,1,128]{4,3,2,1,0:T(1,128)} %positions_ref.1) | copy-start | bytes 18436
  0.7 5.9 %copy-start.9 = (f32[3,2,2,1,128]{4,3,2,1,0:T(1,128)S(1)}, f32[3,2,2,1,128]{4,3,2,1,0:T(1,128)}, u32[]{:S(2)}) copy-start(f32[3,2,2,1,128]{4,3,2,1,0:T(1,128)} %velocity_ref.1) | copy-start | bytes 18436
  0.7 5.9 %copy-start.11 = (s32[2,2,1,128]{3,2,1,0:T(1,128)S(1)}, s32[2,2,1,128]{3,2,1,0:T(1,128)}, u32[]{:S(2)}) copy-start(s32[2,2,1,128]{3,2,1,0:T(1,128)} %owners_ref.1) | copy-start | bytes 6148
  0.7 5.9 %copy-start.2 = (bf16[5,128,128]{2,1,0:T(8,128)(2,1)S(1)}, bf16[5,128,128]{2,1,0:T(8,128)(2,1)}, u32[]{:S(2)}) copy-start(bf16[5,128,128]{2,1,0:T(8,128)(2,1)} %edge_w_ref.1) | copy-start | bytes 491524
  0.7 5.9 %copy-start.3 = (bf16[256,128]{1,0:T(8,128)(2,1)S(1)}, bf16[256,128]{1,0:T(8,128)(2,1)}, u32[]{:S(2)}) copy-start(bf16[256,128]{1,0:T(8,128)(2,1)} %node_in_ref.1) | copy-start | bytes 196612
  0.7 5.9 %copy-start.4 = (bf16[2,128,128]{2,1,0:T(8,128)(2,1)S(1)}, bf16[2,128,128]{2,1,0:T(8,128)(2,1)}, u32[]{:S(2)}) copy-start(bf16[2,128,128]{2,1,0:T(8,128)(2,1)} %node_w_ref.1) | copy-start | bytes 196612
  0.7 5.9 %copy-start.5 = (bf16[2,128,128]{2,1,0:T(8,128)(2,1)S(1)}, bf16[2,128,128]{2,1,0:T(8,128)(2,1)}, u32[]{:S(2)}) copy-start(bf16[2,128,128]{2,1,0:T(8,128)(2,1)} %decoder_w_ref.1) | copy-start | bytes 196612
  0.7 5.9 %copy-start.10 = (bf16[12,128]{1,0:T(8,128)(2,1)S(1)}, bf16[12,128]{1,0:T(8,128)(2,1)}, u32[]{:S(2)}) copy-start(bf16[12,128]{1,0:T(8,128)(2,1)} %encoder_in_ref.1) | copy-start | bytes 9220
  0.8 3.1 %collective-permute-start = (bf16[2,2,1,128,128]{4,3,2,1,0:T(8,128)(2,1)}, bf16[2,2,1,128,128]{4,3,2,1,0:T(8,128)(2,1)S(1)}, u32[]{:S(2)}, u32[]{:S(2)}) collective-permute-start(bf16[2,2,1,128,128]{4,3,2,1,0:T(8,128)(2,1)} %latent_ref), channel_id=1, source_target_pairs={{0,1},{1,0},{2,3},{3,2},{4,5},{5,4},{6,7},{7,6},{8,9},{9,8},{10,11... | collective-permute-start | bytes 393224 | tf_op jit(solution)/shard_map/ppermute | solution.py:591
  1.3 8.8 %collective-permute-start.3 = (bf16[2,2,1,128,128]{4,3,2,1,0:T(8,128)(2,1)}, bf16[2,2,1,128,128]{4,3,2,1,0:T(8,128)(2,1)S(1)}, u32[]{:S(2)}, u32[]{:S(2)}) collective-permute-start(bf16[2,2,1,128,128]{4,3,2,1,0:T(8,128)(2,1)} %latent_ref), channel_id=1, source_target_pairs={{0,2},{2,0},{1,3},{3,1},{4,6},{6,4},{5,7},{7,5},{8,10},{10,8},{9,1... | collective-permute-start | bytes 393224 | tf_op jit(solution)/shard_map/ppermute | solution.py:591
  4.0 6.1 %collective-permute-start.1 = (bf16[2,2,128,128]{3,2,1,0:T(8,128)(2,1)S(1)}, bf16[2,2,128,128]{3,2,1,0:T(8,128)(2,1)S(1)}, u32[]{:S(2)}, u32[]{:S(2)}) collective-permute-start(bf16[2,2,128,128]{3,2,1,0:T(8,128)(2,1)S(1)} %pad_maximum_fusion.1), channel_id=1, source_target_pairs={{0,5},{1,17},{2,7},{3,19},{4,9},{5,0},{6,11},{7,2},{8,13},{9,4},{1... | collective-permute-start | bytes 393224 | tf_op jit(solution)/shard_map/ppermute | solution.py:618
  5.4 4.7 %collective-permute-start.2 = (bf16[2,1,128,128]{3,2,1,0:T(8,128)(2,1)S(1)}, bf16[2,1,128,128]{3,2,1,0:T(8,128)(2,1)S(1)}, u32[]{:S(2)}, u32[]{:S(2)}) collective-permute-start(bf16[2,1,128,128]{3,2,1,0:T(8,128)(2,1)S(1)} %fusion), channel_id=1, source_target_pairs={{0,7},{1,17},{2,5},{3,19},{4,11},{5,2},{6,9},{7,0},{8,15},{9,6},{1... | collective-permute-start | bytes 196616 | tf_op jit(solution)/shard_map/ppermute | solution.py:618
  10.2 1.6 %copy-start.13 = (bf16[3,128]{1,0:T(4,128)(2,1)S(1)}, bf16[3,128]{1,0:T(4,128)(2,1)}, u32[]{:S(2)}) copy-start(bf16[3,128]{1,0:T(4,128)(2,1)} %decoder_out_ref.1) | copy-start | bytes 2308
  10.2 1.6 %collective-permute-start.4 = (bf16[8,128,128]{2,1,0:T(8,128)(2,1)S(1)}, bf16[8,128,128]{2,1,0:T(8,128)(2,1)S(1)}, u32[]{:S(2)}, u32[]{:S(2)}) collective-permute-start(bf16[8,128,128]{2,1,0:T(8,128)(2,1)S(1)} %pad_maximum_fusion), channel_id=1, source_target_pairs={{0,1},{1,0},{2,3},{3,2},{4,5},{5,4},{6,7},{7,6},{8,9},{9,8},{10,11... | collective-permute-start | bytes 786440 | tf_op jit(solution)/shard_map/ppermute | solution.py:591
  14.0 1.4 %collective-permute-start.6 = (f32[16,128]{1,0:T(8,128)S(1)}, f32[16,128]{1,0:T(8,128)S(1)}, u32[]{:S(2)}, u32[]{:S(2)}) collective-permute-start(f32[16,128]{1,0:T(8,128)S(1)} %get-tuple-element.90), channel_id=1, source_target_pairs={{0,1},{1,0},{2,3},{3,2},{4,5},{5,4},{6,7},{7,6},{8,9},{9,8},{10,11... | collective-permute-start | bytes 24584 | tf_op jit(solution)/shard_map/ppermute | solution.py:591
  14.2 7.3 %collective-permute-start.5 = (f32[16,128]{1,0:T(8,128)S(1)}, f32[16,128]{1,0:T(8,128)S(1)}, u32[]{:S(2)}, u32[]{:S(2)}) collective-permute-start(f32[16,128]{1,0:T(8,128)S(1)} %get-tuple-element.90), channel_id=1, source_target_pairs={{0,2},{2,0},{1,3},{3,1},{4,6},{6,4},{5,7},{7,5},{8,10},{10,8},{9,1... | collective-permute-start | bytes 24584 | tf_op jit(solution)/shard_map/ppermute | solution.py:591
  15.4 6.0 %collective-permute-start.7 = (f32[2,16,128]{2,1,0:T(8,128)S(1)}, f32[2,16,128]{2,1,0:T(8,128)S(1)}, u32[]{:S(2)}, u32[]{:S(2)}) collective-permute-start(f32[2,16,128]{2,1,0:T(8,128)S(1)} %pad_maximum_fusion.3), channel_id=1, source_target_pairs={{0,7},{1,17},{2,5},{3,19},{4,11},{5,2},{6,9},{7,0},{8,15},{9,6},{1... | collective-permute-start | bytes 49160 | tf_op jit(solution)/shard_map/ppermute | solution.py:618
  17.6 3.9 %collective-permute-start.8 = (f32[2,16,128]{2,1,0:T(8,128)S(1)}, f32[2,16,128]{2,1,0:T(8,128)S(1)}, u32[]{:S(2)}, u32[]{:S(2)}) collective-permute-start(f32[2,16,128]{2,1,0:T(8,128)S(1)} %pad_maximum_fusion.3), channel_id=1, source_target_pairs={{0,5},{1,17},{2,7},{3,19},{4,9},{5,0},{6,11},{7,2},{8,13},{9,4},{1... | collective-permute-start | bytes 49160 | tf_op jit(solution)/shard_map/ppermute | solution.py:618
  21.4 1.3 %copy-start.6 = (bf16[2,128,128]{2,1,0:T(8,128)(2,1)S(1)}, bf16[2,128,128]{2,1,0:T(8,128)(2,1)}, u32[]{:S(2)}) copy-start(bf16[2,128,128]{2,1,0:T(8,128)(2,1)} %refs_6_.1) | copy-start | bytes 196612
  21.5 1.3 %collective-permute-start.9 = (f32[5,16,128]{2,1,0:T(8,128)S(1)}, f32[5,16,128]{2,1,0:T(8,128)S(1)}, u32[]{:S(2)}, u32[]{:S(2)}) collective-permute-start(f32[5,16,128]{2,1,0:T(8,128)S(1)} %pad_maximum_fusion.2), channel_id=1, source_target_pairs={{0,1},{1,0},{2,3},{3,2},{4,5},{5,4},{6,7},{7,6},{8,9},{9,8},{10,11... | collective-permute-start | bytes 122888 | tf_op jit(solution)/shard_map/ppermute | solution.py:591

commit v19 on v18

--- a/solution.py
+++ b/solution.py
@@ -447,7 +447,6 @@
 
 def edges_kernel(
     sizes,
-    a,
     alive_ref,
     neighbours_ref,
     far_ref,
@@ -459,10 +458,9 @@
     fold_y = sizes[1] == 2
     window = Window(fold_y, None, far_ref)
     index_y = lax.axis_index("gy")
-    alive_ref, neighbours_ref = alive_ref.at[a], neighbours_ref.at[a]
     slots = alive_ref.shape[-1]
-    neighbour_count = neighbours_ref.shape[1]
-    for bt in range(2):
+    neighbour_count = neighbours_ref.shape[2]
+    for a, bt in CELLS:
         if fold_y:
             b = index_y if bt == 0 else 1 - index_y
             rows = (0, 1) if bt == 0 else (0, 1, 2)
@@ -471,9 +469,8 @@
             rows = (bt, bt + 1, bt + 2)
         columns = [(ex, row) for ex in range(a, a + 3) for row in rows]
         columns = [column for column in columns if column not in window.own_columns()]
-        ids = jnp.concatenate([neighbours_ref[b, k] for k in range(neighbour_count)], axis=1)
+        ids = jnp.concatenate([neighbours_ref[a, b, k] for k in range(neighbour_count)], axis=1)
         place, key = places(ids & 127, ids >> 7, fold_y)
-
         message = messages(
             window.cells(columns),
             place,
@@ -481,15 +478,14 @@
             lambda tile, i=2 * a + bt: pre_ref[i, :, tile * TILE : (tile + 1) * TILE],
             weights_ref[MIDDLE],
             weights_ref[FINAL],
-            hidden_ref.at[bt],
+            hidden_ref.at[2 * a + bt],
         )
-        total = jnp.where(alive_ref[b] > 0.5, slot_sum(message, slots), 0.0)
-        total_ref[b] = total.astype(BF16)
+        total = jnp.where(alive_ref[a, b] > 0.5, slot_sum(message, slots), 0.0)
+        total_ref[2 * a + b] = total.astype(BF16)
 
 
 def nodes_kernel(
-    first_ref,
-    second_ref,
+    total_ref,
     node_pre_ref,
     latent_t_ref,
     state_ref,
@@ -497,7 +493,7 @@
     decoder_out_ref,
     moved_ref,
 ):
-    aggregate = jnp.concatenate([first_ref[0], first_ref[1], second_ref[0], second_ref[1]], axis=1)
+    aggregate = jnp.concatenate([total_ref[i] for i in range(4)], axis=1)
     acceleration = advance(
         node_pre_ref[...], aggregate, latent_t_ref[...], weights_ref, decoder_out_ref[...]
     )
@@ -785,17 +781,6 @@
         3_000_000_000,
     )
 
-    def edges(a):
-        return call(
-            functools.partial(edges_kernel, sizes, a),
-            "edges",
-            [VMEM] * 5,
-            [((2, width, slots), BF16)],
-            [pltpu.VMEM((2, width, neighbour_count * slots), BF16)],
-            (alive, neighbours, far_rest, edge_pre, weights),
-            4_000_000_000,
-        )[0]
-
     zed = swap(bucket, "gz")
     if fold_y:
         sides = [swap(bucket, "gy")]
@@ -806,8 +791,16 @@
         both = jnp.stack([bucket, zed])
         sides = [shift(both, "gy", 0), shift(both, "gy", 1)]
         ends = [swap_chips(jnp.stack([both, *sides], axis=1), False)]
-    first, second = edges(0), edges(1)
-    sides, ends, first, second = lax.optimization_barrier((sides, ends, first, second))
+    total = call(
+        functools.partial(edges_kernel, sizes),
+        "edges",
+        [VMEM] * 5,
+        [((4, width, slots), BF16)],
+        [pltpu.VMEM((4, width, neighbour_count * slots), BF16)],
+        (alive, neighbours, far_rest, edge_pre, weights),
+        8_000_000_000,
+    )[0]
+    sides, ends, total = lax.optimization_barrier((sides, ends, total))
     if fold_y:
         packed = swap(jnp.concatenate([*ends, sides[0][None]], axis=0), "gz")
     else:
@@ -815,10 +808,10 @@
     state = call(
         nodes_kernel,
         "nodes",
-        [VMEM] * 7,
+        [VMEM] * 6,
         [((ROWS, particles), F32)],
         [],
-        (first, second, node_pre, latent_t, state, weights, decoder_out),
+        (total, node_pre, latent_t, state, weights, decoder_out),
         1_000_000_000,
     )[0]
     packed, state = lax.optimization_barrier((packed, state))

time: 24.4 us -> 24.3 us (level)
    pallas_call x8 -> x7, Pallas kernels: 12.9 us -> 12.8 us  [call(): pl.pallas_call(kernel, out_shape=tuple((jax.ShapeDtypeStruct(shape, kind)...]
where the time goes in v19:
time: 24.3 us; the launch traced here: 24.2 us
  Pallas kernels  12.8 us (53%)
  starting transfers between devices  9.49 us (39%)
  between operations  1.02 us (4%)
  waiting for transfers between devices  0.64 us (3%)
    pallas_call x7, Pallas kernels, call(): pl.pallas_call(kernel, out_shape=tuple((jax.ShapeDtypeStruct(shape, kind)...  12.8 us
    ppermute x4, starting transfers between devices, swap_chips(): return lax.ppermute(values, axes, pairs)  4.83 us
    ppermute x6, starting transfers between devices, swap(): return lax.ppermute(values, axis, [(0, 1), (1, 0)])  4.65 us
    ppermute x6, waiting for transfers between devices, swap(): return lax.ppermute(values, axis, [(0, 1), (1, 0)])  0.63 us
  transfers between devices with their start and end apart: 10, of which 2 were waited for; matrix products, arithmetic and copies ran while one was open for 0% of the time, Pallas kernels for 38%

profile of v19, /device:TPU:0, one launch (start us, length us, event | category | flops | bytes accessed | tf_op | source)
XLA Modules:
  0.0 24.2 jit_solution(7008092878641870704)
XLA Ops:
  0.8 0.5 %collective-permute-start = (bf16[2,2,1,128,128]{4,3,2,1,0:T(8,128)(2,1)}, bf16[2,2,1,128,128]{4,3,2,1,0:T(8,128)(2,1)S(1)}, u32[]{:S(2)}, u32[]{:S(2)}) collective-permute-start(bf16[2,2,1,128,128]{4,3,2,1,0:T(8,128)(2,1)} %latent_ref), channel_id=1, source_target_pairs={{0,1},{1,0},{2,3},{3,2},{4,5},{5,4},{6,7},{7,6},{8,9},{9,8},{10,11... | collective-permute-start | bytes 393224 | tf_op jit(solution)/shard_map/ppermute | solution.py:587
  1.3 2.6 %collective-permute-start.3 = (bf16[2,2,1,128,128]{4,3,2,1,0:T(8,128)(2,1)}, bf16[2,2,1,128,128]{4,3,2,1,0:T(8,128)(2,1)S(1)}, u32[]{:S(2)}, u32[]{:S(2)}) collective-permute-start(bf16[2,2,1,128,128]{4,3,2,1,0:T(8,128)(2,1)} %latent_ref), channel_id=1, source_target_pairs={{0,2},{2,0},{1,3},{3,1},{4,6},{6,4},{5,7},{7,5},{8,10},{10,8},{9,1... | collective-permute-start | bytes 393224 | tf_op jit(solution)/shard_map/ppermute | solution.py:587
  3.9 0.0 collective-permute-done.own_zed
  4.0 1.4 %collective-permute-start.1 = (bf16[2,2,128,128]{3,2,1,0:T(8,128)(2,1)S(1)}, bf16[2,2,128,128]{3,2,1,0:T(8,128)(2,1)S(1)}, u32[]{:S(2)}, u32[]{:S(2)}) collective-permute-start(bf16[2,2,128,128]{3,2,1,0:T(8,128)(2,1)S(1)} %pad_maximum_fusion.1), channel_id=1, source_target_pairs={{0,5},{1,17},{2,7},{3,19},{4,9},{5,0},{6,11},{7,2},{8,13},{9,4},{1... | collective-permute-start | bytes 393224 | tf_op jit(solution)/shard_map/ppermute | solution.py:614
  5.4 1.2 %collective-permute-start.2 = (bf16[2,1,128,128]{3,2,1,0:T(8,128)(2,1)S(1)}, bf16[2,1,128,128]{3,2,1,0:T(8,128)(2,1)S(1)}, u32[]{:S(2)}, u32[]{:S(2)}) collective-permute-start(bf16[2,1,128,128]{3,2,1,0:T(8,128)(2,1)S(1)} %fusion), channel_id=1, source_target_pairs={{0,7},{1,17},{2,5},{3,19},{4,11},{5,2},{6,9},{7,0},{8,15},{9,6},{1... | collective-permute-start | bytes 196616 | tf_op jit(solution)/shard_map/ppermute | solution.py:614
  6.7 3.3 %ranks.1 = (bf16[11,128,128]{2,1,0:T(8,128)(2,1)S(1)}, bf16[48,128]{1,0:T(8,128)(2,1)S(1)}, f32[2,2,1,128]{3,2,1,0:T(1,128)S(1)}, f32[128,512]{1,0:T(8,128)S(1)}...) custom-call(bf16[2,2,1,12,128,128]{5,4,3,2,1,0:T(8,128)(2,1)S(1)} %c, ...), custom_call_target="tpu_custom_call" | custom-call | flops 5000000000 | tf_op jit(solution)/shard_map/ranks/pallas_call | solution.py:618
  10.1 0.0 collective-permute-done.1
  10.2 0.0 copy-start.13
  10.2 0.1 collective-permute-start.4
  10.3 1.1 %prepare.1 = (bf16[3,128,256]{2,1,0:T(8,128)(2,1)S(1)}, f32[128,1536]{1,0:T(8,128)S(1)}) custom-call(bf16[4,128,256]{2,1,0:T(8,128)(2,1)S(1)} %get-tuple-element.75.far_ref, bf16[2,3,128,128]{3,2,1,0:T(8,128)(2,1)S(1)} %constant_dynamic-update-slice_fusion.mine_ref, bf16[11,128,128]{2,1,0:T(8,128)(2,1)S(1)} %get-tuple-element.76.weights_ref.refs_4_, ...), custom_call_target="tpu_custom_call" | custom-call | flops 5000000000 | tf_op jit(solution)/shard_map/prepare/pallas_call | solution.py:618
  11.3 0.4 %collective-permute-done.4 = bf16[8,128,128]{2,1,0:T(8,128)(2,1)S(1)} collective-permute-done((bf16[8,128,128]{2,1,0:T(8,128)(2,1)S(1)}, bf16[8,128,128]{2,1,0:T(8,128)(2,1)S(1)}, u32[]{:S(2)}, u32[]{:S(2)}) %collective-permute-start.4) | collective-permute-done | bytes 262176 | tf_op jit(solution)/shard_map/ppermute | solution.py:587
  11.8 2.2 %movers.1 = (bf16[8,128,256]{2,1,0:T(8,128)(2,1)S(1)}, f32[16,128]{1,0:T(8,128)S(1)}) custom-call(bf16[2,128,128]{2,1,0:T(8,128)(2,1)S(1)} %dynamic-slice_bitcast_fusion.refs_0_, bf16[2,128,128]{2,1,0:T(8,128)(2,1)S(1)} %slice.6.refs_1_, bf16[2,3,128,128]{3,2,1,0:T(8,128)(2,1)S(1)} %bitcast.16, bf16[3,128,256]{2,1,0:T(8,128)(2,1)S(1)} %get-tuple-element.84.refs_3_, ...), custom_call_target="tpu_custom_call" | custom-call | flops 3000000000 | tf_op jit(solution)/shard_map/movers/pallas_call | solution.py:618
  14.0 0.1 collective-permute-start.6
  14.2 1.3 %collective-permute-start.5 = (f32[16,128]{1,0:T(8,128)S(1)}, f32[16,128]{1,0:T(8,128)S(1)}, u32[]{:S(2)}, u32[]{:S(2)}) collective-permute-start(f32[16,128]{1,0:T(8,128)S(1)} %get-tuple-element.89), channel_id=1, source_target_pairs={{0,2},{2,0},{1,3},{3,1},{4,6},{6,4},{5,7},{7,5},{8,10},{10,8},{9,1... | collective-permute-start | bytes 24584 | tf_op jit(solution)/shard_map/ppermute | solution.py:587
  15.4 2.1 %collective-permute-start.7 = (f32[2,16,128]{2,1,0:T(8,128)S(1)}, f32[2,16,128]{2,1,0:T(8,128)S(1)}, u32[]{:S(2)}, u32[]{:S(2)}) collective-permute-start(f32[2,16,128]{2,1,0:T(8,128)S(1)} %pad_maximum_fusion.3), channel_id=1, source_target_pairs={{0,7},{1,17},{2,5},{3,19},{4,11},{5,2},{6,9},{7,0},{8,15},{9,6},{1... | collective-permute-start | bytes 49160 | tf_op jit(solution)/shard_map/ppermute | solution.py:614
  17.6 0.1 collective-permute-start.8
  17.7 3.7 %edges.1.total_ref = bf16[4,128,128]{2,1,0:T(8,128)(2,1)S(1)} custom-call(f32[2,2,1,128]{3,2,1,0:T(1,128)S(1)} %get-tuple-element.92.alive_ref, s32[2,2,12,1,128]{4,3,2,1,0:T(1,128)S(1)} %bitcast.21, bf16[8,128,256]{2,1,0:T(8,128)(2,1)S(1)} %get-tuple-element.93.far_ref, f32[4,128,1536]{2,1,0:T(8,128)S(1)} %get-tuple-element.94.pre_ref, ...), custom_call_target="tpu_custom_call" | custom-call | flops 8000000000 | tf_op jit(solution)/shard_map/edges/pallas_call | solution.py:618
  21.3 0.0 copy-start.6
  21.3 0.0 collective-permute-done.7.refs_1_
  21.4 0.0 collective-permute-done.8.refs_2_
  21.4 0.1 collective-permute-start.9
  21.5 1.0 %nodes.1.moved_ref = f32[16,512]{1,0:T(8,128)S(1)} custom-call(bf16[4,128,128]{2,1,0:T(8,128)(2,1)S(1)} %edges.1.total_ref, f32[128,512]{1,0:T(8,128)S(1)} %get-tuple-element.99.node_pre_ref, f32[128,512]{1,0:T(8,128)S(1)} %get-tuple-element.100.latent_t_ref, f32[8,512]{1,0:T(8,128)S(1)} %get-tuple-element.101.state_ref, ...), custom_call_target="tpu_custom_call" | custom-call | flops 1000000000 | tf_op jit(solution)/shard_map/nodes/pallas_call | solution.py:618
  22.5 0.2 collective-permute-done.9.refs_3_
  22.7 1.5 %finish.1 = (bf16[2,2,1,128,128]{4,3,2,1,0:T(8,128)(2,1)}, f32[9,2,2,1,128]{4,3,2,1,0:T(1,128)}, bf16[1,1,1,208,128]{4,3,2,1,0:T(8,128)(2,1)}, f32[9,1,1,1,208]{4,3,2,1,0:T(1,128)}) custom-call(f32[16,512]{1,0:T(8,128)S(1)} %nodes.1.moved_ref, f32[16,128]{1,0:T(8,128)S(1)} %collective-permute-done.6.zed_ref, f32[16,128]{1,0:T(8,128)S(1)} %collective-permute-done.5.refs_0_, ...), custom_call_target="tpu_custom_call" | custom-call | flops 1000000000 | tf_op jit(solution)/shard_map/finish/pallas_call | solution.py:618
  (43 shorter events, 0.2 us)
Async XLA Ops:
  0.6 3.2 %copy-start = (bf16[2,2,1,128,128]{4,3,2,1,0:T(8,128)(2,1)S(1)}, bf16[2,2,1,128,128]{4,3,2,1,0:T(8,128)(2,1)}, u32[]{:S(2)}) copy-start(bf16[2,2,1,128,128]{4,3,2,1,0:T(8,128)(2,1)} %latent_ref) | copy-start | bytes 393220
  0.6 6.0 %copy-start.7 = (s32[2,2,1,12,128]{4,2,3,1,0:T(1,128)S(1)}, s32[2,2,1,12,128]{4,2,3,1,0:T(1,128)}, u32[]{:S(2)}) copy-start(s32[2,2,1,12,128]{4,2,3,1,0:T(1,128)} %param.19) | copy-start | bytes 73732
  0.7 6.0 %copy-start.12 = (s32[2,2,1]{1,2,0:T(1,128)S(1)}, s32[2,2,1]{1,2,0:T(1,128)}, u32[]{:S(2)}) copy-start(s32[2,2,1]{1,2,0:T(1,128)} %param.18) | copy-start | bytes 52
  0.7 6.0 %copy-start.1 = (bf16[2,2,1,12,128,128]{5,4,3,2,1,0:T(8,128)(2,1)S(1)}, bf16[2,2,1,12,128,128]{5,4,3,2,1,0:T(8,128)(2,1)}, u32[]{:S(2)}) copy-start(bf16[2,2,1,12,128,128]{5,4,3,2,1,0:T(8,128)(2,1)} %edge_ref.1) | copy-start | bytes 4718596
  0.7 5.9 %copy-start.8 = (f32[3,2,2,1,128]{4,3,2,1,0:T(1,128)S(1)}, f32[3,2,2,1,128]{4,3,2,1,0:T(1,128)}, u32[]{:S(2)}) copy-start(f32[3,2,2,1,128]{4,3,2,1,0:T(1,128)} %positions_ref.1) | copy-start | bytes 18436
  0.7 5.9 %copy-start.9 = (f32[3,2,2,1,128]{4,3,2,1,0:T(1,128)S(1)}, f32[3,2,2,1,128]{4,3,2,1,0:T(1,128)}, u32[]{:S(2)}) copy-start(f32[3,2,2,1,128]{4,3,2,1,0:T(1,128)} %velocity_ref.1) | copy-start | bytes 18436
  0.7 5.9 %copy-start.11 = (s32[2,2,1,128]{3,2,1,0:T(1,128)S(1)}, s32[2,2,1,128]{3,2,1,0:T(1,128)}, u32[]{:S(2)}) copy-start(s32[2,2,1,128]{3,2,1,0:T(1,128)} %owners_ref.1) | copy-start | bytes 6148
  0.7 5.9 %copy-start.2 = (bf16[5,128,128]{2,1,0:T(8,128)(2,1)S(1)}, bf16[5,128,128]{2,1,0:T(8,128)(2,1)}, u32[]{:S(2)}) copy-start(bf16[5,128,128]{2,1,0:T(8,128)(2,1)} %edge_w_ref.1) | copy-start | bytes 491524
  0.7 5.9 %copy-start.3 = (bf16[256,128]{1,0:T(8,128)(2,1)S(1)}, bf16[256,128]{1,0:T(8,128)(2,1)}, u32[]{:S(2)}) copy-start(bf16[256,128]{1,0:T(8,128)(2,1)} %node_in_ref.1) | copy-start | bytes 196612
  0.7 5.9 %copy-start.4 = (bf16[2,128,128]{2,1,0:T(8,128)(2,1)S(1)}, bf16[2,128,128]{2,1,0:T(8,128)(2,1)}, u32[]{:S(2)}) copy-start(bf16[2,128,128]{2,1,0:T(8,128)(2,1)} %node_w_ref.1) | copy-start | bytes 196612
  0.7 5.9 %copy-start.5 = (bf16[2,128,128]{2,1,0:T(8,128)(2,1)S(1)}, bf16[2,128,128]{2,1,0:T(8,128)(2,1)}, u32[]{:S(2)}) copy-start(bf16[2,128,128]{2,1,0:T(8,128)(2,1)} %decoder_w_ref.1) | copy-start | bytes 196612
  0.7 5.9 %copy-start.10 = (bf16[12,128]{1,0:T(8,128)(2,1)S(1)}, bf16[12,128]{1,0:T(8,128)(2,1)}, u32[]{:S(2)}) copy-start(bf16[12,128]{1,0:T(8,128)(2,1)} %encoder_in_ref.1) | copy-start | bytes 9220
  0.8 3.1 %collective-permute-start = (bf16[2,2,1,128,128]{4,3,2,1,0:T(8,128)(2,1)}, bf16[2,2,1,128,128]{4,3,2,1,0:T(8,128)(2,1)S(1)}, u32[]{:S(2)}, u32[]{:S(2)}) collective-permute-start(bf16[2,2,1,128,128]{4,3,2,1,0:T(8,128)(2,1)} %latent_ref), channel_id=1, source_target_pairs={{0,1},{1,0},{2,3},{3,2},{4,5},{5,4},{6,7},{7,6},{8,9},{9,8},{10,11... | collective-permute-start | bytes 393224 | tf_op jit(solution)/shard_map/ppermute | solution.py:587
  1.3 8.8 %collective-permute-start.3 = (bf16[2,2,1,128,128]{4,3,2,1,0:T(8,128)(2,1)}, bf16[2,2,1,128,128]{4,3,2,1,0:T(8,128)(2,1)S(1)}, u32[]{:S(2)}, u32[]{:S(2)}) collective-permute-start(bf16[2,2,1,128,128]{4,3,2,1,0:T(8,128)(2,1)} %latent_ref), channel_id=1, source_target_pairs={{0,2},{2,0},{1,3},{3,1},{4,6},{6,4},{5,7},{7,5},{8,10},{10,8},{9,1... | collective-permute-start | bytes 393224 | tf_op jit(solution)/shard_map/ppermute | solution.py:587
  4.0 6.1 %collective-permute-start.1 = (bf16[2,2,128,128]{3,2,1,0:T(8,128)(2,1)S(1)}, bf16[2,2,128,128]{3,2,1,0:T(8,128)(2,1)S(1)}, u32[]{:S(2)}, u32[]{:S(2)}) collective-permute-start(bf16[2,2,128,128]{3,2,1,0:T(8,128)(2,1)S(1)} %pad_maximum_fusion.1), channel_id=1, source_target_pairs={{0,5},{1,17},{2,7},{3,19},{4,9},{5,0},{6,11},{7,2},{8,13},{9,4},{1... | collective-permute-start | bytes 393224 | tf_op jit(solution)/shard_map/ppermute | solution.py:614
  5.4 4.7 %collective-permute-start.2 = (bf16[2,1,128,128]{3,2,1,0:T(8,128)(2,1)S(1)}, bf16[2,1,128,128]{3,2,1,0:T(8,128)(2,1)S(1)}, u32[]{:S(2)}, u32[]{:S(2)}) collective-permute-start(bf16[2,1,128,128]{3,2,1,0:T(8,128)(2,1)S(1)} %fusion), channel_id=1, source_target_pairs={{0,7},{1,17},{2,5},{3,19},{4,11},{5,2},{6,9},{7,0},{8,15},{9,6},{1... | collective-permute-start | bytes 196616 | tf_op jit(solution)/shard_map/ppermute | solution.py:614
  10.2 1.6 %copy-start.13 = (bf16[3,128]{1,0:T(4,128)(2,1)S(1)}, bf16[3,128]{1,0:T(4,128)(2,1)}, u32[]{:S(2)}) copy-start(bf16[3,128]{1,0:T(4,128)(2,1)} %decoder_out_ref.1) | copy-start | bytes 2308
  10.2 1.6 %collective-permute-start.4 = (bf16[8,128,128]{2,1,0:T(8,128)(2,1)S(1)}, bf16[8,128,128]{2,1,0:T(8,128)(2,1)S(1)}, u32[]{:S(2)}, u32[]{:S(2)}) collective-permute-start(bf16[8,128,128]{2,1,0:T(8,128)(2,1)S(1)} %pad_maximum_fusion), channel_id=1, source_target_pairs={{0,1},{1,0},{2,3},{3,2},{4,5},{5,4},{6,7},{7,6},{8,9},{9,8},{10,11... | collective-permute-start | bytes 786440 | tf_op jit(solution)/shard_map/ppermute | solution.py:587
  14.0 1.4 %collective-permute-start.6 = (f32[16,128]{1,0:T(8,128)S(1)}, f32[16,128]{1,0:T(8,128)S(1)}, u32[]{:S(2)}, u32[]{:S(2)}) collective-permute-start(f32[16,128]{1,0:T(8,128)S(1)} %get-tuple-element.89), channel_id=1, source_target_pairs={{0,1},{1,0},{2,3},{3,2},{4,5},{5,4},{6,7},{7,6},{8,9},{9,8},{10,11... | collective-permute-start | bytes 24584 | tf_op jit(solution)/shard_map/ppermute | solution.py:587
  14.2 7.2 %collective-permute-start.5 = (f32[16,128]{1,0:T(8,128)S(1)}, f32[16,128]{1,0:T(8,128)S(1)}, u32[]{:S(2)}, u32[]{:S(2)}) collective-permute-start(f32[16,128]{1,0:T(8,128)S(1)} %get-tuple-element.89), channel_id=1, source_target_pairs={{0,2},{2,0},{1,3},{3,1},{4,6},{6,4},{5,7},{7,5},{8,10},{10,8},{9,1... | collective-permute-start | bytes 24584 | tf_op jit(solution)/shard_map/ppermute | solution.py:587
  15.4 5.9 %collective-permute-start.7 = (f32[2,16,128]{2,1,0:T(8,128)S(1)}, f32[2,16,128]{2,1,0:T(8,128)S(1)}, u32[]{:S(2)}, u32[]{:S(2)}) collective-permute-start(f32[2,16,128]{2,1,0:T(8,128)S(1)} %pad_maximum_fusion.3), channel_id=1, source_target_pairs={{0,7},{1,17},{2,5},{3,19},{4,11},{5,2},{6,9},{7,0},{8,15},{9,6},{1... | collective-permute-start | bytes 49160 | tf_op jit(solution)/shard_map/ppermute | solution.py:614
  17.6 3.8 %collective-permute-start.8 = (f32[2,16,128]{2,1,0:T(8,128)S(1)}, f32[2,16,128]{2,1,0:T(8,128)S(1)}, u32[]{:S(2)}, u32[]{:S(2)}) collective-permute-start(f32[2,16,128]{2,1,0:T(8,128)S(1)} %pad_maximum_fusion.3), channel_id=1, source_target_pairs={{0,5},{1,17},{2,7},{3,19},{4,9},{5,0},{6,11},{7,2},{8,13},{9,4},{1... | collective-permute-start | bytes 49160 | tf_op jit(solution)/shard_map/ppermute | solution.py:614
  21.3 1.3 %copy-start.6 = (bf16[2,128,128]{2,1,0:T(8,128)(2,1)S(1)}, bf16[2,128,128]{2,1,0:T(8,128)(2,1)}, u32[]{:S(2)}) copy-start(bf16[2,128,128]{2,1,0:T(8,128)(2,1)} %refs_6_.1) | copy-start | bytes 196612
  21.4 1.3 %collective-permute-start.9 = (f32[5,16,128]{2,1,0:T(8,128)S(1)}, f32[5,16,128]{2,1,0:T(8,128)S(1)}, u32[]{:S(2)}, u32[]{:S(2)}) collective-permute-start(f32[5,16,128]{2,1,0:T(8,128)S(1)} %pad_maximum_fusion.2), channel_id=1, source_target_pairs={{0,1},{1,0},{2,3},{3,2},{4,5},{5,4},{6,7},{7,6},{8,9},{9,8},{10,11... | collective-permute-start | bytes 122888 | tf_op jit(solution)/shard_map/ppermute | solution.py:587

commit v20 on v19

--- a/solution.py
+++ b/solution.py
@@ -131,7 +131,10 @@
 def messages(cells, place, key, pre, middle_t, final_t, hidden_ref):
     for tile in range(place.shape[1] // TILE):
         at = slice(tile * TILE, (tile + 1) * TILE)
-        hidden_ref[:, at] = relu16(pre(tile) + pick(cells, place[:, at], key[:, at]))
+        terms = pre(tile)
+        if cells:
+            terms = terms + pick(cells, place[:, at], key[:, at])
+        hidden_ref[:, at] = relu16(terms)
     hidden = relu16(dot(middle_t, hidden_ref[...]))
     return norm(dot(final_t, hidden), 0)
 
@@ -142,6 +145,11 @@
         self.own_rows = (0, 1) if fold_y else (1, 2)
         self.outer_rows = (2,) if fold_y else (0, 3)
         self.own_ref, self.rest_ref = own_ref, rest_ref
+
+    def rows(self, bt):
+        if self.row_count == 3:
+            return (0, 1, 2)[: 2 + bt]
+        return (bt, bt + 1, bt + 2)
 
     def own_columns(self):
         return [(ex, row) for ex in (1, 2) for row in self.own_rows]
@@ -363,8 +371,11 @@
     place_ref,
     key_ref,
     near_ref,
+    neighbours_ref,
+    edge_pre_ref,
     far_mine_ref,
     pre_ref,
+    border_ref,
 ):
     window = Window(sizes[1] == 2, far_ref)
     core = lax.axis_index("gz")
@@ -383,6 +394,15 @@
         pre_ref[:, at] = (
             dot_nt(weights_ref[EDGE], edges) + near + pick(cells, place_ref[:, at], key_ref[:, at])
         )
+
+    a = 1 - core
+    b = lax.axis_index("gy") if sizes[1] == 2 else 0
+    side = [(12 * a + row, far_mine_ref.at[row]) for row in window.rows(0)]
+    ids = jnp.concatenate([neighbours_ref[a, b, k] for k in range(neighbour_count)], axis=1)
+    place, key = places(ids & 127, ids >> 7, sizes[1] == 2)
+    for tile in range(ids.shape[1] // TILE):
+        at = slice(tile * TILE, (tile + 1) * TILE)
+        border_ref[:, at] = edge_pre_ref[2 * a, :, at] + pick(side, place[:, at], key[:, at])
 
 
 def movers_kernel(
@@ -451,6 +471,7 @@
     neighbours_ref,
     far_ref,
     pre_ref,
+    border_ref,
     weights_ref,
     total_ref,
     hidden_ref,
@@ -460,25 +481,30 @@
     index_y = lax.axis_index("gy")
     slots = alive_ref.shape[-1]
     neighbour_count = neighbours_ref.shape[2]
-    for a, bt in CELLS:
-        if fold_y:
-            b = index_y if bt == 0 else 1 - index_y
-            rows = (0, 1) if bt == 0 else (0, 1, 2)
-        else:
-            b = bt
-            rows = (bt, bt + 1, bt + 2)
-        columns = [(ex, row) for ex in range(a, a + 3) for row in rows]
-        columns = [column for column in columns if column not in window.own_columns()]
+    core = lax.axis_index("gz")
+    for other, bt in CELLS:
+        a = core if other else 1 - core
+        b = (index_y if bt == 0 else 1 - index_y) if fold_y else bt
+        rows = window.rows(bt)
+        cells = window.cells([(ex, row) for ex in (1, 2) for row in rows if row in window.outer_rows])
+        picked = other == 0 and bt == 0
+        if not picked:
+            cells += [(12 * a + row, far_ref.at[a * window.row_count + row]) for row in rows]
         ids = jnp.concatenate([neighbours_ref[a, b, k] for k in range(neighbour_count)], axis=1)
         place, key = places(ids & 127, ids >> 7, fold_y)
+
+        def pre(tile, picked=picked, i=2 * a + bt):
+            at = slice(tile * TILE, (tile + 1) * TILE)
+            return border_ref[:, at] if picked else pre_ref[i, :, at]
+
         message = messages(
-            window.cells(columns),
+            cells,
             place,
             key,
-            lambda tile, i=2 * a + bt: pre_ref[i, :, tile * TILE : (tile + 1) * TILE],
+            pre,
             weights_ref[MIDDLE],
             weights_ref[FINAL],
-            hidden_ref.at[2 * a + bt],
+            hidden_ref.at[2 * other + bt],
         )
         total = jnp.where(alive_ref[a, b] > 0.5, slot_sum(message, slots), 0.0)
         total_ref[2 * a + b] = total.astype(BF16)
@@ -748,17 +774,31 @@
     prepared = call(
         functools.partial(prepare_kernel, sizes),
         "prepare",
-        [VMEM] * 7,
-        [((rows, width, 2 * slots), BF16), ((width, neighbour_count * movers), F32)],
+        [VMEM] * 9,
+        [
+            ((rows, width, 2 * slots), BF16),
+            ((width, neighbour_count * movers), F32),
+            ((width, neighbour_count * slots), F32),
+        ],
         [],
-        (far_own, mine, weights, mover_edges, mover_place, mover_key, mover_near),
+        (
+            far_own,
+            mine,
+            weights,
+            mover_edges,
+            mover_place,
+            mover_key,
+            mover_near,
+            neighbours,
+            edge_pre,
+        ),
         5_000_000_000,
     )
     packed, prepared = lax.optimization_barrier((packed, prepared))
     cells = mine.shape[0] * mine.shape[1]
     if fold_y:
         side_zeds = [packed[cells:]]
-    far_mine, mover_pre = prepared
+    far_mine, mover_pre, border = prepared
     halo = [*sides, *side_zeds, packed[:cells].reshape(mine.shape), far_mine]
 
     far_rest, bucket = call(
@@ -794,10 +834,10 @@
     total = call(
         functools.partial(edges_kernel, sizes),
         "edges",
-        [VMEM] * 5,
+        [VMEM] * 6,
         [((4, width, slots), BF16)],
         [pltpu.VMEM((4, width, neighbour_count * slots), BF16)],
-        (alive, neighbours, far_rest, edge_pre, weights),
+        (alive, neighbours, far_rest, edge_pre, border, weights),
         8_000_000_000,
     )[0]
     sides, ends, total = lax.optimization_barrier((sides, ends, total))

time: 24.3 us -> 24.1 us (level)
  no operation moved by 1% of the time
where the time goes in v20:
time: 24.1 us; the launch traced here: 23.9 us
  Pallas kernels  12.8 us (53%)
  starting transfers between devices  9.44 us (39%)
  between operations  1.02 us (4%)
  waiting for transfers between devices  0.43 us (2%)
    pallas_call x7, Pallas kernels, call(): pl.pallas_call(kernel, out_shape=tuple((jax.ShapeDtypeStruct(shape, kind)...  12.8 us
    ppermute x4, starting transfers between devices, swap_chips(): return lax.ppermute(values, axes, pairs)  4.73 us
    ppermute x6, starting transfers between devices, swap(): return lax.ppermute(values, axis, [(0, 1), (1, 0)])  4.72 us
  transfers between devices with their start and end apart: 10, of which 2 were waited for; matrix products, arithmetic and copies ran while one was open for 0% of the time, Pallas kernels for 38%

profile of v20, /device:TPU:0, one launch (start us, length us, event | category | flops | bytes accessed | tf_op | source)
XLA Modules:
  0.0 23.9 jit_solution(14565116300567113017)
XLA Ops:
  0.8 0.5 %collective-permute-start = (bf16[2,2,1,128,128]{4,3,2,1,0:T(8,128)(2,1)}, bf16[2,2,1,128,128]{4,3,2,1,0:T(8,128)(2,1)S(1)}, u32[]{:S(2)}, u32[]{:S(2)}) collective-permute-start(bf16[2,2,1,128,128]{4,3,2,1,0:T(8,128)(2,1)} %latent_ref), channel_id=1, source_target_pairs={{0,1},{1,0},{2,3},{3,2},{4,5},{5,4},{6,7},{7,6},{8,9},{9,8},{10,11... | collective-permute-start | bytes 393224 | tf_op jit(solution)/shard_map/ppermute | solution.py:613
  1.3 2.6 %collective-permute-start.3 = (bf16[2,2,1,128,128]{4,3,2,1,0:T(8,128)(2,1)}, bf16[2,2,1,128,128]{4,3,2,1,0:T(8,128)(2,1)S(1)}, u32[]{:S(2)}, u32[]{:S(2)}) collective-permute-start(bf16[2,2,1,128,128]{4,3,2,1,0:T(8,128)(2,1)} %latent_ref), channel_id=1, source_target_pairs={{0,2},{2,0},{1,3},{3,1},{4,6},{6,4},{5,7},{7,5},{8,10},{10,8},{9,1... | collective-permute-start | bytes 393224 | tf_op jit(solution)/shard_map/ppermute | solution.py:613
  3.9 0.0 collective-permute-done.own_zed
  4.0 1.4 %collective-permute-start.1 = (bf16[2,2,128,128]{3,2,1,0:T(8,128)(2,1)S(1)}, bf16[2,2,128,128]{3,2,1,0:T(8,128)(2,1)S(1)}, u32[]{:S(2)}, u32[]{:S(2)}) collective-permute-start(bf16[2,2,128,128]{3,2,1,0:T(8,128)(2,1)S(1)} %pad_maximum_fusion.1), channel_id=1, source_target_pairs={{0,5},{1,17},{2,7},{3,19},{4,9},{5,0},{6,11},{7,2},{8,13},{9,4},{1... | collective-permute-start | bytes 393224 | tf_op jit(solution)/shard_map/ppermute | solution.py:640
  5.4 1.2 %collective-permute-start.2 = (bf16[2,1,128,128]{3,2,1,0:T(8,128)(2,1)S(1)}, bf16[2,1,128,128]{3,2,1,0:T(8,128)(2,1)S(1)}, u32[]{:S(2)}, u32[]{:S(2)}) collective-permute-start(bf16[2,1,128,128]{3,2,1,0:T(8,128)(2,1)S(1)} %fusion), channel_id=1, source_target_pairs={{0,7},{1,17},{2,5},{3,19},{4,11},{5,2},{6,9},{7,0},{8,15},{9,6},{1... | collective-permute-start | bytes 196616 | tf_op jit(solution)/shard_map/ppermute | solution.py:640
  6.7 3.4 %ranks.1 = (bf16[11,128,128]{2,1,0:T(8,128)(2,1)S(1)}, bf16[48,128]{1,0:T(8,128)(2,1)S(1)}, f32[2,2,1,128]{3,2,1,0:T(1,128)S(1)}, f32[128,512]{1,0:T(8,128)S(1)}...) custom-call(bf16[2,2,1,12,128,128]{5,4,3,2,1,0:T(8,128)(2,1)S(1)} %c, ...), custom_call_target="tpu_custom_call" | custom-call | flops 5000000000 | tf_op jit(solution)/shard_map/ranks/pallas_call | solution.py:644
  10.1 0.0 collective-permute-done.3
  10.2 0.0 copy-start.13
  10.3 0.1 collective-permute-start.4
  10.3 1.3 %prepare.1 = (bf16[3,128,256]{2,1,0:T(8,128)(2,1)S(1)}, f32[128,1536]{1,0:T(8,128)S(1)}, f32[128,1536]{1,0:T(8,128)S(1)}) custom-call(bf16[4,128,256]{2,1,0:T(8,128)(2,1)S(1)} %get-tuple-element.77.far_ref, bf16[2,3,128,128]{3,2,1,0:T(8,128)(2,1)S(1)} %constant_dynamic-update-slice_fusion.mine_ref, ...), custom_call_target="tpu_custom_call" | custom-call | flops 5000000000 | tf_op jit(solution)/shard_map/prepare/pallas_call | solution.py:644
  11.6 0.2 collective-permute-done.4
  11.9 2.2 %movers.1 = (bf16[8,128,256]{2,1,0:T(8,128)(2,1)S(1)}, f32[16,128]{1,0:T(8,128)S(1)}) custom-call(bf16[2,128,128]{2,1,0:T(8,128)(2,1)S(1)} %dynamic-slice_bitcast_fusion.refs_0_, bf16[2,128,128]{2,1,0:T(8,128)(2,1)S(1)} %slice.6.refs_1_, bf16[2,3,128,128]{3,2,1,0:T(8,128)(2,1)S(1)} %bitcast.16, bf16[3,128,256]{2,1,0:T(8,128)(2,1)S(1)} %get-tuple-element.88.refs_3_, ...), custom_call_target="tpu_custom_call" | custom-call | flops 3000000000 | tf_op jit(solution)/shard_map/movers/pallas_call | solution.py:644
  14.1 0.3 %collective-permute-start.6 = (f32[16,128]{1,0:T(8,128)S(1)}, f32[16,128]{1,0:T(8,128)S(1)}, u32[]{:S(2)}, u32[]{:S(2)}) collective-permute-start(f32[16,128]{1,0:T(8,128)S(1)} %get-tuple-element.93), channel_id=1, source_target_pairs={{0,1},{1,0},{2,3},{3,2},{4,5},{5,4},{6,7},{7,6},{8,9},{9,8},{10,11... | collective-permute-start | bytes 24584 | tf_op jit(solution)/shard_map/ppermute | solution.py:613
  14.4 1.2 %collective-permute-start.5 = (f32[16,128]{1,0:T(8,128)S(1)}, f32[16,128]{1,0:T(8,128)S(1)}, u32[]{:S(2)}, u32[]{:S(2)}) collective-permute-start(f32[16,128]{1,0:T(8,128)S(1)} %get-tuple-element.93), channel_id=1, source_target_pairs={{0,2},{2,0},{1,3},{3,1},{4,6},{6,4},{5,7},{7,5},{8,10},{10,8},{9,1... | collective-permute-start | bytes 24584 | tf_op jit(solution)/shard_map/ppermute | solution.py:613
  15.6 0.0 collective-permute-done.6.zed_ref
  15.6 2.1 %collective-permute-start.7 = (f32[2,16,128]{2,1,0:T(8,128)S(1)}, f32[2,16,128]{2,1,0:T(8,128)S(1)}, u32[]{:S(2)}, u32[]{:S(2)}) collective-permute-start(f32[2,16,128]{2,1,0:T(8,128)S(1)} %pad_maximum_fusion.3), channel_id=1, source_target_pairs={{0,7},{1,17},{2,5},{3,19},{4,11},{5,2},{6,9},{7,0},{8,15},{9,6},{1... | collective-permute-start | bytes 49160 | tf_op jit(solution)/shard_map/ppermute | solution.py:640
  17.7 3.4 %edges.1.total_ref = bf16[4,128,128]{2,1,0:T(8,128)(2,1)S(1)} custom-call(f32[2,2,1,128]{3,2,1,0:T(1,128)S(1)} %get-tuple-element.96.alive_ref, s32[2,2,12,1,128]{4,3,2,1,0:T(1,128)S(1)} %bitcast.22, bf16[8,128,256]{2,1,0:T(8,128)(2,1)S(1)} %get-tuple-element.97.far_ref, f32[4,128,1536]{2,1,0:T(8,128)S(1)} %get-tuple-element.83.edge_pre_ref.pre_ref, ...), custom_call_target="tpu_custom_call" | custom-call | flops 8000000000 | tf_op jit(solution)/shard_map/edges/pallas_call | solution.py:644
  21.1 0.0 copy-start.6
  21.1 0.0 collective-permute-done.7.refs_1_
  21.1 0.0 collective-permute-done.8.refs_2_
  21.1 0.1 collective-permute-start.9
  21.2 1.0 %nodes.1.moved_ref = f32[16,512]{1,0:T(8,128)S(1)} custom-call(bf16[4,128,128]{2,1,0:T(8,128)(2,1)S(1)} %edges.1.total_ref, f32[128,512]{1,0:T(8,128)S(1)} %get-tuple-element.103.node_pre_ref, f32[128,512]{1,0:T(8,128)S(1)} %get-tuple-element.104.latent_t_ref, f32[8,512]{1,0:T(8,128)S(1)} %get-tuple-element.105.state_ref, ...), custom_call_target="tpu_custom_call" | custom-call | flops 1000000000 | tf_op jit(solution)/shard_map/nodes/pallas_call | solution.py:644
  22.2 0.2 collective-permute-done.9.refs_3_
  22.4 1.5 %finish.1 = (bf16[2,2,1,128,128]{4,3,2,1,0:T(8,128)(2,1)}, f32[9,2,2,1,128]{4,3,2,1,0:T(1,128)}, bf16[1,1,1,208,128]{4,3,2,1,0:T(8,128)(2,1)}, f32[9,1,1,1,208]{4,3,2,1,0:T(1,128)}) custom-call(f32[16,512]{1,0:T(8,128)S(1)} %nodes.1.moved_ref, f32[16,128]{1,0:T(8,128)S(1)} %collective-permute-done.6.zed_ref, f32[16,128]{1,0:T(8,128)S(1)} %collective-permute-done.5.refs_0_, ...), custom_call_target="tpu_custom_call" | custom-call | flops 1000000000 | tf_op jit(solution)/shard_map/finish/pallas_call | solution.py:644
  (43 shorter events, 0.2 us)
Async XLA Ops:
  0.6 3.2 %copy-start = (bf16[2,2,1,128,128]{4,3,2,1,0:T(8,128)(2,1)S(1)}, bf16[2,2,1,128,128]{4,3,2,1,0:T(8,128)(2,1)}, u32[]{:S(2)}) copy-start(bf16[2,2,1,128,128]{4,3,2,1,0:T(8,128)(2,1)} %latent_ref) | copy-start | bytes 393220
  0.6 6.0 %copy-start.7 = (s32[2,2,1,12,128]{4,2,3,1,0:T(1,128)S(1)}, s32[2,2,1,12,128]{4,2,3,1,0:T(1,128)}, u32[]{:S(2)}) copy-start(s32[2,2,1,12,128]{4,2,3,1,0:T(1,128)} %param.19) | copy-start | bytes 73732
  0.7 6.0 %copy-start.12 = (s32[2,2,1]{1,2,0:T(1,128)S(1)}, s32[2,2,1]{1,2,0:T(1,128)}, u32[]{:S(2)}) copy-start(s32[2,2,1]{1,2,0:T(1,128)} %param.18) | copy-start | bytes 52
  0.7 6.0 %copy-start.1 = (bf16[2,2,1,12,128,128]{5,4,3,2,1,0:T(8,128)(2,1)S(1)}, bf16[2,2,1,12,128,128]{5,4,3,2,1,0:T(8,128)(2,1)}, u32[]{:S(2)}) copy-start(bf16[2,2,1,12,128,128]{5,4,3,2,1,0:T(8,128)(2,1)} %edge_ref.1) | copy-start | bytes 4718596
  0.7 5.9 %copy-start.8 = (f32[3,2,2,1,128]{4,3,2,1,0:T(1,128)S(1)}, f32[3,2,2,1,128]{4,3,2,1,0:T(1,128)}, u32[]{:S(2)}) copy-start(f32[3,2,2,1,128]{4,3,2,1,0:T(1,128)} %positions_ref.1) | copy-start | bytes 18436
  0.7 5.9 %copy-start.9 = (f32[3,2,2,1,128]{4,3,2,1,0:T(1,128)S(1)}, f32[3,2,2,1,128]{4,3,2,1,0:T(1,128)}, u32[]{:S(2)}) copy-start(f32[3,2,2,1,128]{4,3,2,1,0:T(1,128)} %velocity_ref.1) | copy-start | bytes 18436
  0.7 5.9 %copy-start.11 = (s32[2,2,1,128]{3,2,1,0:T(1,128)S(1)}, s32[2,2,1,128]{3,2,1,0:T(1,128)}, u32[]{:S(2)}) copy-start(s32[2,2,1,128]{3,2,1,0:T(1,128)} %owners_ref.1) | copy-start | bytes 6148
  0.7 5.9 %copy-start.2 = (bf16[5,128,128]{2,1,0:T(8,128)(2,1)S(1)}, bf16[5,128,128]{2,1,0:T(8,128)(2,1)}, u32[]{:S(2)}) copy-start(bf16[5,128,128]{2,1,0:T(8,128)(2,1)} %edge_w_ref.1) | copy-start | bytes 491524
  0.7 5.9 %copy-start.3 = (bf16[256,128]{1,0:T(8,128)(2,1)S(1)}, bf16[256,128]{1,0:T(8,128)(2,1)}, u32[]{:S(2)}) copy-start(bf16[256,128]{1,0:T(8,128)(2,1)} %node_in_ref.1) | copy-start | bytes 196612
  0.7 5.9 %copy-start.4 = (bf16[2,128,128]{2,1,0:T(8,128)(2,1)S(1)}, bf16[2,128,128]{2,1,0:T(8,128)(2,1)}, u32[]{:S(2)}) copy-start(bf16[2,128,128]{2,1,0:T(8,128)(2,1)} %node_w_ref.1) | copy-start | bytes 196612
  0.7 5.9 %copy-start.5 = (bf16[2,128,128]{2,1,0:T(8,128)(2,1)S(1)}, bf16[2,128,128]{2,1,0:T(8,128)(2,1)}, u32[]{:S(2)}) copy-start(bf16[2,128,128]{2,1,0:T(8,128)(2,1)} %decoder_w_ref.1) | copy-start | bytes 196612
  0.7 5.9 %copy-start.10 = (bf16[12,128]{1,0:T(8,128)(2,1)S(1)}, bf16[12,128]{1,0:T(8,128)(2,1)}, u32[]{:S(2)}) copy-start(bf16[12,128]{1,0:T(8,128)(2,1)} %encoder_in_ref.1) | copy-start | bytes 9220
  0.8 3.1 %collective-permute-start = (bf16[2,2,1,128,128]{4,3,2,1,0:T(8,128)(2,1)}, bf16[2,2,1,128,128]{4,3,2,1,0:T(8,128)(2,1)S(1)}, u32[]{:S(2)}, u32[]{:S(2)}) collective-permute-start(bf16[2,2,1,128,128]{4,3,2,1,0:T(8,128)(2,1)} %latent_ref), channel_id=1, source_target_pairs={{0,1},{1,0},{2,3},{3,2},{4,5},{5,4},{6,7},{7,6},{8,9},{9,8},{10,11... | collective-permute-start | bytes 393224 | tf_op jit(solution)/shard_map/ppermute | solution.py:613
  1.3 8.8 %collective-permute-start.3 = (bf16[2,2,1,128,128]{4,3,2,1,0:T(8,128)(2,1)}, bf16[2,2,1,128,128]{4,3,2,1,0:T(8,128)(2,1)S(1)}, u32[]{:S(2)}, u32[]{:S(2)}) collective-permute-start(bf16[2,2,1,128,128]{4,3,2,1,0:T(8,128)(2,1)} %latent_ref), channel_id=1, source_target_pairs={{0,2},{2,0},{1,3},{3,1},{4,6},{6,4},{5,7},{7,5},{8,10},{10,8},{9,1... | collective-permute-start | bytes 393224 | tf_op jit(solution)/shard_map/ppermute | solution.py:613
  4.0 6.2 %collective-permute-start.1 = (bf16[2,2,128,128]{3,2,1,0:T(8,128)(2,1)S(1)}, bf16[2,2,128,128]{3,2,1,0:T(8,128)(2,1)S(1)}, u32[]{:S(2)}, u32[]{:S(2)}) collective-permute-start(bf16[2,2,128,128]{3,2,1,0:T(8,128)(2,1)S(1)} %pad_maximum_fusion.1), channel_id=1, source_target_pairs={{0,5},{1,17},{2,7},{3,19},{4,9},{5,0},{6,11},{7,2},{8,13},{9,4},{1... | collective-permute-start | bytes 393224 | tf_op jit(solution)/shard_map/ppermute | solution.py:640
  5.4 4.7 %collective-permute-start.2 = (bf16[2,1,128,128]{3,2,1,0:T(8,128)(2,1)S(1)}, bf16[2,1,128,128]{3,2,1,0:T(8,128)(2,1)S(1)}, u32[]{:S(2)}, u32[]{:S(2)}) collective-permute-start(bf16[2,1,128,128]{3,2,1,0:T(8,128)(2,1)S(1)} %fusion), channel_id=1, source_target_pairs={{0,7},{1,17},{2,5},{3,19},{4,11},{5,2},{6,9},{7,0},{8,15},{9,6},{1... | collective-permute-start | bytes 196616 | tf_op jit(solution)/shard_map/ppermute | solution.py:640
  10.2 1.6 %copy-start.13 = (bf16[3,128]{1,0:T(4,128)(2,1)S(1)}, bf16[3,128]{1,0:T(4,128)(2,1)}, u32[]{:S(2)}) copy-start(bf16[3,128]{1,0:T(4,128)(2,1)} %decoder_out_ref.1) | copy-start | bytes 2308
  10.3 1.6 %collective-permute-start.4 = (bf16[8,128,128]{2,1,0:T(8,128)(2,1)S(1)}, bf16[8,128,128]{2,1,0:T(8,128)(2,1)S(1)}, u32[]{:S(2)}, u32[]{:S(2)}) collective-permute-start(bf16[8,128,128]{2,1,0:T(8,128)(2,1)S(1)} %pad_maximum_fusion), channel_id=1, source_target_pairs={{0,1},{1,0},{2,3},{3,2},{4,5},{5,4},{6,7},{7,6},{8,9},{9,8},{10,11... | collective-permute-start | bytes 786440 | tf_op jit(solution)/shard_map/ppermute | solution.py:613
  14.1 1.5 %collective-permute-start.6 = (f32[16,128]{1,0:T(8,128)S(1)}, f32[16,128]{1,0:T(8,128)S(1)}, u32[]{:S(2)}, u32[]{:S(2)}) collective-permute-start(f32[16,128]{1,0:T(8,128)S(1)} %get-tuple-element.93), channel_id=1, source_target_pairs={{0,1},{1,0},{2,3},{3,2},{4,5},{5,4},{6,7},{7,6},{8,9},{9,8},{10,11... | collective-permute-start | bytes 24584 | tf_op jit(solution)/shard_map/ppermute | solution.py:613
  14.4 6.7 %collective-permute-start.5 = (f32[16,128]{1,0:T(8,128)S(1)}, f32[16,128]{1,0:T(8,128)S(1)}, u32[]{:S(2)}, u32[]{:S(2)}) collective-permute-start(f32[16,128]{1,0:T(8,128)S(1)} %get-tuple-element.93), channel_id=1, source_target_pairs={{0,2},{2,0},{1,3},{3,1},{4,6},{6,4},{5,7},{7,5},{8,10},{10,8},{9,1... | collective-permute-start | bytes 24584 | tf_op jit(solution)/shard_map/ppermute | solution.py:613
  15.6 5.5 %collective-permute-start.7 = (f32[2,16,128]{2,1,0:T(8,128)S(1)}, f32[2,16,128]{2,1,0:T(8,128)S(1)}, u32[]{:S(2)}, u32[]{:S(2)}) collective-permute-start(f32[2,16,128]{2,1,0:T(8,128)S(1)} %pad_maximum_fusion.3), channel_id=1, source_target_pairs={{0,7},{1,17},{2,5},{3,19},{4,11},{5,2},{6,9},{7,0},{8,15},{9,6},{1... | collective-permute-start | bytes 49160 | tf_op jit(solution)/shard_map/ppermute | solution.py:640
  17.7 3.4 %collective-permute-start.8 = (f32[2,16,128]{2,1,0:T(8,128)S(1)}, f32[2,16,128]{2,1,0:T(8,128)S(1)}, u32[]{:S(2)}, u32[]{:S(2)}) collective-permute-start(f32[2,16,128]{2,1,0:T(8,128)S(1)} %pad_maximum_fusion.3), channel_id=1, source_target_pairs={{0,5},{1,17},{2,7},{3,19},{4,9},{5,0},{6,11},{7,2},{8,13},{9,4},{1... | collective-permute-start | bytes 49160 | tf_op jit(solution)/shard_map/ppermute | solution.py:640
  21.1 1.3 %copy-start.6 = (bf16[2,128,128]{2,1,0:T(8,128)(2,1)S(1)}, bf16[2,128,128]{2,1,0:T(8,128)(2,1)}, u32[]{:S(2)}) copy-start(bf16[2,128,128]{2,1,0:T(8,128)(2,1)} %refs_6_.1) | copy-start | bytes 196612
  21.1 1.3 %collective-permute-start.9 = (f32[5,16,128]{2,1,0:T(8,128)S(1)}, f32[5,16,128]{2,1,0:T(8,128)S(1)}, u32[]{:S(2)}, u32[]{:S(2)}) collective-permute-start(f32[5,16,128]{2,1,0:T(8,128)S(1)} %pad_maximum_fusion.2), channel_id=1, source_target_pairs={{0,1},{1,0},{2,3},{3,2},{4,5},{5,4},{6,7},{7,6},{8,9},{9,8},{10,11... | collective-permute-start | bytes 122888 | tf_op jit(solution)/shard_map/ppermute | solution.py:613

commit v21 on v20

--- a/solution.py
+++ b/solution.py
@@ -75,7 +75,7 @@
     return copies
 
 
-def encode(state, mask, inward, encoder_w, extent):
+def encode_first(state, inward, extent):
     width = state.shape[1]
     position = state[0:3]
     row = lax.broadcasted_iota(I32, (3, width), 0)
@@ -89,7 +89,11 @@
         ],
         axis=0,
     )
-    hidden = relu16(dot_tn(thirds(features), inward))
+    return relu16(dot_tn(thirds(features), inward))
+
+
+def encode_rest(hidden, mask, encoder_w):
+    width = hidden.shape[0]
     hidden = relu16(dot(hidden, encoder_w[0]))
     column = jnp.broadcast_to(mask, (8, width)).T[:, 0:1]
     return (norm(dot(hidden, encoder_w[1]), 1) * column).astype(BF16)
@@ -511,13 +515,16 @@
 
 
 def nodes_kernel(
+    sizes,
     total_ref,
     node_pre_ref,
     latent_t_ref,
     state_ref,
     weights_ref,
     decoder_out_ref,
+    inward_ref,
     moved_ref,
+    hidden_ref,
 ):
     aggregate = jnp.concatenate([total_ref[i] for i in range(4)], axis=1)
     acceleration = advance(
@@ -527,9 +534,11 @@
     moved_ref[...] = jnp.concatenate(
         [state, state_ref[6:7], jnp.zeros((ROWS - 10, state.shape[1]), F32)], axis=0
     )
-
-
-def finish_kernel(sizes, moved_ref, zed_ref, *refs):
+    extent = (2.0 * sizes[0], 2.0 * sizes[1], 1.0 * sizes[2])
+    hidden_ref[...] = encode_first(state, inward_ref[...], extent)
+
+
+def finish_kernel(sizes, moved_ref, hidden_ref, zed_ref, *refs):
     count_x, count_y, count_z = sizes
     fold_y = count_y == 2
     options_y = 2 if fold_y else 3
@@ -569,7 +578,7 @@
     slots = kept_latent_ref.shape[-2]
     stays = moved_ref[9:10]
     kept = moved_ref[:9] * stays
-    latents = encode(moved_ref[:9], stays, inward_ref[...], encoder_w_ref[...], extent)
+    latents = encode_rest(hidden_ref[...], stays, encoder_w_ref[...])
     for i, (a, b) in enumerate(CELLS):
         kept_latent_ref[a, b, 0] = latents[i * slots : (i + 1) * slots]
         for j in range(9):
@@ -604,9 +613,8 @@
     arrived = jnp.concatenate(halves, axis=1)[:, : 26 * CAP]
     for j in range(9):
         arrived_state_ref[j, 0, 0] = arrived[j : j + 1]
-    arrived_latent_ref[0, 0, 0] = encode(
-        arrived[:9], arrived[9:10], inward_ref[...], encoder_w_ref[...], extent
-    )
+    hidden = encode_first(arrived[:9], inward_ref[...], extent)
+    arrived_latent_ref[0, 0, 0] = encode_rest(hidden, arrived[9:10], encoder_w_ref[...])
 
 
 def swap(values, axis):
@@ -845,20 +853,20 @@
         packed = swap(jnp.concatenate([*ends, sides[0][None]], axis=0), "gz")
     else:
         packed = swap(ends[0], "gz")
-    state = call(
-        nodes_kernel,
+    state, hidden = call(
+        functools.partial(nodes_kernel, sizes),
         "nodes",
-        [VMEM] * 6,
-        [((ROWS, particles), F32)],
+        [VMEM] * 7,
+        [((ROWS, particles), F32), ((particles, width), BF16)],
         [],
-        (total, node_pre, latent_t, state, weights, decoder_out),
+        (total, node_pre, latent_t, state, weights, decoder_out, inward),
         1_000_000_000,
-    )[0]
-    packed, state = lax.optimization_barrier((packed, state))
+    )
+    packed, state, hidden = lax.optimization_barrier((packed, state, hidden))
     return call(
         functools.partial(finish_kernel, sizes),
         "finish",
-        [VMEM] * (len(sides) + len(ends) + 6),
+        [VMEM] * (len(sides) + len(ends) + 7),
         [
             (node_latent.shape, BF16),
             ((9,) + node_latent.shape[:4], F32),
@@ -866,7 +874,7 @@
             ((9, 1, 1, 1, 26 * CAP), F32),
         ],
         [],
-        (state, zed, *sides, *ends, packed, spread, inward, encoder_weights),
+        (state, hidden, zed, *sides, *ends, packed, spread, inward, encoder_weights),
         1_000_000_000,
     )
 

time: 24.1 us -> 24.1 us (level)
  transfers between devices with their start and end apart: 10 -> 10, of which waited for: 2 -> 1; matrix products, arithmetic and copies ran while one was open for 0% -> 0% of each run, Pallas kernels for 38% -> 39%
where the time goes in v21:
time: 24.1 us; the launch traced here: 23.9 us
  Pallas kernels  13 us (54%)
  starting transfers between devices  9.46 us (39%)
  between operations  1.03 us (4%)
    pallas_call x7, Pallas kernels, call(): pl.pallas_call(kernel, out_shape=tuple((jax.ShapeDtypeStruct(shape, kind)...  13 us
    ppermute x4, starting transfers between devices, swap_chips(): return lax.ppermute(values, axes, pairs)  4.73 us
    ppermute x6, starting transfers between devices, swap(): return lax.ppermute(values, axis, [(0, 1), (1, 0)])  4.73 us
  transfers between devices with their start and end apart: 10, of which 1 were waited for; matrix products, arithmetic and copies ran while one was open for 0% of the time, Pallas kernels for 39%

profile of v21, /device:TPU:0, one launch (start us, length us, event | category | flops | bytes accessed | tf_op | source)
XLA Modules:
  0.0 23.9 jit_solution(14728353929795832034)
XLA Ops:
  0.8 0.5 %collective-permute-start = (bf16[2,2,1,128,128]{4,3,2,1,0:T(8,128)(2,1)}, bf16[2,2,1,128,128]{4,3,2,1,0:T(8,128)(2,1)S(1)}, u32[]{:S(2)}, u32[]{:S(2)}) collective-permute-start(bf16[2,2,1,128,128]{4,3,2,1,0:T(8,128)(2,1)} %latent_ref), channel_id=1, source_target_pairs={{0,1},{1,0},{2,3},{3,2},{4,5},{5,4},{6,7},{7,6},{8,9},{9,8},{10,11... | collective-permute-start | bytes 393224 | tf_op jit(solution)/shard_map/ppermute | solution.py:621
  1.3 2.6 %collective-permute-start.3 = (bf16[2,2,1,128,128]{4,3,2,1,0:T(8,128)(2,1)}, bf16[2,2,1,128,128]{4,3,2,1,0:T(8,128)(2,1)S(1)}, u32[]{:S(2)}, u32[]{:S(2)}) collective-permute-start(bf16[2,2,1,128,128]{4,3,2,1,0:T(8,128)(2,1)} %latent_ref), channel_id=1, source_target_pairs={{0,2},{2,0},{1,3},{3,1},{4,6},{6,4},{5,7},{7,5},{8,10},{10,8},{9,1... | collective-permute-start | bytes 393224 | tf_op jit(solution)/shard_map/ppermute | solution.py:621
  3.9 0.0 collective-permute-done.own_zed
  4.0 1.4 %collective-permute-start.1 = (bf16[2,2,128,128]{3,2,1,0:T(8,128)(2,1)S(1)}, bf16[2,2,128,128]{3,2,1,0:T(8,128)(2,1)S(1)}, u32[]{:S(2)}, u32[]{:S(2)}) collective-permute-start(bf16[2,2,128,128]{3,2,1,0:T(8,128)(2,1)S(1)} %pad_maximum_fusion.1), channel_id=1, source_target_pairs={{0,5},{1,17},{2,7},{3,19},{4,9},{5,0},{6,11},{7,2},{8,13},{9,4},{1... | collective-permute-start | bytes 393224 | tf_op jit(solution)/shard_map/ppermute | solution.py:648
  5.4 1.2 %collective-permute-start.2 = (bf16[2,1,128,128]{3,2,1,0:T(8,128)(2,1)S(1)}, bf16[2,1,128,128]{3,2,1,0:T(8,128)(2,1)S(1)}, u32[]{:S(2)}, u32[]{:S(2)}) collective-permute-start(bf16[2,1,128,128]{3,2,1,0:T(8,128)(2,1)S(1)} %fusion), channel_id=1, source_target_pairs={{0,7},{1,17},{2,5},{3,19},{4,11},{5,2},{6,9},{7,0},{8,15},{9,6},{1... | collective-permute-start | bytes 196616 | tf_op jit(solution)/shard_map/ppermute | solution.py:648
  6.7 3.4 %ranks.1 = (bf16[11,128,128]{2,1,0:T(8,128)(2,1)S(1)}, bf16[48,128]{1,0:T(8,128)(2,1)S(1)}, f32[2,2,1,128]{3,2,1,0:T(1,128)S(1)}, f32[128,512]{1,0:T(8,128)S(1)}...) custom-call(bf16[2,2,1,12,128,128]{5,4,3,2,1,0:T(8,128)(2,1)S(1)} %c, ...), custom_call_target="tpu_custom_call" | custom-call | flops 5000000000 | tf_op jit(solution)/shard_map/ranks/pallas_call | solution.py:652
  10.1 0.0 collective-permute-done.2
  10.1 0.0 collective-permute-done.1
  10.2 0.0 copy-start.13
  10.3 0.1 collective-permute-start.4
  10.3 1.3 %prepare.1 = (bf16[3,128,256]{2,1,0:T(8,128)(2,1)S(1)}, f32[128,1536]{1,0:T(8,128)S(1)}, f32[128,1536]{1,0:T(8,128)S(1)}) custom-call(bf16[4,128,256]{2,1,0:T(8,128)(2,1)S(1)} %get-tuple-element.80.far_ref, bf16[2,3,128,128]{3,2,1,0:T(8,128)(2,1)S(1)} %constant_dynamic-update-slice_fusion.mine_ref, ...), custom_call_target="tpu_custom_call" | custom-call | flops 5000000000 | tf_op jit(solution)/shard_map/prepare/pallas_call | solution.py:652
  11.6 0.2 collective-permute-done.4
  11.9 2.2 %movers.1 = (bf16[8,128,256]{2,1,0:T(8,128)(2,1)S(1)}, f32[16,128]{1,0:T(8,128)S(1)}) custom-call(bf16[2,128,128]{2,1,0:T(8,128)(2,1)S(1)} %dynamic-slice_bitcast_fusion.refs_0_, bf16[2,128,128]{2,1,0:T(8,128)(2,1)S(1)} %slice.6.refs_1_, bf16[2,3,128,128]{3,2,1,0:T(8,128)(2,1)S(1)} %bitcast.16, bf16[3,128,256]{2,1,0:T(8,128)(2,1)S(1)} %get-tuple-element.91.refs_3_, ...), custom_call_target="tpu_custom_call" | custom-call | flops 3000000000 | tf_op jit(solution)/shard_map/movers/pallas_call | solution.py:652
  14.1 0.3 %collective-permute-start.6 = (f32[16,128]{1,0:T(8,128)S(1)}, f32[16,128]{1,0:T(8,128)S(1)}, u32[]{:S(2)}, u32[]{:S(2)}) collective-permute-start(f32[16,128]{1,0:T(8,128)S(1)} %get-tuple-element.96), channel_id=1, source_target_pairs={{0,1},{1,0},{2,3},{3,2},{4,5},{5,4},{6,7},{7,6},{8,9},{9,8},{10,11... | collective-permute-start | bytes 24584 | tf_op jit(solution)/shard_map/ppermute | solution.py:621
  14.4 1.2 %collective-permute-start.5 = (f32[16,128]{1,0:T(8,128)S(1)}, f32[16,128]{1,0:T(8,128)S(1)}, u32[]{:S(2)}, u32[]{:S(2)}) collective-permute-start(f32[16,128]{1,0:T(8,128)S(1)} %get-tuple-element.96), channel_id=1, source_target_pairs={{0,2},{2,0},{1,3},{3,1},{4,6},{6,4},{5,7},{7,5},{8,10},{10,8},{9,1... | collective-permute-start | bytes 24584 | tf_op jit(solution)/shard_map/ppermute | solution.py:621
  15.6 0.0 collective-permute-done.6.zed_ref
  15.6 2.1 %collective-permute-start.7 = (f32[2,16,128]{2,1,0:T(8,128)S(1)}, f32[2,16,128]{2,1,0:T(8,128)S(1)}, u32[]{:S(2)}, u32[]{:S(2)}) collective-permute-start(f32[2,16,128]{2,1,0:T(8,128)S(1)} %pad_maximum_fusion.3), channel_id=1, source_target_pairs={{0,7},{1,17},{2,5},{3,19},{4,11},{5,2},{6,9},{7,0},{8,15},{9,6},{1... | collective-permute-start | bytes 49160 | tf_op jit(solution)/shard_map/ppermute | solution.py:648
  17.7 0.0 collective-permute-start.8
  17.7 3.4 %edges.1.total_ref = bf16[4,128,128]{2,1,0:T(8,128)(2,1)S(1)} custom-call(f32[2,2,1,128]{3,2,1,0:T(1,128)S(1)} %get-tuple-element.99.alive_ref, s32[2,2,12,1,128]{4,3,2,1,0:T(1,128)S(1)} %bitcast.22, bf16[8,128,256]{2,1,0:T(8,128)(2,1)S(1)} %get-tuple-element.100.far_ref, f32[4,128,1536]{2,1,0:T(8,128)S(1)} %get-tuple-element.86.edge_pre_ref.pre_ref, ...), custom_call_target="tpu_custom_call" | custom-call | flops 8000000000 | tf_op jit(solution)/shard_map/edges/pallas_call | solution.py:652
  21.1 0.0 copy-start.6
  21.1 0.0 collective-permute-done.5.refs_0_
  21.2 0.1 collective-permute-start.9
  21.2 1.2 %nodes.1 = (f32[16,512]{1,0:T(8,128)S(1)}, bf16[512,128]{1,0:T(8,128)(2,1)S(1)}) custom-call(bf16[4,128,128]{2,1,0:T(8,128)(2,1)S(1)} %edges.1.total_ref, f32[128,512]{1,0:T(8,128)S(1)} %get-tuple-element.106.node_pre_ref, f32[128,512]{1,0:T(8,128)S(1)} %get-tuple-element.107.latent_t_ref, f32[8,512]{1,0:T(8,128)S(1)} %get-tuple-element.108.state_ref, ...), custom_call_target="tpu_custom_call" | custom-call | flops 1000000000 | tf_op jit(solution)/shard_map/nodes/pallas_call | solution.py:652
  22.5 1.4 %finish.1 = (bf16[2,2,1,128,128]{4,3,2,1,0:T(8,128)(2,1)}, f32[9,2,2,1,128]{4,3,2,1,0:T(1,128)}, bf16[1,1,1,208,128]{4,3,2,1,0:T(8,128)(2,1)}, f32[9,1,1,1,208]{4,3,2,1,0:T(1,128)}) custom-call(f32[16,512]{1,0:T(8,128)S(1)} %get-tuple-element.112.moved_ref, bf16[512,128]{1,0:T(8,128)(2,1)S(1)} %get-tuple-element.113.hidden_ref, ...), custom_call_target="tpu_custom_call" | custom-call | flops 1000000000 | tf_op jit(solution)/shard_map/finish/pallas_call | solution.py:652
  (43 shorter events, 0.2 us)
Async XLA Ops:
  0.6 3.2 %copy-start = (bf16[2,2,1,128,128]{4,3,2,1,0:T(8,128)(2,1)S(1)}, bf16[2,2,1,128,128]{4,3,2,1,0:T(8,128)(2,1)}, u32[]{:S(2)}) copy-start(bf16[2,2,1,128,128]{4,3,2,1,0:T(8,128)(2,1)} %latent_ref) | copy-start | bytes 393220
  0.6 6.0 %copy-start.7 = (s32[2,2,1,12,128]{4,2,3,1,0:T(1,128)S(1)}, s32[2,2,1,12,128]{4,2,3,1,0:T(1,128)}, u32[]{:S(2)}) copy-start(s32[2,2,1,12,128]{4,2,3,1,0:T(1,128)} %param.19) | copy-start | bytes 73732
  0.7 6.0 %copy-start.12 = (s32[2,2,1]{1,2,0:T(1,128)S(1)}, s32[2,2,1]{1,2,0:T(1,128)}, u32[]{:S(2)}) copy-start(s32[2,2,1]{1,2,0:T(1,128)} %param.18) | copy-start | bytes 52
  0.7 6.0 %copy-start.1 = (bf16[2,2,1,12,128,128]{5,4,3,2,1,0:T(8,128)(2,1)S(1)}, bf16[2,2,1,12,128,128]{5,4,3,2,1,0:T(8,128)(2,1)}, u32[]{:S(2)}) copy-start(bf16[2,2,1,12,128,128]{5,4,3,2,1,0:T(8,128)(2,1)} %edge_ref.1) | copy-start | bytes 4718596
  0.7 5.9 %copy-start.8 = (f32[3,2,2,1,128]{4,3,2,1,0:T(1,128)S(1)}, f32[3,2,2,1,128]{4,3,2,1,0:T(1,128)}, u32[]{:S(2)}) copy-start(f32[3,2,2,1,128]{4,3,2,1,0:T(1,128)} %positions_ref.1) | copy-start | bytes 18436
  0.7 5.9 %copy-start.9 = (f32[3,2,2,1,128]{4,3,2,1,0:T(1,128)S(1)}, f32[3,2,2,1,128]{4,3,2,1,0:T(1,128)}, u32[]{:S(2)}) copy-start(f32[3,2,2,1,128]{4,3,2,1,0:T(1,128)} %velocity_ref.1) | copy-start | bytes 18436
  0.7 5.9 %copy-start.11 = (s32[2,2,1,128]{3,2,1,0:T(1,128)S(1)}, s32[2,2,1,128]{3,2,1,0:T(1,128)}, u32[]{:S(2)}) copy-start(s32[2,2,1,128]{3,2,1,0:T(1,128)} %owners_ref.1) | copy-start | bytes 6148
  0.7 5.9 %copy-start.2 = (bf16[5,128,128]{2,1,0:T(8,128)(2,1)S(1)}, bf16[5,128,128]{2,1,0:T(8,128)(2,1)}, u32[]{:S(2)}) copy-start(bf16[5,128,128]{2,1,0:T(8,128)(2,1)} %edge_w_ref.1) | copy-start | bytes 491524
  0.7 5.9 %copy-start.3 = (bf16[256,128]{1,0:T(8,128)(2,1)S(1)}, bf16[256,128]{1,0:T(8,128)(2,1)}, u32[]{:S(2)}) copy-start(bf16[256,128]{1,0:T(8,128)(2,1)} %node_in_ref.1) | copy-start | bytes 196612
  0.7 5.9 %copy-start.4 = (bf16[2,128,128]{2,1,0:T(8,128)(2,1)S(1)}, bf16[2,128,128]{2,1,0:T(8,128)(2,1)}, u32[]{:S(2)}) copy-start(bf16[2,128,128]{2,1,0:T(8,128)(2,1)} %node_w_ref.1) | copy-start | bytes 196612
  0.7 5.9 %copy-start.5 = (bf16[2,128,128]{2,1,0:T(8,128)(2,1)S(1)}, bf16[2,128,128]{2,1,0:T(8,128)(2,1)}, u32[]{:S(2)}) copy-start(bf16[2,128,128]{2,1,0:T(8,128)(2,1)} %decoder_w_ref.1) | copy-start | bytes 196612
  0.7 5.9 %copy-start.10 = (bf16[12,128]{1,0:T(8,128)(2,1)S(1)}, bf16[12,128]{1,0:T(8,128)(2,1)}, u32[]{:S(2)}) copy-start(bf16[12,128]{1,0:T(8,128)(2,1)} %encoder_in_ref.1) | copy-start | bytes 9220
  0.8 3.1 %collective-permute-start = (bf16[2,2,1,128,128]{4,3,2,1,0:T(8,128)(2,1)}, bf16[2,2,1,128,128]{4,3,2,1,0:T(8,128)(2,1)S(1)}, u32[]{:S(2)}, u32[]{:S(2)}) collective-permute-start(bf16[2,2,1,128,128]{4,3,2,1,0:T(8,128)(2,1)} %latent_ref), channel_id=1, source_target_pairs={{0,1},{1,0},{2,3},{3,2},{4,5},{5,4},{6,7},{7,6},{8,9},{9,8},{10,11... | collective-permute-start | bytes 393224 | tf_op jit(solution)/shard_map/ppermute | solution.py:621
  1.3 8.8 %collective-permute-start.3 = (bf16[2,2,1,128,128]{4,3,2,1,0:T(8,128)(2,1)}, bf16[2,2,1,128,128]{4,3,2,1,0:T(8,128)(2,1)S(1)}, u32[]{:S(2)}, u32[]{:S(2)}) collective-permute-start(bf16[2,2,1,128,128]{4,3,2,1,0:T(8,128)(2,1)} %latent_ref), channel_id=1, source_target_pairs={{0,2},{2,0},{1,3},{3,1},{4,6},{6,4},{5,7},{7,5},{8,10},{10,8},{9,1... | collective-permute-start | bytes 393224 | tf_op jit(solution)/shard_map/ppermute | solution.py:621
  4.0 6.2 %collective-permute-start.1 = (bf16[2,2,128,128]{3,2,1,0:T(8,128)(2,1)S(1)}, bf16[2,2,128,128]{3,2,1,0:T(8,128)(2,1)S(1)}, u32[]{:S(2)}, u32[]{:S(2)}) collective-permute-start(bf16[2,2,128,128]{3,2,1,0:T(8,128)(2,1)S(1)} %pad_maximum_fusion.1), channel_id=1, source_target_pairs={{0,5},{1,17},{2,7},{3,19},{4,9},{5,0},{6,11},{7,2},{8,13},{9,4},{1... | collective-permute-start | bytes 393224 | tf_op jit(solution)/shard_map/ppermute | solution.py:648
  5.4 4.7 %collective-permute-start.2 = (bf16[2,1,128,128]{3,2,1,0:T(8,128)(2,1)S(1)}, bf16[2,1,128,128]{3,2,1,0:T(8,128)(2,1)S(1)}, u32[]{:S(2)}, u32[]{:S(2)}) collective-permute-start(bf16[2,1,128,128]{3,2,1,0:T(8,128)(2,1)S(1)} %fusion), channel_id=1, source_target_pairs={{0,7},{1,17},{2,5},{3,19},{4,11},{5,2},{6,9},{7,0},{8,15},{9,6},{1... | collective-permute-start | bytes 196616 | tf_op jit(solution)/shard_map/ppermute | solution.py:648
  10.2 1.6 %copy-start.13 = (bf16[3,128]{1,0:T(4,128)(2,1)S(1)}, bf16[3,128]{1,0:T(4,128)(2,1)}, u32[]{:S(2)}) copy-start(bf16[3,128]{1,0:T(4,128)(2,1)} %decoder_out_ref.1) | copy-start | bytes 2308
  10.3 1.6 %collective-permute-start.4 = (bf16[8,128,128]{2,1,0:T(8,128)(2,1)S(1)}, bf16[8,128,128]{2,1,0:T(8,128)(2,1)S(1)}, u32[]{:S(2)}, u32[]{:S(2)}) collective-permute-start(bf16[8,128,128]{2,1,0:T(8,128)(2,1)S(1)} %pad_maximum_fusion), channel_id=1, source_target_pairs={{0,1},{1,0},{2,3},{3,2},{4,5},{5,4},{6,7},{7,6},{8,9},{9,8},{10,11... | collective-permute-start | bytes 786440 | tf_op jit(solution)/shard_map/ppermute | solution.py:621
  14.1 1.5 %collective-permute-start.6 = (f32[16,128]{1,0:T(8,128)S(1)}, f32[16,128]{1,0:T(8,128)S(1)}, u32[]{:S(2)}, u32[]{:S(2)}) collective-permute-start(f32[16,128]{1,0:T(8,128)S(1)} %get-tuple-element.96), channel_id=1, source_target_pairs={{0,1},{1,0},{2,3},{3,2},{4,5},{5,4},{6,7},{7,6},{8,9},{9,8},{10,11... | collective-permute-start | bytes 24584 | tf_op jit(solution)/shard_map/ppermute | solution.py:621
  14.4 6.7 %collective-permute-start.5 = (f32[16,128]{1,0:T(8,128)S(1)}, f32[16,128]{1,0:T(8,128)S(1)}, u32[]{:S(2)}, u32[]{:S(2)}) collective-permute-start(f32[16,128]{1,0:T(8,128)S(1)} %get-tuple-element.96), channel_id=1, source_target_pairs={{0,2},{2,0},{1,3},{3,1},{4,6},{6,4},{5,7},{7,5},{8,10},{10,8},{9,1... | collective-permute-start | bytes 24584 | tf_op jit(solution)/shard_map/ppermute | solution.py:621
  15.6 5.5 %collective-permute-start.7 = (f32[2,16,128]{2,1,0:T(8,128)S(1)}, f32[2,16,128]{2,1,0:T(8,128)S(1)}, u32[]{:S(2)}, u32[]{:S(2)}) collective-permute-start(f32[2,16,128]{2,1,0:T(8,128)S(1)} %pad_maximum_fusion.3), channel_id=1, source_target_pairs={{0,7},{1,17},{2,5},{3,19},{4,11},{5,2},{6,9},{7,0},{8,15},{9,6},{1... | collective-permute-start | bytes 49160 | tf_op jit(solution)/shard_map/ppermute | solution.py:648
  17.7 3.4 %collective-permute-start.8 = (f32[2,16,128]{2,1,0:T(8,128)S(1)}, f32[2,16,128]{2,1,0:T(8,128)S(1)}, u32[]{:S(2)}, u32[]{:S(2)}) collective-permute-start(f32[2,16,128]{2,1,0:T(8,128)S(1)} %pad_maximum_fusion.3), channel_id=1, source_target_pairs={{0,5},{1,17},{2,7},{3,19},{4,9},{5,0},{6,11},{7,2},{8,13},{9,4},{1... | collective-permute-start | bytes 49160 | tf_op jit(solution)/shard_map/ppermute | solution.py:648
  21.1 1.4 %copy-start.6 = (bf16[2,128,128]{2,1,0:T(8,128)(2,1)S(1)}, bf16[2,128,128]{2,1,0:T(8,128)(2,1)}, u32[]{:S(2)}) copy-start(bf16[2,128,128]{2,1,0:T(8,128)(2,1)} %refs_6_.1) | copy-start | bytes 196612
  21.2 1.3 %collective-permute-start.9 = (f32[5,16,128]{2,1,0:T(8,128)S(1)}, f32[5,16,128]{2,1,0:T(8,128)S(1)}, u32[]{:S(2)}, u32[]{:S(2)}) collective-permute-start(f32[5,16,128]{2,1,0:T(8,128)S(1)} %pad_maximum_fusion.2), channel_id=1, source_target_pairs={{0,1},{1,0},{2,3},{3,2},{4,5},{5,4},{6,7},{7,6},{8,9},{9,8},{10,11... | collective-permute-start | bytes 122888 | tf_op jit(solution)/shard_map/ppermute | solution.py:621

commit v22 on v20

--- a/solution.py
+++ b/solution.py
@@ -413,7 +413,7 @@
     fold_y = sizes[1] == 2
     side_refs, refs = refs[:side_count], refs[side_count:]
     side_zeds, refs = refs[:side_count], refs[side_count:]
-    other_ref, far_mine_ref, refs = refs[0], refs[1], refs[2:]
+    other_ref, refs = refs[0], refs[1:]
     (
         weights_ref,
         decoder_out_ref,
@@ -443,8 +443,6 @@
             far(window.side(ex, row), side_refs[side][ex - 1], side_zeds[side][ex - 1])
 
     movers = state_ref.shape[1]
-    for row in range(row_count):
-        far_ref[(1 - core) * row_count + row] = far_mine_ref[row]
     cells = [(12 * core + row, far_ref.at[core * row_count + row]) for row in range(row_count)]
     cells += window.cells([(ex, row) for ex in (1, 2) for row in window.outer_rows])
     message = messages(
@@ -470,6 +468,7 @@
     alive_ref,
     neighbours_ref,
     far_ref,
+    far_mine_ref,
     pre_ref,
     border_ref,
     weights_ref,
@@ -489,7 +488,9 @@
         cells = window.cells([(ex, row) for ex in (1, 2) for row in rows if row in window.outer_rows])
         picked = other == 0 and bt == 0
         if not picked:
-            cells += [(12 * a + row, far_ref.at[a * window.row_count + row]) for row in rows]
+            for row in rows:
+                end = far_ref.at[a * window.row_count + row] if other else far_mine_ref.at[row]
+                cells.append((12 * a + row, end))
         ids = jnp.concatenate([neighbours_ref[a, b, k] for k in range(neighbour_count)], axis=1)
         place, key = places(ids & 127, ids >> 7, fold_y)
 
@@ -799,7 +800,7 @@
     if fold_y:
         side_zeds = [packed[cells:]]
     far_mine, mover_pre, border = prepared
-    halo = [*sides, *side_zeds, packed[:cells].reshape(mine.shape), far_mine]
+    halo = [*sides, *side_zeds, packed[:cells].reshape(mine.shape)]
 
     far_rest, bucket = call(
         functools.partial(movers_kernel, sizes, len(sides)),
@@ -834,10 +835,10 @@
     total = call(
         functools.partial(edges_kernel, sizes),
         "edges",
-        [VMEM] * 6,
+        [VMEM] * 7,
         [((4, width, slots), BF16)],
         [pltpu.VMEM((4, width, neighbour_count * slots), BF16)],
-        (alive, neighbours, far_rest, edge_pre, border, weights),
+        (alive, neighbours, far_rest, far_mine, edge_pre, border, weights),
         8_000_000_000,
     )[0]
     sides, ends, total = lax.optimization_barrier((sides, ends, total))

time: 24.1 us -> 24.1 us (level)
  no operation moved by 1% of the time
where the time goes in v22:
time: 24.1 us; the launch traced here: 23.9 us
  Pallas kernels  12.8 us (53%)
  starting transfers between devices  9.47 us (39%)
  between operations  1.02 us (4%)
  waiting for transfers between devices  0.42 us (2%)
    pallas_call x7, Pallas kernels, call(): pl.pallas_call(kernel, out_shape=tuple((jax.ShapeDtypeStruct(shape, kind)...  12.8 us
    ppermute x6, starting transfers between devices, swap(): return lax.ppermute(values, axis, [(0, 1), (1, 0)])  4.73 us
    ppermute x4, starting transfers between devices, swap_chips(): return lax.ppermute(values, axes, pairs)  4.73 us
  transfers between devices with their start and end apart: 10, of which 2 were waited for; matrix products, arithmetic and copies ran while one was open for 0% of the time, Pallas kernels for 38%

profile of v22, /device:TPU:0, one launch (start us, length us, event | category | flops | bytes accessed | tf_op | source)
XLA Modules:
  0.0 23.9 jit_solution(6671040128458354002)
XLA Ops:
  0.8 0.5 %collective-permute-start = (bf16[2,2,1,128,128]{4,3,2,1,0:T(8,128)(2,1)}, bf16[2,2,1,128,128]{4,3,2,1,0:T(8,128)(2,1)S(1)}, u32[]{:S(2)}, u32[]{:S(2)}) collective-permute-start(bf16[2,2,1,128,128]{4,3,2,1,0:T(8,128)(2,1)} %latent_ref), channel_id=1, source_target_pairs={{0,1},{1,0},{2,3},{3,2},{4,5},{5,4},{6,7},{7,6},{8,9},{9,8},{10,11... | collective-permute-start | bytes 393224 | tf_op jit(solution)/shard_map/ppermute | solution.py:614
  1.3 2.6 %collective-permute-start.3 = (bf16[2,2,1,128,128]{4,3,2,1,0:T(8,128)(2,1)}, bf16[2,2,1,128,128]{4,3,2,1,0:T(8,128)(2,1)S(1)}, u32[]{:S(2)}, u32[]{:S(2)}) collective-permute-start(bf16[2,2,1,128,128]{4,3,2,1,0:T(8,128)(2,1)} %latent_ref), channel_id=1, source_target_pairs={{0,2},{2,0},{1,3},{3,1},{4,6},{6,4},{5,7},{7,5},{8,10},{10,8},{9,1... | collective-permute-start | bytes 393224 | tf_op jit(solution)/shard_map/ppermute | solution.py:614
  3.9 0.0 collective-permute-done.own_zed
  4.0 1.4 %collective-permute-start.1 = (bf16[2,2,128,128]{3,2,1,0:T(8,128)(2,1)S(1)}, bf16[2,2,128,128]{3,2,1,0:T(8,128)(2,1)S(1)}, u32[]{:S(2)}, u32[]{:S(2)}) collective-permute-start(bf16[2,2,128,128]{3,2,1,0:T(8,128)(2,1)S(1)} %pad_maximum_fusion.1), channel_id=1, source_target_pairs={{0,5},{1,17},{2,7},{3,19},{4,9},{5,0},{6,11},{7,2},{8,13},{9,4},{1... | collective-permute-start | bytes 393224 | tf_op jit(solution)/shard_map/ppermute | solution.py:641
  5.4 1.2 %collective-permute-start.2 = (bf16[2,1,128,128]{3,2,1,0:T(8,128)(2,1)S(1)}, bf16[2,1,128,128]{3,2,1,0:T(8,128)(2,1)S(1)}, u32[]{:S(2)}, u32[]{:S(2)}) collective-permute-start(bf16[2,1,128,128]{3,2,1,0:T(8,128)(2,1)S(1)} %fusion), channel_id=1, source_target_pairs={{0,7},{1,17},{2,5},{3,19},{4,11},{5,2},{6,9},{7,0},{8,15},{9,6},{1... | collective-permute-start | bytes 196616 | tf_op jit(solution)/shard_map/ppermute | solution.py:641
  6.7 3.4 %ranks.1 = (bf16[11,128,128]{2,1,0:T(8,128)(2,1)S(1)}, bf16[48,128]{1,0:T(8,128)(2,1)S(1)}, f32[2,2,1,128]{3,2,1,0:T(1,128)S(1)}, f32[128,512]{1,0:T(8,128)S(1)}...) custom-call(bf16[2,2,1,12,128,128]{5,4,3,2,1,0:T(8,128)(2,1)S(1)} %c, ...), custom_call_target="tpu_custom_call" | custom-call | flops 5000000000 | tf_op jit(solution)/shard_map/ranks/pallas_call | solution.py:645
  10.1 0.0 collective-permute-done.2
  10.1 0.0 collective-permute-done.1
  10.2 0.0 copy-start.13
  10.3 0.1 collective-permute-start.4
  10.3 1.3 %prepare.1 = (bf16[3,128,256]{2,1,0:T(8,128)(2,1)S(1)}, f32[128,1536]{1,0:T(8,128)S(1)}, f32[128,1536]{1,0:T(8,128)S(1)}) custom-call(bf16[4,128,256]{2,1,0:T(8,128)(2,1)S(1)} %get-tuple-element.77.far_ref, bf16[2,3,128,128]{3,2,1,0:T(8,128)(2,1)S(1)} %constant_dynamic-update-slice_fusion.mine_ref, ...), custom_call_target="tpu_custom_call" | custom-call | flops 5000000000 | tf_op jit(solution)/shard_map/prepare/pallas_call | solution.py:645
  11.6 0.2 collective-permute-done.4
  11.9 2.1 %movers.1 = (bf16[8,128,256]{2,1,0:T(8,128)(2,1)S(1)}, f32[16,128]{1,0:T(8,128)S(1)}) custom-call(bf16[2,128,128]{2,1,0:T(8,128)(2,1)S(1)} %dynamic-slice_bitcast_fusion.refs_0_, bf16[2,128,128]{2,1,0:T(8,128)(2,1)S(1)} %slice.6.refs_1_, bf16[2,3,128,128]{3,2,1,0:T(8,128)(2,1)S(1)} %bitcast.16, ...), custom_call_target="tpu_custom_call" | custom-call | flops 3000000000 | tf_op jit(solution)/shard_map/movers/pallas_call | solution.py:645
  14.0 0.3 %collective-permute-start.6 = (f32[16,128]{1,0:T(8,128)S(1)}, f32[16,128]{1,0:T(8,128)S(1)}, u32[]{:S(2)}, u32[]{:S(2)}) collective-permute-start(f32[16,128]{1,0:T(8,128)S(1)} %get-tuple-element.92), channel_id=1, source_target_pairs={{0,1},{1,0},{2,3},{3,2},{4,5},{5,4},{6,7},{7,6},{8,9},{9,8},{10,11... | collective-permute-start | bytes 24584 | tf_op jit(solution)/shard_map/ppermute | solution.py:614
  14.4 1.2 %collective-permute-start.5 = (f32[16,128]{1,0:T(8,128)S(1)}, f32[16,128]{1,0:T(8,128)S(1)}, u32[]{:S(2)}, u32[]{:S(2)}) collective-permute-start(f32[16,128]{1,0:T(8,128)S(1)} %get-tuple-element.92), channel_id=1, source_target_pairs={{0,2},{2,0},{1,3},{3,1},{4,6},{6,4},{5,7},{7,5},{8,10},{10,8},{9,1... | collective-permute-start | bytes 24584 | tf_op jit(solution)/shard_map/ppermute | solution.py:614
  15.6 0.0 collective-permute-done.6.zed_ref
  15.6 2.1 %collective-permute-start.7 = (f32[2,16,128]{2,1,0:T(8,128)S(1)}, f32[2,16,128]{2,1,0:T(8,128)S(1)}, u32[]{:S(2)}, u32[]{:S(2)}) collective-permute-start(f32[2,16,128]{2,1,0:T(8,128)S(1)} %pad_maximum_fusion.3), channel_id=1, source_target_pairs={{0,7},{1,17},{2,5},{3,19},{4,11},{5,2},{6,9},{7,0},{8,15},{9,6},{1... | collective-permute-start | bytes 49160 | tf_op jit(solution)/shard_map/ppermute | solution.py:641
  17.7 3.4 %edges.1.total_ref = bf16[4,128,128]{2,1,0:T(8,128)(2,1)S(1)} custom-call(f32[2,2,1,128]{3,2,1,0:T(1,128)S(1)} %get-tuple-element.95.alive_ref, s32[2,2,12,1,128]{4,3,2,1,0:T(1,128)S(1)} %bitcast.22, bf16[8,128,256]{2,1,0:T(8,128)(2,1)S(1)} %get-tuple-element.96.far_ref, bf16[3,128,256]{2,1,0:T(8,128)(2,1)S(1)} %get-tuple-element.97.far_mine_ref, ...), custom_call_target="tpu_custom_call" | custom-call | flops 8000000000 | tf_op jit(solution)/shard_map/edges/pallas_call | solution.py:645
  21.1 0.0 copy-start.6
  21.1 0.0 collective-permute-done.8.refs_2_
  21.1 0.1 collective-permute-start.9
  21.2 1.0 %nodes.1.moved_ref = f32[16,512]{1,0:T(8,128)S(1)} custom-call(bf16[4,128,128]{2,1,0:T(8,128)(2,1)S(1)} %edges.1.total_ref, f32[128,512]{1,0:T(8,128)S(1)} %get-tuple-element.103.node_pre_ref, f32[128,512]{1,0:T(8,128)S(1)} %get-tuple-element.104.latent_t_ref, f32[8,512]{1,0:T(8,128)S(1)} %get-tuple-element.105.state_ref, ...), custom_call_target="tpu_custom_call" | custom-call | flops 1000000000 | tf_op jit(solution)/shard_map/nodes/pallas_call | solution.py:645
  22.2 0.2 collective-permute-done.9.refs_3_
  22.4 1.5 %finish.1 = (bf16[2,2,1,128,128]{4,3,2,1,0:T(8,128)(2,1)}, f32[9,2,2,1,128]{4,3,2,1,0:T(1,128)}, bf16[1,1,1,208,128]{4,3,2,1,0:T(8,128)(2,1)}, f32[9,1,1,1,208]{4,3,2,1,0:T(1,128)}) custom-call(f32[16,512]{1,0:T(8,128)S(1)} %nodes.1.moved_ref, f32[16,128]{1,0:T(8,128)S(1)} %collective-permute-done.6.zed_ref, f32[16,128]{1,0:T(8,128)S(1)} %collective-permute-done.5.refs_0_, ...), custom_call_target="tpu_custom_call" | custom-call | flops 1000000000 | tf_op jit(solution)/shard_map/finish/pallas_call | solution.py:645
  (43 shorter events, 0.2 us)
Async XLA Ops:
  0.6 3.2 %copy-start = (bf16[2,2,1,128,128]{4,3,2,1,0:T(8,128)(2,1)S(1)}, bf16[2,2,1,128,128]{4,3,2,1,0:T(8,128)(2,1)}, u32[]{:S(2)}) copy-start(bf16[2,2,1,128,128]{4,3,2,1,0:T(8,128)(2,1)} %latent_ref) | copy-start | bytes 393220
  0.6 6.0 %copy-start.7 = (s32[2,2,1,12,128]{4,2,3,1,0:T(1,128)S(1)}, s32[2,2,1,12,128]{4,2,3,1,0:T(1,128)}, u32[]{:S(2)}) copy-start(s32[2,2,1,12,128]{4,2,3,1,0:T(1,128)} %param.19) | copy-start | bytes 73732
  0.7 6.0 %copy-start.12 = (s32[2,2,1]{1,2,0:T(1,128)S(1)}, s32[2,2,1]{1,2,0:T(1,128)}, u32[]{:S(2)}) copy-start(s32[2,2,1]{1,2,0:T(1,128)} %param.18) | copy-start | bytes 52
  0.7 6.0 %copy-start.1 = (bf16[2,2,1,12,128,128]{5,4,3,2,1,0:T(8,128)(2,1)S(1)}, bf16[2,2,1,12,128,128]{5,4,3,2,1,0:T(8,128)(2,1)}, u32[]{:S(2)}) copy-start(bf16[2,2,1,12,128,128]{5,4,3,2,1,0:T(8,128)(2,1)} %edge_ref.1) | copy-start | bytes 4718596
  0.7 5.9 %copy-start.8 = (f32[3,2,2,1,128]{4,3,2,1,0:T(1,128)S(1)}, f32[3,2,2,1,128]{4,3,2,1,0:T(1,128)}, u32[]{:S(2)}) copy-start(f32[3,2,2,1,128]{4,3,2,1,0:T(1,128)} %positions_ref.1) | copy-start | bytes 18436
  0.7 5.9 %copy-start.9 = (f32[3,2,2,1,128]{4,3,2,1,0:T(1,128)S(1)}, f32[3,2,2,1,128]{4,3,2,1,0:T(1,128)}, u32[]{:S(2)}) copy-start(f32[3,2,2,1,128]{4,3,2,1,0:T(1,128)} %velocity_ref.1) | copy-start | bytes 18436
  0.7 5.9 %copy-start.11 = (s32[2,2,1,128]{3,2,1,0:T(1,128)S(1)}, s32[2,2,1,128]{3,2,1,0:T(1,128)}, u32[]{:S(2)}) copy-start(s32[2,2,1,128]{3,2,1,0:T(1,128)} %owners_ref.1) | copy-start | bytes 6148
  0.7 5.9 %copy-start.2 = (bf16[5,128,128]{2,1,0:T(8,128)(2,1)S(1)}, bf16[5,128,128]{2,1,0:T(8,128)(2,1)}, u32[]{:S(2)}) copy-start(bf16[5,128,128]{2,1,0:T(8,128)(2,1)} %edge_w_ref.1) | copy-start | bytes 491524
  0.7 5.9 %copy-start.3 = (bf16[256,128]{1,0:T(8,128)(2,1)S(1)}, bf16[256,128]{1,0:T(8,128)(2,1)}, u32[]{:S(2)}) copy-start(bf16[256,128]{1,0:T(8,128)(2,1)} %node_in_ref.1) | copy-start | bytes 196612
  0.7 5.9 %copy-start.4 = (bf16[2,128,128]{2,1,0:T(8,128)(2,1)S(1)}, bf16[2,128,128]{2,1,0:T(8,128)(2,1)}, u32[]{:S(2)}) copy-start(bf16[2,128,128]{2,1,0:T(8,128)(2,1)} %node_w_ref.1) | copy-start | bytes 196612
  0.7 5.9 %copy-start.5 = (bf16[2,128,128]{2,1,0:T(8,128)(2,1)S(1)}, bf16[2,128,128]{2,1,0:T(8,128)(2,1)}, u32[]{:S(2)}) copy-start(bf16[2,128,128]{2,1,0:T(8,128)(2,1)} %decoder_w_ref.1) | copy-start | bytes 196612
  0.7 5.9 %copy-start.10 = (bf16[12,128]{1,0:T(8,128)(2,1)S(1)}, bf16[12,128]{1,0:T(8,128)(2,1)}, u32[]{:S(2)}) copy-start(bf16[12,128]{1,0:T(8,128)(2,1)} %encoder_in_ref.1) | copy-start | bytes 9220
  0.8 3.1 %collective-permute-start = (bf16[2,2,1,128,128]{4,3,2,1,0:T(8,128)(2,1)}, bf16[2,2,1,128,128]{4,3,2,1,0:T(8,128)(2,1)S(1)}, u32[]{:S(2)}, u32[]{:S(2)}) collective-permute-start(bf16[2,2,1,128,128]{4,3,2,1,0:T(8,128)(2,1)} %latent_ref), channel_id=1, source_target_pairs={{0,1},{1,0},{2,3},{3,2},{4,5},{5,4},{6,7},{7,6},{8,9},{9,8},{10,11... | collective-permute-start | bytes 393224 | tf_op jit(solution)/shard_map/ppermute | solution.py:614
  1.3 8.8 %collective-permute-start.3 = (bf16[2,2,1,128,128]{4,3,2,1,0:T(8,128)(2,1)}, bf16[2,2,1,128,128]{4,3,2,1,0:T(8,128)(2,1)S(1)}, u32[]{:S(2)}, u32[]{:S(2)}) collective-permute-start(bf16[2,2,1,128,128]{4,3,2,1,0:T(8,128)(2,1)} %latent_ref), channel_id=1, source_target_pairs={{0,2},{2,0},{1,3},{3,1},{4,6},{6,4},{5,7},{7,5},{8,10},{10,8},{9,1... | collective-permute-start | bytes 393224 | tf_op jit(solution)/shard_map/ppermute | solution.py:614
  4.0 6.2 %collective-permute-start.1 = (bf16[2,2,128,128]{3,2,1,0:T(8,128)(2,1)S(1)}, bf16[2,2,128,128]{3,2,1,0:T(8,128)(2,1)S(1)}, u32[]{:S(2)}, u32[]{:S(2)}) collective-permute-start(bf16[2,2,128,128]{3,2,1,0:T(8,128)(2,1)S(1)} %pad_maximum_fusion.1), channel_id=1, source_target_pairs={{0,5},{1,17},{2,7},{3,19},{4,9},{5,0},{6,11},{7,2},{8,13},{9,4},{1... | collective-permute-start | bytes 393224 | tf_op jit(solution)/shard_map/ppermute | solution.py:641
  5.4 4.7 %collective-permute-start.2 = (bf16[2,1,128,128]{3,2,1,0:T(8,128)(2,1)S(1)}, bf16[2,1,128,128]{3,2,1,0:T(8,128)(2,1)S(1)}, u32[]{:S(2)}, u32[]{:S(2)}) collective-permute-start(bf16[2,1,128,128]{3,2,1,0:T(8,128)(2,1)S(1)} %fusion), channel_id=1, source_target_pairs={{0,7},{1,17},{2,5},{3,19},{4,11},{5,2},{6,9},{7,0},{8,15},{9,6},{1... | collective-permute-start | bytes 196616 | tf_op jit(solution)/shard_map/ppermute | solution.py:641
  10.2 1.6 %copy-start.13 = (bf16[3,128]{1,0:T(4,128)(2,1)S(1)}, bf16[3,128]{1,0:T(4,128)(2,1)}, u32[]{:S(2)}) copy-start(bf16[3,128]{1,0:T(4,128)(2,1)} %decoder_out_ref.1) | copy-start | bytes 2308
  10.3 1.6 %collective-permute-start.4 = (bf16[8,128,128]{2,1,0:T(8,128)(2,1)S(1)}, bf16[8,128,128]{2,1,0:T(8,128)(2,1)S(1)}, u32[]{:S(2)}, u32[]{:S(2)}) collective-permute-start(bf16[8,128,128]{2,1,0:T(8,128)(2,1)S(1)} %pad_maximum_fusion), channel_id=1, source_target_pairs={{0,1},{1,0},{2,3},{3,2},{4,5},{5,4},{6,7},{7,6},{8,9},{9,8},{10,11... | collective-permute-start | bytes 786440 | tf_op jit(solution)/shard_map/ppermute | solution.py:614
  14.0 1.5 %collective-permute-start.6 = (f32[16,128]{1,0:T(8,128)S(1)}, f32[16,128]{1,0:T(8,128)S(1)}, u32[]{:S(2)}, u32[]{:S(2)}) collective-permute-start(f32[16,128]{1,0:T(8,128)S(1)} %get-tuple-element.92), channel_id=1, source_target_pairs={{0,1},{1,0},{2,3},{3,2},{4,5},{5,4},{6,7},{7,6},{8,9},{9,8},{10,11... | collective-permute-start | bytes 24584 | tf_op jit(solution)/shard_map/ppermute | solution.py:614
  14.4 6.7 %collective-permute-start.5 = (f32[16,128]{1,0:T(8,128)S(1)}, f32[16,128]{1,0:T(8,128)S(1)}, u32[]{:S(2)}, u32[]{:S(2)}) collective-permute-start(f32[16,128]{1,0:T(8,128)S(1)} %get-tuple-element.92), channel_id=1, source_target_pairs={{0,2},{2,0},{1,3},{3,1},{4,6},{6,4},{5,7},{7,5},{8,10},{10,8},{9,1... | collective-permute-start | bytes 24584 | tf_op jit(solution)/shard_map/ppermute | solution.py:614
  15.6 5.5 %collective-permute-start.7 = (f32[2,16,128]{2,1,0:T(8,128)S(1)}, f32[2,16,128]{2,1,0:T(8,128)S(1)}, u32[]{:S(2)}, u32[]{:S(2)}) collective-permute-start(f32[2,16,128]{2,1,0:T(8,128)S(1)} %pad_maximum_fusion.3), channel_id=1, source_target_pairs={{0,7},{1,17},{2,5},{3,19},{4,11},{5,2},{6,9},{7,0},{8,15},{9,6},{1... | collective-permute-start | bytes 49160 | tf_op jit(solution)/shard_map/ppermute | solution.py:641
  17.7 3.4 %collective-permute-start.8 = (f32[2,16,128]{2,1,0:T(8,128)S(1)}, f32[2,16,128]{2,1,0:T(8,128)S(1)}, u32[]{:S(2)}, u32[]{:S(2)}) collective-permute-start(f32[2,16,128]{2,1,0:T(8,128)S(1)} %pad_maximum_fusion.3), channel_id=1, source_target_pairs={{0,5},{1,17},{2,7},{3,19},{4,9},{5,0},{6,11},{7,2},{8,13},{9,4},{1... | collective-permute-start | bytes 49160 | tf_op jit(solution)/shard_map/ppermute | solution.py:641
  21.1 1.3 %copy-start.6 = (bf16[2,128,128]{2,1,0:T(8,128)(2,1)S(1)}, bf16[2,128,128]{2,1,0:T(8,128)(2,1)}, u32[]{:S(2)}) copy-start(bf16[2,128,128]{2,1,0:T(8,128)(2,1)} %refs_6_.1) | copy-start | bytes 196612
  21.1 1.3 %collective-permute-start.9 = (f32[5,16,128]{2,1,0:T(8,128)S(1)}, f32[5,16,128]{2,1,0:T(8,128)S(1)}, u32[]{:S(2)}, u32[]{:S(2)}) collective-permute-start(f32[5,16,128]{2,1,0:T(8,128)S(1)} %pad_maximum_fusion.2), channel_id=1, source_target_pairs={{0,1},{1,0},{2,3},{3,2},{4,5},{5,4},{6,7},{7,6},{8,9},{9,8},{10,11... | collective-permute-start | bytes 122888 | tf_op jit(solution)/shard_map/ppermute | solution.py:614
